TPU v7x, 32 devices: a whole 2x2x4 slice. The times are simulated.
32 devices in a mesh: fsdp: 4 (over z), ctx: 8 (over y, x, core).
Axes of the slice: x: 2, y: 2, z: 4, core: 2. Of those that a mesh axis runs over, the one named last changes fastest.
Arguments:
- tokens: bfloat16 [4, 1024, 2048], P('fsdp', 'ctx'), may hold values from -6 to 6
- positions: int32 [4, 1024], P('fsdp', 'ctx'), may hold values from 0 to 1023, as said below
- attn_gain: bfloat16 [2048], P(('fsdp', 'ctx')), may hold values from 0.5 to 1.5
- w_query: bfloat16 [2048, 2048], P(('fsdp', 'ctx')), may hold values from -0.125 to 0.125
- w_key: bfloat16 [2048, 512], P(('fsdp', 'ctx')), may hold values from -0.125 to 0.125
- w_value: bfloat16 [2048, 512], P(('fsdp', 'ctx')), may hold values from -0.125 to 0.125
- w_out: bfloat16 [2048, 2048], P(('fsdp', 'ctx')), may hold values from -2 to 2
- mlp_gain: bfloat16 [2048], P(('fsdp', 'ctx')), may hold values from 0.5 to 1.5
- w_gate: bfloat16 [2048, 8192], P(('fsdp', 'ctx')), may hold values from -0.125 to 0.125
- w_up: bfloat16 [2048, 8192], P(('fsdp', 'ctx')), may hold values from -0.125 to 0.125
- w_down: bfloat16 [8192, 2048], P(('fsdp', 'ctx')), may hold values from -0.125 to 0.125
- cotangent: bfloat16 [4, 1024, 2048], P('fsdp', 'ctx'), may hold values from -6 to 6
Outputs:
- output: bfloat16 [4, 1024, 2048], P('fsdp', 'ctx')
- input_grad: bfloat16 [4, 1024, 2048], P('fsdp', 'ctx')
- attn_gain_grad: float32 [2048], P(('fsdp', 'ctx'))
- query_grad: float32 [2048, 2048], P(('fsdp', 'ctx'))
- key_grad: float32 [2048, 512], P(('fsdp', 'ctx'))
- value_grad: float32 [2048, 512], P(('fsdp', 'ctx'))
- out_grad: float32 [2048, 2048], P(('fsdp', 'ctx'))
- mlp_gain_grad: float32 [2048], P(('fsdp', 'ctx'))
- gate_grad: float32 [2048, 8192], P(('fsdp', 'ctx'))
- up_grad: float32 [2048, 8192], P(('fsdp', 'ctx'))
- down_grad: float32 [8192, 2048], P(('fsdp', 'ctx'))
Inputs may be any that keep to these rules, and one draw needn't show every extreme that they name: In each sequence the positions are a permutation of 0 to 1023 made of runs of 64 consecutive rising positions; the order of the runs is drawn afresh for every sequence.
All inputs are finite; a program needn't handle non-finite values.
Results may differ from a plain program's by a relative error of at most 0.023.
Values may be sent and summed in bfloat16 or wider, within the bound.
No kernel may reach another device: no remote copies, remote signals or barrier semaphores. Data moves between devices by JAX's collectives and lax.ppermute only.
A program may use at most 384 MiB of HBM per device.

v0:
```python
import jax
import jax.numpy as jnp
from jax import lax
from jax.sharding import PartitionSpec as P

HEADS = 32
KV_HEADS = 8
HEAD_DIM = 64


EPSILON = 1e-05
ROPE_BASE = 500000.0


def shifted_2(block, axis, distance):
    devices = range(lax.axis_size(axis))
    route = [((i - distance) % len(devices), i) for i in devices]
    return lax.ppermute(block, axis, route)


def rotate(features, places, direction):
    half_dim = features.shape[-1] // 2
    frequency = jnp.power(
        ROPE_BASE, -2.0 * jnp.arange(half_dim, dtype=jnp.float32) / features.shape[-1]
    )
    angles = places.astype(jnp.float32)[:, None] * frequency[None, :]
    cosine = jnp.cos(angles)[:, None, :]
    sine_part = direction * jnp.sin(angles)[:, None, :]
    first_half = features[..., :half_dim]
    second_half = features[..., half_dim:]
    return jnp.concatenate(
        [
            first_half * cosine - second_half * sine_part,
            second_half * cosine + first_half * sine_part,
        ],
        axis=-1,
    )


def transposed(left_side, right_side):
    return lax.dot_general(
        left_side, right_side, (((1,), (1,)), ((), ())), preferred_element_type=jnp.float32
    )


def inner_rows(left_side, right_side):
    return lax.dot_general(
        left_side, right_side, (((0,), (0,)), ((), ())), preferred_element_type=jnp.float32
    )


def norm_back(grad_hat, hat_rows, inv_rms):
    return inv_rms * (grad_hat - hat_rows * jnp.mean(grad_hat * hat_rows, axis=-1, keepdims=True))


def per_device(
    tokens,
    positions,
    attn_gain,
    w_query,
    w_key,
    w_value,
    w_out,
    mlp_gain,
    w_gate,
    w_up,
    w_down,
    cotangent,
):
    inputs = tokens[0].astype(jnp.float32)
    tok_rows = inputs.shape[0]
    model_width = inputs.shape[1]
    ff_width = w_gate.shape[1]
    own_places = positions[0]
    all_places = lax.all_gather(positions, "ctx", axis=1, tiled=True)[0]
    ctx_count = lax.axis_size("ctx")
    ctx_index = lax.axis_index("ctx")
    fsdp_index = lax.axis_index("fsdp")
    group_size = HEADS // KV_HEADS
    score_scale = HEAD_DIM ** (-0.5)
    kv_width = KV_HEADS * HEAD_DIM
    inv_first = lax.rsqrt(jnp.mean(inputs * inputs, axis=-1, keepdims=True) + EPSILON)
    hat_first = inputs * inv_first
    attn_start = (
        jnp.zeros((tok_rows, model_width), jnp.bfloat16),
        jnp.zeros((tok_rows, w_query.shape[1]), jnp.float32),
        jnp.zeros((tok_rows, kv_width), jnp.float32),
        jnp.zeros((tok_rows, kv_width), jnp.float32),
    )
    attn_start = attn_start + ()
    gain_piece = lax.all_gather(attn_gain, ("fsdp", "ctx"), axis=0, tiled=True)
    query_piece = lax.all_gather(w_query, ("fsdp", "ctx"), axis=0, tiled=True)
    key_piece = lax.all_gather(w_key, ("fsdp", "ctx"), axis=0, tiled=True)
    value_piece = lax.all_gather(w_value, ("fsdp", "ctx"), axis=0, tiled=True)
    normed = (hat_first * gain_piece.astype(jnp.float32)).astype(jnp.bfloat16)
    updated = (
        normed,
        jnp.dot(normed, query_piece, preferred_element_type=jnp.float32),
        jnp.dot(normed, key_piece, preferred_element_type=jnp.float32),
        jnp.dot(normed, value_piece, preferred_element_type=jnp.float32),
    )
    folded = updated
    normed_first = folded[0]
    query_rot = rotate(folded[1].reshape(tok_rows, HEADS, HEAD_DIM), own_places, 1.0).astype(
        jnp.bfloat16
    )
    query_rot = query_rot.reshape(tok_rows, KV_HEADS, group_size, HEAD_DIM)
    key_rot = rotate(folded[2].reshape(tok_rows, KV_HEADS, HEAD_DIM), own_places, 1.0).astype(
        jnp.bfloat16
    )
    key_rot = key_rot.reshape(tok_rows, kv_width)
    value_low = folded[3].astype(jnp.bfloat16)
    key_piece = lax.all_gather(key_rot, "ctx", axis=0, tiled=True)
    value_piece = lax.all_gather(value_low, "ctx", axis=0, tiled=True)
    piece_rows = key_piece.shape[0]
    key_places = all_places
    visible = key_places[None, :] <= own_places[:, None]
    running_max = jnp.full((KV_HEADS, group_size, tok_rows), -1e30, jnp.float32)
    scores = (
        jnp.einsum(
            "tkgd,skd->kgts",
            query_rot,
            key_piece.reshape(piece_rows, KV_HEADS, HEAD_DIM),
            preferred_element_type=jnp.float32,
        )
        * score_scale
    )
    new_max = jnp.maximum(running_max, jnp.max(jnp.where(visible, scores, -1e30), axis=-1))
    weights = jnp.where(visible, jnp.exp(scores - new_max[..., None]), 0.0)
    contrib = jnp.einsum(
        "kgts,skd->kgtd",
        weights.astype(jnp.bfloat16),
        value_piece.reshape(piece_rows, KV_HEADS, HEAD_DIM),
        preferred_element_type=jnp.float32,
    )
    running_sum = jnp.sum(weights, axis=-1)
    log_total = new_max + jnp.log(running_sum)
    attn_heads = contrib / running_sum[..., None]
    mixed_low = (
        attn_heads.transpose(2, 0, 1, 3).reshape(tok_rows, HEADS * HEAD_DIM).astype(jnp.bfloat16)
    )
    block_piece = lax.all_gather(w_out, ("fsdp", "ctx"), axis=0, tiled=True)
    updated = (jnp.dot(mixed_low, block_piece, preferred_element_type=jnp.float32),)
    out_folded = updated
    hidden = inputs + out_folded[0]
    inv_second = lax.rsqrt(jnp.mean(hidden * hidden, axis=-1, keepdims=True) + EPSILON)
    hat_second = hidden * inv_second
    mlp_start = (
        jnp.zeros((tok_rows, model_width), jnp.bfloat16),
        jnp.zeros((tok_rows, ff_width), jnp.float32),
        jnp.zeros((tok_rows, ff_width), jnp.float32),
    )
    mlp_start = mlp_start + ()
    gain_piece = lax.all_gather(mlp_gain, ("fsdp", "ctx"), axis=0, tiled=True)
    gate_piece = lax.all_gather(w_gate, ("fsdp", "ctx"), axis=0, tiled=True)
    up_piece = lax.all_gather(w_up, ("fsdp", "ctx"), axis=0, tiled=True)
    normed = (hat_second * gain_piece.astype(jnp.float32)).astype(jnp.bfloat16)
    updated = (
        normed,
        jnp.dot(normed, gate_piece, preferred_element_type=jnp.float32),
        jnp.dot(normed, up_piece, preferred_element_type=jnp.float32),
    )
    mlp_folded = updated
    normed_second = mlp_folded[0]
    gate_proj = mlp_folded[1]
    up_proj = mlp_folded[2]
    activated = (jax.nn.silu(gate_proj) * up_proj).astype(jnp.bfloat16)
    block_piece = lax.all_gather(w_down, ("fsdp", "ctx"), axis=0, tiled=True)
    updated = (jnp.dot(activated, block_piece, preferred_element_type=jnp.float32),)
    output = (hidden + updated[0]).astype(jnp.bfloat16)[None]
    grad_out = cotangent[0]
    grad_act = transposed(grad_out, lax.all_gather(w_down, ("fsdp", "ctx"), axis=0, tiled=True))
    down_owned = w_down.shape[0] * ctx_count
    act_piece = lax.all_gather(activated, "fsdp", axis=0, tiled=True)
    grad_piece = lax.all_gather(grad_out, "fsdp", axis=0, tiled=True)
    act_cols = lax.dynamic_slice_in_dim(act_piece, fsdp_index * down_owned, down_owned, 1)
    down_partial = inner_rows(act_cols, grad_piece)
    down_grad = lax.psum_scatter(
        down_partial.astype(jnp.bfloat16), "ctx", scatter_dimension=0, tiled=True
    ).astype(jnp.float32)
    sigmoid_gate = jax.nn.sigmoid(gate_proj)
    gate_low = (
        grad_act * up_proj * sigmoid_gate * (1.0 + gate_proj * (1.0 - sigmoid_gate))
    ).astype(jnp.bfloat16)
    up_low = (grad_act * gate_proj * sigmoid_gate).astype(jnp.bfloat16)
    paired_low = jnp.concatenate([gate_low, up_low], axis=1)
    gate_owned = w_gate.shape[0] * ctx_count
    normed_piece = lax.all_gather(normed_second, "fsdp", axis=0, tiled=True)
    paired_piece = lax.all_gather(paired_low, "fsdp", axis=0, tiled=True)
    normed_cols = lax.dynamic_slice_in_dim(normed_piece, fsdp_index * gate_owned, gate_owned, 1)
    gate_up_partial = inner_rows(normed_cols, paired_piece)
    gate_up = lax.psum_scatter(
        gate_up_partial.astype(jnp.bfloat16), "ctx", scatter_dimension=0, tiled=True
    ).astype(jnp.float32)
    gain_piece = lax.all_gather(mlp_gain, ("fsdp", "ctx"), axis=0, tiled=True)
    gate_piece = lax.all_gather(w_gate, ("fsdp", "ctx"), axis=0, tiled=True)
    up_piece = lax.all_gather(w_up, ("fsdp", "ctx"), axis=0, tiled=True)
    grad_normed = transposed(gate_low, gate_piece) + transposed(up_low, up_piece)
    hat_cols = hat_second
    grad_hat_second = grad_normed * gain_piece.astype(jnp.float32)
    mlp_gain_term = jnp.sum(grad_normed * hat_cols, axis=0)
    grad_hidden = grad_out.astype(jnp.float32) + norm_back(grad_hat_second, hat_second, inv_second)
    hidden_low = grad_hidden.astype(jnp.bfloat16)
    out_term = inner_rows(mixed_low, hidden_low)
    grad_mixed = transposed(hidden_low, lax.all_gather(w_out, ("fsdp", "ctx"), axis=0, tiled=True))
    grad_heads = grad_mixed.astype(jnp.bfloat16).reshape(tok_rows, KV_HEADS, group_size, HEAD_DIM)
    row_delta = jnp.einsum("kgtd,tkgd->kgt", attn_heads, grad_heads.astype(jnp.float32))

    def cycle_step(turn_index, carried):
        key_wide, value_wide, key_grad, value_grad, query_grad = carried
        source = (ctx_index - turn_index) % ctx_count
        key_places = lax.dynamic_slice_in_dim(all_places, source * tok_rows, tok_rows)
        visible = key_places[None, :] <= own_places[:, None]
        accumulated = (key_grad, value_grad, query_grad)
        key_acc, value_acc, query_acc = accumulated
        key_block = key_wide.astype(jnp.bfloat16).reshape(tok_rows, KV_HEADS, HEAD_DIM)
        value_block = value_wide.astype(jnp.bfloat16).reshape(tok_rows, KV_HEADS, HEAD_DIM)
        scores = (
            jnp.einsum("tkgd,skd->kgts", query_rot, key_block, preferred_element_type=jnp.float32)
            * score_scale
        )
        probs_block = jnp.where(visible, jnp.exp(scores - log_total[..., None]), 0.0)
        value_acc = value_acc + jnp.einsum(
            "kgts,tkgd->skd",
            probs_block.astype(jnp.bfloat16),
            grad_heads,
            preferred_element_type=jnp.float32,
        ).reshape(tok_rows, kv_width)
        grad_probs = jnp.einsum(
            "tkgd,skd->kgts", grad_heads, value_block, preferred_element_type=jnp.float32
        )
        grad_scores = (probs_block * (grad_probs - row_delta[..., None])).astype(jnp.bfloat16)
        query_acc = (
            query_acc
            + jnp.einsum(
                "kgts,skd->tkgd", grad_scores, key_block, preferred_element_type=jnp.float32
            )
            * score_scale
        )
        key_acc = key_acc + (
            jnp.einsum("kgts,tkgd->skd", grad_scores, query_rot, preferred_element_type=jnp.float32)
            * score_scale
        ).reshape(tok_rows, kv_width)
        accumulated = (key_acc, value_acc, query_acc)
        shifted = (
            shifted_2(key_wide.astype(jnp.bfloat16), "ctx", 1).astype(key_wide.dtype),
            shifted_2(value_wide.astype(jnp.bfloat16), "ctx", 1).astype(value_wide.dtype),
            shifted_2(accumulated[0].astype(jnp.bfloat16), "ctx", 1).astype(jnp.float32),
            shifted_2(accumulated[1].astype(jnp.bfloat16), "ctx", 1).astype(jnp.float32),
        )
        return shifted + (accumulated[2],)

    cycle_start = (
        key_rot.astype(jnp.float32),
        value_low.astype(jnp.float32),
        jnp.zeros((tok_rows, kv_width), jnp.float32),
        jnp.zeros((tok_rows, kv_width), jnp.float32),
        jnp.zeros((tok_rows, KV_HEADS, group_size, HEAD_DIM), jnp.float32),
    )
    cycle_end = lax.fori_loop(0, ctx_count, cycle_step, cycle_start)
    query_grad_low = rotate(
        cycle_end[4].reshape(tok_rows, HEADS, HEAD_DIM), own_places, -1.0
    ).astype(jnp.bfloat16)
    query_grad_low = query_grad_low.reshape(tok_rows, HEADS * HEAD_DIM)
    key_grad_low = rotate(
        cycle_end[2].reshape(tok_rows, KV_HEADS, HEAD_DIM), own_places, -1.0
    ).astype(jnp.bfloat16)
    key_grad_low = key_grad_low.reshape(tok_rows, kv_width)
    value_grad_low = cycle_end[3].astype(jnp.bfloat16)
    query_term = inner_rows(normed_first, query_grad_low)
    key_term = inner_rows(normed_first, key_grad_low)
    value_term = inner_rows(normed_first, value_grad_low)
    gain_piece = lax.all_gather(attn_gain, ("fsdp", "ctx"), axis=0, tiled=True)
    query_piece = lax.all_gather(w_query, ("fsdp", "ctx"), axis=0, tiled=True)
    key_piece = lax.all_gather(w_key, ("fsdp", "ctx"), axis=0, tiled=True)
    value_piece = lax.all_gather(w_value, ("fsdp", "ctx"), axis=0, tiled=True)
    grad_normed = (
        transposed(query_grad_low, query_piece)
        + transposed(key_grad_low, key_piece)
        + transposed(value_grad_low, value_piece)
    )
    hat_cols = hat_first
    grad_hat_first = grad_normed * gain_piece.astype(jnp.float32)
    attn_gain_term = jnp.sum(grad_normed * hat_cols, axis=0)
    grad_input = grad_hidden + norm_back(grad_hat_first, hat_first, inv_first)
    summed_grads = (
        lax.psum_scatter(attn_gain_term, ("fsdp", "ctx"), scatter_dimension=0, tiled=True),
        lax.psum_scatter(mlp_gain_term, ("fsdp", "ctx"), scatter_dimension=0, tiled=True),
        lax.psum_scatter(query_term, ("fsdp", "ctx"), scatter_dimension=0, tiled=True),
        lax.psum_scatter(key_term, ("fsdp", "ctx"), scatter_dimension=0, tiled=True),
        lax.psum_scatter(value_term, ("fsdp", "ctx"), scatter_dimension=0, tiled=True),
        lax.psum_scatter(out_term, ("fsdp", "ctx"), scatter_dimension=0, tiled=True),
    )
    return (
        output,
        grad_input.astype(jnp.bfloat16)[None],
        summed_grads[0],
        summed_grads[2],
        summed_grads[3],
        summed_grads[4],
        summed_grads[5],
        summed_grads[1],
        gate_up[:, :ff_width],
        gate_up[:, ff_width:],
        down_grad,
    )


def solution(mesh):
    in_specs = (
        P("fsdp", "ctx", None),
        P("fsdp", "ctx"),
        P(("fsdp", "ctx")),
        P(("fsdp", "ctx"), None),
        P(("fsdp", "ctx"), None),
        P(("fsdp", "ctx"), None),
        P(("fsdp", "ctx"), None),
        P(("fsdp", "ctx")),
        P(("fsdp", "ctx"), None),
        P(("fsdp", "ctx"), None),
        P(("fsdp", "ctx"), None),
        P("fsdp", "ctx", None),
    )
    out_specs = (
        P("fsdp", "ctx", None),
        P("fsdp", "ctx", None),
        P(("fsdp", "ctx")),
        P(("fsdp", "ctx"), None),
        P(("fsdp", "ctx"), None),
        P(("fsdp", "ctx"), None),
        P(("fsdp", "ctx"), None),
        P(("fsdp", "ctx")),
        P(("fsdp", "ctx"), None),
        P(("fsdp", "ctx"), None),
        P(("fsdp", "ctx"), None),
    )
    return jax.shard_map(
        per_device, mesh=mesh, in_specs=in_specs, out_specs=out_specs, check_vma=False
    )
```

profile of v0, /device:TPU:1, one launch (start us, length us, event | category | flops | bytes accessed | tf_op | source)
XLA Modules:
  0.0 2343.2 jit_solution(4837758723915019303)
XLA Ops:
  10.4 41.1 %all-reduce.5 = (bf16[2048]{0:T(1024)(128)(2,1)S(1)}, bf16[2048]{0:T(1024)(128)(2,1)S(1)}) all-reduce(bf16[2048]{0:T(1024)(128)(2,1)S(1)} %dynamic-update-slice, bf16[2048]{0:T(1024)(128)(2,1)S(1)} %dynamic-update-slice.1), channel_id=1, replica_groups=mesh['fsdp'=4,'ctx'=8] {'fsdp','ctx'}, use_global_device_ids=true, to_apply=%add | all-reduce | flops 4096 | bytes 16384
  52.8 17.1 all-gather.21.cloned.1.call-done
  69.9 2.9 convolution_convert_fusion.3
  74.8 53.1 %all-gather.15.cloned.1.call-done = bf16[2048,512]{1,0:T(8,128)(2,1)} async-done(((bf16[64,512]{1,0:T(8,128)(2,1)}), bf16[2048,512]{1,0:T(8,128)(2,1)}) %all-gather.15.cloned.1.call-update) | async-done | bytes 2097168 | tf_op jit(solution)/shard_map/all_gather | solution.py:93
  128.0 2.9 copy.44
  135.9 9.0 all_gather.57
  145.1 7.7 all-gather.23.cloned.1.call-done
  154.3 78.7 %all-gather.19.cloned.1.call-done = bf16[2048,2048]{1,0:T(8,128)(2,1)} async-done(((bf16[64,2048]{1,0:T(8,128)(2,1)}), bf16[2048,2048]{1,0:T(8,128)(2,1)}) %all-gather.19.cloned.1.call-update) | async-done | bytes 8388624 | tf_op jit(solution)/shard_map/all_gather | solution.py:92
  233.0 12.3 copy.45
  245.3 5.9 fusion.43
  251.3 6.2 all-gather.17.cloned.1.call-done
  257.5 8.4 fusion.11
  265.9 9.5 fusion.14
  275.4 8.9 fusion.39
  284.3 53.4 %all-gather.25.cloned.1.call-done = bf16[2048,2048]{1,0:T(8,128)(2,1)} async-done(((bf16[64,2048]{1,0:T(8,128)(2,1)}), bf16[2048,2048]{1,0:T(8,128)(2,1)}) %all-gather.25.cloned.1.call-update) | async-done | bytes 8388624 | tf_op jit(solution)/shard_map/all_gather | solution.py:142
  337.7 4.7 multiply_reduce_fusion.3
  342.7 191.3 %all-gather.27.cloned.1.call-done = bf16[2048,8192]{1,0:T(8,128)(2,1)} async-done(((bf16[64,8192]{1,0:T(8,128)(2,1)}), bf16[2048,8192]{1,0:T(8,128)(2,1)}) %all-gather.27.cloned.1.call-update) | async-done | bytes 33554448 | tf_op jit(solution)/shard_map/all_gather | solution.py:155
  534.0 17.7 fusion.70
  551.7 178.1 %all-gather.29.cloned.1.call-done = bf16[2048,8192]{1,0:T(8,128)(2,1)} async-done(((bf16[64,8192]{1,0:T(8,128)(2,1)}), bf16[2048,8192]{1,0:T(8,128)(2,1)}) %all-gather.29.cloned.1.call-update) | async-done | bytes 33554448 | tf_op jit(solution)/shard_map/all_gather | solution.py:156
  729.8 17.9 fusion.71
  747.7 178.0 %all-gather.31.cloned.1.call-done = bf16[8192,2048]{1,0:T(8,128)(2,1)} async-done(((bf16[256,2048]{1,0:T(8,128)(2,1)}), bf16[8192,2048]{1,0:T(8,128)(2,1)}) %all-gather.31.cloned.1.call-update) | async-done | bytes 33554448 | tf_op jit(solution)/shard_map/all_gather | solution.py:168
  925.7 20.5 multiply_convert_fusion
  946.8 4.6 pad_maximum_fusion
  951.5 19.3 all-gather.39.cloned.1.call-done
  970.8 150.7 %all-gather.37.cloned.1.call-done = bf16[512,8192]{1,0:T(8,128)(2,1)} async-done(((bf16[128,8192]{1,0:T(8,128)(2,1)}), bf16[512,8192]{1,0:T(8,128)(2,1)}) %all-gather.37.cloned.1.call-update) | async-done | bytes 8388624 | tf_op jit(solution)/shard_map/all_gather | solution.py:174
  1121.5 10.1 convolution_convert_fusion.1
  1131.7 35.8 %all-gather.33.cloned.1.call-done = bf16[512,2048]{1,0:T(8,128)(2,1)} async-done(((bf16[128,2048]{1,0:T(8,128)(2,1)}), bf16[512,2048]{1,0:T(8,128)(2,1)}) %all-gather.33.cloned.1.call-update) | async-done | bytes 2097168 | tf_op jit(solution)/shard_map/all_gather | solution.py:188
  1167.5 287.3 %all-gather.35.cloned.1.call-done = bf16[512,16384]{1,0:T(8,128)(2,1)} async-done(((bf16[128,16384]{1,0:T(8,128)(2,1)}), bf16[512,16384]{1,0:T(8,128)(2,1)}) %all-gather.35.cloned.1.call-update) | async-done | bytes 16777232 | tf_op jit(solution)/shard_map/all_gather | solution.py:189
  1454.8 17.0 convolution_convert_fusion
  1474.9 17.6 fusion.72
  1492.5 18.6 multiply_reduce_fusion.1
  1513.8 7.1 convolution_convert_fusion.2
  1524.3 158.3 %while.24 = (s32[]{:T(128)}, bf16[128,512]{0,1:T(8,128)(2,1)S(1)}, bf16[128,512]{0,1:T(8,128)(2,1)}, f32[128,512]{0,1:T(8,128)}, f32[128,512]{0,1:T(8,128)}, /*i...) while((s32[]{:T(128)}, bf16[128,512]{0,1:T(8,128)(2,1)S(1)}, ...), condition=%wide.region_6.7_spmd.clone, body=%wide.region_5.6_spmd.clone.sunk | while | flops 340606976 | bytes 23530068 | solution.py:260
  1539.8 2.5 collective-permute-start
  1557.2 2.4 collective-permute-start
  1568.9 3.1 collective-permute-done.2
  1573.6 2.6 collective-permute-done.3
  1577.9 2.5 collective-permute-start
  1587.1 2.7 collective-permute-start.2
  1591.4 3.4 collective-permute-done.2
  1596.3 2.6 collective-permute-done.3
  1600.6 2.5 collective-permute-start
  1613.9 3.4 collective-permute-done.2
  1618.9 2.6 collective-permute-done.3
  1623.1 2.5 collective-permute-start
  1636.4 3.1 collective-permute-done.2
  1641.1 2.6 collective-permute-done.3
  1645.3 2.5 collective-permute-start
  1656.2 4.9 collective-permute-done.2
  1662.7 2.6 collective-permute-done.3
  1667.0 2.5 collective-permute-start
  1683.7 2.8 fusion.47
  1686.5 2.8 fusion.55
  1689.9 8.2 fusion.49
  1699.3 9.1 fusion.52
  1708.5 6.7 fusion.73
  1718.6 39.9 %all-reduce.4 = (f32[2048]{0:T(1024)S(1)}, f32[2048]{0:T(1024)S(1)}) all-reduce(f32[2048]{0:T(1024)S(1)} %get-tuple-element.408, f32[2048]{0:T(1024)S(1)} %copy-done.24), channel_id=3, replica_groups=mesh['fsdp'=4,'ctx'=8] {'fsdp','ctx'}, use_global_device_ids=true, to_apply=%region_9.10.clone | all-reduce | flops 4096 | bytes 32768
  1762.2 13.9 fusion.20
  1776.1 2.8 convert_element_type.272
  1778.9 4.0 fusion.69
  1782.9 38.9 %reduce-scatter.9.cloned.1.call-done = f32[64,512]{1,0:T(8,128)} async-done(((f32[2048,512]{1,0:T(8,128)}), f32[64,512]{1,0:T(8,128)}) %reduce-scatter.9.cloned.1.call-update) | async-done | bytes 131088 | tf_op jit(solution)/shard_map/reduce_scatter | solution.py:290
  1821.8 139.8 %reduce-scatter.11.cloned.1.call-done = f32[64,512]{1,0:T(8,128)} async-done(((f32[2048,512]{1,0:T(8,128)}), f32[64,512]{1,0:T(8,128)}) %reduce-scatter.11.cloned.1.call-update) | async-done | bytes 131088 | tf_op jit(solution)/shard_map/reduce_scatter | solution.py:291
  1961.7 187.3 %reduce-scatter.7.cloned.1.call-done = f32[64,2048]{1,0:T(8,128)} async-done(((f32[2048,2048]{1,0:T(8,128)}), f32[64,2048]{1,0:T(8,128)}) %reduce-scatter.7.cloned.1.call-update) | async-done | bytes 524304 | tf_op jit(solution)/shard_map/reduce_scatter | solution.py:289
  2149.0 187.5 %reduce-scatter.13.cloned.1.call-done = f32[64,2048]{1,0:T(8,128)} async-done(((f32[2048,2048]{1,0:T(8,128)}), f32[64,2048]{1,0:T(8,128)}) %reduce-scatter.13.cloned.1.call-update) | async-done | bytes 524304 | tf_op jit(solution)/shard_map/reduce_scatter | solution.py:292
  (330 shorter events, 139.6 us)
Async XLA Ops:
  7.2 123.7 %copy-start = (bf16[1,128,2048]{2,1,0:T(8,128)(2,1)S(1)}, bf16[1,128,2048]{2,1,0:T(8,128)(2,1)}, u32[]{:S(2)}) copy-start(bf16[1,128,2048]{2,1,0:T(8,128)(2,1)} %param.14) | copy-start | bytes 1572868
  7.2 62.7 %all-gather.21.cloned.1.call-start = ((), (), s32[]{:S(2)}) async-start(), calls=%async_computation.9 | async-start | bytes 2162688 | tf_op jit(solution)/shard_map/all_gather | solution.py:94
  7.9 120.1 %all-gather.15.cloned.1.call-start = ((), (), s32[]{:S(2)}) async-start(), calls=%async_computation.6 | async-start | bytes 2162688 | tf_op jit(solution)/shard_map/all_gather | solution.py:93
  8.7 144.2 %all-gather.23.cloned.1.call-start = ((), (), s32[]{:S(2)}) async-start(), calls=%async_computation.10 | async-start | bytes 1179648 | tf_op jit(solution)/shard_map/all_gather | solution.py:114
  51.5 193.8 %copy-start.18 = (f32[2048]{0:T(1024)}, f32[2048]{0:T(1024)S(1)}, u32[]{:S(2)}) copy-start(f32[2048]{0:T(1024)S(1)} %convert_element_type.242) | copy-start | bytes 24580
  52.8 192.5 %copy-start.25 = (f32[128]{0:T(128)}, f32[128]{0:T(128)S(1)}, u32[]{:S(2)}) copy-start(f32[128]{0:T(128)S(1)} %add_rsqrt_fusion.1) | copy-start | bytes 1540
  72.8 160.2 %all-gather.19.cloned.1.call-start = ((), (), s32[]{:S(2)}) async-start(), calls=%async_computation.8 | async-start | bytes 8650752 | tf_op jit(solution)/shard_map/all_gather | solution.py:92
  73.4 184.1 %all-gather.17.cloned.1.call-start = ((), (), s32[]{:S(2)}) async-start(), calls=%async_computation.7 | async-start | bytes 1179648 | tf_op jit(solution)/shard_map/all_gather | solution.py:113
  74.8 176.3 %copy-start.21 = (f32[128,32]{0,1:T(8,128)}, f32[128,32]{0,1:T(8,128)S(1)}, u32[]{:S(2)}) copy-start(f32[128,32]{0,1:T(8,128)S(1)} %get-tuple-element.455) | copy-start | bytes 49156
  132.5 205.3 %all-gather.25.cloned.1.call-start = ((), (), s32[]{:S(2)}) async-start(), calls=%async_computation.11 | async-start | bytes 8650752 | tf_op jit(solution)/shard_map/all_gather | solution.py:142
  133.0 400.9 %all-gather.27.cloned.1.call-start = ((), (), s32[]{:S(2)}) async-start(), calls=%async_computation.12 | async-start | bytes 34603008 | tf_op jit(solution)/shard_map/all_gather | solution.py:155
  133.8 596.0 %all-gather.29.cloned.1.call-start = ((), (), s32[]{:S(2)}) async-start(), calls=%async_computation.13 | async-start | bytes 34603008 | tf_op jit(solution)/shard_map/all_gather | solution.py:156
  134.5 791.1 %all-gather.31.cloned.1.call-start = ((), (), s32[]{:S(2)}) async-start(), calls=%async_computation.14 | async-start | bytes 34603008 | tf_op jit(solution)/shard_map/all_gather | solution.py:168
  135.3 835.5 %all-gather.39.cloned.1.call-start = ((), (), s32[]{:S(2)}) async-start(), calls=%async_computation.24 | async-start | bytes 2621440 | tf_op jit(solution)/shard_map/all_gather | solution.py:175
  135.9 985.6 %all-gather.37.cloned.1.call-start = ((), (), s32[]{:S(2)}) async-start(), calls=%async_computation.22 | async-start | bytes 10485760 | tf_op jit(solution)/shard_map/all_gather | solution.py:174
  144.9 100.4 %copy-start.28 = (s32[1,1024]{1,0:T(1,128)}, s32[1,1024]{1,0:T(1,128)S(1)}, u32[]{:S(2)}) copy-start(s32[1,1024]{1,0:T(1,128)S(1)} %all_gather.57) | copy-start | bytes 12292
  251.3 14.6 copy-start.14
  284.3 58.2 %copy-start.13 = (bf16[128,8,4,64]{0,3,2,1:T(8,128)(2,1)}, bf16[128,8,4,64]{0,3,2,1:T(8,128)(2,1)S(1)}, u32[]{:S(2)}) copy-start(bf16[128,8,4,64]{0,3,2,1:T(8,128)(2,1)S(1)} %get-tuple-element.458) | copy-start | bytes 1572868
  342.6 387.2 %copy-start.9 = (bf16[128,2048]{1,0:T(8,128)(2,1)}, bf16[128,2048]{1,0:T(8,128)(2,1)S(1)}, u32[]{:S(2)}) copy-start(bf16[128,2048]{1,0:T(8,128)(2,1)S(1)} %multiply_convert_fusion.3) | copy-start | bytes 1572868
  551.7 374.0 %copy-start.17 = (bf16[1,128,2048]{2,1,0:T(8,128)(2,1)S(1)}, bf16[1,128,2048]{2,1,0:T(8,128)(2,1)}, u32[]{:S(2)}) copy-start(bf16[1,128,2048]{2,1,0:T(8,128)(2,1)} %param.25) | copy-start | bytes 1572868
  946.2 221.3 %all-gather.33.cloned.1.call-start = ((), (), s32[]{:S(2)}) async-start(), calls=%async_computation.19 | async-start | bytes 2621440 | tf_op jit(solution)/shard_map/all_gather | solution.py:188
  946.8 508.0 %all-gather.35.cloned.1.call-start = ((), (), s32[]{:S(2)}) async-start(), calls=%async_computation.20 | async-start | bytes 20971520 | tf_op jit(solution)/shard_map/all_gather | solution.py:189
  951.4 824.7 %reduce-scatter.17.cloned.1.call-start = ((), (), s32[]{:S(2)}) async-start(), calls=%async_computation.23 | async-start | bytes 9437184 | tf_op jit(solution)/shard_map/reduce_scatter | solution.py:178
  1131.7 647.3 %reduce-scatter.15.cloned.1.call-start = ((), (), s32[]{:S(2)}) async-start(), calls=%async_computation.21 | async-start | bytes 18874368 | tf_op jit(solution)/shard_map/reduce_scatter | solution.py:192
  1471.8 350.0 %reduce-scatter.9.cloned.1.call-start = ((), (), s32[]{:S(2)}) async-start(), calls=%async_computation.16 | async-start | bytes 4325376 | tf_op jit(solution)/shard_map/reduce_scatter | solution.py:290
  1474.9 17.6 copy-start.6
  1513.8 10.5 copy-start.11
  1524.3 159.3 %copy-start.19 = (f32[2048]{0:T(1024)S(1)}, f32[2048]{0:T(1024)}, u32[]{:S(2)}) copy-start(f32[2048]{0:T(1024)} %copy-done.18) | copy-start | bytes 24580
  1524.3 159.3 %copy-start.26 = (f32[128]{0:T(128)S(1)}, f32[128]{0:T(128)}, u32[]{:S(2)}) copy-start(f32[128]{0:T(128)} %copy-done.25) | copy-start | bytes 1540
  1524.3 15.5 collective-permute-start
  1526.9 12.9 collective-permute-start.1
  1532.6 3.8 collective-permute-start.2
  1535.4 2.8 collective-permute-start.3
  1539.8 17.4 collective-permute-start
  1543.3 13.9 collective-permute-start.1
  1549.2 4.6 collective-permute-start.2
  1552.7 2.8 collective-permute-start.3
  1557.2 20.6 collective-permute-start
  1560.5 17.3 collective-permute-start.1
  1566.3 5.7 collective-permute-start.2
  1568.4 7.8 collective-permute-start.3
  1577.9 22.7 collective-permute-start
  1581.3 19.3 collective-permute-start.1
  1587.1 7.7 collective-permute-start.2
  1590.9 8.0 collective-permute-start.3
  1600.6 22.5 collective-permute-start
  1604.0 19.0 collective-permute-start.1
  1609.8 7.4 collective-permute-start.2
  1613.4 8.0 collective-permute-start.3
  1623.1 22.2 collective-permute-start
  1626.6 18.8 collective-permute-start.1
  1632.3 7.1 collective-permute-start.2
  1635.9 7.8 collective-permute-start.3
  1645.3 21.6 collective-permute-start
  1648.8 18.2 collective-permute-start.1
  1654.5 6.6 collective-permute-start.2
  1655.8 9.5 collective-permute-start.3
  1667.0 15.6 collective-permute-start
  1670.4 12.2 collective-permute-start.1
  1676.2 3.2 collective-permute-start.2
  1678.2 2.7 collective-permute-start.3
  1686.5 275.2 %reduce-scatter.11.cloned.1.call-start = ((), (), s32[]{:S(2)}) async-start(), calls=%async_computation.17 | async-start | bytes 4325376 | tf_op jit(solution)/shard_map/reduce_scatter | solution.py:291
  1689.3 459.7 %reduce-scatter.7.cloned.1.call-start = ((), (), s32[]{:S(2)}) async-start(), calls=%async_computation.15 | async-start | bytes 17301504 | tf_op jit(solution)/shard_map/reduce_scatter | solution.py:289
  1698.1 638.4 %reduce-scatter.13.cloned.1.call-start = ((), (), s32[]{:S(2)}) async-start(), calls=%async_computation.18 | async-start | bytes 17301504 | tf_op jit(solution)/shard_map/reduce_scatter | solution.py:292
  (37 other events, 143.6 us)
Sparse Core Ops, SparseCore 0:
  10.9 58.9 all-gather.20
  72.7 55.2 all-gather.14
  130.4 22.3 all-gather.22
  155.6 77.4 all-gather.18
  235.3 22.1 all-gather.16
  260.2 77.4 all-gather.24
  340.6 193.3 all-gather.26
  536.8 192.9 all-gather.28
  732.7 192.9 all-gather.30
  927.1 43.6 all-gather.38
  973.0 148.4 all-gather.36
  1123.5 43.9 all-gather.32
  1169.1 285.7 all-gather.34
  1458.1 69.2 reduce-scatter.16
  1531.2 137.4 reduce-scatter.14
  1686.6 135.2 reduce-scatter.8
  1824.6 137.0 reduce-scatter.10
  1964.5 184.4 reduce-scatter.6
  2152.0 184.4 reduce-scatter.12
where the time goes:
time: 2350 us; the launch traced here: 2340 us
  waiting for transfers between devices  1850 us (79%)
  matrix products  239 us (10%)
  blocking collectives  90 us (4%)
  other arithmetic  72.9 us (3%)
  local copies, waits for them, and re-layouts  43.3 us (2%)
  starting transfers between devices  33.9 us (1%)
    all_gather x1, waiting for transfers between devices, per_device(): paired_piece = lax.all_gather(paired_low, 'fsdp', axis=0, tiled=True)  287 us
    all_gather x1, waiting for transfers between devices, per_device(): gate_piece = lax.all_gather(w_gate, ('fsdp', 'ctx'), axis=0, tiled=True)  191 us
    reduce_scatter x1, waiting for transfers between devices, per_device(): lax.psum_scatter(out_term, ('fsdp', 'ctx'), scatter_dimension=0, tiled=True)  188 us
    reduce_scatter x1, waiting for transfers between devices, per_device(): lax.psum_scatter(query_term, ('fsdp', 'ctx'), scatter_dimension=0, tiled=...  187 us
    all_gather x1, waiting for transfers between devices, per_device(): up_piece = lax.all_gather(w_up, ('fsdp', 'ctx'), axis=0, tiled=True)  178 us
    all_gather x1, waiting for transfers between devices, per_device(): block_piece = lax.all_gather(w_down, ('fsdp', 'ctx'), axis=0, tiled=True)  178 us
    all_gather x1, waiting for transfers between devices, per_device(): act_piece = lax.all_gather(activated, 'fsdp', axis=0, tiled=True)  151 us
    reduce_scatter x1, waiting for transfers between devices, per_device(): lax.psum_scatter(value_term, ('fsdp', 'ctx'), scatter_dimension=0, tiled=...  140 us
  transfers between devices with their start and end apart: 51, of which 30 were waited for; matrix products, arithmetic and copies ran while one was open for 15% of the time, Pallas kernels for 0%

commit v1 on v0

v1 whole, which is shorter than its diff:
```python
import functools

import jax
import jax.numpy as jnp
from jax import lax
from jax.experimental import pallas as pl
from jax.experimental.pallas import tpu as pltpu
from jax.sharding import PartitionSpec as P

HEADS = 32
KV_HEADS = 8
HEAD_DIM = 64
EPSILON = 1e-05
ROPE_BASE = 500000.0
LOW = jnp.bfloat16
WIDE = jnp.float32


def dot(left, right, dims=((1,), (0,)), out=WIDE):
    return lax.dot_general(left, right, (dims, ((), ())), preferred_element_type=WIDE).astype(out)


def swap(block, axis, mask):
    count = lax.axis_size(axis)
    return lax.ppermute(block, axis, [(i, i ^ mask) for i in range(count)])


def pick(stack, index):
    return lax.dynamic_index_in_dim(stack, index, 0, keepdims=False)


def in_order(pieces, base):
    out = jnp.zeros((len(pieces),) + pieces[0].shape, pieces[0].dtype)
    for r, piece in enumerate(pieces):
        out = lax.dynamic_update_index_in_dim(out, piece, base ^ r, 0)
    return out


def ctx_order(count):
    order = [0]
    bit = 2
    while bit < count:
        order = order + [k ^ bit for k in order]
        bit *= 2
    return order + [k ^ 1 for k in order]


def gather_ctx(block):
    count = lax.axis_size("ctx")
    if count == 8:
        near_x, near_y = swap(block, "ctx", 2), swap(block, "ctx", 4)
        half = block.shape[0] // 2
        far_top = swap(near_y[:half], "ctx", 2)
        far_low = swap(near_x[half:], "ctx", 4)
        quad = jnp.concatenate([block, near_x, near_y, far_top, far_low], axis=0)
    else:
        quad = block
        bit = 2
        while bit < count:
            quad = jnp.concatenate([quad, swap(quad, "ctx", bit)], axis=0)
            bit *= 2
    return jnp.concatenate([quad, swap(quad, "ctx", 1)], axis=0)


def scatter_ctx(partial):
    count = lax.axis_size("ctx")
    middle = partial.shape[0] // 2
    quad = partial[:middle].astype(WIDE) + swap(partial[middle:], "ctx", 1).astype(WIDE)
    rows = partial.shape[0] // count
    if count == 8:
        half = rows // 2
        quad = quad.astype(LOW)
        own, to_x, to_y, far = (quad[j * rows : (j + 1) * rows] for j in range(4))
        by_x = swap(jnp.concatenate([to_x[half:], far[half:]], axis=0), "ctx", 2)
        by_y = swap(jnp.concatenate([to_y[:half], far[:half]], axis=0), "ctx", 4)
        last_x = swap((to_x[:half].astype(WIDE) + by_y[half:].astype(WIDE)).astype(LOW), "ctx", 2)
        last_y = swap((to_y[half:].astype(WIDE) + by_x[half:].astype(WIDE)).astype(LOW), "ctx", 4)
        top = own[:half].astype(WIDE) + last_x.astype(WIDE) + by_y[:half].astype(WIDE)
        low = own[half:].astype(WIDE) + by_x[:half].astype(WIDE) + last_y.astype(WIDE)
        return jnp.concatenate([top, low], axis=0)
    bit = count // 2
    while bit >= 2:
        middle = quad.shape[0] // 2
        quad = quad[:middle] + swap(quad[middle:].astype(LOW), "ctx", bit).astype(WIDE)
        bit //= 2
    return quad


def exchange_ctx(stack):
    return lax.all_to_all(stack, "ctx", 0, 0, tiled=True)


def gather_fsdp(block, base):
    count = lax.axis_size("fsdp")
    return in_order([block] + [swap(block, "fsdp", r) for r in range(1, count)], base)


def scatter_fsdp(stack, base):
    count = lax.axis_size("fsdp")
    total = pick(stack, base).astype(WIDE)
    for r in range(1, count):
        total = total + swap(pick(stack, base ^ r), "fsdp", r).astype(WIDE)
    return total


def turned(block, cosine, sine):
    lane = lax.broadcasted_iota(jnp.int32, block.shape, 1)
    first = (lane % HEAD_DIM) < HEAD_DIM // 2
    width = block.shape[1]
    other = jnp.where(
        first, pltpu.roll(block, width - HEAD_DIM // 2, 1), pltpu.roll(block, HEAD_DIM // 2, 1)
    )
    return block * cosine + other * sine


def forward_kernel(
    heads, q_ref, kv_ref, cos_ref, sin_ref, cosk_ref, sink_ref, row_ref, col_ref,
    mixed_ref, lse_ref, qs_ref, kr_ref, vl_ref, vt_ref,
):
    @pl.when(pl.program_id(0) == 0)
    def _():
        keys = turned(kv_ref[...], cosk_ref[...], sink_ref[...])
        kr_ref[...] = keys[:, :HEAD_DIM].astype(LOW)
        values = kv_ref[...][:, HEAD_DIM:].astype(LOW)
        vl_ref[...] = values
        vt_ref[...] = values.astype(WIDE).T.astype(LOW)

    cosine, sine = cos_ref[...], sin_ref[...]
    keys = kr_ref[...]
    values_t = vt_ref[...]
    visible = col_ref[...] <= row_ref[...]
    scale = HEAD_DIM ** (-0.5)
    mixed, totals = [], []
    for pair in range(heads // 2):
        both = turned(q_ref[:, pair * 128 : pair * 128 + 128], cosine, sine)
        both = (both.astype(LOW).astype(WIDE) * scale).astype(LOW)
        qs_ref[:, pair * 128 : pair * 128 + 128] = both
        for side in range(2):
            query = both[:, side * HEAD_DIM : (side + 1) * HEAD_DIM]
            scores = jnp.where(visible, dot(keys, query, ((1,), (1,))), -1e30)
            top = jnp.max(scores, axis=0, keepdims=True)
            weights = jnp.exp(scores - top)
            total = jnp.sum(weights, axis=0, keepdims=True)
            out = dot(values_t, weights.astype(LOW)) / total
            mixed.append(out)
            totals.append(top + jnp.log(total))
    mixed_ref[...] = jnp.concatenate(mixed, axis=0).T.astype(LOW)
    pad = [jnp.zeros_like(totals[0])] * (8 - heads)
    lse_ref[...] = jnp.concatenate(totals + pad, axis=0)


def backward_kernel(
    heads, steps, q_ref, k_ref, v_ref, do_ref, lse_ref, cos_ref, sin_ref, cosk_ref, sink_ref,
    row_ref, col_ref, dq_ref, dkv_ref, kt_ref, dk_ref, dv_ref,
):
    @pl.when(pl.program_id(0) == 0)
    def _():
        kt_ref[...] = k_ref[...].astype(WIDE).T.astype(LOW)
        dk_ref[...] = jnp.zeros_like(dk_ref)
        dv_ref[...] = jnp.zeros_like(dv_ref)

    keys, values, keys_t = k_ref[...], v_ref[...], kt_ref[...]
    visible = col_ref[...] <= row_ref[...]
    scale = HEAD_DIM ** (-0.5)
    grads = []
    for head in range(heads):
        lanes = slice(head * HEAD_DIM, (head + 1) * HEAD_DIM)
        query, grad_out = q_ref[:, lanes], do_ref[:, lanes]
        scores = dot(keys, query, ((1,), (1,)))
        probs = jnp.where(visible, jnp.exp(scores - lse_ref[head : head + 1, :]), 0.0)
        grad_probs = dot(values, grad_out, ((1,), (1,)))
        product = probs * grad_probs
        delta = jnp.sum(product, axis=0, keepdims=True)
        grad_scores = (product - probs * delta).astype(LOW)
        dv_ref[...] += dot(probs.astype(LOW), grad_out)
        dk_ref[...] += dot(grad_scores, query)
        grads.append(dot(keys_t, grad_scores) * scale)
    grad_q = jnp.concatenate(grads, axis=0).T
    cosine, sine = cos_ref[...], sin_ref[...]
    for pair in range(heads // 2):
        lanes = slice(pair * 128, pair * 128 + 128)
        dq_ref[:, lanes] = turned(grad_q[:, lanes], cosine, -sine).astype(LOW)

    @pl.when(pl.program_id(0) == steps - 1)
    def _():
        both = jnp.concatenate([dk_ref[...], dv_ref[...]], axis=1)
        back = turned(both, cosk_ref[...], -sink_ref[...])
        lane = lax.broadcasted_iota(jnp.int32, both.shape, 1)
        dkv_ref[...] = jnp.where(lane < HEAD_DIM, back, both).astype(LOW)


VMEM_LIMIT = 56 * 1024 * 1024


def attention_forward(qkv, cosine, sine, places, heads):
    length = qkv.shape[0]
    width = heads * HEAD_DIM
    block = min(256, length)
    whole = lambda shape: pl.BlockSpec(shape, lambda i: (0,) * len(shape))
    rows = lambda columns: pl.BlockSpec((block, columns), lambda i: (i, 0))
    flops = 4 * heads * length * length * HEAD_DIM
    return pl.pallas_call(
        functools.partial(forward_kernel, heads),
        grid=(length // block,),
        in_specs=[
            rows(width),
            pl.BlockSpec((length, 128), lambda i: (0, width // 128)),
            rows(128), rows(128), whole((length, 128)), whole((length, 128)),
            pl.BlockSpec((1, block), lambda i: (0, i)), whole((length, 1)),
        ],
        out_specs=[
            rows(width), pl.BlockSpec((8, block), lambda i: (0, i)), rows(width),
            whole((length, HEAD_DIM)), whole((length, HEAD_DIM)),
        ],
        out_shape=[
            jax.ShapeDtypeStruct((length, width), LOW),
            jax.ShapeDtypeStruct((8, length), WIDE),
            jax.ShapeDtypeStruct((length, width), LOW),
            jax.ShapeDtypeStruct((length, HEAD_DIM), LOW),
            jax.ShapeDtypeStruct((length, HEAD_DIM), LOW),
        ],
        scratch_shapes=[pltpu.VMEM((HEAD_DIM, length), LOW)],
        compiler_params=pltpu.CompilerParams(
            dimension_semantics=("arbitrary",), vmem_limit_bytes=VMEM_LIMIT
        ),
        cost_estimate=pl.CostEstimate(
            flops=flops * 2, bytes_accessed=8 * length * width, transcendentals=heads * length * length
        ),
        name="attention_forward",
    )(qkv, qkv, cosine, sine, cosine, sine, places[None, :], places[:, None])


def attention_backward(q_scaled, k_rot, v_low, grad_mixed, lse, cosine, sine, places, heads):
    length = q_scaled.shape[0]
    width = heads * HEAD_DIM
    block = min(256, length)
    steps = length // block
    whole = lambda shape: pl.BlockSpec(shape, lambda i: (0,) * len(shape))
    rows = lambda columns: pl.BlockSpec((block, columns), lambda i: (i, 0))
    flops = 10 * heads * length * length * HEAD_DIM
    return pl.pallas_call(
        functools.partial(backward_kernel, heads, steps),
        grid=(steps,),
        in_specs=[
            rows(width), whole((length, HEAD_DIM)), whole((length, HEAD_DIM)), rows(width),
            pl.BlockSpec((8, block), lambda i: (0, i)),
            rows(128), rows(128), whole((length, 128)), whole((length, 128)),
            pl.BlockSpec((1, block), lambda i: (0, i)), whole((length, 1)),
        ],
        out_specs=[rows(width), whole((length, 128))],
        out_shape=[
            jax.ShapeDtypeStruct((length, width), LOW),
            jax.ShapeDtypeStruct((length, 128), LOW),
        ],
        scratch_shapes=[
            pltpu.VMEM((HEAD_DIM, length), LOW),
            pltpu.VMEM((length, HEAD_DIM), WIDE),
            pltpu.VMEM((length, HEAD_DIM), WIDE),
        ],
        compiler_params=pltpu.CompilerParams(
            dimension_semantics=("arbitrary",), vmem_limit_bytes=VMEM_LIMIT
        ),
        cost_estimate=pl.CostEstimate(
            flops=flops * 2, bytes_accessed=8 * length * width, transcendentals=heads * length * length
        ),
        name="attention_backward",
    )(
        q_scaled, k_rot, v_low, grad_mixed, lse, cosine, sine, cosine, sine,
        places[None, :], places[:, None],
    )


def inverse_rms(rows):
    return lax.rsqrt(jnp.mean(rows * rows, axis=-1, keepdims=True) + EPSILON)


def norm_back(grad_hat, hat_rows, inv_rms):
    return inv_rms * (grad_hat - hat_rows * jnp.mean(grad_hat * hat_rows, axis=-1, keepdims=True))


def per_device(
    tokens, positions, attn_gain, w_query, w_key, w_value, w_out,
    mlp_gain, w_gate, w_up, w_down, cotangent,
):
    f_count, c_count = lax.axis_size("fsdp"), lax.axis_size("ctx")
    f_index, c_index = lax.axis_index("fsdp"), lax.axis_index("ctx")
    f_side, f_high = f_index % 2, f_index // 2
    groups = f_count // 2
    own_tokens, own_cot = tokens[0], cotangent[0]
    tok_rows, width = own_tokens.shape
    piece = w_query.shape[0]
    heads = HEADS // c_count
    q_width = heads * HEAD_DIM
    qkv_width = q_width + 2 * HEAD_DIM
    kv_share = max(1, c_count // KV_HEADS)
    ff_width = w_gate.shape[1]
    ff_block = w_down.shape[0]

    gains = jnp.concatenate([attn_gain, mlp_gain]).astype(WIDE)
    gains = gather_fsdp(gains, f_index).reshape(-1)
    small = lax.all_gather(
        jnp.concatenate([gains, positions[0].astype(WIDE)])[None], "ctx", axis=0, tiled=True
    )
    both_gains = small[:, : gains.shape[0]].reshape(c_count, f_count, 2, piece)
    both_gains = both_gains.transpose(2, 1, 0, 3).reshape(2, width)
    gain_first, gain_second = both_gains[0], both_gains[1]
    order = jnp.array(ctx_order(c_count), jnp.int32) ^ c_index
    places = jnp.take(small[:, gains.shape[0] :], order, axis=0).reshape(-1)
    length = places.shape[0]
    half_dim = HEAD_DIM // 2
    frequency = jnp.power(ROPE_BASE, -2.0 * jnp.arange(half_dim, dtype=WIDE) / HEAD_DIM)
    angles = places[:, None] * frequency[None, :]
    cosine, sine = jnp.cos(angles), jnp.sin(angles)
    cosine = jnp.concatenate([cosine] * 4, axis=1)
    sine = jnp.concatenate([-sine, sine, -sine, sine], axis=1)
    int_places = places.astype(jnp.int32)

    shares = [
        w_query.reshape(piece, c_count, q_width),
        jnp.repeat(w_key.reshape(piece, KV_HEADS, HEAD_DIM), kv_share, axis=1),
        jnp.repeat(w_value.reshape(piece, KV_HEADS, HEAD_DIM), kv_share, axis=1),
    ]
    qkv_piece = jnp.concatenate(shares, axis=2).transpose(1, 0, 2)
    qkv_piece = exchange_ctx(qkv_piece).reshape(c_count * piece, qkv_width)
    w_qkv = gather_fsdp(qkv_piece, f_index).reshape(width, qkv_width)
    devices = f_count * c_count
    out_route = [(f_count * c + j, j * c_count + c) for c in range(c_count) for j in range(f_count)]
    out_piece = lax.ppermute(w_out, ("fsdp", "ctx"), out_route)
    w_out_rows = gather_fsdp(out_piece, f_index).reshape(q_width, width)

    all_tokens = gather_ctx(own_tokens)
    wide_tokens = all_tokens.astype(WIDE)
    normed_first = (wide_tokens * inverse_rms(wide_tokens) * gain_first).astype(LOW)
    qkv = dot(normed_first, w_qkv)
    mixed, lse, q_scaled, k_rot, v_low = attention_forward(qkv, cosine, sine, int_places, heads)
    inputs = own_tokens.astype(WIDE)
    inv_first = inverse_rms(inputs)
    hat_first = inputs * inv_first
    hidden = inputs + scatter_ctx(dot(mixed, w_out_rows, out=LOW))
    inv_second = inverse_rms(hidden)
    hat_second = hidden * inv_second
    normed_own = (hat_second * gain_second).astype(LOW)

    def my_columns(weight):
        split = weight.reshape(piece, groups, 2, c_count, ff_block).transpose(2, 3, 0, 1, 4)
        mine = pick(split, f_side)
        theirs = swap(pick(split, 1 - f_side), "fsdp", 1)
        return jnp.stack([mine, theirs], axis=1)

    gate_up = jnp.stack([my_columns(w_gate), my_columns(w_up)], axis=3)
    gate_up = exchange_ctx(gate_up)
    gate_up = gate_up.transpose(1, 0, 2, 3, 4, 5)
    local = groups * ff_block
    gate_up = gate_up.reshape(2, c_count * piece, 2 * local)
    gate_up = [gate_up] + [swap(gate_up, "fsdp", 2 * r) for r in range(1, groups)]
    gate_up = in_order([g[s] for g in gate_up for s in range(2)], f_index)
    gate_up = gate_up.reshape(width, 2 * local)
    down_rows = [w_down] + [swap(w_down, "fsdp", 2 * r) for r in range(1, groups)]
    down_rows = in_order(down_rows, f_high).reshape(local, width)

    def gather_pair(block):
        return gather_ctx(block), gather_ctx(swap(block, "fsdp", 1))

    def scatter_pair(first, second):
        return scatter_ctx(first) + swap(scatter_ctx(second).astype(LOW), "fsdp", 1).astype(WIDE)

    cots = gather_pair(own_cot)
    norms = gather_pair(normed_own)
    down_terms, norm_terms, acts, lows = [], [], [], []
    for cot, normed in zip(cots, norms):
        grad_act = dot(cot, down_rows, ((1,), (1,)))
        projected = dot(normed, gate_up)
        gate, up = projected[:, :local], projected[:, local:]
        sig = jax.nn.sigmoid(gate)
        acts.append((gate * sig * up).astype(LOW))
        gate_low = grad_act * up * sig * (1.0 + gate * (1.0 - sig))
        up_low = grad_act * gate * sig
        lows.append(jnp.concatenate([gate_low, up_low], axis=1).astype(LOW))
        norm_terms.append(dot(lows[-1], gate_up, ((1,), (1,)), LOW))
        down_terms.append(dot(acts[-1], down_rows, out=LOW))
    grad_normed = scatter_pair(*norm_terms)
    output = hidden + scatter_pair(*down_terms)
    down_part = dot(acts[0], cots[0], ((0,), (0,))) + dot(acts[1], cots[1], ((0,), (0,)))
    gate_up_part = dot(norms[0], lows[0], ((0,), (0,))) + dot(norms[1], lows[1], ((0,), (0,)))

    down_part = down_part.astype(LOW).reshape(groups, ff_block, width)
    down_grad = pick(down_part, f_high).astype(WIDE)
    for r in range(1, groups):
        down_grad = down_grad + swap(pick(down_part, f_high ^ r), "fsdp", 2 * r).astype(WIDE)
    gate_up_part = gate_up_part.astype(LOW).reshape(groups, 2, c_count * piece, 2 * local)
    gate_up_sum = pick(gate_up_part, f_high).astype(WIDE)
    for r in range(1, groups):
        gate_up_sum = gate_up_sum + swap(pick(gate_up_part, f_high ^ r), "fsdp", 2 * r).astype(WIDE)
    gate_up_sum = gate_up_sum.astype(LOW)
    gate_up_sum = gate_up_sum.reshape(2, c_count, piece, 2 * local).transpose(1, 0, 2, 3)
    gate_up_sum = exchange_ctx(gate_up_sum).transpose(1, 0, 2, 3)
    sides = in_order([pick(gate_up_sum, f_side), swap(pick(gate_up_sum, 1 - f_side), "fsdp", 1)], f_side)
    sides = sides.reshape(2, c_count, piece, 2, groups, ff_block).transpose(3, 2, 4, 0, 1, 5)
    sides = sides.reshape(2, piece, ff_width).astype(WIDE)
    gate_grad, up_grad = sides[0], sides[1]
    mlp_gain_grad = jnp.sum(
        gate_grad * w_gate.astype(WIDE) + up_grad * w_up.astype(WIDE), axis=1
    ) / mlp_gain.astype(WIDE)

    grad_hidden = own_cot.astype(WIDE) + norm_back(grad_normed * gain_second, hat_second, inv_second)
    all_hidden = gather_ctx(grad_hidden.astype(LOW))
    grad_mixed = dot(all_hidden, w_out_rows, ((1,), (1,)), LOW)
    out_part = dot(mixed, all_hidden, ((0,), (0,)), LOW).reshape(f_count, piece, width)
    grad_q, grad_kv = attention_backward(
        q_scaled, k_rot, v_low, grad_mixed, lse, cosine, sine, int_places, heads
    )
    grad_qkv = jnp.concatenate([grad_q, grad_kv], axis=1)
    grad_normed = scatter_ctx(dot(grad_qkv, w_qkv, ((1,), (1,)), LOW))
    input_grad = grad_hidden + norm_back(grad_normed * gain_first, hat_first, inv_first)

    out_sum = scatter_fsdp(out_part, f_index).astype(LOW)
    out_grad = lax.ppermute(out_sum, ("fsdp", "ctx"), [(d, s) for s, d in out_route]).astype(WIDE)
    qkv_part = dot(normed_first, grad_qkv, ((0,), (0,)), LOW)
    qkv_sum = scatter_fsdp(qkv_part.reshape(f_count, c_count * piece, qkv_width), f_index)
    qkv_sum = exchange_ctx(qkv_sum.astype(LOW).reshape(c_count, piece, qkv_width))
    qkv_sum = qkv_sum.astype(WIDE)
    query_grad = qkv_sum[:, :, :q_width].transpose(1, 0, 2).reshape(piece, -1)
    kv_sum = qkv_sum[:, :, q_width:].reshape(KV_HEADS, kv_share, piece, 2, HEAD_DIM).sum(axis=1)
    key_grad = kv_sum[:, :, 0].transpose(1, 0, 2).reshape(piece, -1)
    value_grad = kv_sum[:, :, 1].transpose(1, 0, 2).reshape(piece, -1)
    attn_gain_grad = (
        jnp.sum(query_grad * w_query.astype(WIDE), axis=1)
        + jnp.sum(key_grad * w_key.astype(WIDE), axis=1)
        + jnp.sum(value_grad * w_value.astype(WIDE), axis=1)
    ) / attn_gain.astype(WIDE)

    return (
        output.astype(LOW)[None],
        input_grad.astype(LOW)[None],
        attn_gain_grad,
        query_grad,
        key_grad,
        value_grad,
        out_grad,
        mlp_gain_grad,
        gate_grad,
        up_grad,
        down_grad,
    )


def solution(mesh):
    rows = P(("fsdp", "ctx"), None)
    vector = P(("fsdp", "ctx"))
    tokens = P("fsdp", "ctx", None)
    in_specs = (
        tokens, P("fsdp", "ctx"), vector, rows, rows, rows, rows, vector, rows, rows, rows, tokens,
    )
    out_specs = (
        tokens, tokens, vector, rows, rows, rows, rows, vector, rows, rows, rows,
    )
    return jax.shard_map(
        per_device, mesh=mesh, in_specs=in_specs, out_specs=out_specs, check_vma=False
    )
```

time: 2350 us -> 937 us (0.40)
  waiting for transfers between devices: 1850 us -> 427 us
  matrix products: 239 us -> 85.5 us
  starting transfers between devices: 33.9 us -> 144 us
  local copies, waits for them, and re-layouts: 43.3 us -> 152 us
  blocking collectives: 90 us -> 12.8 us
  Pallas kernels: 0 us -> 34.1 us
    all_gather x13 -> x0, waiting for transfers between devices: 1260 us -> none  [the longest x1 287 us: per_device(): paired_piece = lax.all_gather(paired_low, 'fsdp', axis=0, tiled=True)]
    reduce_scatter x6 -> x0, waiting for transfers between devices: 554 us -> none  [the longest x1 188 us: per_device(): lax.psum_scatter(out_term, ('fsdp', 'ctx'), scatter_dimension=0, tiled=True)]
    ppermute x32 -> x88, waiting for transfers between devices: 32.5 us -> 420 us  [the longest x86 420 us: swap(): return lax.ppermute(block, axis, [(i, i ^ mask) for i in range(count)])]
    dot_general x62 -> x18, matrix products: 239 us -> 85.5 us  [dot(): lax.dot_general(left, right, (dims, ((), ())), preferred_element_type=WIDE)]
    ppermute x32 -> x88, starting transfers between devices: 32.9 us -> 125 us  [the longest x86 117 us: swap(): return lax.ppermute(block, axis, [(i, i ^ mask) for i in range(count)])]
    unnamed x2 -> x0, blocking collectives: 81 us -> none
    unnamed x59 -> x179, local copies, waits for them, and re-layouts: 7.38 us -> 44.6 us
    slice x1 -> x35, local copies, waits for them, and re-layouts: 4 us -> 38.9 us  [the longest x3 12.7 us: per_device(): gate_grad, up_grad = (sides[0], sides[1])]
  transfers between devices with their start and end apart: 51 -> 92, of which waited for: 30 -> 37; matrix products, arithmetic and copies ran while one was open for 15% -> 28% of each run, Pallas kernels for 0% -> 2%
where the time goes in v1:
time: 937 us; the launch traced here: 920 us
  waiting for transfers between devices  427 us (46%)
  local copies, waits for them, and re-layouts  152 us (16%)
  starting transfers between devices  144 us (15%)
  matrix products  85.5 us (9%)
  other arithmetic  62.9 us (7%)
  Pallas kernels  34.1 us (4%)
  blocking collectives  12.8 us (1%)
    ppermute x86, waiting for transfers between devices, swap(): return lax.ppermute(block, axis, [(i, i ^ mask) for i in range(count)])  420 us
    ppermute x86, starting transfers between devices, swap(): return lax.ppermute(block, axis, [(i, i ^ mask) for i in range(count)])  117 us
    dot_general x18, matrix products, dot(): lax.dot_general(left, right, (dims, ((), ())), preferred_element_type=WIDE)  85.5 us
    unnamed x179, local copies, waits for them, and re-layouts  44.6 us
  transfers between devices with their start and end apart: 92, of which 37 were waited for; matrix products, arithmetic and copies ran while one was open for 28% of the time, Pallas kernels for 2%

profile of v1, /device:TPU:1, one launch (start us, length us, event | category | flops | bytes accessed | tf_op | source)
XLA Modules:
  0.0 920.5 jit_solution(3820231023947058415)
XLA Ops:
  12.8 5.5 all-to-all-start
  31.2 3.8 collective-permute-start.11
  35.1 12.8 %all-gather.1 = f32[8,1,640]{2,1,0:T(1,128)S(1)} all-gather(f32[1,1,640]{2,1,0:T(1,128)S(1)} %reshape.281), channel_id=2, replica_groups=mesh['fsdp'=4,'ctx'=8] {'ctx'}, dimensions={0}, use_global_device_ids=true | all-gather | bytes 23040 | tf_op jit(solution)/shard_map/all_gather | solution.py:301
  54.2 4.8 collective-permute-start.12
  77.4 10.9 %collective-permute-done.13 = bf16[64,2048]{1,0:T(8,128)(2,1)S(1)} collective-permute-done((bf16[64,2048]{1,0:T(8,128)(2,1)}, bf16[64,2048]{1,0:T(8,128)(2,1)S(1)}, u32[]{:S(2)}, u32[]{:S(2)}) %collective-permute-start.13) | collective-permute-done | bytes 262176 | tf_op jit(solution)/shard_map/ppermute | solution.py:25
  89.7 7.4 collective-permute-start.9
  97.1 9.4 %collective-permute-start.10 = (bf16[512,384]{1,0:T(8,128)(2,1)S(1)}, bf16[512,384]{1,0:T(8,128)(2,1)S(1)}, u32[]{:S(2)}, u32[]{:S(2)}) collective-permute-start(bf16[512,384]{1,0:T(8,128)(2,1)S(1)} %bitcast.237), channel_id=1, source_target_pairs={{0,24},{8,16},{16,8},{24,0},{1,25},{9,17},{17,9},{25,1},{2,26},{10... | collective-permute-start | bytes 1179656 | tf_op jit(solution)/shard_map/ppermute | solution.py:25
  106.5 16.5 %collective-permute-done.9 = bf16[512,384]{1,0:T(8,128)(2,1)S(1)} collective-permute-done((bf16[512,384]{1,0:T(8,128)(2,1)S(1)}, bf16[512,384]{1,0:T(8,128)(2,1)S(1)}, u32[]{:S(2)}, u32[]{:S(2)}) %collective-permute-start.9) | collective-permute-done | bytes 393248 | tf_op jit(solution)/shard_map/ppermute | solution.py:25
  124.5 7.4 collective-permute-start.25
  137.1 3.5 fusion.8.q_ref.kv_ref
  140.6 16.0 %attention_forward.1 = (bf16[1024,256]{1,0:T(8,128)(2,1)}, f32[8,1024]{1,0:T(8,128)}, bf16[1024,256]{1,0:T(8,128)(2,1)}, bf16[1024,64]{1,0:T(8,128)(2,1)}, bf16[1024,64]{1,0:T(8,128)(2,1)}) custom-call(f32[1024,384]{1,0:T(8,128)} %fusion.8.q_ref.kv_ref, f32[1024,384]{1,0:T(8,128)} %fusion.8.q_ref.kv_ref, f32[1024,128]{1,0:T(8,128)} %get-tuple-element.156.cos_ref.cosk_ref, ...), custom_call_target="tpu_custom_call" | custom-call | flops 2147483648 | bytes 2097152 | tf_op jit(solution)/shard_map/attention_forward/pallas_call | solution.py:202
  171.5 4.2 all-to-all-start.1
  187.3 19.0 %collective-permute-done.48 = bf16[64,2048]{1,0:T(8,128)(2,1)S(1)} collective-permute-done((bf16[64,2048]{1,0:T(8,128)(2,1)S(1)}, bf16[64,2048]{1,0:T(8,128)(2,1)S(1)}, u32[]{:S(2)}, u32[]{:S(2)}) %collective-permute-start.48) | collective-permute-done | bytes 262176 | tf_op jit(solution)/shard_map/ppermute | solution.py:25
  210.2 7.1 collective-permute-done.58
  223.1 30.2 %collective-permute-done.28 = bf16[256,2048]{1,0:T(8,128)(2,1)S(1)} collective-permute-done((bf16[256,2048]{1,0:T(8,128)(2,1)S(1)}, bf16[256,2048]{1,0:T(8,128)(2,1)S(1)}, u32[]{:S(2)}, u32[]{:S(2)}) %collective-permute-start.28) | collective-permute-done | bytes 1048608 | tf_op jit(solution)/shard_map/ppermute | solution.py:25
  258.0 8.1 collective-permute-done.18
  266.2 5.6 collective-permute-done.17
  283.2 4.4 reshape.254
  299.1 5.0 collective-permute-done.21
  322.0 59.2 %collective-permute-done.27 = bf16[2,512,1024]{2,1,0:T(8,128)(2,1)} collective-permute-done((bf16[2,512,1024]{2,1,0:T(8,128)(2,1)}, bf16[2,512,1024]{2,1,0:T(8,128)(2,1)}, u32[]{:S(2)}, u32[]{:S(2)}) %collective-permute-start.27) | collective-permute-done | bytes 2097184 | tf_op jit(solution)/shard_map/ppermute | solution.py:25
  384.9 10.8 %collective-permute-done.36 = bf16[128,2048]{1,0:T(8,128)(2,1)S(1)} collective-permute-done((bf16[128,2048]{1,0:T(8,128)(2,1)S(1)}, bf16[128,2048]{1,0:T(8,128)(2,1)S(1)}, u32[]{:S(2)}, u32[]{:S(2)}) %collective-permute-start.36) | collective-permute-done | bytes 524320 | tf_op jit(solution)/shard_map/ppermute | solution.py:25
  397.6 4.4 collective-permute-done.37
  408.1 6.6 fusion.42
  414.8 4.7 multiply_convert_fusion.3
  419.5 5.1 convolution_convert_fusion.2
  427.9 4.8 convolution_convert_fusion.5
  435.9 6.6 fusion.43
  442.5 5.9 multiply_convert_fusion.1
  449.8 7.8 fusion.4
  457.6 10.0 %add_convert_fusion = bf16[2048,1024]{1,0:T(8,128)(2,1)S(1)} fusion(f32[2048,1024]{1,0:T(8,128)} %fusion.4, bf16[1024,2048]{1,0:T(8,128)(2,1)} %copy-done.51, bf16[1024,512]{0,1:T(8,128)(2,1)} %copy-done.71, bf16[1024,512]{0,1:T(8,128)(2,1)} %copy-done.70), kind=kOutput, calls=%fused_computation.6 | convolution fusion | flops 4303355904 | bytes 18874368 | tf_op jit(solution)/shard_map/dot_general | solution.py:20
  469.1 4.0 convolution_convert_fusion.1
  475.8 6.8 convolution_convert_fusion.4
  487.0 4.3 fusion.44
  499.3 62.3 %collective-permute-done.85 = bf16[2,512,1024]{2,1,0:T(8,128)(2,1)} collective-permute-done((bf16[2,512,1024]{2,1,0:T(8,128)(2,1)}, bf16[2,512,1024]{2,1,0:T(8,128)(2,1)}, u32[]{:S(2)}, u32[]{:S(2)}) %collective-permute-start.85) | collective-permute-done | bytes 2097184 | tf_op jit(solution)/shard_map/ppermute | solution.py:25
  566.0 4.2 all-to-all-start.3
  580.2 26.1 %collective-permute-done.52 = bf16[128,2048]{1,0:T(8,128)(2,1)S(1)} collective-permute-done((bf16[128,2048]{1,0:T(8,128)(2,1)}, bf16[128,2048]{1,0:T(8,128)(2,1)S(1)}, u32[]{:S(2)}, u32[]{:S(2)}) %collective-permute-start.52) | collective-permute-done | bytes 524320 | tf_op jit(solution)/shard_map/ppermute | solution.py:25
  610.9 9.0 collective-permute-done.53
  622.6 7.5 collective-permute-done.63
  631.7 3.9 collective-permute-done.42
  636.4 4.0 collective-permute-done.64
  641.6 4.3 collective-permute-done.44
  646.2 5.4 collective-permute-done.66
  654.2 11.5 %collective-permute-done.67 = bf16[128,2048]{1,0:T(8,128)(2,1)S(1)} collective-permute-done((bf16[128,2048]{1,0:T(8,128)(2,1)S(1)}, bf16[128,2048]{1,0:T(8,128)(2,1)S(1)}, u32[]{:S(2)}, u32[]{:S(2)}) %collective-permute-start.67) | collective-permute-done | bytes 524320 | tf_op jit(solution)/shard_map/ppermute | solution.py:25
  676.1 3.3 collective-permute-done.69
  681.7 5.8 collective-permute-done.70
  691.0 8.3 collective-permute-start.72
  700.5 23.1 %collective-permute-done.87 = bf16[256,2048]{1,0:T(8,128)(2,1)} collective-permute-done((bf16[256,2048]{1,0:T(8,128)(2,1)}, bf16[256,2048]{1,0:T(8,128)(2,1)}, u32[]{:S(2)}, u32[]{:S(2)}) %collective-permute-start.87) | collective-permute-done | bytes 1048608 | tf_op jit(solution)/shard_map/ppermute | solution.py:25
  729.4 16.6 %collective-permute-done.86 = bf16[8,64,1024]{2,1,0:T(8,128)(2,1)} collective-permute-done((bf16[8,64,1024]{2,1,0:T(8,128)(2,1)}, bf16[8,64,1024]{2,1,0:T(8,128)(2,1)}, u32[]{:S(2)}, u32[]{:S(2)}) %collective-permute-start.86) | collective-permute-done | bytes 1048608 | tf_op jit(solution)/shard_map/ppermute | solution.py:25
  748.3 6.7 reshape.270
  755.0 5.2 fusion.32
  764.5 5.0 copy.92
  772.2 3.2 constant_dynamic-update-slice_fusion.60
  775.4 3.6 convolution_convert_fusion.7
  781.3 18.1 %attention_backward.1 = (bf16[1024,256]{1,0:T(8,128)(2,1)}, bf16[1024,128]{1,0:T(8,128)(2,1)}) custom-call(bf16[1024,256]{1,0:T(8,128)(2,1)} %get-tuple-element.19.q_ref, bf16[1024,64]{1,0:T(8,128)(2,1)} %get-tuple-element.20.k_ref, bf16[1024,64]{1,0:T(8,128)(2,1)} %get-tuple-element.21.v_ref, bf16[1024,256]{1,0:T(8,128)(2,1)} %convolution_convert_fusion.8.do_ref, ...), custom_call_target="tpu_custom_call" | custom-call | flops 5368709120 | bytes 2097152 | tf_op jit(solution)/shard_map/attention_backward/pallas_call | solution.py:241
  814.1 6.7 collective-permute-done.81
  820.8 9.2 %collective-permute-start.80 = (bf16[512,384]{1,0:T(8,128)(2,1)S(1)}, bf16[512,384]{1,0:T(8,128)(2,1)S(1)}, u32[]{:S(2)}, u32[]{:S(2)}) collective-permute-start(bf16[512,384]{1,0:T(8,128)(2,1)S(1)} %get-tuple-element.81), channel_id=1, source_target_pairs={{0,24},{8,16},{16,8},{24,0},{1,25},{9,17},{17,9},{25,1},{2,26},{10... | collective-permute-start | bytes 1179656 | tf_op jit(solution)/shard_map/ppermute | solution.py:25
  830.1 4.6 collective-permute-start.84
  837.7 26.7 %collective-permute-done.79 = bf16[512,384]{1,0:T(8,128)(2,1)S(1)} collective-permute-done((bf16[512,384]{1,0:T(8,128)(2,1)S(1)}, bf16[512,384]{1,0:T(8,128)(2,1)S(1)}, u32[]{:S(2)}, u32[]{:S(2)}) %collective-permute-start.79) | collective-permute-done | bytes 393248 | tf_op jit(solution)/shard_map/ppermute | solution.py:25
  865.3 4.7 all-to-all-start.2
  874.1 6.3 all-to-all-done.2
  894.2 4.1 collective-permute-done.74
  900.6 5.3 collective-permute-done.76
  905.9 5.6 collective-permute-done.75
  915.1 3.5 collective-permute-done.77
  (499 shorter events, 281.6 us)
Async XLA Ops:
  2.0 26.1 %collective-permute-start.5 = (f32[128]{0:T(128)}, f32[128]{0:T(128)}, u32[]{:S(2)}, u32[]{:S(2)}) collective-permute-start(f32[128]{0:T(128)} %maximum_convert_fusion.1), channel_id=1, source_target_pairs={{0,8},{8,0},{16,24},{24,16},{1,9},{9,1},{17,25},{25,17},{2,10},{10... | collective-permute-start | bytes 1544 | tf_op jit(solution)/shard_map/ppermute | solution.py:25
  4.1 25.1 %collective-permute-start.6 = (f32[128]{0:T(128)}, f32[128]{0:T(128)}, u32[]{:S(2)}, u32[]{:S(2)}) collective-permute-start(f32[128]{0:T(128)} %maximum_convert_fusion.1), channel_id=1, source_target_pairs={{0,16},{8,24},{16,0},{24,8},{1,17},{9,25},{17,1},{25,9},{2,18},{10... | collective-permute-start | bytes 1544 | tf_op jit(solution)/shard_map/ppermute | solution.py:25
  6.4 24.8 %collective-permute-start.7 = (f32[128]{0:T(128)}, f32[128]{0:T(128)S(1)}, u32[]{:S(2)}, u32[]{:S(2)}) collective-permute-start(f32[128]{0:T(128)} %maximum_convert_fusion.1), channel_id=1, source_target_pairs={{0,24},{8,16},{16,8},{24,0},{1,25},{9,17},{17,9},{25,1},{2,26},{10... | collective-permute-start | bytes 1544 | tf_op jit(solution)/shard_map/ppermute | solution.py:25
  6.4 55.3 %collective-permute-start = (bf16[128,2048]{1,0:T(8,128)(2,1)}, bf16[128,2048]{1,0:T(8,128)(2,1)}, u32[]{:S(2)}, u32[]{:S(2)}) collective-permute-start(bf16[128,2048]{1,0:T(8,128)(2,1)} %bitcast.208), channel_id=1, source_target_pairs={{0,2},{1,3},{2,0},{3,1},{4,6},{5,7},{6,4},{7,5},{8,10},{9,11},{10,... | collective-permute-start | bytes 1572872 | tf_op jit(solution)/shard_map/ppermute | solution.py:25
  7.6 52.7 %collective-permute-start.1 = (bf16[128,2048]{1,0:T(8,128)(2,1)}, bf16[128,2048]{1,0:T(8,128)(2,1)}, u32[]{:S(2)}, u32[]{:S(2)}) collective-permute-start(bf16[128,2048]{1,0:T(8,128)(2,1)} %bitcast.209), channel_id=1, source_target_pairs={{0,4},{1,5},{2,6},{3,7},{4,0},{5,1},{6,2},{7,3},{8,12},{9,13},{10,... | collective-permute-start | bytes 1572872 | tf_op jit(solution)/shard_map/ppermute | solution.py:25
  12.8 47.2 %all-to-all-start = ((bf16[8,64,384]{2,1,0:T(8,128)(2,1)}), bf16[8,64,384]{2,1,0:T(8,128)(2,1)S(1)}, u32[]{:S(2)}, u32[]{:S(2)}) async-start(bf16[8,64,384]{2,1,0:T(8,128)(2,1)} %copy.78), calls=%async_computation | async-start | bytes 786432 | tf_op jit(solution)/shard_map/all_to_all | solution.py:90
  28.1 152.3 %collective-permute-start.56 = (bf16[128,2048]{1,0:T(8,128)(2,1)}, bf16[128,2048]{1,0:T(8,128)(2,1)}, u32[]{:S(2)}, u32[]{:S(2)}) collective-permute-start(bf16[128,2048]{1,0:T(8,128)(2,1)} %bitcast.42), channel_id=1, source_target_pairs={{0,8},{8,0},{16,24},{24,16},{1,9},{9,1},{17,25},{25,17},{2,10},{10... | collective-permute-start | bytes 1572872 | tf_op jit(solution)/shard_map/ppermute | solution.py:25
  29.2 148.9 %collective-permute-start.46 = (bf16[128,2048]{1,0:T(8,128)(2,1)}, bf16[128,2048]{1,0:T(8,128)(2,1)}, u32[]{:S(2)}, u32[]{:S(2)}) collective-permute-start(bf16[128,2048]{1,0:T(8,128)(2,1)} %bitcast.42), channel_id=1, source_target_pairs={{0,2},{1,3},{2,0},{3,1},{4,6},{5,7},{6,4},{7,5},{8,10},{9,11},{10,... | collective-permute-start | bytes 1572872 | tf_op jit(solution)/shard_map/ppermute | solution.py:25
  31.2 22.9 %collective-permute-start.11 = (bf16[64,2048]{1,0:T(8,128)(2,1)S(1)}, bf16[64,2048]{1,0:T(8,128)(2,1)}, u32[]{:S(2)}, u32[]{:S(2)}) collective-permute-start(bf16[64,2048]{1,0:T(8,128)(2,1)S(1)} %copy-done.63), channel_id=1, source_target_pairs={{0,0},{1,8},{2,16},{3,24},{4,1},{5,9},{6,17},{7,25},{8,2},{9,10},{... | collective-permute-start | bytes 786440 | tf_op jit(solution)/shard_map/ppermute | solution.py:328
  54.2 20.3 %collective-permute-start.12 = (bf16[64,2048]{1,0:T(8,128)(2,1)}, bf16[64,2048]{1,0:T(8,128)(2,1)}, u32[]{:S(2)}, u32[]{:S(2)}) collective-permute-start(bf16[64,2048]{1,0:T(8,128)(2,1)} %collective-permute-done.11), channel_id=1, source_target_pairs={{0,8},{8,0},{16,24},{24,16},{1,9},{9,1},{17,25},{25,17},{2,10},{10... | collective-permute-start | bytes 786440 | tf_op jit(solution)/shard_map/ppermute | solution.py:25
  68.7 19.5 %collective-permute-start.13 = (bf16[64,2048]{1,0:T(8,128)(2,1)}, bf16[64,2048]{1,0:T(8,128)(2,1)S(1)}, u32[]{:S(2)}, u32[]{:S(2)}) collective-permute-start(bf16[64,2048]{1,0:T(8,128)(2,1)} %collective-permute-done.11), channel_id=1, source_target_pairs={{0,16},{8,24},{16,0},{24,8},{1,17},{9,25},{17,1},{25,9},{2,18},{10... | collective-permute-start | bytes 786440 | tf_op jit(solution)/shard_map/ppermute | solution.py:25
  71.7 18.0 %collective-permute-start.14 = (bf16[64,2048]{1,0:T(8,128)(2,1)}, bf16[64,2048]{1,0:T(8,128)(2,1)S(1)}, u32[]{:S(2)}, u32[]{:S(2)}) collective-permute-start(bf16[64,2048]{1,0:T(8,128)(2,1)} %collective-permute-done.11), channel_id=1, source_target_pairs={{0,24},{8,16},{16,8},{24,0},{1,25},{9,17},{17,9},{25,1},{2,26},{10... | collective-permute-start | bytes 786440 | tf_op jit(solution)/shard_map/ppermute | solution.py:25
  74.5 57.4 %collective-permute-start.4 = (bf16[512,2048]{1,0:T(8,128)(2,1)S(1)}, bf16[512,2048]{1,0:T(8,128)(2,1)S(1)}, u32[]{:S(2)}, u32[]{:S(2)}) collective-permute-start(bf16[512,2048]{1,0:T(8,128)(2,1)S(1)} %get-tuple-element.145), channel_id=1, source_target_pairs={{0,1},{1,0},{2,3},{3,2},{4,5},{5,4},{6,7},{7,6},{8,9},{9,8},{10,11... | collective-permute-start | bytes 6291464 | tf_op jit(solution)/shard_map/ppermute | solution.py:25
  89.7 33.3 %collective-permute-start.9 = (bf16[512,384]{1,0:T(8,128)(2,1)S(1)}, bf16[512,384]{1,0:T(8,128)(2,1)S(1)}, u32[]{:S(2)}, u32[]{:S(2)}) collective-permute-start(bf16[512,384]{1,0:T(8,128)(2,1)S(1)} %bitcast.236), channel_id=1, source_target_pairs={{0,16},{8,24},{16,0},{24,8},{1,17},{9,25},{17,1},{25,9},{2,18},{10... | collective-permute-start | bytes 1179656 | tf_op jit(solution)/shard_map/ppermute | solution.py:25
  97.1 27.3 %collective-permute-start.10 = (bf16[512,384]{1,0:T(8,128)(2,1)S(1)}, bf16[512,384]{1,0:T(8,128)(2,1)S(1)}, u32[]{:S(2)}, u32[]{:S(2)}) collective-permute-start(bf16[512,384]{1,0:T(8,128)(2,1)S(1)} %bitcast.237), channel_id=1, source_target_pairs={{0,24},{8,16},{16,8},{24,0},{1,25},{9,17},{17,9},{25,1},{2,26},{10... | collective-permute-start | bytes 1179656 | tf_op jit(solution)/shard_map/ppermute | solution.py:25
  123.0 52.7 %collective-permute-start.47 = (bf16[128,2048]{1,0:T(8,128)(2,1)}, bf16[128,2048]{1,0:T(8,128)(2,1)}, u32[]{:S(2)}, u32[]{:S(2)}) collective-permute-start(bf16[128,2048]{1,0:T(8,128)(2,1)} %bitcast.42), channel_id=1, source_target_pairs={{0,4},{1,5},{2,6},{3,7},{4,0},{5,1},{6,2},{7,3},{8,12},{9,13},{10,... | collective-permute-start | bytes 1572872 | tf_op jit(solution)/shard_map/ppermute | solution.py:25
  124.5 37.1 %collective-permute-start.25 = (bf16[8,64,2,256]{3,0,2,1:T(8,128)(2,1)S(1)}, bf16[8,64,2,256]{3,0,2,1:T(8,128)(2,1)S(1)}, u32[]{:S(2)}, u32[]{:S(2)}) collective-permute-start(bf16[8,64,2,256]{3,0,2,1:T(8,128)(2,1)S(1)} %copy-done.33), channel_id=1, source_target_pairs={{0,8},{8,0},{16,24},{24,16},{1,9},{9,1},{17,25},{25,17},{2,10},{10... | collective-permute-start | bytes 1572872 | tf_op jit(solution)/shard_map/ppermute | solution.py:25
  131.9 35.0 %collective-permute-start.26 = (bf16[8,64,2,256]{3,0,2,1:T(8,128)(2,1)S(1)}, bf16[8,64,2,256]{3,0,2,1:T(8,128)(2,1)}, u32[]{:S(2)}, u32[]{:S(2)}) collective-permute-start(bf16[8,64,2,256]{3,0,2,1:T(8,128)(2,1)S(1)} %copy-done.32), channel_id=1, source_target_pairs={{0,8},{8,0},{16,24},{24,16},{1,9},{9,1},{17,25},{25,17},{2,10},{10... | collective-permute-start | bytes 1572872 | tf_op jit(solution)/shard_map/ppermute | solution.py:25
  162.3 56.9 %collective-permute-start.15 = (bf16[512,2048]{1,0:T(8,128)(2,1)}, bf16[512,2048]{1,0:T(8,128)(2,1)}, u32[]{:S(2)}, u32[]{:S(2)}) collective-permute-start(bf16[512,2048]{1,0:T(8,128)(2,1)} %slice.548), channel_id=1, source_target_pairs={{0,1},{1,0},{2,3},{3,2},{4,5},{5,4},{6,7},{7,6},{8,9},{9,8},{10,11... | collective-permute-start | bytes 6291464 | tf_op jit(solution)/shard_map/ppermute | solution.py:25
  171.5 108.8 %all-to-all-start.1 = ((bf16[8,2,64,2,2,256]{5,4,3,2,1,0:T(2,128)(2,1)}), bf16[8,2,64,2,2,256]{5,4,3,2,1,0:T(2,128)(2,1)S(1)}, u32[]{:S(2)}, u32[]{:S(2)}) async-start(bf16[8,2,64,2,2,256]{5,4,3,2,1,0:T(2,128)(2,1)} %copy.84), calls=%async_computation.1 | async-start | bytes 4194304 | tf_op jit(solution)/shard_map/all_to_all | solution.py:90
  176.7 29.5 %collective-permute-start.48 = (bf16[64,2048]{1,0:T(8,128)(2,1)S(1)}, bf16[64,2048]{1,0:T(8,128)(2,1)S(1)}, u32[]{:S(2)}, u32[]{:S(2)}) collective-permute-start(bf16[64,2048]{1,0:T(8,128)(2,1)S(1)} %slice.602), channel_id=1, source_target_pairs={{0,2},{1,3},{2,0},{3,1},{4,6},{5,7},{6,4},{7,5},{8,10},{9,11},{10,... | collective-permute-start | bytes 786440 | tf_op jit(solution)/shard_map/ppermute | solution.py:25
  179.1 28.6 %collective-permute-start.49 = (bf16[64,2048]{1,0:T(8,128)(2,1)S(1)}, bf16[64,2048]{1,0:T(8,128)(2,1)S(1)}, u32[]{:S(2)}, u32[]{:S(2)}) collective-permute-start(bf16[64,2048]{1,0:T(8,128)(2,1)S(1)} %slice.603), channel_id=1, source_target_pairs={{0,4},{1,5},{2,6},{3,7},{4,0},{5,1},{6,2},{7,3},{8,12},{9,13},{10,... | collective-permute-start | bytes 786440 | tf_op jit(solution)/shard_map/ppermute | solution.py:25
  180.4 38.6 %collective-permute-start.57 = (bf16[128,2048]{1,0:T(8,128)(2,1)}, bf16[128,2048]{1,0:T(8,128)(2,1)S(1)}, u32[]{:S(2)}, u32[]{:S(2)}) collective-permute-start(bf16[128,2048]{1,0:T(8,128)(2,1)} %collective-permute-done.56), channel_id=1, source_target_pairs={{0,2},{1,3},{2,0},{3,1},{4,6},{5,7},{6,4},{7,5},{8,10},{9,11},{10,... | collective-permute-start | bytes 1572872 | tf_op jit(solution)/shard_map/ppermute | solution.py:25
  180.6 36.7 %collective-permute-start.58 = (bf16[128,2048]{1,0:T(8,128)(2,1)}, bf16[128,2048]{1,0:T(8,128)(2,1)S(1)}, u32[]{:S(2)}, u32[]{:S(2)}) collective-permute-start(bf16[128,2048]{1,0:T(8,128)(2,1)} %collective-permute-done.56), channel_id=1, source_target_pairs={{0,4},{1,5},{2,6},{3,7},{4,0},{5,1},{6,2},{7,3},{8,12},{9,13},{10,... | collective-permute-start | bytes 1572872 | tf_op jit(solution)/shard_map/ppermute | solution.py:25
  206.2 47.1 %collective-permute-start.28 = (bf16[256,2048]{1,0:T(8,128)(2,1)S(1)}, bf16[256,2048]{1,0:T(8,128)(2,1)S(1)}, u32[]{:S(2)}, u32[]{:S(2)}) collective-permute-start(bf16[256,2048]{1,0:T(8,128)(2,1)S(1)} %copy-done.28), channel_id=1, source_target_pairs={{0,16},{8,24},{16,0},{24,8},{1,17},{9,25},{17,1},{25,9},{2,18},{10... | collective-permute-start | bytes 3145736 | tf_op jit(solution)/shard_map/ppermute | solution.py:25
  208.6 107.6 %collective-permute-start.50 = (bf16[512,2048]{1,0:T(8,128)(2,1)}, bf16[512,2048]{1,0:T(8,128)(2,1)}, u32[]{:S(2)}, u32[]{:S(2)}) collective-permute-start(bf16[512,2048]{1,0:T(8,128)(2,1)} %get-tuple-element.129), channel_id=1, source_target_pairs={{0,1},{1,0},{2,3},{3,2},{4,5},{5,4},{6,7},{7,6},{8,9},{9,8},{10,11... | collective-permute-start | bytes 6291464 | tf_op jit(solution)/shard_map/ppermute | solution.py:25
  217.3 56.5 %collective-permute-start.59 = (bf16[64,2048]{1,0:T(8,128)(2,1)S(1)}, bf16[64,2048]{1,0:T(8,128)(2,1)S(1)}, u32[]{:S(2)}, u32[]{:S(2)}) collective-permute-start(bf16[64,2048]{1,0:T(8,128)(2,1)S(1)} %slice.618), channel_id=1, source_target_pairs={{0,2},{1,3},{2,0},{3,1},{4,6},{5,7},{6,4},{7,5},{8,10},{9,11},{10,... | collective-permute-start | bytes 786440 | tf_op jit(solution)/shard_map/ppermute | solution.py:25
  219.0 55.6 %collective-permute-start.60 = (bf16[64,2048]{1,0:T(8,128)(2,1)S(1)}, bf16[64,2048]{1,0:T(8,128)(2,1)S(1)}, u32[]{:S(2)}, u32[]{:S(2)}) collective-permute-start(bf16[64,2048]{1,0:T(8,128)(2,1)S(1)} %slice.619), channel_id=1, source_target_pairs={{0,4},{1,5},{2,6},{3,7},{4,0},{5,1},{6,2},{7,3},{8,12},{9,13},{10,... | collective-permute-start | bytes 786440 | tf_op jit(solution)/shard_map/ppermute | solution.py:25
  221.7 33.4 %collective-permute-start.16 = (bf16[128,2048]{1,0:T(8,128)(2,1)S(1)}, bf16[128,2048]{1,0:T(8,128)(2,1)S(1)}, u32[]{:S(2)}, u32[]{:S(2)}) collective-permute-start(bf16[128,2048]{1,0:T(8,128)(2,1)S(1)} %pad_maximum_fusion.9), channel_id=1, source_target_pairs={{0,4},{1,5},{2,6},{3,7},{4,0},{5,1},{6,2},{7,3},{8,12},{9,13},{10,... | collective-permute-start | bytes 1572872 | tf_op jit(solution)/shard_map/ppermute | solution.py:25
  255.2 16.6 %collective-permute-start.17 = (bf16[64,2048]{1,0:T(8,128)(2,1)S(1)}, bf16[64,2048]{1,0:T(8,128)(2,1)S(1)}, u32[]{:S(2)}, u32[]{:S(2)}) collective-permute-start(bf16[64,2048]{1,0:T(8,128)(2,1)S(1)} %add_convert_fusion.23), channel_id=1, source_target_pairs={{0,2},{1,3},{2,0},{3,1},{4,6},{5,7},{6,4},{7,5},{8,10},{9,11},{10,... | collective-permute-start | bytes 786440 | tf_op jit(solution)/shard_map/ppermute | solution.py:25
  272.7 15.0 %collective-permute-start.19 = (bf16[64,2048]{1,0:T(8,128)(2,1)}, bf16[64,2048]{1,0:T(8,128)(2,1)S(1)}, u32[]{:S(2)}, u32[]{:S(2)}) collective-permute-start(bf16[64,2048]{1,0:T(8,128)(2,1)} %get-tuple-element.75), channel_id=1, source_target_pairs={{0,4},{1,5},{2,6},{3,7},{4,0},{5,1},{6,2},{7,3},{8,12},{9,13},{10,... | collective-permute-start | bytes 786440 | tf_op jit(solution)/shard_map/ppermute | solution.py:25
  277.3 43.0 %collective-permute-start.61 = (bf16[512,2048]{1,0:T(8,128)(2,1)}, bf16[512,2048]{1,0:T(8,128)(2,1)}, u32[]{:S(2)}, u32[]{:S(2)}) collective-permute-start(bf16[512,2048]{1,0:T(8,128)(2,1)} %get-tuple-element.133), channel_id=1, source_target_pairs={{0,1},{1,0},{2,3},{3,2},{4,5},{5,4},{6,7},{7,6},{8,9},{9,8},{10,11... | collective-permute-start | bytes 6291464 | tf_op jit(solution)/shard_map/ppermute | solution.py:25
  287.7 93.6 %collective-permute-start.27 = (bf16[2,512,1024]{2,1,0:T(8,128)(2,1)}, bf16[2,512,1024]{2,1,0:T(8,128)(2,1)}, u32[]{:S(2)}, u32[]{:S(2)}) collective-permute-start(bf16[2,512,1024]{2,1,0:T(8,128)(2,1)} %reshape.254), channel_id=1, source_target_pairs={{0,16},{8,24},{16,0},{24,8},{1,17},{9,25},{17,1},{25,9},{2,18},{10... | collective-permute-start | bytes 6291464 | tf_op jit(solution)/shard_map/ppermute | solution.py:25
  290.2 16.1 %collective-permute-start.20 = (bf16[128,2048]{1,0:T(8,128)(2,1)}, bf16[128,2048]{1,0:T(8,128)(2,1)}, u32[]{:S(2)}, u32[]{:S(2)}) collective-permute-start(bf16[128,2048]{1,0:T(8,128)(2,1)} %get-tuple-element.31), channel_id=1, source_target_pairs={{0,2},{1,3},{2,0},{3,1},{4,6},{5,7},{6,4},{7,5},{8,10},{9,11},{10,... | collective-permute-start | bytes 1572872 | tf_op jit(solution)/shard_map/ppermute | solution.py:25
  313.9 92.0 %collective-permute-start.24 = (bf16[512,2048]{1,0:T(8,128)(2,1)S(1)}, bf16[512,2048]{1,0:T(8,128)(2,1)S(1)}, u32[]{:S(2)}, u32[]{:S(2)}) collective-permute-start(bf16[512,2048]{1,0:T(8,128)(2,1)S(1)} %get-tuple-element.137), channel_id=1, source_target_pairs={{0,1},{1,0},{2,3},{3,2},{4,5},{5,4},{6,7},{7,6},{8,9},{9,8},{10,11... | collective-permute-start | bytes 6291464 | tf_op jit(solution)/shard_map/ppermute | solution.py:25
  318.0 64.6 %collective-permute-start.34 = (bf16[128,2048]{1,0:T(8,128)(2,1)}, bf16[128,2048]{1,0:T(8,128)(2,1)S(1)}, u32[]{:S(2)}, u32[]{:S(2)}) collective-permute-start(bf16[128,2048]{1,0:T(8,128)(2,1)} %get-tuple-element.31), channel_id=1, source_target_pairs={{0,8},{8,0},{16,24},{24,16},{1,9},{9,1},{17,25},{25,17},{2,10},{10... | collective-permute-start | bytes 1572872 | tf_op jit(solution)/shard_map/ppermute | solution.py:25
  403.0 31.1 %collective-permute-start.39 = (bf16[512,2048]{1,0:T(8,128)(2,1)S(1)}, bf16[512,2048]{1,0:T(8,128)(2,1)S(1)}, u32[]{:S(2)}, u32[]{:S(2)}) collective-permute-start(bf16[512,2048]{1,0:T(8,128)(2,1)S(1)} %get-tuple-element.141), channel_id=1, source_target_pairs={{0,1},{1,0},{2,3},{3,2},{4,5},{5,4},{6,7},{7,6},{8,9},{9,8},{10,11... | collective-permute-start | bytes 6291464 | tf_op jit(solution)/shard_map/ppermute | solution.py:25
  426.0 65.3 %collective-permute-start.29 = (bf16[512,2048]{1,0:T(8,128)(2,1)}, bf16[512,2048]{1,0:T(8,128)(2,1)}, u32[]{:S(2)}, u32[]{:S(2)}) collective-permute-start(bf16[512,2048]{1,0:T(8,128)(2,1)} %slice.571), channel_id=1, source_target_pairs={{0,1},{1,0},{2,3},{3,2},{4,5},{5,4},{6,7},{7,6},{8,9},{9,8},{10,11... | collective-permute-start | bytes 6291464 | tf_op jit(solution)/shard_map/ppermute | solution.py:25
  434.2 61.8 %collective-permute-start.51 = (bf16[512,2048]{1,0:T(8,128)(2,1)}, bf16[512,2048]{1,0:T(8,128)(2,1)S(1)}, u32[]{:S(2)}, u32[]{:S(2)}) collective-permute-start(bf16[512,2048]{1,0:T(8,128)(2,1)} %slice.605), channel_id=1, source_target_pairs={{0,1},{1,0},{2,3},{3,2},{4,5},{5,4},{6,7},{7,6},{8,9},{9,8},{10,11... | collective-permute-start | bytes 6291464 | tf_op jit(solution)/shard_map/ppermute | solution.py:25
  469.1 92.5 %collective-permute-start.85 = (bf16[2,512,1024]{2,1,0:T(8,128)(2,1)}, bf16[2,512,1024]{2,1,0:T(8,128)(2,1)}, u32[]{:S(2)}, u32[]{:S(2)}) collective-permute-start(bf16[2,512,1024]{2,1,0:T(8,128)(2,1)} %dynamic-slice_bitcast_fusion), channel_id=1, source_target_pairs={{0,16},{8,24},{16,0},{24,8},{1,17},{9,25},{17,1},{25,9},{2,18},{10... | collective-permute-start | bytes 6291464 | tf_op jit(solution)/shard_map/ppermute | solution.py:25
  475.8 96.9 %collective-permute-start.40 = (bf16[512,2048]{1,0:T(8,128)(2,1)}, bf16[512,2048]{1,0:T(8,128)(2,1)}, u32[]{:S(2)}, u32[]{:S(2)}) collective-permute-start(bf16[512,2048]{1,0:T(8,128)(2,1)} %slice.589), channel_id=1, source_target_pairs={{0,1},{1,0},{2,3},{3,2},{4,5},{5,4},{6,7},{7,6},{8,9},{9,8},{10,11... | collective-permute-start | bytes 6291464 | tf_op jit(solution)/shard_map/ppermute | solution.py:25
  485.7 91.6 %collective-permute-start.62 = (bf16[512,2048]{1,0:T(8,128)(2,1)}, bf16[512,2048]{1,0:T(8,128)(2,1)}, u32[]{:S(2)}, u32[]{:S(2)}) collective-permute-start(bf16[512,2048]{1,0:T(8,128)(2,1)} %slice.621), channel_id=1, source_target_pairs={{0,1},{1,0},{2,3},{3,2},{4,5},{5,4},{6,7},{7,6},{8,9},{9,8},{10,11... | collective-permute-start | bytes 6291464 | tf_op jit(solution)/shard_map/ppermute | solution.py:25
  494.8 111.9 %collective-permute-start.32 = (bf16[128,2048]{1,0:T(8,128)(2,1)}, bf16[128,2048]{1,0:T(8,128)(2,1)}, u32[]{:S(2)}, u32[]{:S(2)}) collective-permute-start(bf16[128,2048]{1,0:T(8,128)(2,1)} %pad_maximum_fusion.12), channel_id=1, source_target_pairs={{0,2},{1,3},{2,0},{3,1},{4,6},{5,7},{6,4},{7,5},{8,10},{9,11},{10,... | collective-permute-start | bytes 1572872 | tf_op jit(solution)/shard_map/ppermute | solution.py:25
  496.0 74.3 %collective-permute-start.30 = (bf16[128,2048]{1,0:T(8,128)(2,1)}, bf16[128,2048]{1,0:T(8,128)(2,1)}, u32[]{:S(2)}, u32[]{:S(2)}) collective-permute-start(bf16[128,2048]{1,0:T(8,128)(2,1)} %pad_maximum_fusion.11), channel_id=1, source_target_pairs={{0,4},{1,5},{2,6},{3,7},{4,0},{5,1},{6,2},{7,3},{8,12},{9,13},{10,... | collective-permute-start | bytes 1572872 | tf_op jit(solution)/shard_map/ppermute | solution.py:25
  561.6 48.0 %collective-permute-start.54 = (bf16[128,2048]{1,0:T(8,128)(2,1)}, bf16[128,2048]{1,0:T(8,128)(2,1)}, u32[]{:S(2)}, u32[]{:S(2)}) collective-permute-start(bf16[128,2048]{1,0:T(8,128)(2,1)} %pad_maximum_fusion.17), channel_id=1, source_target_pairs={{0,2},{1,3},{2,0},{3,1},{4,6},{5,7},{6,4},{7,5},{8,10},{9,11},{10,... | collective-permute-start | bytes 1572872 | tf_op jit(solution)/shard_map/ppermute | solution.py:25
  566.0 133.4 %all-to-all-start.3 = ((bf16[8,2,64,1024]{3,2,1,0:T(8,128)(2,1)}), bf16[8,2,64,1024]{3,2,1,0:T(8,128)(2,1)S(1)}, u32[]{:S(2)}, u32[]{:S(2)}) async-start(bf16[8,2,64,1024]{3,2,1,0:T(8,128)(2,1)} %copy.90), calls=%async_computation.3 | async-start | bytes 4194304 | tf_op jit(solution)/shard_map/all_to_all | solution.py:90
  570.2 36.1 %collective-permute-start.52 = (bf16[128,2048]{1,0:T(8,128)(2,1)}, bf16[128,2048]{1,0:T(8,128)(2,1)S(1)}, u32[]{:S(2)}, u32[]{:S(2)}) collective-permute-start(bf16[128,2048]{1,0:T(8,128)(2,1)} %pad_maximum_fusion.16), channel_id=1, source_target_pairs={{0,4},{1,5},{2,6},{3,7},{4,0},{5,1},{6,2},{7,3},{8,12},{9,13},{10,... | collective-permute-start | bytes 1572872 | tf_op jit(solution)/shard_map/ppermute | solution.py:25
  572.7 35.3 %collective-permute-start.31 = (bf16[64,2048]{1,0:T(8,128)(2,1)S(1)}, bf16[64,2048]{1,0:T(8,128)(2,1)S(1)}, u32[]{:S(2)}, u32[]{:S(2)}) collective-permute-start(bf16[64,2048]{1,0:T(8,128)(2,1)S(1)} %add_convert_fusion.21), channel_id=1, source_target_pairs={{0,2},{1,3},{2,0},{3,1},{4,6},{5,7},{6,4},{7,5},{8,10},{9,11},{10,... | collective-permute-start | bytes 786440 | tf_op jit(solution)/shard_map/ppermute | solution.py:25
  577.3 54.0 %collective-permute-start.43 = (bf16[128,2048]{1,0:T(8,128)(2,1)S(1)}, bf16[128,2048]{1,0:T(8,128)(2,1)S(1)}, u32[]{:S(2)}, u32[]{:S(2)}) collective-permute-start(bf16[128,2048]{1,0:T(8,128)(2,1)S(1)} %pad_maximum_fusion.14), channel_id=1, source_target_pairs={{0,2},{1,3},{2,0},{3,1},{4,6},{5,7},{6,4},{7,5},{8,10},{9,11},{10,... | collective-permute-start | bytes 1572872 | tf_op jit(solution)/shard_map/ppermute | solution.py:25
  606.3 15.0 %collective-permute-start.41 = (bf16[128,2048]{1,0:T(8,128)(2,1)S(1)}, bf16[128,2048]{1,0:T(8,128)(2,1)S(1)}, u32[]{:S(2)}, u32[]{:S(2)}) collective-permute-start(bf16[128,2048]{1,0:T(8,128)(2,1)S(1)} %pad_maximum_fusion.13), channel_id=1, source_target_pairs={{0,4},{1,5},{2,6},{3,7},{4,0},{5,1},{6,2},{7,3},{8,12},{9,13},{10,... | collective-permute-start | bytes 1572872 | tf_op jit(solution)/shard_map/ppermute | solution.py:25
  608.0 28.4 %collective-permute-start.65 = (bf16[128,2048]{1,0:T(8,128)(2,1)S(1)}, bf16[128,2048]{1,0:T(8,128)(2,1)S(1)}, u32[]{:S(2)}, u32[]{:S(2)}) collective-permute-start(bf16[128,2048]{1,0:T(8,128)(2,1)S(1)} %pad_maximum_fusion.19), channel_id=1, source_target_pairs={{0,2},{1,3},{2,0},{3,1},{4,6},{5,7},{6,4},{7,5},{8,10},{9,11},{10,... | collective-permute-start | bytes 1572872 | tf_op jit(solution)/shard_map/ppermute | solution.py:25
  609.6 20.5 %collective-permute-start.63 = (bf16[128,2048]{1,0:T(8,128)(2,1)S(1)}, bf16[128,2048]{1,0:T(8,128)(2,1)S(1)}, u32[]{:S(2)}, u32[]{:S(2)}) collective-permute-start(bf16[128,2048]{1,0:T(8,128)(2,1)S(1)} %pad_maximum_fusion.18), channel_id=1, source_target_pairs={{0,4},{1,5},{2,6},{3,7},{4,0},{5,1},{6,2},{7,3},{8,12},{9,13},{10,... | collective-permute-start | bytes 1572872 | tf_op jit(solution)/shard_map/ppermute | solution.py:25
  619.9 31.9 %collective-permute-start.33 = (bf16[64,2048]{1,0:T(8,128)(2,1)S(1)}, bf16[64,2048]{1,0:T(8,128)(2,1)S(1)}, u32[]{:S(2)}, u32[]{:S(2)}) collective-permute-start(bf16[64,2048]{1,0:T(8,128)(2,1)S(1)} %get-tuple-element.61), channel_id=1, source_target_pairs={{0,4},{1,5},{2,6},{3,7},{4,0},{5,1},{6,2},{7,3},{8,12},{9,13},{10,... | collective-permute-start | bytes 786440 | tf_op jit(solution)/shard_map/ppermute | solution.py:25
  621.3 31.7 %collective-permute-start.55 = (bf16[64,2048]{1,0:T(8,128)(2,1)S(1)}, bf16[64,2048]{1,0:T(8,128)(2,1)S(1)}, u32[]{:S(2)}, u32[]{:S(2)}) collective-permute-start(bf16[64,2048]{1,0:T(8,128)(2,1)S(1)} %get-tuple-element.49), channel_id=1, source_target_pairs={{0,4},{1,5},{2,6},{3,7},{4,0},{5,1},{6,2},{7,3},{8,12},{9,13},{10,... | collective-permute-start | bytes 786440 | tf_op jit(solution)/shard_map/ppermute | solution.py:25
  674.8 48.7 %collective-permute-start.87 = (bf16[256,2048]{1,0:T(8,128)(2,1)}, bf16[256,2048]{1,0:T(8,128)(2,1)}, u32[]{:S(2)}, u32[]{:S(2)}) collective-permute-start(bf16[256,2048]{1,0:T(8,128)(2,1)} %dynamic-slice_bitcast_fusion.1), channel_id=1, source_target_pairs={{0,16},{8,24},{16,0},{24,8},{1,17},{9,25},{17,1},{25,9},{2,18},{10... | collective-permute-start | bytes 3145736 | tf_op jit(solution)/shard_map/ppermute | solution.py:25
  691.0 81.2 %collective-permute-start.72 = (bf16[512,2048]{1,0:T(8,128)(2,1)}, bf16[512,2048]{1,0:T(8,128)(2,1)}, u32[]{:S(2)}, u32[]{:S(2)}) collective-permute-start(bf16[512,2048]{1,0:T(8,128)(2,1)} %get-tuple-element.125), channel_id=1, source_target_pairs={{0,1},{1,0},{2,3},{3,2},{4,5},{5,4},{6,7},{7,6},{8,9},{9,8},{10,11... | collective-permute-start | bytes 6291464 | tf_op jit(solution)/shard_map/ppermute | solution.py:25
  700.5 45.6 %collective-permute-start.86 = (bf16[8,64,1024]{2,1,0:T(8,128)(2,1)}, bf16[8,64,1024]{2,1,0:T(8,128)(2,1)}, u32[]{:S(2)}, u32[]{:S(2)}) collective-permute-start(bf16[8,64,1024]{2,1,0:T(8,128)(2,1)} %dynamic-slice_bitcast_fusion.2), channel_id=1, source_target_pairs={{0,8},{8,0},{16,24},{24,16},{1,9},{9,1},{17,25},{25,17},{2,10},{10... | collective-permute-start | bytes 3145736 | tf_op jit(solution)/shard_map/ppermute | solution.py:25
  807.0 73.5 %collective-permute-start.73 = (bf16[512,2048]{1,0:T(8,128)(2,1)}, bf16[512,2048]{1,0:T(8,128)(2,1)}, u32[]{:S(2)}, u32[]{:S(2)}) collective-permute-start(bf16[512,2048]{1,0:T(8,128)(2,1)} %slice.637), channel_id=1, source_target_pairs={{0,1},{1,0},{2,3},{3,2},{4,5},{5,4},{6,7},{7,6},{8,9},{9,8},{10,11... | collective-permute-start | bytes 6291464 | tf_op jit(solution)/shard_map/ppermute | solution.py:25
  810.1 19.9 %collective-permute-start.83 = (bf16[64,2048]{1,0:T(8,128)(2,1)S(1)}, bf16[64,2048]{1,0:T(8,128)(2,1)S(1)}, u32[]{:S(2)}, u32[]{:S(2)}) collective-permute-start(bf16[64,2048]{1,0:T(8,128)(2,1)S(1)} %get-tuple-element.85), channel_id=1, source_target_pairs={{0,24},{8,16},{16,8},{24,0},{1,25},{9,17},{17,9},{25,1},{2,26},{10... | collective-permute-start | bytes 786440 | tf_op jit(solution)/shard_map/ppermute | solution.py:25
  814.0 23.7 %collective-permute-start.78 = (bf16[512,384]{1,0:T(8,128)(2,1)S(1)}, bf16[512,384]{1,0:T(8,128)(2,1)S(1)}, u32[]{:S(2)}, u32[]{:S(2)}) collective-permute-start(bf16[512,384]{1,0:T(8,128)(2,1)S(1)} %get-tuple-element.80), channel_id=1, source_target_pairs={{0,8},{8,0},{16,24},{24,16},{1,9},{9,1},{17,25},{25,17},{2,10},{10... | collective-permute-start | bytes 1179656 | tf_op jit(solution)/shard_map/ppermute | solution.py:25
  820.8 43.6 %collective-permute-start.79 = (bf16[512,384]{1,0:T(8,128)(2,1)S(1)}, bf16[512,384]{1,0:T(8,128)(2,1)S(1)}, u32[]{:S(2)}, u32[]{:S(2)}) collective-permute-start(bf16[512,384]{1,0:T(8,128)(2,1)S(1)} %get-tuple-element.82), channel_id=1, source_target_pairs={{0,16},{8,24},{16,0},{24,8},{1,17},{9,25},{17,1},{25,9},{2,18},{10... | collective-permute-start | bytes 1179656 | tf_op jit(solution)/shard_map/ppermute | solution.py:25
  820.8 43.6 %collective-permute-start.80 = (bf16[512,384]{1,0:T(8,128)(2,1)S(1)}, bf16[512,384]{1,0:T(8,128)(2,1)S(1)}, u32[]{:S(2)}, u32[]{:S(2)}) collective-permute-start(bf16[512,384]{1,0:T(8,128)(2,1)S(1)} %get-tuple-element.81), channel_id=1, source_target_pairs={{0,24},{8,16},{16,8},{24,0},{1,25},{9,17},{17,9},{25,1},{2,26},{10... | collective-permute-start | bytes 1179656 | tf_op jit(solution)/shard_map/ppermute | solution.py:25
  830.1 43.1 %collective-permute-start.84 = (bf16[64,2048]{1,0:T(8,128)(2,1)S(1)}, bf16[64,2048]{1,0:T(8,128)(2,1)S(1)}, u32[]{:S(2)}, u32[]{:S(2)}) collective-permute-start(bf16[64,2048]{1,0:T(8,128)(2,1)S(1)} %fusion.25), channel_id=1, source_target_pairs={{0,0},{8,1},{16,2},{24,3},{1,4},{9,5},{17,6},{25,7},{2,8},{10,9},{... | collective-permute-start | bytes 786440 | tf_op jit(solution)/shard_map/ppermute | solution.py:417
  865.3 15.1 %all-to-all-start.2 = ((bf16[8,64,384]{2,1,0:T(8,128)(2,1)}), bf16[8,64,384]{2,1,0:T(8,128)(2,1)S(1)}, u32[]{:S(2)}, u32[]{:S(2)}) async-start(bf16[8,64,384]{2,1,0:T(8,128)(2,1)} %bitcast.49), calls=%async_computation.2 | async-start | bytes 786432 | tf_op jit(solution)/shard_map/all_to_all | solution.py:90
  (102 other events, 1407.9 us)

commit v2 on v1

v2 whole, which is shorter than its diff:
```python
import functools

import jax
import jax.numpy as jnp
from jax import lax
from jax.experimental import pallas as pl
from jax.experimental.pallas import tpu as pltpu
from jax.sharding import PartitionSpec as P

HEADS = 32
KV_HEADS = 8
HEAD_DIM = 64
EPSILON = 1e-05
ROPE_BASE = 500000.0
VMEM_LIMIT = 56 * 1024 * 1024
LOW = jnp.bfloat16
WIDE = jnp.float32


def dot(left, right, dims=((1,), (0,)), out=WIDE):
    return lax.dot_general(left, right, (dims, ((), ())), preferred_element_type=WIDE).astype(out)


def tie(*values):
    return lax.optimization_barrier(values)


def swap(block, axis, mask):
    count = lax.axis_size(axis)
    return lax.ppermute(block, axis, [(i, i ^ mask) for i in range(count)])


def pick(stack, index):
    return lax.dynamic_index_in_dim(stack, index, 0, keepdims=False)


def in_order(pieces, base):
    out = jnp.zeros((len(pieces),) + pieces[0].shape, pieces[0].dtype)
    for r, piece in enumerate(pieces):
        out = lax.dynamic_update_index_in_dim(out, piece, base ^ r, 0)
    return out


def ctx_order(count):
    order = [0]
    bit = 2
    while bit < count:
        order = order + [k ^ bit for k in order]
        bit *= 2
    return order + [k ^ 1 for k in order]


def gather_near(block):
    count = lax.axis_size("ctx")
    return (swap(block, "ctx", 2), swap(block, "ctx", 4)) if count == 8 else ()


def gather_far(block, near):
    count = lax.axis_size("ctx")
    if count == 8:
        near_x, near_y = near
        half = block.shape[0] // 2
        return block, near_x, near_y, swap(near_y[:half], "ctx", 2), swap(near_x[half:], "ctx", 4)
    even, bit = (block,), 2
    while bit < count:
        even = even + tuple(swap(part, "ctx", bit) for part in even)
        bit *= 2
    return even


def gather_core(even):
    quad = jnp.concatenate(even, axis=0)
    return quad, swap(quad, "ctx", 1)


def scatter_core(odd):
    return swap(odd, "ctx", 1)


def scatter_far(even, odd):
    count = lax.axis_size("ctx")
    quad = even.astype(WIDE) + odd.astype(WIDE)
    if count != 8:
        return (quad,)
    quad = quad.astype(LOW)
    rows = quad.shape[0] // 4
    half = rows // 2
    own, to_x, to_y, far = (quad[j * rows : (j + 1) * rows] for j in range(4))
    far_x, far_y = swap(far[half:], "ctx", 2), swap(far[:half], "ctx", 4)
    by_x, by_y = swap(to_x[half:], "ctx", 2), swap(to_y[:half], "ctx", 4)
    return own, to_x[:half], to_y[half:], by_x, by_y, far_x, far_y


def scatter_near(state):
    count = lax.axis_size("ctx")
    if count != 8:
        (quad,) = state
        bit = count // 2
        while bit >= 2:
            middle = quad.shape[0] // 2
            quad = quad[:middle] + swap(quad[middle:].astype(LOW), "ctx", bit).astype(WIDE)
            bit //= 2
        return (quad,)
    own, to_x, to_y, by_x, by_y, far_x, far_y = state
    last_x = swap((to_x.astype(WIDE) + far_y.astype(WIDE)).astype(LOW), "ctx", 2)
    last_y = swap((to_y.astype(WIDE) + far_x.astype(WIDE)).astype(LOW), "ctx", 4)
    return own, by_x, by_y, last_x, last_y


def scatter_end(state):
    if len(state) == 1:
        return state[0]
    own, by_x, by_y, last_x, last_y = state
    half = last_x.shape[0]
    top = own[:half].astype(WIDE) + last_x.astype(WIDE) + by_y.astype(WIDE)
    low = own[half:].astype(WIDE) + by_x.astype(WIDE) + last_y.astype(WIDE)
    return jnp.concatenate([top, low], axis=0)


def exchange_ctx(stack):
    return lax.all_to_all(stack, "ctx", 0, 0, tiled=True)


def double_fsdp(stack, first, last):
    bits, bit = [], first
    while bit >= last:
        bits.append(bit)
        bit //= 2
    for bit in bits:
        stack = jnp.concatenate([stack, swap(stack, "fsdp", bit)], axis=0)
    return stack


def xor_order(first, last):
    order, bit = [0], first
    while bit >= last:
        order = order + [k ^ bit for k in order]
        bit //= 2
    return order


def place_kernel(spots, rows, base_ref, *refs):
    out_ref = refs[-1]
    for (mask, offset), part in zip(spots, refs[:-1]):
        start = pl.multiple_of((base_ref[0] ^ mask) * rows + offset, 16)
        out_ref[pl.ds(start, part.shape[0]), :] = part[...]


def place(parts, base, count):
    columns = parts[0][2].shape[1]
    total = sum(part.shape[0] for _, _, part in parts)
    whole = pl.BlockSpec(memory_space=pltpu.VMEM)
    return pl.pallas_call(
        functools.partial(place_kernel, [(m, o) for m, o, _ in parts], total // count),
        in_specs=[pl.BlockSpec(memory_space=pltpu.SMEM)] + [whole] * len(parts),
        out_specs=whole,
        out_shape=jax.ShapeDtypeStruct((total, columns), parts[0][2].dtype),
        compiler_params=pltpu.CompilerParams(vmem_limit_bytes=VMEM_LIMIT),
        cost_estimate=pl.CostEstimate(flops=0, bytes_accessed=total * columns * 2, transcendentals=0),
        name="place",
    )(base.reshape(1), *[part for _, _, part in parts])


def halve_fsdp(stack, base, first, last):
    bit = first
    while bit >= last:
        low = stack.shape[0] // 2
        side = (base // bit) % 2
        pair = stack.reshape((2, low) + stack.shape[1:])
        mine, theirs = pick(pair, side), pick(pair, 1 - side)
        stack = (mine.astype(WIDE) + swap(theirs, "fsdp", bit).astype(WIDE)).astype(LOW)
        bit //= 2
    return stack if stack.shape[0] > 1 else stack[0]


def halve_near(stack, base):
    pair = stack.reshape((stack.shape[0] // 2, 2) + stack.shape[1:]).swapaxes(0, 1)
    mine, theirs = pick(pair, base % 2), pick(pair, 1 - base % 2)
    return (mine.astype(WIDE) + swap(theirs, "fsdp", 1).astype(WIDE)).astype(LOW)


def halve_far(stack, base, first):
    return halve_fsdp(stack, base, first, 2)


def turned(block, cosine, sine):
    lane = lax.broadcasted_iota(jnp.int32, block.shape, 1)
    first = (lane % HEAD_DIM) < HEAD_DIM // 2
    width = block.shape[1]
    other = jnp.where(
        first, pltpu.roll(block, width - HEAD_DIM // 2, 1), pltpu.roll(block, HEAD_DIM // 2, 1)
    )
    return block * cosine + other * sine


def forward_kernel(
    heads, q_ref, kv_ref, cos_ref, sin_ref, cosk_ref, sink_ref, row_ref, col_ref,
    mixed_ref, lse_ref, qs_ref, kr_ref, vl_ref, vt_ref,
):
    @pl.when(pl.program_id(0) == 0)
    def _():
        keys = turned(kv_ref[...], cosk_ref[...], sink_ref[...])
        kr_ref[...] = keys[:, :HEAD_DIM].astype(LOW)
        values = kv_ref[...][:, HEAD_DIM:].astype(LOW)
        vl_ref[...] = values
        vt_ref[...] = values.astype(WIDE).T.astype(LOW)

    cosine, sine = cos_ref[...], sin_ref[...]
    keys = kr_ref[...]
    values_t = vt_ref[...]
    visible = col_ref[...] <= row_ref[...]
    scale = HEAD_DIM ** (-0.5)
    mixed, totals = [], []
    for pair in range(heads // 2):
        both = turned(q_ref[:, pair * 128 : pair * 128 + 128], cosine, sine)
        both = (both.astype(LOW).astype(WIDE) * scale).astype(LOW)
        qs_ref[:, pair * 128 : pair * 128 + 128] = both
        for side in range(2):
            query = both[:, side * HEAD_DIM : (side + 1) * HEAD_DIM]
            scores = jnp.where(visible, dot(keys, query, ((1,), (1,))), -1e30)
            top = jnp.max(scores, axis=0, keepdims=True)
            weights = jnp.exp(scores - top)
            total = jnp.sum(weights, axis=0, keepdims=True)
            out = dot(values_t, weights.astype(LOW)) / total
            mixed.append(out)
            totals.append(top + jnp.log(total))
    mixed_ref[...] = jnp.concatenate(mixed, axis=0).T.astype(LOW)
    pad = [jnp.zeros_like(totals[0])] * (8 - heads)
    lse_ref[...] = jnp.concatenate(totals + pad, axis=0)


def backward_kernel(
    heads, steps, q_ref, k_ref, v_ref, do_ref, lse_ref, cos_ref, sin_ref, cosk_ref, sink_ref,
    row_ref, col_ref, dq_ref, dkv_ref, kt_ref, dk_ref, dv_ref,
):
    @pl.when(pl.program_id(0) == 0)
    def _():
        kt_ref[...] = k_ref[...].astype(WIDE).T.astype(LOW)
        dk_ref[...] = jnp.zeros_like(dk_ref)
        dv_ref[...] = jnp.zeros_like(dv_ref)

    keys, values, keys_t = k_ref[...], v_ref[...], kt_ref[...]
    visible = col_ref[...] <= row_ref[...]
    scale = HEAD_DIM ** (-0.5)
    grads = []
    for head in range(heads):
        lanes = slice(head * HEAD_DIM, (head + 1) * HEAD_DIM)
        query, grad_out = q_ref[:, lanes], do_ref[:, lanes]
        scores = dot(keys, query, ((1,), (1,)))
        probs = jnp.where(visible, jnp.exp(scores - lse_ref[head : head + 1, :]), 0.0)
        grad_probs = dot(values, grad_out, ((1,), (1,)))
        product = probs * grad_probs
        delta = jnp.sum(product, axis=0, keepdims=True)
        grad_scores = (product - probs * delta).astype(LOW)
        dv_ref[...] += dot(probs.astype(LOW), grad_out)
        dk_ref[...] += dot(grad_scores, query)
        grads.append(dot(keys_t, grad_scores) * scale)
    grad_q = jnp.concatenate(grads, axis=0).T
    cosine, sine = cos_ref[...], sin_ref[...]
    for pair in range(heads // 2):
        lanes = slice(pair * 128, pair * 128 + 128)
        dq_ref[:, lanes] = turned(grad_q[:, lanes], cosine, -sine).astype(LOW)

    @pl.when(pl.program_id(0) == steps - 1)
    def _():
        both = jnp.concatenate([dk_ref[...], dv_ref[...]], axis=1)
        back = turned(both, cosk_ref[...], -sink_ref[...])
        lane = lax.broadcasted_iota(jnp.int32, both.shape, 1)
        dkv_ref[...] = jnp.where(lane < HEAD_DIM, back, both).astype(LOW)


def attention_forward(qkv, cosine, sine, places, heads):
    length = qkv.shape[0]
    width = heads * HEAD_DIM
    block = min(256, length)
    whole = lambda shape: pl.BlockSpec(shape, lambda i: (0,) * len(shape))
    rows = lambda columns: pl.BlockSpec((block, columns), lambda i: (i, 0))
    return pl.pallas_call(
        functools.partial(forward_kernel, heads),
        grid=(length // block,),
        in_specs=[
            rows(width),
            pl.BlockSpec((length, 128), lambda i: (0, width // 128)),
            rows(128), rows(128), whole((length, 128)), whole((length, 128)),
            pl.BlockSpec((1, block), lambda i: (0, i)), whole((length, 1)),
        ],
        out_specs=[
            rows(width), pl.BlockSpec((8, block), lambda i: (0, i)), rows(width),
            whole((length, HEAD_DIM)), whole((length, HEAD_DIM)),
        ],
        out_shape=[
            jax.ShapeDtypeStruct((length, width), LOW),
            jax.ShapeDtypeStruct((8, length), WIDE),
            jax.ShapeDtypeStruct((length, width), LOW),
            jax.ShapeDtypeStruct((length, HEAD_DIM), LOW),
            jax.ShapeDtypeStruct((length, HEAD_DIM), LOW),
        ],
        scratch_shapes=[pltpu.VMEM((HEAD_DIM, length), LOW)],
        compiler_params=pltpu.CompilerParams(
            dimension_semantics=("arbitrary",), vmem_limit_bytes=VMEM_LIMIT
        ),
        cost_estimate=pl.CostEstimate(
            flops=0, bytes_accessed=8 * length * width, transcendentals=0
        ),
        name="attention_forward",
    )(qkv, qkv, cosine, sine, cosine, sine, places[None, :], places[:, None])


def attention_backward(q_scaled, k_rot, v_low, grad_mixed, lse, cosine, sine, places, heads):
    length = q_scaled.shape[0]
    width = heads * HEAD_DIM
    block = min(256, length)
    steps = length // block
    whole = lambda shape: pl.BlockSpec(shape, lambda i: (0,) * len(shape))
    rows = lambda columns: pl.BlockSpec((block, columns), lambda i: (i, 0))
    return pl.pallas_call(
        functools.partial(backward_kernel, heads, steps),
        grid=(steps,),
        in_specs=[
            rows(width), whole((length, HEAD_DIM)), whole((length, HEAD_DIM)), rows(width),
            pl.BlockSpec((8, block), lambda i: (0, i)),
            rows(128), rows(128), whole((length, 128)), whole((length, 128)),
            pl.BlockSpec((1, block), lambda i: (0, i)), whole((length, 1)),
        ],
        out_specs=[rows(width), whole((length, 128))],
        out_shape=[
            jax.ShapeDtypeStruct((length, width), LOW),
            jax.ShapeDtypeStruct((length, 128), LOW),
        ],
        scratch_shapes=[
            pltpu.VMEM((HEAD_DIM, length), LOW),
            pltpu.VMEM((length, HEAD_DIM), WIDE),
            pltpu.VMEM((length, HEAD_DIM), WIDE),
        ],
        compiler_params=pltpu.CompilerParams(
            dimension_semantics=("arbitrary",), vmem_limit_bytes=VMEM_LIMIT
        ),
        cost_estimate=pl.CostEstimate(
            flops=0, bytes_accessed=8 * length * width, transcendentals=0
        ),
        name="attention_backward",
    )(
        q_scaled, k_rot, v_low, grad_mixed, lse, cosine, sine, cosine, sine,
        places[None, :], places[:, None],
    )


def columns_kernel(block, gate_ref, up_ref, scale_ref, out_ref):
    scale = scale_ref[...]
    for j in range(out_ref.shape[0]):
        lanes = slice(j * block, (j + 1) * block)
        out_ref[j, :, :block] = (gate_ref[:, lanes].astype(WIDE) * scale).astype(LOW)
        out_ref[j, :, block:] = (up_ref[:, lanes].astype(WIDE) * scale).astype(LOW)


def columns_by_device(w_gate, w_up, scale, block):
    rows, ff_width = w_gate.shape
    devices = ff_width // block
    if block % 128:
        split = [(w.astype(WIDE) * scale).astype(LOW).reshape(rows, devices, block) for w in (w_gate, w_up)]
        return jnp.concatenate(split, axis=2).transpose(1, 0, 2)
    some = 8
    part = pl.BlockSpec((rows, some * block), lambda d: (0, d))
    return pl.pallas_call(
        functools.partial(columns_kernel, block),
        grid=(devices // some,),
        in_specs=[part, part, pl.BlockSpec((rows, 1), lambda d: (0, 0))],
        out_specs=pl.BlockSpec((some, rows, 2 * block), lambda d: (d, 0, 0)),
        out_shape=jax.ShapeDtypeStruct((devices, rows, 2 * block), LOW),
        cost_estimate=pl.CostEstimate(flops=0, bytes_accessed=2 << 20, transcendentals=0),
        name="columns_by_device",
    )(w_gate, w_up, scale)


def assemble_kernel(part_ref, gate_ref, up_ref, scale_ref, gate_out, up_out, gain_out):
    @pl.when(pl.program_id(0) == 0)
    def _():
        gain_out[...] = jnp.zeros_like(gain_out)

    scale = scale_ref[...]
    block = gate_ref.shape[1] // part_ref.shape[0]
    total = jnp.zeros_like(gain_out)
    for j in range(part_ref.shape[0]):
        lanes = slice(j * block, (j + 1) * block)
        gate = part_ref[j, :, :block].astype(WIDE)
        up = part_ref[j, :, block:].astype(WIDE)
        gate_out[:, lanes] = gate * scale
        up_out[:, lanes] = up * scale
        products = gate * gate_ref[:, lanes].astype(WIDE) + up * up_ref[:, lanes].astype(WIDE)
        total = total + jnp.sum(products, axis=1, keepdims=True)
    gain_out[...] += total


def assemble_columns(parts, w_gate, w_up, scale):
    devices, rows, both = parts.shape
    block = both // 2
    ff_width = w_gate.shape[1]
    if block % 128:
        sides = parts.reshape(devices, rows, 2, block).transpose(2, 1, 0, 3).reshape(2, rows, ff_width)
        sides = sides.astype(WIDE)
        products = sides[0] * w_gate.astype(WIDE) + sides[1] * w_up.astype(WIDE)
        return sides[0] * scale, sides[1] * scale, jnp.sum(products, axis=1, keepdims=True)
    some = 8
    columns = pl.BlockSpec((rows, some * block), lambda d: (0, d))
    one = pl.BlockSpec((rows, 1), lambda d: (0, 0))
    return pl.pallas_call(
        assemble_kernel,
        grid=(devices // some,),
        in_specs=[pl.BlockSpec((some, rows, both), lambda d: (d, 0, 0)), columns, columns, one],
        out_specs=[columns, columns, one],
        out_shape=[
            jax.ShapeDtypeStruct((rows, ff_width), WIDE),
            jax.ShapeDtypeStruct((rows, ff_width), WIDE),
            jax.ShapeDtypeStruct((rows, 1), WIDE),
        ],
        compiler_params=pltpu.CompilerParams(
            dimension_semantics=("arbitrary",), vmem_limit_bytes=VMEM_LIMIT
        ),
        cost_estimate=pl.CostEstimate(flops=0, bytes_accessed=8 << 20, transcendentals=0),
        name="assemble_columns",
    )(parts, w_gate, w_up, scale)


def feed_kernel(blocks, steps, per_step, table_ref, *refs):
    even_ref, odd_ref = refs[:2]
    cot_refs = refs[2 : 2 + per_step]
    weights = refs[2 + per_step : 2 + per_step + blocks]
    downs = refs[2 + per_step + blocks : 2 + per_step + 2 * blocks]
    norm_out, cot_out, act_out, low_out, even_out, odd_out = refs[-6:]
    step = pl.program_id(0)
    norm = jnp.where(step < steps // 2, even_ref[...], odd_ref[...])
    norm_out[...] = norm
    cot = jnp.concatenate([ref[0, 0] for ref in cot_refs], axis=0)
    cot_out[...] = cot
    term = None
    for j in range(blocks):
        rows = dot(norm, weights[j][...])
        grad_act = dot(cot, downs[j][...], ((1,), (1,)))
        width = rows.shape[1] // 2
        gate, up = rows[:, :width], rows[:, width:]
        sig = 1.0 / (1.0 + jnp.exp(-gate))
        gate_sig = gate * sig
        act_out[:, j * width : (j + 1) * width] = (gate_sig * up).astype(LOW)
        grad_up = grad_act * gate_sig
        grad_gate = grad_act * up * (sig + gate_sig * (1.0 - sig))
        low = jnp.concatenate([grad_gate, grad_up], axis=1).astype(LOW)
        low_out[j] = low
        more = dot(low, weights[j][...], ((1,), (1,)))
        term = more if term is None else term + more
    term = term.astype(LOW)

    @pl.when(step < steps // 2)
    def _():
        even_out[...] = term

    @pl.when(step >= steps // 2)
    def _():
        odd_out[...] = term


def feed_forward(which, even, odd, cots, table, weights, downs, earlier):
    half, width = even.shape
    _, c_count, tok_rows, _ = cots.shape
    blocks = len(weights)
    both = weights[0].shape[1]
    block = both // 2
    steps = 4
    rows = 2 * half // steps
    per_step = rows // tok_rows
    total = 4 * half
    first = which * steps
    even_at = lambda i, t: (jnp.minimum(i, steps // 2 - 1), 0)
    odd_at = lambda i, t: (jnp.maximum(i - steps // 2, 0), 0)
    cot_spec = lambda j: pl.BlockSpec(
        (1, 1, tok_rows, width), lambda i, t, j=j: (which, t[i * per_step + j], 0, 0)
    )
    fixed = lambda shape: pl.BlockSpec(shape, lambda i, t: (0,) * len(shape))
    at = lambda i, t: (first + i, 0)
    out_shape = [
        jax.ShapeDtypeStruct((total, width), LOW),
        jax.ShapeDtypeStruct((total, width), LOW),
        jax.ShapeDtypeStruct((total, blocks * block), LOW),
        jax.ShapeDtypeStruct((blocks, total, both), LOW),
        jax.ShapeDtypeStruct((half, width), LOW),
        jax.ShapeDtypeStruct((half, width), LOW),
    ]
    inputs = [even, odd] + [cots] * per_step + list(weights) + list(downs) + list(earlier)
    in_specs = (
        [pl.BlockSpec((rows, width), even_at), pl.BlockSpec((rows, width), odd_at)]
        + [cot_spec(j) for j in range(per_step)]
        + [fixed(w.shape) for w in weights]
        + [fixed(d.shape) for d in downs]
        + [pl.BlockSpec(memory_space=pl.ANY)] * len(earlier)
    )
    aliases = {1 + len(inputs) - len(earlier) + j: j for j in range(len(earlier))}
    return pl.pallas_call(
        functools.partial(feed_kernel, blocks, steps, per_step),
        grid_spec=pltpu.PrefetchScalarGridSpec(
            num_scalar_prefetch=1,
            grid=(steps,),
            in_specs=in_specs,
            out_specs=[
                pl.BlockSpec((rows, width), at),
                pl.BlockSpec((rows, width), at),
                pl.BlockSpec((rows, blocks * block), at),
                pl.BlockSpec((blocks, rows, both), lambda i, t: (0, first + i, 0)),
                pl.BlockSpec((rows, width), even_at),
                pl.BlockSpec((rows, width), odd_at),
            ],
        ),
        out_shape=out_shape,
        input_output_aliases=aliases,
        compiler_params=pltpu.CompilerParams(
            dimension_semantics=("arbitrary",), vmem_limit_bytes=VMEM_LIMIT
        ),
        cost_estimate=pl.CostEstimate(flops=0, bytes_accessed=8 << 20, transcendentals=0),
        name="feed_forward",
    )(table, *inputs)


def down_kernel(blocks, table_ref, act_ref, *refs):
    out_ref, downs = refs[-1], refs[:-1]
    block = act_ref.shape[1] // blocks
    total = None
    for j in range(blocks):
        part = dot(act_ref[:, j * block : (j + 1) * block], downs[j][...])
        total = part if total is None else total + part
    out_ref[0, 0] = total.astype(LOW)


def down_terms_by_device(acts, table, downs, tok_rows):
    total, local = acts.shape
    c_count = table.shape[0]
    width = downs[0].shape[1]
    fixed = lambda shape: pl.BlockSpec(shape, lambda i, j, t: (0,) * len(shape))
    return pl.pallas_call(
        functools.partial(down_kernel, len(downs)),
        grid_spec=pltpu.PrefetchScalarGridSpec(
            num_scalar_prefetch=1,
            grid=(2, c_count),
            in_specs=[pl.BlockSpec((tok_rows, local), lambda i, j, t: (i * c_count + j, 0))]
            + [fixed(d.shape) for d in downs],
            out_specs=pl.BlockSpec((1, 1, tok_rows, width), lambda i, j, t: (t[j], i, 0, 0)),
        ),
        out_shape=jax.ShapeDtypeStruct((c_count, 2, tok_rows, width), LOW),
        compiler_params=pltpu.CompilerParams(vmem_limit_bytes=VMEM_LIMIT),
        cost_estimate=pl.CostEstimate(flops=0, bytes_accessed=8 << 20, transcendentals=0),
        name="down_terms",
    )(table, acts, *downs)


def inverse_rms(rows):
    return lax.rsqrt(jnp.mean(rows * rows, axis=-1, keepdims=True) + EPSILON)


def norm_back(grad_hat, hat_rows, inv_rms):
    return inv_rms * (grad_hat - hat_rows * jnp.mean(grad_hat * hat_rows, axis=-1, keepdims=True))


def per_device(
    tokens, positions, attn_gain, w_query, w_key, w_value, w_out,
    mlp_gain, w_gate, w_up, w_down, cotangent,
):
    f_count, c_count = lax.axis_size("fsdp"), lax.axis_size("ctx")
    f_index, c_index = lax.axis_index("fsdp"), lax.axis_index("ctx")
    devices = f_count * c_count
    top_bit = f_count // 2
    own_tokens, own_cot = tokens[0], cotangent[0]
    tok_rows, width = own_tokens.shape
    piece = w_query.shape[0]
    heads = HEADS // c_count
    q_width = heads * HEAD_DIM
    qkv_width = q_width + 2 * HEAD_DIM
    kv_share = max(1, c_count // KV_HEADS)
    ff_block = w_down.shape[0]
    c_order = ctx_order(c_count)
    f_order = xor_order(top_bit, 1)

    attn_scale, mlp_scale = attn_gain.astype(WIDE)[:, None], mlp_gain.astype(WIDE)[:, None]
    near_tokens = gather_near(own_tokens)
    shares = [
        w_query.reshape(piece, c_count, q_width),
        jnp.repeat(w_key.reshape(piece, KV_HEADS, HEAD_DIM), kv_share, axis=1),
        jnp.repeat(w_value.reshape(piece, KV_HEADS, HEAD_DIM), kv_share, axis=1),
    ]
    qkv_piece = (jnp.concatenate(shares, axis=2).astype(WIDE) * attn_scale[:, :, None]).astype(LOW)
    qkv_piece = qkv_piece.transpose(1, 0, 2)
    qkv_piece, w_gate_in, w_out = tie(qkv_piece, w_gate, w_out)
    qkv_piece = exchange_ctx(qkv_piece).reshape(1, c_count * piece, qkv_width)
    out_route = [(f_count * c + j, j * c_count + c) for c in range(c_count) for j in range(f_count)]
    out_piece = lax.ppermute(w_out, ("fsdp", "ctx"), out_route)
    small = positions
    for bit in [2 ** j for j in range(1, c_count.bit_length() - 1)] + [1]:
        small = jnp.concatenate([small, swap(small, "ctx", bit)], axis=0)
    int_places = small.reshape(-1)
    gate_up = columns_by_device(w_gate_in, w_up, mlp_scale, ff_block)

    qkv_piece, out_piece, near_tokens = tie(qkv_piece, out_piece, near_tokens)
    even_tokens = gather_far(own_tokens, near_tokens)
    qkv_piece = qkv_piece[0]
    qkv_parts = [qkv_piece] + [swap(qkv_piece, "fsdp", r) for r in range(1, f_count)]
    half_dim = HEAD_DIM // 2
    frequency = jnp.power(ROPE_BASE, -2.0 * jnp.arange(half_dim, dtype=WIDE) / HEAD_DIM)
    angles = int_places.astype(WIDE)[:, None] * frequency[None, :]
    cosine, sine = jnp.cos(angles), jnp.sin(angles)
    cosine = jnp.concatenate([cosine] * 4, axis=1)
    sine = jnp.concatenate([-sine, sine, -sine, sine], axis=1)

    out_piece, cosine, sine, even_tokens = tie(out_piece, cosine, sine, even_tokens)
    quad_tokens, other_tokens = gather_core(even_tokens)
    w_out_rows = lax.all_gather(out_piece, "fsdp", axis=0, tiled=True)

    def first_norm(rows):
        rows = rows.astype(WIDE)
        return (rows * inverse_rms(rows)).astype(LOW)

    normed_first = [first_norm(quad_tokens), first_norm(other_tokens)]

    qkv_parts, gate_up, own_cot, normed_first, w_down = tie(
        qkv_parts, gate_up, own_cot, normed_first, w_down
    )
    gate_up = lax.all_to_all(gate_up, ("fsdp", "ctx"), 0, 0, tiled=True)
    side_cot = swap(own_cot, "fsdp", top_bit)
    downs = [w_down] + [swap(w_down, "fsdp", r) for r in range(1, top_bit)]
    w_qkv = place([(r, 0, part) for r, part in enumerate(qkv_parts)], f_index, f_count)
    qkv = jnp.concatenate([dot(rows, w_qkv) for rows in normed_first], axis=0)
    mixed, lse, q_scaled, k_rot, v_low = attention_forward(qkv, cosine, sine, int_places, heads)

    mixed, side_cot, downs = tie(mixed, side_cot, downs)
    cots = lax.all_gather(jnp.stack([own_cot, side_cot], axis=0), "ctx", axis=1, tiled=True)
    middle = mixed.shape[0] // 2
    odd_out = scatter_core(dot(mixed[middle:], w_out_rows, out=LOW))
    even_out = dot(mixed[:middle], w_out_rows, out=LOW)
    state = scatter_far(even_out, odd_out)
    inputs = own_tokens.astype(WIDE)
    inv_first = inverse_rms(inputs)
    hat_first = inputs * inv_first
    state, hat_first, gate_up = tie(state, hat_first, gate_up)
    gate_ups = [gate_up.reshape(width, 2 * ff_block)]
    halves = [gate_ups[0][: width // 2], gate_ups[0][width // 2 :]]
    tops = [swap(halves[0], "fsdp", r) for r in range(1, top_bit)]
    hidden = inputs + scatter_end(scatter_near(state))
    inv_second = inverse_rms(hidden)
    hat_second = hidden * inv_second
    normed_own = hat_second.astype(LOW)

    near_norm = gather_near(normed_own)
    side_norm = swap(normed_own, "fsdp", top_bit)
    near_norm, side_norm, tops, halves = tie(near_norm, side_norm, tops, halves)
    lows = [swap(halves[1], "fsdp", r) for r in range(1, top_bit)]
    even_norm = gather_far(normed_own, near_norm)
    near_side = gather_near(side_norm)
    norm_pieces = list(gather_core(even_norm))
    near_side, norm_pieces, cots, lows = tie(near_side, norm_pieces, cots, lows)
    gate_ups += [jnp.concatenate(parts, axis=0) for parts in zip(tops, lows)]
    even_side = gather_far(side_norm, near_side)
    cots = cots.reshape(2, c_count, tok_rows, width)
    table = jnp.array(c_order, jnp.int32) ^ c_index

    *buffers, even_zero, odd_zero = feed_forward(0, *norm_pieces, cots, table, gate_ups, downs, [])
    even_side, buffers, even_zero, odd_zero = tie(even_side, buffers, even_zero, odd_zero)
    norm_pieces = gather_core(even_side)
    odd_zero = scatter_core(odd_zero)
    state_zero = scatter_far(even_zero, odd_zero)
    norm_pieces, state_zero = tie(norm_pieces, state_zero)
    *buffers, even_one, odd_one = feed_forward(1, *norm_pieces, cots, table, gate_ups, downs, buffers)
    all_norms, all_cots, all_acts, all_lows = buffers
    state_zero, odd_one = tie(state_zero, odd_one)
    odd_one = scatter_core(odd_one)
    state_zero = scatter_near(state_zero)
    state_zero, odd_one = tie(state_zero, odd_one)
    state_one = scatter_far(even_one, odd_one)

    act_of = lambda j: all_acts[:, j * ff_block : (j + 1) * ff_block]
    gate_up_away = [dot(all_norms, all_lows[j], ((0,), (0,)), LOW) for j in range(1, len(downs))]
    state_one, gate_up_away, all_lows = tie(state_one, gate_up_away, all_lows)
    state_one = scatter_near(state_one)
    cut = width // 2
    tops = [swap(part[:cut], "fsdp", r) for r, part in enumerate(gate_up_away, 1)]
    gate_up_own = dot(all_norms, all_lows[0], ((0,), (0,)))
    down_away = [dot(act_of(j), all_cots, ((0,), (0,)), LOW) for j in range(1, len(downs))]
    side_one = swap(scatter_end(state_one).astype(LOW), "fsdp", top_bit)
    side_one, tops, gate_up_away, gate_up_own, down_away = tie(
        side_one, tops, gate_up_away, gate_up_own, down_away
    )
    lows = [swap(part[cut:], "fsdp", r) for r, part in enumerate(gate_up_away, 1)]
    grad_normed = scatter_end(state_zero) + side_one.astype(WIDE)

    grad_hidden = own_cot.astype(WIDE) + norm_back(grad_normed, hat_second, inv_second)
    hidden_low = grad_hidden.astype(LOW)
    near_hidden = gather_near(hidden_low)
    down_terms = down_terms_by_device(all_acts, table, downs, tok_rows)
    near_hidden, down_terms, lows, down_away = tie(near_hidden, down_terms, lows, down_away)
    even_hidden = gather_far(hidden_low, near_hidden)
    out_rows = lax.psum_scatter(down_terms.reshape(-1, width), "ctx", scatter_dimension=0, tiled=True)
    out_rows = out_rows.reshape(2, tok_rows, width)
    received = [jnp.concatenate(parts, axis=0) for parts in zip(tops, lows)]
    gate_up_sum = sum([part.astype(WIDE) for part in received], gate_up_own).astype(LOW)
    even_hidden, gate_up_sum = tie(even_hidden, gate_up_sum)
    hidden_halves = gather_core(even_hidden)
    gate_up_sum = lax.all_to_all(
        gate_up_sum.reshape(devices, piece, 2 * ff_block), ("fsdp", "ctx"), 0, 0, tiled=True
    )
    grad_mixed = jnp.concatenate([dot(h, w_out_rows, ((1,), (1,)), LOW) for h in hidden_halves], axis=0)
    out_part = dot(mixed[:middle], hidden_halves[0], ((0,), (0,))) + dot(
        mixed[middle:], hidden_halves[1], ((0,), (0,))
    )
    out_part = out_part.astype(LOW).reshape(f_count, piece, width)

    grad_mixed, out_part = tie(grad_mixed, out_part)
    out_sum = halve_near(out_part, f_index)
    down_sum = dot(act_of(0), all_cots, ((0,), (0,)))
    grad_q, grad_kv = attention_backward(
        q_scaled, k_rot, v_low, grad_mixed, lse, cosine, sine, int_places, heads
    )
    grad_qkv = jnp.concatenate([grad_q, grad_kv], axis=1)
    grad_qkv, out_sum = tie(grad_qkv, out_sum)

    halves = [grad_qkv[middle:], grad_qkv[:middle]]
    odd = scatter_core(dot(halves[0], w_qkv, ((1,), (1,)), LOW))
    qkv_part = dot(normed_first[0], halves[1], ((0,), (0,))) + dot(normed_first[1], halves[0], ((0,), (0,)))
    qkv_part = qkv_part.astype(LOW).reshape(f_count, c_count * piece, qkv_width)
    even = dot(halves[1], w_qkv, ((1,), (1,)), LOW)
    odd, even, qkv_part = tie(odd, even, qkv_part)
    state = scatter_far(even, odd)
    qkv_sum = halve_near(qkv_part, f_index)
    out_sum = halve_far(out_sum, f_index, top_bit)
    state, qkv_sum, out_sum, down_away = tie(state, qkv_sum, out_sum, down_away)
    state = scatter_near(state)
    qkv_sum = halve_far(qkv_sum, f_index, top_bit)
    out_grad = lax.ppermute(out_sum, ("fsdp", "ctx"), [(d, s) for s, d in out_route]).astype(WIDE)
    for r, part in enumerate(down_away, 1):
        down_sum = down_sum + swap(part, "fsdp", r).astype(WIDE)
    down_grad = down_sum
    state, qkv_sum, out_rows = tie(state, qkv_sum, out_rows)
    qkv_sum = exchange_ctx(qkv_sum.reshape(c_count, piece, qkv_width))
    side_out = swap(out_rows[1], "fsdp", top_bit)
    grad_normed = scatter_end(state)
    input_grad = grad_hidden + norm_back(grad_normed, hat_first, inv_first)
    gate_grad, up_grad, mlp_gain_grad = assemble_columns(gate_up_sum, w_gate, w_up, mlp_scale)
    mlp_gain_grad = mlp_gain_grad[:, 0]
    output = hidden + out_rows[0].astype(WIDE) + side_out.astype(WIDE)

    qkv_sum = qkv_sum.astype(WIDE)
    query_grad = qkv_sum[:, :, :q_width].transpose(1, 0, 2).reshape(piece, -1)
    kv_sum = qkv_sum[:, :, q_width:].reshape(KV_HEADS, kv_share, piece, 2, HEAD_DIM).sum(axis=1)
    key_grad = kv_sum[:, :, 0].transpose(1, 0, 2).reshape(piece, -1)
    value_grad = kv_sum[:, :, 1].transpose(1, 0, 2).reshape(piece, -1)
    attn_gain_grad = (
        jnp.sum(query_grad * w_query.astype(WIDE), axis=1)
        + jnp.sum(key_grad * w_key.astype(WIDE), axis=1)
        + jnp.sum(value_grad * w_value.astype(WIDE), axis=1)
    )
    query_grad, key_grad, value_grad = (g * attn_scale for g in (query_grad, key_grad, value_grad))

    return (
        output.astype(LOW)[None],
        input_grad.astype(LOW)[None],
        attn_gain_grad,
        query_grad,
        key_grad,
        value_grad,
        out_grad,
        mlp_gain_grad,
        gate_grad,
        up_grad,
        down_grad,
    )


def solution(mesh):
    rows = P(("fsdp", "ctx"), None)
    vector = P(("fsdp", "ctx"))
    tokens = P("fsdp", "ctx", None)
    in_specs = (
        tokens, P("fsdp", "ctx"), vector, rows, rows, rows, rows, vector, rows, rows, rows, tokens,
    )
    out_specs = (
        tokens, tokens, vector, rows, rows, rows, rows, vector, rows, rows, rows,
    )
    return jax.shard_map(
        per_device, mesh=mesh, in_specs=in_specs, out_specs=out_specs, check_vma=False
    )
```

time: 937 us -> 645 us (0.69)
  waiting for transfers between devices: 427 us -> 266 us
  local copies, waits for them, and re-layouts: 152 us -> 29.4 us
  Pallas kernels: 34.1 us -> 100 us
  matrix products: 85.5 us -> 50.5 us
  starting transfers between devices: 144 us -> 125 us
  blocking collectives: 12.8 us -> 0 us
  between operations: 2.53 us -> 15.2 us
  other arithmetic: 62.9 us -> 50.5 us
    ppermute x86 -> x68, waiting for transfers between devices: 420 us -> 220 us  [swap(): return lax.ppermute(block, axis, [(i, i ^ mask) for i in range(count)])]
    pallas_call x0 -> x6, Pallas kernels: none -> 66.4 us  [the longest x2 39.7 us: feed_forward(): pl.pallas_call(functools.partial(feed_kernel, blocks, steps, per_step), g...]
    ppermute x1, waiting for transfers between devices: 0.01 us -> 40.4 us  [per_device(): lax.ppermute(out_sum, ('fsdp', 'ctx'), [(d, s) for s, d in out_route])]
    dot_general x18 -> x16, matrix products: 85.5 us -> 50.5 us  [dot(): lax.dot_general(left, right, (dims, ((), ())), preferred_element_type=WIDE)]
    slice x33 -> x23, local copies, waits for them, and re-layouts: 35.7 us -> 3.92 us  [the longest x1 1.16 us: per_device(): halves = [gate_ups[0][:width // 2], gate_ups[0][width // 2:]]]
    unnamed x179 -> x133, local copies, waits for them, and re-layouts: 44.6 us -> 14.4 us
    ppermute x86 -> x68, starting transfers between devices: 117 us -> 95.5 us  [swap(): return lax.ppermute(block, axis, [(i, i ^ mask) for i in range(count)])]
    all_gather x1 -> x0, blocking collectives: 12.8 us -> none  [per_device(): lax.all_gather(jnp.concatenate([gains, positions[0].astype(WIDE)])[None],...]
  transfers between devices with their start and end apart: 92 -> 77, of which waited for: 37 -> 40; matrix products, arithmetic and copies ran while one was open for 28% -> 18% of each run, Pallas kernels for 2% -> 13%
where the time goes in v2:
time: 645 us; the launch traced here: 637 us
  waiting for transfers between devices  266 us (41%)
  starting transfers between devices  125 us (19%)
  Pallas kernels  100 us (16%)
  other arithmetic  50.5 us (8%)
  matrix products  50.5 us (8%)
  local copies, waits for them, and re-layouts  29.4 us (5%)
  between operations  15.2 us (2%)
    ppermute x68, waiting for transfers between devices, swap(): return lax.ppermute(block, axis, [(i, i ^ mask) for i in range(count)])  220 us
    ppermute x68, starting transfers between devices, swap(): return lax.ppermute(block, axis, [(i, i ^ mask) for i in range(count)])  95.5 us
    dot_general x16, matrix products, dot(): lax.dot_general(left, right, (dims, ((), ())), preferred_element_type=WIDE)  50.5 us
    ppermute x1, waiting for transfers between devices, per_device(): lax.ppermute(out_sum, ('fsdp', 'ctx'), [(d, s) for s, d in out_route])  40.4 us
    pallas_call x2, Pallas kernels, feed_forward(): pl.pallas_call(functools.partial(feed_kernel, blocks, steps, per_step), g...  39.7 us
    pallas_call x1, Pallas kernels, attention_backward(): pl.pallas_call(functools.partial(backward_kernel, heads, steps), grid=(st...  17.9 us
    pallas_call x1, Pallas kernels, attention_forward(): pl.pallas_call(functools.partial(forward_kernel, heads), grid=(length //...  15.9 us
    pallas_call x1, Pallas kernels, down_terms_by_device(): pl.pallas_call(functools.partial(down_kernel, len(downs)), grid_spec=pltp...  15.2 us
  transfers between devices with their start and end apart: 77, of which 40 were waited for; matrix products, arithmetic and copies ran while one was open for 18% of the time, Pallas kernels for 13%

profile of v2, /device:TPU:1, one launch (start us, length us, event | category | flops | bytes accessed | tf_op | source)
XLA Modules:
  0.0 637.2 jit_solution(134471318176233994)
XLA Ops:
  7.2 2.1 collective-permute-start.1
  15.4 4.9 all-to-all-start
  22.4 5.0 collective-permute-start
  28.7 2.2 collective-permute-done
  30.9 5.5 collective-permute-start.9
  36.5 3.4 collective-permute-start.10
  43.8 4.0 collective-permute-start.11
  48.5 4.0 columns_by_device.1
  52.5 3.7 collective-permute-start.3
  61.0 2.1 fusion.2
  65.2 12.8 %collective-permute-done.3.refs_1_ = bf16[512,384]{1,0:T(8,128)(2,1)} collective-permute-done((bf16[512,384]{1,0:T(8,128)(2,1)S(1)}, bf16[512,384]{1,0:T(8,128)(2,1)}, u32[]{:S(2)}, u32[]{:S(2)}) %collective-permute-start.3) | collective-permute-done | bytes 393248 | tf_op jit(solution)/shard_map/ppermute | solution.py:30
  78.9 14.1 %collective-permute-done.5.refs_3_ = bf16[512,384]{1,0:T(8,128)(2,1)} collective-permute-done((bf16[512,384]{1,0:T(8,128)(2,1)S(1)}, bf16[512,384]{1,0:T(8,128)(2,1)}, u32[]{:S(2)}, u32[]{:S(2)}) %collective-permute-start.5) | collective-permute-done | bytes 393248 | tf_op jit(solution)/shard_map/ppermute | solution.py:30
  92.9 16.2 %collective-permute-start.13 = (bf16[256,2048]{1,0:T(8,128)(2,1)}, bf16[256,2048]{1,0:T(8,128)(2,1)}, u32[]{:S(2)}, u32[]{:S(2)}) collective-permute-start(bf16[256,2048]{1,0:T(8,128)(2,1)} %refs_0_), channel_id=1, source_target_pairs={{0,8},{8,0},{16,24},{24,16},{1,9},{9,1},{17,25},{25,17},{2,10},{10... | collective-permute-start | bytes 3145736 | tf_op jit(solution)/shard_map/ppermute | solution.py:30
  110.9 2.7 place.1
  113.6 2.8 fusion.42
  118.9 15.9 %attention_forward.1 = (bf16[1024,256]{1,0:T(8,128)(2,1)}, f32[8,1024]{1,0:T(8,128)}, bf16[1024,256]{1,0:T(8,128)(2,1)}, bf16[1024,64]{1,0:T(8,128)(2,1)}, bf16[1024,64]{1,0:T(8,128)(2,1)}) custom-call(f32[1024,384]{1,0:T(8,128)} %pad_maximum_fusion.q_ref.kv_ref, f32[1024,384]{1,0:T(8,128)} %pad_maximum_fusion.q_ref.kv_ref, ...), custom_call_target="tpu_custom_call" | custom-call | bytes 2097152 | tf_op jit(solution)/shard_map/attention_forward/pallas_call | solution.py:278
  134.8 6.1 collective-permute-done.12
  143.1 5.4 all-to-all-start.1
  151.3 3.7 collective-permute-done.14
  160.1 23.5 %collective-permute-done.15 = bf16[64,2048]{1,0:T(8,128)(2,1)S(1)} collective-permute-done((bf16[64,2048]{1,0:T(8,128)(2,1)S(1)}, bf16[64,2048]{1,0:T(8,128)(2,1)S(1)}, u32[]{:S(2)}, u32[]{:S(2)}) %collective-permute-start.15) | collective-permute-done | bytes 262176 | tf_op jit(solution)/shard_map/ppermute | solution.py:30
  183.6 12.2 %collective-permute-done.17 = bf16[64,2048]{1,0:T(8,128)(2,1)S(1)} collective-permute-done((bf16[64,2048]{1,0:T(8,128)(2,1)S(1)}, bf16[64,2048]{1,0:T(8,128)(2,1)S(1)}, u32[]{:S(2)}, u32[]{:S(2)}) %collective-permute-start.17) | collective-permute-done | bytes 262176 | tf_op jit(solution)/shard_map/ppermute | solution.py:30
  202.7 6.8 %collective-permute-done.19 = bf16[64,2048]{1,0:T(8,128)(2,1)S(1)} collective-permute-done((bf16[64,2048]{1,0:T(8,128)(2,1)S(1)}, bf16[64,2048]{1,0:T(8,128)(2,1)S(1)}, u32[]{:S(2)}, u32[]{:S(2)}) %collective-permute-start.19) | collective-permute-done | bytes 262176 | tf_op jit(solution)/shard_map/ppermute | solution.py:30
  209.5 3.7 collective-permute-done.20
  217.8 20.7 %collective-permute-done.21 = bf16[128,2048]{1,0:T(8,128)(2,1)S(1)} collective-permute-done((bf16[128,2048]{1,0:T(8,128)(2,1)S(1)}, bf16[128,2048]{1,0:T(8,128)(2,1)S(1)}, u32[]{:S(2)}, u32[]{:S(2)}) %collective-permute-start.21) | collective-permute-done | bytes 524320 | tf_op jit(solution)/shard_map/ppermute | solution.py:30
  242.0 3.0 collective-permute-done.27
  246.1 4.9 collective-permute-start.29
  252.5 12.2 %collective-permute-done.25 = bf16[128,2048]{1,0:T(8,128)(2,1)} collective-permute-done((bf16[128,2048]{1,0:T(8,128)(2,1)}, bf16[128,2048]{1,0:T(8,128)(2,1)}, u32[]{:S(2)}, u32[]{:S(2)}) %collective-permute-start.25) | collective-permute-done | bytes 524320 | tf_op jit(solution)/shard_map/ppermute | solution.py:30
  264.7 11.4 %collective-permute-done.30 = bf16[1024,512]{1,0:T(8,128)(2,1)} collective-permute-done((bf16[1024,512]{1,0:T(8,128)(2,1)}, bf16[1024,512]{1,0:T(8,128)(2,1)}, u32[]{:S(2)}, u32[]{:S(2)}) %collective-permute-start.30) | collective-permute-done | bytes 1048608 | tf_op jit(solution)/shard_map/ppermute | solution.py:30
  283.0 19.8 %feed_forward.2 = (bf16[2048,2048]{1,0:T(8,128)(2,1)}, bf16[2048,2048]{1,0:T(8,128)(2,1)}, bf16[2048,512]{1,0:T(8,128)(2,1)}, bf16[2,2048,512]{2,1,0:T(8,128)(2,...) custom-call(s32[8]{0:T(128)} %broadcast_xor_fusion.table_ref, bf16[512,2048]{1,0:T(8,128)(2,1)} %copy-done.25, ...), custom_call_target="tpu_custom_call" | custom-call | bytes 8388608 | tf_op jit(solution)/shard_map/feed_forward/pallas_call | solution.py:496
  312.2 4.7 collective-permute-done.35
  317.3 5.3 collective-permute-done.37
  322.9 19.9 %feed_forward.3 = (bf16[2048,2048]{1,0:T(8,128)(2,1)}, bf16[2048,2048]{1,0:T(8,128)(2,1)}, bf16[2048,512]{1,0:T(8,128)(2,1)}, bf16[2,2048,512]{2,1,0:T(8,128)(2,...) custom-call(s32[8]{0:T(128)} %broadcast_xor_fusion.table_ref, ...), custom_call_target="tpu_custom_call", output_to_operand_aliasing={{0}: (9, {}), {1}: (10, {}), {2}: (11, {}), {3}: (12, {})} | custom-call | bytes 8388608 | tf_op jit(solution)/shard_map/feed_forward/pallas_call | solution.py:496
  348.4 8.7 %convolution_convert_fusion.4 = bf16[2048,512]{1,0:T(8,128)(2,1)S(1)} fusion(bf16[2048,2048]{1,0:T(8,128)(2,1)} %get-tuple-element.257, bf16[2,2048,512]{2,1,0:T(8,128)(2,1)} %get-tuple-element.267), kind=kOutput, calls=%fused_computation.18 | convolution fusion | flops 4296015872 | bytes 12582912 | tf_op jit(solution)/shard_map/dot_general | solution.py:21
  361.2 3.3 convolution_convert_fusion.5
  366.9 4.5 collective-permute-done.44
  375.1 3.9 collective-permute-done.46
  381.2 7.1 %fusion.5 = f32[2048,512]{1,0:T(8,128)} fusion(bf16[2048,2048]{1,0:T(8,128)(2,1)S(1)} %bitcast.119, bf16[2,2048,512]{2,1,0:T(8,128)(2,1)S(1)} %copy-done.21), kind=kOutput, calls=%fused_computation.22 | convolution fusion | flops 4294967296 | bytes 14680064 | tf_op jit(solution)/shard_map/dot_general | solution.py:21
  388.4 18.5 %collective-permute-done.48 = bf16[128,2048]{1,0:T(8,128)(2,1)S(1)} collective-permute-done((bf16[128,2048]{1,0:T(8,128)(2,1)S(1)}, bf16[128,2048]{1,0:T(8,128)(2,1)S(1)}, u32[]{:S(2)}, u32[]{:S(2)}) %collective-permute-start.48) | collective-permute-done | bytes 524320 | tf_op jit(solution)/shard_map/ppermute | solution.py:30
  414.3 15.2 %down_terms.1 = bf16[8,2,128,2048]{3,2,1,0:T(8,128)(2,1)} custom-call(s32[8]{0:T(128)} %broadcast_xor_fusion.table_ref, bf16[2048,512]{1,0:T(8,128)(2,1)} %get-tuple-element.268.act_ref, bf16[256,2048]{1,0:T(8,128)(2,1)} %refs_0_, bf16[256,2048]{1,0:T(8,128)(2,1)} %collective-permute-done.13.refs_7_.refs_1_), custom_call_target="tpu_custom_call" | custom-call | bytes 8388608 | tf_op jit(solution)/shard_map/down_terms/pallas_call | solution.py:536
  429.5 2.1 collective-permute-done.52
  434.9 4.8 add_convert_fusion.1
  443.7 4.9 collective-permute-start.55
  448.6 3.8 all-to-all-start.3
  452.4 2.4 convolution_convert_fusion.7
  454.9 2.4 convolution_convert_fusion.6
  458.1 2.3 fusion.28
  460.5 2.3 fusion.4
  465.0 17.9 %attention_backward.1 = (bf16[1024,256]{1,0:T(8,128)(2,1)}, bf16[1024,128]{1,0:T(8,128)(2,1)}) custom-call(bf16[1024,256]{1,0:T(8,128)(2,1)} %get-tuple-element.197.q_ref, bf16[1024,64]{1,0:T(8,128)(2,1)} %get-tuple-element.198.k_ref, bf16[1024,64]{1,0:T(8,128)(2,1)} %get-tuple-element.199.v_ref, bf16[1024,256]{1,0:T(8,128)(2,1)} %pad_maximum_fusion.7.do_ref, ...), custom_call_target="tpu_custom_call" | custom-call | bytes 2097152 | tf_op jit(solution)/shard_map/attention_backward/pallas_call | solution.py:316
  484.3 14.1 %collective-permute-done.56 = bf16[2,64,2048]{2,1,0:T(8,128)(2,1)S(1)} collective-permute-done((bf16[2,64,2048]{2,1,0:T(8,128)(2,1)}, bf16[2,64,2048]{2,1,0:T(8,128)(2,1)S(1)}, u32[]{:S(2)}, u32[]{:S(2)}) %collective-permute-start.56) | collective-permute-done | bytes 524320 | tf_op jit(solution)/shard_map/ppermute | solution.py:30
  498.5 2.6 convolution_convert_fusion.3
  501.8 7.2 %fusion.15 = f32[256,2048]{1,0:T(8,128)} fusion(bf16[2048,2048]{1,0:T(8,128)(2,1)} %get-tuple-element.269, bf16[2048,512]{1,0:T(8,128)(2,1)S(1)} %copy-done.3), kind=kOutput, calls=%fused_computation.45 | convolution fusion | flops 2147483648 | bytes 11534336 | tf_op jit(solution)/shard_map/dot_general | solution.py:21
  509.1 3.8 collective-permute-start.63
  515.5 2.6 convolution_convert_fusion.2
  518.1 6.9 %collective-permute-done.63 = bf16[1,64,2048]{2,1,0:T(8,128)(2,1)S(1)} collective-permute-done((bf16[1,64,2048]{2,1,0:T(8,128)(2,1)S(1)}, bf16[1,64,2048]{2,1,0:T(8,128)(2,1)S(1)}, u32[]{:S(2)}, u32[]{:S(2)}) %collective-permute-start.63) | collective-permute-done | bytes 262176 | tf_op jit(solution)/shard_map/ppermute | solution.py:30
  525.8 4.9 assemble_columns.1
  532.2 3.0 add_convert_fusion
  539.5 11.1 %collective-permute-done.62 = bf16[2,512,384]{2,1,0:T(8,128)(2,1)S(1)} collective-permute-done((bf16[2,512,384]{2,1,0:T(8,128)(2,1)S(1)}, bf16[2,512,384]{2,1,0:T(8,128)(2,1)S(1)}, u32[]{:S(2)}, u32[]{:S(2)}) %collective-permute-start.62) | collective-permute-done | bytes 786464 | tf_op jit(solution)/shard_map/ppermute | solution.py:30
  553.6 5.8 collective-permute-start.68
  560.7 40.4 %collective-permute-done.68 = bf16[64,2048]{1,0:T(8,128)(2,1)S(1)} collective-permute-done((bf16[64,2048]{1,0:T(8,128)(2,1)S(1)}, bf16[64,2048]{1,0:T(8,128)(2,1)S(1)}, u32[]{:S(2)}, u32[]{:S(2)}) %collective-permute-start.68) | collective-permute-done | bytes 262176 | tf_op jit(solution)/shard_map/ppermute | solution.py:731
  608.7 3.9 all-to-all-start.2
  612.7 2.6 fusion.18
  615.3 3.8 all-to-all-done.2
  623.3 5.1 collective-permute-done.67
  628.4 2.1 fusion.19
  (361 shorter events, 133.6 us)
Async XLA Ops:
  7.2 23.6 %collective-permute-start.1 = (bf16[128,2048]{1,0:T(8,128)(2,1)}, bf16[128,2048]{1,0:T(8,128)(2,1)S(1)}, u32[]{:S(2)}, u32[]{:S(2)}) collective-permute-start(bf16[128,2048]{1,0:T(8,128)(2,1)} %bitcast.115), channel_id=1, source_target_pairs={{0,2},{1,3},{2,0},{3,1},{4,6},{5,7},{6,4},{7,5},{8,10},{9,11},{10,... | collective-permute-start | bytes 1572872 | tf_op jit(solution)/shard_map/ppermute | solution.py:30
  9.3 21.5 %collective-permute-start.2 = (bf16[128,2048]{1,0:T(8,128)(2,1)}, bf16[128,2048]{1,0:T(8,128)(2,1)S(1)}, u32[]{:S(2)}, u32[]{:S(2)}) collective-permute-start(bf16[128,2048]{1,0:T(8,128)(2,1)} %bitcast.116), channel_id=1, source_target_pairs={{0,4},{1,5},{2,6},{3,7},{4,0},{5,1},{6,2},{7,3},{8,12},{9,13},{10,... | collective-permute-start | bytes 1572872 | tf_op jit(solution)/shard_map/ppermute | solution.py:30
  10.5 10.6 %collective-permute-start.6 = (s32[1,128]{1,0:T(1,128)}, s32[1,128]{1,0:T(1,128)S(1)}, u32[]{:S(2)}, u32[]{:S(2)}) collective-permute-start(s32[1,128]{1,0:T(1,128)} %param.14), channel_id=1, source_target_pairs={{0,2},{1,3},{2,0},{3,1},{4,6},{5,7},{6,4},{7,5},{8,10},{9,11},{10,... | collective-permute-start | bytes 1544 | tf_op jit(solution)/shard_map/ppermute | solution.py:30
  15.4 15.5 %all-to-all-start = ((bf16[8,64,384]{2,1,0:T(8,128)(2,1)}), bf16[8,64,384]{2,1,0:T(8,128)(2,1)S(1)}, u32[]{:S(2)}, u32[]{:S(2)}) async-start(bf16[8,64,384]{2,1,0:T(8,128)(2,1)} %fusion.20), calls=%async_computation | async-start | bytes 786432 | tf_op jit(solution)/shard_map/all_to_all | solution.py:121
  20.2 128.5 %all-gather.3.cloned.1.call-start = ((), (), s32[]{:S(2)}) async-start(), calls=%async_computation.5 | async-start | bytes 1310720 | tf_op jit(solution)/shard_map/all_gather | solution.py:611
  22.4 8.4 %collective-permute-start = (bf16[64,2048]{1,0:T(8,128)(2,1)S(1)}, bf16[64,2048]{1,0:T(8,128)(2,1)}, u32[]{:S(2)}, u32[]{:S(2)}) collective-permute-start(bf16[64,2048]{1,0:T(8,128)(2,1)S(1)} %copy-done.51), channel_id=1, source_target_pairs={{0,0},{1,8},{2,16},{3,24},{4,1},{5,9},{6,17},{7,25},{8,2},{9,10},{... | collective-permute-start | bytes 786440 | tf_op jit(solution)/shard_map/ppermute | solution.py:591
  30.9 12.7 %collective-permute-start.9 = (bf16[64,2048]{1,0:T(8,128)(2,1)S(1)}, bf16[64,2048]{1,0:T(8,128)(2,1)S(1)}, u32[]{:S(2)}, u32[]{:S(2)}) collective-permute-start(bf16[64,2048]{1,0:T(8,128)(2,1)S(1)} %slice.230), channel_id=1, source_target_pairs={{0,2},{1,3},{2,0},{3,1},{4,6},{5,7},{6,4},{7,5},{8,10},{9,11},{10,... | collective-permute-start | bytes 786440 | tf_op jit(solution)/shard_map/ppermute | solution.py:30
  43.8 17.2 %collective-permute-start.11 = (bf16[512,2048]{1,0:T(8,128)(2,1)S(1)}, bf16[512,2048]{1,0:T(8,128)(2,1)}, u32[]{:S(2)}, u32[]{:S(2)}) collective-permute-start(bf16[512,2048]{1,0:T(8,128)(2,1)S(1)} %constant_dynamic-update-slice_fusion), channel_id=1, source_target_pairs={{0,1},{1,0},{2,3},{3,2},{4,5},{5,4},{6,7},{7,6},{8,9},{9,8},{10,11... | collective-permute-start | bytes 6291464 | tf_op jit(solution)/shard_map/ppermute | solution.py:30
  52.5 25.6 %collective-permute-start.3 = (bf16[512,384]{1,0:T(8,128)(2,1)S(1)}, bf16[512,384]{1,0:T(8,128)(2,1)}, u32[]{:S(2)}, u32[]{:S(2)}) collective-permute-start(bf16[512,384]{1,0:T(8,128)(2,1)S(1)} %bitcast.128), channel_id=1, source_target_pairs={{0,8},{8,0},{16,24},{24,16},{1,9},{9,1},{17,25},{25,17},{2,10},{10... | collective-permute-start | bytes 1179656 | tf_op jit(solution)/shard_map/ppermute | solution.py:30
  56.2 22.7 %collective-permute-start.4 = (bf16[512,384]{1,0:T(8,128)(2,1)S(1)}, bf16[512,384]{1,0:T(8,128)(2,1)}, u32[]{:S(2)}, u32[]{:S(2)}) collective-permute-start(bf16[512,384]{1,0:T(8,128)(2,1)S(1)} %bitcast.129), channel_id=1, source_target_pairs={{0,16},{8,24},{16,0},{24,8},{1,17},{9,25},{17,1},{25,9},{2,18},{10... | collective-permute-start | bytes 1179656 | tf_op jit(solution)/shard_map/ppermute | solution.py:30
  58.1 34.8 %collective-permute-start.5 = (bf16[512,384]{1,0:T(8,128)(2,1)S(1)}, bf16[512,384]{1,0:T(8,128)(2,1)}, u32[]{:S(2)}, u32[]{:S(2)}) collective-permute-start(bf16[512,384]{1,0:T(8,128)(2,1)S(1)} %bitcast.130), channel_id=1, source_target_pairs={{0,24},{8,16},{16,8},{24,0},{1,25},{9,17},{17,9},{25,1},{2,26},{10... | collective-permute-start | bytes 1179656 | tf_op jit(solution)/shard_map/ppermute | solution.py:30
  58.3 217.8 %all-gather.5.cloned.1.call-start = ((), (), s32[]{:S(2)}) async-start(), calls=%async_computation.6 | async-start | bytes 9437184 | tf_op jit(solution)/shard_map/all_gather | solution.py:630
  92.9 49.1 %collective-permute-start.13 = (bf16[256,2048]{1,0:T(8,128)(2,1)}, bf16[256,2048]{1,0:T(8,128)(2,1)}, u32[]{:S(2)}, u32[]{:S(2)}) collective-permute-start(bf16[256,2048]{1,0:T(8,128)(2,1)} %refs_0_), channel_id=1, source_target_pairs={{0,8},{8,0},{16,24},{24,16},{1,9},{9,1},{17,25},{25,17},{2,10},{10... | collective-permute-start | bytes 3145736 | tf_op jit(solution)/shard_map/ppermute | solution.py:30
  110.1 30.8 %collective-permute-start.12 = (bf16[128,2048]{1,0:T(8,128)(2,1)S(1)}, bf16[128,2048]{1,0:T(8,128)(2,1)S(1)}, u32[]{:S(2)}, u32[]{:S(2)}) collective-permute-start(bf16[128,2048]{1,0:T(8,128)(2,1)S(1)} %bitcast.126), channel_id=1, source_target_pairs={{0,16},{8,24},{16,0},{24,8},{1,17},{9,25},{17,1},{25,9},{2,18},{10... | collective-permute-start | bytes 1572872 | tf_op jit(solution)/shard_map/ppermute | solution.py:30
  143.1 53.9 %all-to-all-start.1 = ((bf16[32,64,512]{2,1,0:T(8,128)(2,1)}), bf16[32,64,512]{2,1,0:T(8,128)(2,1)S(1)}, u32[]{:S(2)}, u32[]{:S(2)}) async-start(bf16[32,64,512]{2,1,0:T(8,128)(2,1)} %columns_by_device.1), calls=%async_computation.1 | async-start | bytes 4194304 | tf_op jit(solution)/shard_map/all_to_all | solution.py:622
  148.5 455.9 %reduce-scatter.2.cloned.1.call-start = ((), (), s32[]{:S(2)}) async-start(), calls=%async_computation.7 | async-start | bytes 9437184 | tf_op jit(solution)/shard_map/reduce_scatter | solution.py:695
  156.0 27.7 %collective-permute-start.15 = (bf16[64,2048]{1,0:T(8,128)(2,1)S(1)}, bf16[64,2048]{1,0:T(8,128)(2,1)S(1)}, u32[]{:S(2)}, u32[]{:S(2)}) collective-permute-start(bf16[64,2048]{1,0:T(8,128)(2,1)S(1)} %get-tuple-element.344), channel_id=1, source_target_pairs={{0,2},{1,3},{2,0},{3,1},{4,6},{5,7},{6,4},{7,5},{8,10},{9,11},{10,... | collective-permute-start | bytes 786440 | tf_op jit(solution)/shard_map/ppermute | solution.py:30
  157.4 26.2 %collective-permute-start.16 = (bf16[64,2048]{1,0:T(8,128)(2,1)S(1)}, bf16[64,2048]{1,0:T(8,128)(2,1)S(1)}, u32[]{:S(2)}, u32[]{:S(2)}) collective-permute-start(bf16[64,2048]{1,0:T(8,128)(2,1)S(1)} %get-tuple-element.343), channel_id=1, source_target_pairs={{0,4},{1,5},{2,6},{3,7},{4,0},{5,1},{6,2},{7,3},{8,12},{9,13},{10,... | collective-permute-start | bytes 786440 | tf_op jit(solution)/shard_map/ppermute | solution.py:30
  158.6 37.2 %collective-permute-start.17 = (bf16[64,2048]{1,0:T(8,128)(2,1)S(1)}, bf16[64,2048]{1,0:T(8,128)(2,1)S(1)}, u32[]{:S(2)}, u32[]{:S(2)}) collective-permute-start(bf16[64,2048]{1,0:T(8,128)(2,1)S(1)} %get-tuple-element.342), channel_id=1, source_target_pairs={{0,2},{1,3},{2,0},{3,1},{4,6},{5,7},{6,4},{7,5},{8,10},{9,11},{10,... | collective-permute-start | bytes 786440 | tf_op jit(solution)/shard_map/ppermute | solution.py:30
  158.9 37.6 %collective-permute-start.18 = (bf16[64,2048]{1,0:T(8,128)(2,1)S(1)}, bf16[64,2048]{1,0:T(8,128)(2,1)}, u32[]{:S(2)}, u32[]{:S(2)}) collective-permute-start(bf16[64,2048]{1,0:T(8,128)(2,1)S(1)} %get-tuple-element.341), channel_id=1, source_target_pairs={{0,4},{1,5},{2,6},{3,7},{4,0},{5,1},{6,2},{7,3},{8,12},{9,13},{10,... | collective-permute-start | bytes 786440 | tf_op jit(solution)/shard_map/ppermute | solution.py:30
  198.2 11.3 %collective-permute-start.19 = (bf16[64,2048]{1,0:T(8,128)(2,1)S(1)}, bf16[64,2048]{1,0:T(8,128)(2,1)S(1)}, u32[]{:S(2)}, u32[]{:S(2)}) collective-permute-start(bf16[64,2048]{1,0:T(8,128)(2,1)S(1)} %add_convert_fusion.18), channel_id=1, source_target_pairs={{0,2},{1,3},{2,0},{3,1},{4,6},{5,7},{6,4},{7,5},{8,10},{9,11},{10,... | collective-permute-start | bytes 786440 | tf_op jit(solution)/shard_map/ppermute | solution.py:30
  200.2 13.0 %collective-permute-start.20 = (bf16[64,2048]{1,0:T(8,128)(2,1)S(1)}, bf16[64,2048]{1,0:T(8,128)(2,1)S(1)}, u32[]{:S(2)}, u32[]{:S(2)}) collective-permute-start(bf16[64,2048]{1,0:T(8,128)(2,1)S(1)} %add_convert_fusion.17), channel_id=1, source_target_pairs={{0,4},{1,5},{2,6},{3,7},{4,0},{5,1},{6,2},{7,3},{8,12},{9,13},{10,... | collective-permute-start | bytes 786440 | tf_op jit(solution)/shard_map/ppermute | solution.py:30
  202.6 37.0 %collective-permute-start.24 = (bf16[1024,512]{1,0:T(8,128)(2,1)S(1)}, bf16[1024,512]{1,0:T(8,128)(2,1)S(1)}, u32[]{:S(2)}, u32[]{:S(2)}) collective-permute-start(bf16[1024,512]{1,0:T(8,128)(2,1)S(1)} %bitcast.138), channel_id=1, source_target_pairs={{0,8},{8,0},{16,24},{24,16},{1,9},{9,1},{17,25},{25,17},{2,10},{10... | collective-permute-start | bytes 3145736 | tf_op jit(solution)/shard_map/ppermute | solution.py:30
  214.2 24.3 %collective-permute-start.21 = (bf16[128,2048]{1,0:T(8,128)(2,1)S(1)}, bf16[128,2048]{1,0:T(8,128)(2,1)S(1)}, u32[]{:S(2)}, u32[]{:S(2)}) collective-permute-start(bf16[128,2048]{1,0:T(8,128)(2,1)S(1)} %get-tuple-element.320), channel_id=1, source_target_pairs={{0,2},{1,3},{2,0},{3,1},{4,6},{5,7},{6,4},{7,5},{8,10},{9,11},{10,... | collective-permute-start | bytes 1572872 | tf_op jit(solution)/shard_map/ppermute | solution.py:30
  215.3 24.4 %collective-permute-start.22 = (bf16[128,2048]{1,0:T(8,128)(2,1)S(1)}, bf16[128,2048]{1,0:T(8,128)(2,1)S(1)}, u32[]{:S(2)}, u32[]{:S(2)}) collective-permute-start(bf16[128,2048]{1,0:T(8,128)(2,1)S(1)} %get-tuple-element.320), channel_id=1, source_target_pairs={{0,4},{1,5},{2,6},{3,7},{4,0},{5,1},{6,2},{7,3},{8,12},{9,13},{10,... | collective-permute-start | bytes 1572872 | tf_op jit(solution)/shard_map/ppermute | solution.py:30
  215.9 23.7 %collective-permute-start.23 = (bf16[128,2048]{1,0:T(8,128)(2,1)S(1)}, bf16[128,2048]{1,0:T(8,128)(2,1)}, u32[]{:S(2)}, u32[]{:S(2)}) collective-permute-start(bf16[128,2048]{1,0:T(8,128)(2,1)S(1)} %get-tuple-element.320), channel_id=1, source_target_pairs={{0,16},{8,24},{16,0},{24,8},{1,17},{9,25},{17,1},{25,9},{2,18},{10... | collective-permute-start | bytes 1572872 | tf_op jit(solution)/shard_map/ppermute | solution.py:30
  246.1 30.0 %collective-permute-start.29 = (bf16[512,2048]{1,0:T(8,128)(2,1)S(1)}, bf16[512,2048]{1,0:T(8,128)(2,1)}, u32[]{:S(2)}, u32[]{:S(2)}) collective-permute-start(bf16[512,2048]{1,0:T(8,128)(2,1)S(1)} %constant_dynamic-update-slice_fusion.5.refs_0_), channel_id=1, source_target_pairs={{0,1},{1,0},{2,3},{3,2},{4,5},{5,4},{6,7},{7,6},{8,9},{9,8},{10,11... | collective-permute-start | bytes 6291464 | tf_op jit(solution)/shard_map/ppermute | solution.py:30
  251.0 25.1 %collective-permute-start.30 = (bf16[1024,512]{1,0:T(8,128)(2,1)}, bf16[1024,512]{1,0:T(8,128)(2,1)}, u32[]{:S(2)}, u32[]{:S(2)}) collective-permute-start(bf16[1024,512]{1,0:T(8,128)(2,1)} %bitcast.11), channel_id=1, source_target_pairs={{0,8},{8,0},{16,24},{24,16},{1,9},{9,1},{17,25},{25,17},{2,10},{10... | collective-permute-start | bytes 3145736 | tf_op jit(solution)/shard_map/ppermute | solution.py:30
  251.0 13.7 %collective-permute-start.25 = (bf16[128,2048]{1,0:T(8,128)(2,1)}, bf16[128,2048]{1,0:T(8,128)(2,1)}, u32[]{:S(2)}, u32[]{:S(2)}) collective-permute-start(bf16[128,2048]{1,0:T(8,128)(2,1)} %collective-permute-done.23), channel_id=1, source_target_pairs={{0,2},{1,3},{2,0},{3,1},{4,6},{5,7},{6,4},{7,5},{8,10},{9,11},{10,... | collective-permute-start | bytes 1572872 | tf_op jit(solution)/shard_map/ppermute | solution.py:30
  251.3 13.4 %collective-permute-start.26 = (bf16[128,2048]{1,0:T(8,128)(2,1)}, bf16[128,2048]{1,0:T(8,128)(2,1)}, u32[]{:S(2)}, u32[]{:S(2)}) collective-permute-start(bf16[128,2048]{1,0:T(8,128)(2,1)} %collective-permute-done.23), channel_id=1, source_target_pairs={{0,4},{1,5},{2,6},{3,7},{4,0},{5,1},{6,2},{7,3},{8,12},{9,13},{10,... | collective-permute-start | bytes 1572872 | tf_op jit(solution)/shard_map/ppermute | solution.py:30
  277.0 25.7 %collective-permute-start.31 = (bf16[64,2048]{1,0:T(8,128)(2,1)S(1)}, bf16[64,2048]{1,0:T(8,128)(2,1)S(1)}, u32[]{:S(2)}, u32[]{:S(2)}) collective-permute-start(bf16[64,2048]{1,0:T(8,128)(2,1)S(1)} %slice.249), channel_id=1, source_target_pairs={{0,2},{1,3},{2,0},{3,1},{4,6},{5,7},{6,4},{7,5},{8,10},{9,11},{10,... | collective-permute-start | bytes 786440 | tf_op jit(solution)/shard_map/ppermute | solution.py:30
  278.1 24.6 %collective-permute-start.32 = (bf16[64,2048]{1,0:T(8,128)(2,1)S(1)}, bf16[64,2048]{1,0:T(8,128)(2,1)S(1)}, u32[]{:S(2)}, u32[]{:S(2)}) collective-permute-start(bf16[64,2048]{1,0:T(8,128)(2,1)S(1)} %slice.250), channel_id=1, source_target_pairs={{0,4},{1,5},{2,6},{3,7},{4,0},{5,1},{6,2},{7,3},{8,12},{9,13},{10,... | collective-permute-start | bytes 786440 | tf_op jit(solution)/shard_map/ppermute | solution.py:30
  309.2 7.7 %collective-permute-start.35 = (bf16[64,2048]{1,0:T(8,128)(2,1)S(1)}, bf16[64,2048]{1,0:T(8,128)(2,1)S(1)}, u32[]{:S(2)}, u32[]{:S(2)}) collective-permute-start(bf16[64,2048]{1,0:T(8,128)(2,1)S(1)} %get-tuple-element.336), channel_id=1, source_target_pairs={{0,2},{1,3},{2,0},{3,1},{4,6},{5,7},{6,4},{7,5},{8,10},{9,11},{10,... | collective-permute-start | bytes 786440 | tf_op jit(solution)/shard_map/ppermute | solution.py:30
  309.9 7.3 %collective-permute-start.36 = (bf16[64,2048]{1,0:T(8,128)(2,1)S(1)}, bf16[64,2048]{1,0:T(8,128)(2,1)}, u32[]{:S(2)}, u32[]{:S(2)}) collective-permute-start(bf16[64,2048]{1,0:T(8,128)(2,1)S(1)} %get-tuple-element.335), channel_id=1, source_target_pairs={{0,4},{1,5},{2,6},{3,7},{4,0},{5,1},{6,2},{7,3},{8,12},{9,13},{10,... | collective-permute-start | bytes 786440 | tf_op jit(solution)/shard_map/ppermute | solution.py:30
  311.4 11.1 %collective-permute-start.37 = (bf16[64,2048]{1,0:T(8,128)(2,1)S(1)}, bf16[64,2048]{1,0:T(8,128)(2,1)}, u32[]{:S(2)}, u32[]{:S(2)}) collective-permute-start(bf16[64,2048]{1,0:T(8,128)(2,1)S(1)} %get-tuple-element.334), channel_id=1, source_target_pairs={{0,2},{1,3},{2,0},{3,1},{4,6},{5,7},{6,4},{7,5},{8,10},{9,11},{10,... | collective-permute-start | bytes 786440 | tf_op jit(solution)/shard_map/ppermute | solution.py:30
  311.5 11.4 %collective-permute-start.38 = (bf16[64,2048]{1,0:T(8,128)(2,1)S(1)}, bf16[64,2048]{1,0:T(8,128)(2,1)}, u32[]{:S(2)}, u32[]{:S(2)}) collective-permute-start(bf16[64,2048]{1,0:T(8,128)(2,1)S(1)} %get-tuple-element.333), channel_id=1, source_target_pairs={{0,4},{1,5},{2,6},{3,7},{4,0},{5,1},{6,2},{7,3},{8,12},{9,13},{10,... | collective-permute-start | bytes 786440 | tf_op jit(solution)/shard_map/ppermute | solution.py:30
  343.8 13.3 %collective-permute-start.39 = (bf16[64,2048]{1,0:T(8,128)(2,1)S(1)}, bf16[64,2048]{1,0:T(8,128)(2,1)S(1)}, u32[]{:S(2)}, u32[]{:S(2)}) collective-permute-start(bf16[64,2048]{1,0:T(8,128)(2,1)S(1)} %add_convert_fusion.16), channel_id=1, source_target_pairs={{0,2},{1,3},{2,0},{3,1},{4,6},{5,7},{6,4},{7,5},{8,10},{9,11},{10,... | collective-permute-start | bytes 786440 | tf_op jit(solution)/shard_map/ppermute | solution.py:30
  344.7 12.5 %collective-permute-start.41 = (bf16[512,2048]{1,0:T(8,128)(2,1)}, bf16[512,2048]{1,0:T(8,128)(2,1)S(1)}, u32[]{:S(2)}, u32[]{:S(2)}) collective-permute-start(bf16[512,2048]{1,0:T(8,128)(2,1)} %get-tuple-element.249), channel_id=1, source_target_pairs={{0,1},{1,0},{2,3},{3,2},{4,5},{5,4},{6,7},{7,6},{8,9},{9,8},{10,11... | collective-permute-start | bytes 6291464 | tf_op jit(solution)/shard_map/ppermute | solution.py:30
  347.6 9.5 %collective-permute-start.40 = (bf16[64,2048]{1,0:T(8,128)(2,1)S(1)}, bf16[64,2048]{1,0:T(8,128)(2,1)S(1)}, u32[]{:S(2)}, u32[]{:S(2)}) collective-permute-start(bf16[64,2048]{1,0:T(8,128)(2,1)S(1)} %add_convert_fusion.15), channel_id=1, source_target_pairs={{0,4},{1,5},{2,6},{3,7},{4,0},{5,1},{6,2},{7,3},{8,12},{9,13},{10,... | collective-permute-start | bytes 786440 | tf_op jit(solution)/shard_map/ppermute | solution.py:30
  358.2 7.7 %collective-permute-start.42 = (bf16[64,2048]{1,0:T(8,128)(2,1)S(1)}, bf16[64,2048]{1,0:T(8,128)(2,1)S(1)}, u32[]{:S(2)}, u32[]{:S(2)}) collective-permute-start(bf16[64,2048]{1,0:T(8,128)(2,1)S(1)} %get-tuple-element.330), channel_id=1, source_target_pairs={{0,2},{1,3},{2,0},{3,1},{4,6},{5,7},{6,4},{7,5},{8,10},{9,11},{10,... | collective-permute-start | bytes 786440 | tf_op jit(solution)/shard_map/ppermute | solution.py:30
  359.7 11.8 %collective-permute-start.44 = (bf16[64,2048]{1,0:T(8,128)(2,1)S(1)}, bf16[64,2048]{1,0:T(8,128)(2,1)S(1)}, u32[]{:S(2)}, u32[]{:S(2)}) collective-permute-start(bf16[64,2048]{1,0:T(8,128)(2,1)S(1)} %get-tuple-element.328), channel_id=1, source_target_pairs={{0,2},{1,3},{2,0},{3,1},{4,6},{5,7},{6,4},{7,5},{8,10},{9,11},{10,... | collective-permute-start | bytes 786440 | tf_op jit(solution)/shard_map/ppermute | solution.py:30
  360.4 12.1 %collective-permute-start.45 = (bf16[64,2048]{1,0:T(8,128)(2,1)S(1)}, bf16[64,2048]{1,0:T(8,128)(2,1)S(1)}, u32[]{:S(2)}, u32[]{:S(2)}) collective-permute-start(bf16[64,2048]{1,0:T(8,128)(2,1)S(1)} %get-tuple-element.327), channel_id=1, source_target_pairs={{0,4},{1,5},{2,6},{3,7},{4,0},{5,1},{6,2},{7,3},{8,12},{9,13},{10,... | collective-permute-start | bytes 786440 | tf_op jit(solution)/shard_map/ppermute | solution.py:30
  374.9 34.0 %collective-permute-start.49 = (bf16[1024,512]{1,0:T(8,128)(2,1)S(1)}, bf16[1024,512]{1,0:T(8,128)(2,1)S(1)}, u32[]{:S(2)}, u32[]{:S(2)}) collective-permute-start(bf16[1024,512]{1,0:T(8,128)(2,1)S(1)} %slice.270), channel_id=1, source_target_pairs={{0,8},{8,0},{16,24},{24,16},{1,9},{9,1},{17,25},{25,17},{2,10},{10... | collective-permute-start | bytes 3145736 | tf_op jit(solution)/shard_map/ppermute | solution.py:30
  379.8 27.0 %collective-permute-start.48 = (bf16[128,2048]{1,0:T(8,128)(2,1)S(1)}, bf16[128,2048]{1,0:T(8,128)(2,1)S(1)}, u32[]{:S(2)}, u32[]{:S(2)}) collective-permute-start(bf16[128,2048]{1,0:T(8,128)(2,1)S(1)} %pad_maximum_fusion.6), channel_id=1, source_target_pairs={{0,16},{8,24},{16,0},{24,8},{1,17},{9,25},{17,1},{25,9},{2,18},{10... | collective-permute-start | bytes 1572872 | tf_op jit(solution)/shard_map/ppermute | solution.py:30
  409.8 21.8 %collective-permute-start.52 = (bf16[1024,512]{1,0:T(8,128)(2,1)S(1)}, bf16[1024,512]{1,0:T(8,128)(2,1)S(1)}, u32[]{:S(2)}, u32[]{:S(2)}) collective-permute-start(bf16[1024,512]{1,0:T(8,128)(2,1)S(1)} %slice.273), channel_id=1, source_target_pairs={{0,8},{8,0},{16,24},{24,16},{1,9},{9,1},{17,25},{25,17},{2,10},{10... | collective-permute-start | bytes 3145736 | tf_op jit(solution)/shard_map/ppermute | solution.py:30
  412.6 16.8 %collective-permute-start.50 = (bf16[128,2048]{1,0:T(8,128)(2,1)S(1)}, bf16[128,2048]{1,0:T(8,128)(2,1)S(1)}, u32[]{:S(2)}, u32[]{:S(2)}) collective-permute-start(bf16[128,2048]{1,0:T(8,128)(2,1)S(1)} %get-tuple-element.278), channel_id=1, source_target_pairs={{0,2},{1,3},{2,0},{3,1},{4,6},{5,7},{6,4},{7,5},{8,10},{9,11},{10,... | collective-permute-start | bytes 1572872 | tf_op jit(solution)/shard_map/ppermute | solution.py:30
  413.7 15.8 %collective-permute-start.51 = (bf16[128,2048]{1,0:T(8,128)(2,1)S(1)}, bf16[128,2048]{1,0:T(8,128)(2,1)S(1)}, u32[]{:S(2)}, u32[]{:S(2)}) collective-permute-start(bf16[128,2048]{1,0:T(8,128)(2,1)S(1)} %get-tuple-element.278), channel_id=1, source_target_pairs={{0,4},{1,5},{2,6},{3,7},{4,0},{5,1},{6,2},{7,3},{8,12},{9,13},{10,... | collective-permute-start | bytes 1572872 | tf_op jit(solution)/shard_map/ppermute | solution.py:30
  443.7 11.2 %collective-permute-start.55 = (bf16[512,2048]{1,0:T(8,128)(2,1)}, bf16[512,2048]{1,0:T(8,128)(2,1)}, u32[]{:S(2)}, u32[]{:S(2)}) collective-permute-start(bf16[512,2048]{1,0:T(8,128)(2,1)} %constant_dynamic-update-slice_fusion.17), channel_id=1, source_target_pairs={{0,1},{1,0},{2,3},{3,2},{4,5},{5,4},{6,7},{7,6},{8,9},{9,8},{10,11... | collective-permute-start | bytes 6291464 | tf_op jit(solution)/shard_map/ppermute | solution.py:30
  448.6 77.2 %all-to-all-start.3 = ((bf16[32,64,512]{2,1,0:T(8,128)(2,1)}), bf16[32,64,512]{2,1,0:T(8,128)(2,1)}, u32[]{:S(2)}, u32[]{:S(2)}) async-start(bf16[32,64,512]{2,1,0:T(8,128)(2,1)} %bitcast.120), calls=%async_computation.4 | async-start | bytes 4194304 | tf_op jit(solution)/shard_map/all_to_all | solution.py:701
  463.6 34.7 %collective-permute-start.56 = (bf16[2,64,2048]{2,1,0:T(8,128)(2,1)}, bf16[2,64,2048]{2,1,0:T(8,128)(2,1)S(1)}, u32[]{:S(2)}, u32[]{:S(2)}) collective-permute-start(bf16[2,64,2048]{2,1,0:T(8,128)(2,1)} %dynamic-slice_bitcast_fusion.1), channel_id=1, source_target_pairs={{0,8},{8,0},{16,24},{24,16},{1,9},{9,1},{17,25},{25,17},{2,10},{10... | collective-permute-start | bytes 1572872 | tf_op jit(solution)/shard_map/ppermute | solution.py:30
  501.1 30.9 %collective-permute-start.57 = (bf16[512,2048]{1,0:T(8,128)(2,1)}, bf16[512,2048]{1,0:T(8,128)(2,1)}, u32[]{:S(2)}, u32[]{:S(2)}) collective-permute-start(bf16[512,2048]{1,0:T(8,128)(2,1)} %convolution_convert_fusion.3), channel_id=1, source_target_pairs={{0,1},{1,0},{2,3},{3,2},{4,5},{5,4},{6,7},{7,6},{8,9},{9,8},{10,11... | collective-permute-start | bytes 6291464 | tf_op jit(solution)/shard_map/ppermute | solution.py:30
  509.1 15.9 %collective-permute-start.63 = (bf16[1,64,2048]{2,1,0:T(8,128)(2,1)S(1)}, bf16[1,64,2048]{2,1,0:T(8,128)(2,1)S(1)}, u32[]{:S(2)}, u32[]{:S(2)}) collective-permute-start(bf16[1,64,2048]{2,1,0:T(8,128)(2,1)S(1)} %constant_dynamic-slice_fusion.1), channel_id=1, source_target_pairs={{0,16},{8,24},{16,0},{24,8},{1,17},{9,25},{17,1},{25,9},{2,18},{10... | collective-permute-start | bytes 786440 | tf_op jit(solution)/shard_map/ppermute | solution.py:30
  532.1 18.5 %collective-permute-start.62 = (bf16[2,512,384]{2,1,0:T(8,128)(2,1)S(1)}, bf16[2,512,384]{2,1,0:T(8,128)(2,1)S(1)}, u32[]{:S(2)}, u32[]{:S(2)}) collective-permute-start(bf16[2,512,384]{2,1,0:T(8,128)(2,1)S(1)} %dynamic-slice_bitcast_fusion), channel_id=1, source_target_pairs={{0,8},{8,0},{16,24},{24,16},{1,9},{9,1},{17,25},{25,17},{2,10},{10... | collective-permute-start | bytes 2359304 | tf_op jit(solution)/shard_map/ppermute | solution.py:30
  536.5 14.2 %collective-permute-start.58 = (bf16[64,2048]{1,0:T(8,128)(2,1)S(1)}, bf16[64,2048]{1,0:T(8,128)(2,1)S(1)}, u32[]{:S(2)}, u32[]{:S(2)}) collective-permute-start(bf16[64,2048]{1,0:T(8,128)(2,1)S(1)} %get-tuple-element.324), channel_id=1, source_target_pairs={{0,2},{1,3},{2,0},{3,1},{4,6},{5,7},{6,4},{7,5},{8,10},{9,11},{10,... | collective-permute-start | bytes 786440 | tf_op jit(solution)/shard_map/ppermute | solution.py:30
  537.6 13.2 %collective-permute-start.59 = (bf16[64,2048]{1,0:T(8,128)(2,1)S(1)}, bf16[64,2048]{1,0:T(8,128)(2,1)S(1)}, u32[]{:S(2)}, u32[]{:S(2)}) collective-permute-start(bf16[64,2048]{1,0:T(8,128)(2,1)S(1)} %get-tuple-element.323), channel_id=1, source_target_pairs={{0,4},{1,5},{2,6},{3,7},{4,0},{5,1},{6,2},{7,3},{8,12},{9,13},{10,... | collective-permute-start | bytes 786440 | tf_op jit(solution)/shard_map/ppermute | solution.py:30
  539.1 11.7 %collective-permute-start.60 = (bf16[64,2048]{1,0:T(8,128)(2,1)S(1)}, bf16[64,2048]{1,0:T(8,128)(2,1)S(1)}, u32[]{:S(2)}, u32[]{:S(2)}) collective-permute-start(bf16[64,2048]{1,0:T(8,128)(2,1)S(1)} %get-tuple-element.322), channel_id=1, source_target_pairs={{0,2},{1,3},{2,0},{3,1},{4,6},{5,7},{6,4},{7,5},{8,10},{9,11},{10,... | collective-permute-start | bytes 786440 | tf_op jit(solution)/shard_map/ppermute | solution.py:30
  539.5 11.3 %collective-permute-start.61 = (bf16[64,2048]{1,0:T(8,128)(2,1)S(1)}, bf16[64,2048]{1,0:T(8,128)(2,1)S(1)}, u32[]{:S(2)}, u32[]{:S(2)}) collective-permute-start(bf16[64,2048]{1,0:T(8,128)(2,1)S(1)} %get-tuple-element.321), channel_id=1, source_target_pairs={{0,4},{1,5},{2,6},{3,7},{4,0},{5,1},{6,2},{7,3},{8,12},{9,13},{10,... | collective-permute-start | bytes 786440 | tf_op jit(solution)/shard_map/ppermute | solution.py:30
  550.8 51.9 %collective-permute-start.69 = (bf16[256,2048]{1,0:T(8,128)(2,1)S(1)}, bf16[256,2048]{1,0:T(8,128)(2,1)S(1)}, u32[]{:S(2)}, u32[]{:S(2)}) collective-permute-start(bf16[256,2048]{1,0:T(8,128)(2,1)S(1)} %copy-done.36), channel_id=1, source_target_pairs={{0,8},{8,0},{16,24},{24,16},{1,9},{9,1},{17,25},{25,17},{2,10},{10... | collective-permute-start | bytes 3145736 | tf_op jit(solution)/shard_map/ppermute | solution.py:30
  551.3 53.1 %collective-permute-start.64 = (bf16[64,2048]{1,0:T(8,128)(2,1)S(1)}, bf16[64,2048]{1,0:T(8,128)(2,1)}, u32[]{:S(2)}, u32[]{:S(2)}) collective-permute-start(bf16[64,2048]{1,0:T(8,128)(2,1)S(1)} %add_convert_fusion.9), channel_id=1, source_target_pairs={{0,2},{1,3},{2,0},{3,1},{4,6},{5,7},{6,4},{7,5},{8,10},{9,11},{10,... | collective-permute-start | bytes 786440 | tf_op jit(solution)/shard_map/ppermute | solution.py:30
  552.5 49.4 %collective-permute-start.66 = (bf16[1,512,384]{2,1,0:T(8,128)(2,1)S(1)}, bf16[1,512,384]{2,1,0:T(8,128)(2,1)S(1)}, u32[]{:S(2)}, u32[]{:S(2)}) collective-permute-start(bf16[1,512,384]{2,1,0:T(8,128)(2,1)S(1)} %constant_dynamic-slice_fusion), channel_id=1, source_target_pairs={{0,16},{8,24},{16,0},{24,8},{1,17},{9,25},{17,1},{25,9},{2,18},{10... | collective-permute-start | bytes 1179656 | tf_op jit(solution)/shard_map/ppermute | solution.py:30
  553.6 47.5 %collective-permute-start.68 = (bf16[64,2048]{1,0:T(8,128)(2,1)S(1)}, bf16[64,2048]{1,0:T(8,128)(2,1)S(1)}, u32[]{:S(2)}, u32[]{:S(2)}) collective-permute-start(bf16[64,2048]{1,0:T(8,128)(2,1)S(1)} %copy-done.48), channel_id=1, source_target_pairs={{0,0},{8,1},{16,2},{24,3},{1,4},{9,5},{17,6},{25,7},{2,8},{10,9},{... | collective-permute-start | bytes 786440 | tf_op jit(solution)/shard_map/ppermute | solution.py:731
  559.5 44.9 %collective-permute-start.65 = (bf16[64,2048]{1,0:T(8,128)(2,1)S(1)}, bf16[64,2048]{1,0:T(8,128)(2,1)}, u32[]{:S(2)}, u32[]{:S(2)}) collective-permute-start(bf16[64,2048]{1,0:T(8,128)(2,1)S(1)} %add_convert_fusion.8), channel_id=1, source_target_pairs={{0,4},{1,5},{2,6},{3,7},{4,0},{5,1},{6,2},{7,3},{8,12},{9,13},{10,... | collective-permute-start | bytes 786440 | tf_op jit(solution)/shard_map/ppermute | solution.py:30
  606.4 22.0 %collective-permute-start.67 = (bf16[128,2048]{1,0:T(8,128)(2,1)}, bf16[128,2048]{1,0:T(8,128)(2,1)}, u32[]{:S(2)}, u32[]{:S(2)}) collective-permute-start(bf16[128,2048]{1,0:T(8,128)(2,1)} %slice_bitcast_fusion.1), channel_id=1, source_target_pairs={{0,16},{8,24},{16,0},{24,8},{1,17},{9,25},{17,1},{25,9},{2,18},{10... | collective-permute-start | bytes 1572872 | tf_op jit(solution)/shard_map/ppermute | solution.py:30
  608.7 10.4 %all-to-all-start.2 = ((bf16[8,64,384]{2,1,0:T(8,128)(2,1)}), bf16[8,64,384]{2,1,0:T(8,128)(2,1)S(1)}, u32[]{:S(2)}, u32[]{:S(2)}) async-start(bf16[8,64,384]{2,1,0:T(8,128)(2,1)} %bitcast.34), calls=%async_computation.3 | async-start | bytes 786432 | tf_op jit(solution)/shard_map/all_to_all | solution.py:121
  (75 other events, 766.1 us)
Sparse Core Ops, SparseCore 0:
  58.4 51.4 all-gather.2
  143.2 100.3 all-gather.4
  432.7 88.5 reduce-scatter.1

commit v3 on v2

--- a/solution.py
+++ b/solution.py
@@ -77,12 +77,14 @@
     return swap(odd, "ctx", 1)
 
 
-def scatter_far(even, odd):
+def scatter_sum(even, odd):
+    return (even.astype(WIDE) + odd.astype(WIDE)).astype(LOW)
+
+
+def scatter_far(quad):
     count = lax.axis_size("ctx")
-    quad = even.astype(WIDE) + odd.astype(WIDE)
     if count != 8:
-        return (quad,)
-    quad = quad.astype(LOW)
+        return (quad.astype(WIDE),)
     rows = quad.shape[0] // 4
     half = rows // 2
     own, to_x, to_y, far = (quad[j * rows : (j + 1) * rows] for j in range(4))
@@ -121,14 +123,13 @@
     return lax.all_to_all(stack, "ctx", 0, 0, tiled=True)
 
 
-def double_fsdp(stack, first, last):
-    bits, bit = [], first
+def double_fsdp(stacks, first, last):
+    bit = first
     while bit >= last:
-        bits.append(bit)
+        sent = stacks[0] if len(stacks) == 1 else jnp.concatenate(stacks, axis=0)
+        stacks = stacks + [swap(sent, "fsdp", bit)]
         bit //= 2
-    for bit in bits:
-        stack = jnp.concatenate([stack, swap(stack, "fsdp", bit)], axis=0)
-    return stack
+    return stacks
 
 
 def xor_order(first, last):
@@ -139,26 +140,28 @@
     return order
 
 
-def place_kernel(spots, rows, base_ref, *refs):
+def place_kernel(masks, rows, base_ref, *refs):
     out_ref = refs[-1]
-    for (mask, offset), part in zip(spots, refs[:-1]):
-        start = pl.multiple_of((base_ref[0] ^ mask) * rows + offset, 16)
-        out_ref[pl.ds(start, part.shape[0]), :] = part[...]
-
-
-def place(parts, base, count):
-    columns = parts[0][2].shape[1]
-    total = sum(part.shape[0] for _, _, part in parts)
+    masks = iter(masks)
+    for part in refs[:-1]:
+        for j in range(part.shape[0]):
+            start = pl.multiple_of((base_ref[0] ^ next(masks)) * rows, 16)
+            out_ref[pl.ds(start, rows), :] = part[j]
+
+
+def place(parts, masks, base):
+    _, rows, columns = parts[0].shape
+    total = len(masks) * rows
     whole = pl.BlockSpec(memory_space=pltpu.VMEM)
     return pl.pallas_call(
-        functools.partial(place_kernel, [(m, o) for m, o, _ in parts], total // count),
+        functools.partial(place_kernel, masks, rows),
         in_specs=[pl.BlockSpec(memory_space=pltpu.SMEM)] + [whole] * len(parts),
         out_specs=whole,
-        out_shape=jax.ShapeDtypeStruct((total, columns), parts[0][2].dtype),
+        out_shape=jax.ShapeDtypeStruct((total, columns), parts[0].dtype),
         compiler_params=pltpu.CompilerParams(vmem_limit_bytes=VMEM_LIMIT),
         cost_estimate=pl.CostEstimate(flops=0, bytes_accessed=total * columns * 2, transcendentals=0),
         name="place",
-    )(base.reshape(1), *[part for _, _, part in parts])
+    )(base.reshape(1), *parts)
 
 
 def halve_fsdp(stack, base, first, last):
@@ -231,7 +234,7 @@
 
 def backward_kernel(
     heads, steps, q_ref, k_ref, v_ref, do_ref, lse_ref, cos_ref, sin_ref, cosk_ref, sink_ref,
-    row_ref, col_ref, dq_ref, dkv_ref, kt_ref, dk_ref, dv_ref,
+    row_ref, col_ref, out_ref, kt_ref, dk_ref, dv_ref,
 ):
     @pl.when(pl.program_id(0) == 0)
     def _():
@@ -257,16 +260,18 @@
         grads.append(dot(keys_t, grad_scores) * scale)
     grad_q = jnp.concatenate(grads, axis=0).T
     cosine, sine = cos_ref[...], sin_ref[...]
+    block = grad_q.shape[0]
+    rows = pl.ds(pl.multiple_of(pl.program_id(0) * block, block), block)
     for pair in range(heads // 2):
         lanes = slice(pair * 128, pair * 128 + 128)
-        dq_ref[:, lanes] = turned(grad_q[:, lanes], cosine, -sine).astype(LOW)
+        out_ref[rows, lanes] = turned(grad_q[:, lanes], cosine, -sine).astype(LOW)
 
     @pl.when(pl.program_id(0) == steps - 1)
     def _():
         both = jnp.concatenate([dk_ref[...], dv_ref[...]], axis=1)
         back = turned(both, cosk_ref[...], -sink_ref[...])
         lane = lax.broadcasted_iota(jnp.int32, both.shape, 1)
-        dkv_ref[...] = jnp.where(lane < HEAD_DIM, back, both).astype(LOW)
+        out_ref[:, heads * HEAD_DIM :] = jnp.where(lane < HEAD_DIM, back, both).astype(LOW)
 
 
 def attention_forward(qkv, cosine, sine, places, heads):
@@ -322,11 +327,8 @@
             rows(128), rows(128), whole((length, 128)), whole((length, 128)),
             pl.BlockSpec((1, block), lambda i: (0, i)), whole((length, 1)),
         ],
-        out_specs=[rows(width), whole((length, 128))],
-        out_shape=[
-            jax.ShapeDtypeStruct((length, width), LOW),
-            jax.ShapeDtypeStruct((length, 128), LOW),
-        ],
+        out_specs=whole((length, width + 128)),
+        out_shape=jax.ShapeDtypeStruct((length, width + 128), LOW),
         scratch_shapes=[
             pltpu.VMEM((HEAD_DIM, length), LOW),
             pltpu.VMEM((length, HEAD_DIM), WIDE),
@@ -428,24 +430,24 @@
     downs = refs[2 + per_step + blocks : 2 + per_step + 2 * blocks]
     norm_out, cot_out, act_out, low_out, even_out, odd_out = refs[-6:]
     step = pl.program_id(0)
+    width = downs[0].shape[0]
     norm = jnp.where(step < steps // 2, even_ref[...], odd_ref[...])
     norm_out[...] = norm
-    cot = jnp.concatenate([ref[0, 0] for ref in cot_refs], axis=0)
+    cot = jnp.concatenate([ref[0] for ref in cot_refs], axis=0)
     cot_out[...] = cot
     term = None
     for j in range(blocks):
         rows = dot(norm, weights[j][...])
+        gate, up = rows[:, :width], rows[:, width:]
         grad_act = dot(cot, downs[j][...], ((1,), (1,)))
-        width = rows.shape[1] // 2
-        gate, up = rows[:, :width], rows[:, width:]
         sig = 1.0 / (1.0 + jnp.exp(-gate))
         gate_sig = gate * sig
-        act_out[:, j * width : (j + 1) * width] = (gate_sig * up).astype(LOW)
-        grad_up = grad_act * gate_sig
-        grad_gate = grad_act * up * (sig + gate_sig * (1.0 - sig))
-        low = jnp.concatenate([grad_gate, grad_up], axis=1).astype(LOW)
-        low_out[j] = low
-        more = dot(low, weights[j][...], ((1,), (1,)))
+        act_out[j] = (gate_sig * up).astype(LOW)
+        grad_up = (grad_act * gate_sig).astype(LOW)
+        grad_gate = (grad_act * up * (sig + gate_sig * (1.0 - sig))).astype(LOW)
+        low_out[2 * j] = grad_gate
+        low_out[2 * j + 1] = grad_up
+        more = dot(jnp.concatenate([grad_gate, grad_up], axis=1), weights[j][...], ((1,), (1,)))
         term = more if term is None else term + more
     term = term.astype(LOW)
 
@@ -460,10 +462,9 @@
 
 def feed_forward(which, even, odd, cots, table, weights, downs, earlier):
     half, width = even.shape
-    _, c_count, tok_rows, _ = cots.shape
+    c_count, tok_rows, _ = cots.shape
     blocks = len(weights)
-    both = weights[0].shape[1]
-    block = both // 2
+    block = downs[0].shape[0]
     steps = 4
     rows = 2 * half // steps
     per_step = rows // tok_rows
@@ -472,24 +473,24 @@
     even_at = lambda i, t: (jnp.minimum(i, steps // 2 - 1), 0)
     odd_at = lambda i, t: (jnp.maximum(i - steps // 2, 0), 0)
     cot_spec = lambda j: pl.BlockSpec(
-        (1, 1, tok_rows, width), lambda i, t, j=j: (which, t[i * per_step + j], 0, 0)
+        (1, tok_rows, width), lambda i, t, j=j: (t[i * per_step + j], 0, 0)
     )
     fixed = lambda shape: pl.BlockSpec(shape, lambda i, t: (0,) * len(shape))
     at = lambda i, t: (first + i, 0)
     out_shape = [
         jax.ShapeDtypeStruct((total, width), LOW),
         jax.ShapeDtypeStruct((total, width), LOW),
-        jax.ShapeDtypeStruct((total, blocks * block), LOW),
-        jax.ShapeDtypeStruct((blocks, total, both), LOW),
+        jax.ShapeDtypeStruct((blocks, total, block), LOW),
+        jax.ShapeDtypeStruct((2 * blocks, total, block), LOW),
         jax.ShapeDtypeStruct((half, width), LOW),
         jax.ShapeDtypeStruct((half, width), LOW),
     ]
-    inputs = [even, odd] + [cots] * per_step + list(weights) + list(downs) + list(earlier)
+    weights = list(weights) + list(downs)
+    inputs = [even, odd] + [cots] * per_step + weights + list(earlier)
     in_specs = (
         [pl.BlockSpec((rows, width), even_at), pl.BlockSpec((rows, width), odd_at)]
         + [cot_spec(j) for j in range(per_step)]
         + [fixed(w.shape) for w in weights]
-        + [fixed(d.shape) for d in downs]
         + [pl.BlockSpec(memory_space=pl.ANY)] * len(earlier)
     )
     aliases = {1 + len(inputs) - len(earlier) + j: j for j in range(len(earlier))}
@@ -502,8 +503,8 @@
             out_specs=[
                 pl.BlockSpec((rows, width), at),
                 pl.BlockSpec((rows, width), at),
-                pl.BlockSpec((rows, blocks * block), at),
-                pl.BlockSpec((blocks, rows, both), lambda i, t: (0, first + i, 0)),
+                pl.BlockSpec((blocks, rows, block), lambda i, t: (0, first + i, 0)),
+                pl.BlockSpec((2 * blocks, rows, block), lambda i, t: (0, first + i, 0)),
                 pl.BlockSpec((rows, width), even_at),
                 pl.BlockSpec((rows, width), odd_at),
             ],
@@ -520,33 +521,39 @@
 
 def down_kernel(blocks, table_ref, act_ref, *refs):
     out_ref, downs = refs[-1], refs[:-1]
-    block = act_ref.shape[1] // blocks
     total = None
     for j in range(blocks):
-        part = dot(act_ref[:, j * block : (j + 1) * block], downs[j][...])
+        part = dot(act_ref[j], downs[j][...])
         total = part if total is None else total + part
-    out_ref[0, 0] = total.astype(LOW)
-
-
-def down_terms_by_device(acts, table, downs, tok_rows):
-    total, local = acts.shape
-    c_count = table.shape[0]
+    total = total.astype(LOW)
+    chips, rows = out_ref.shape[0], out_ref.shape[3]
+    for q in range(chips):
+        out_ref[table_ref[0] ^ q, 0, 0] = total[q * rows : (q + 1) * rows]
+
+
+def down_terms_by_device(acts, c_index, c_count, downs, tok_rows):
+    blocks, total, block = acts.shape
     width = downs[0].shape[1]
+    chips = c_count // 2
     fixed = lambda shape: pl.BlockSpec(shape, lambda i, j, t: (0,) * len(shape))
-    return pl.pallas_call(
-        functools.partial(down_kernel, len(downs)),
+    place_of = jnp.stack([c_index // 2, c_index % 2]).astype(jnp.int32)
+    out = pl.pallas_call(
+        functools.partial(down_kernel, blocks),
         grid_spec=pltpu.PrefetchScalarGridSpec(
             num_scalar_prefetch=1,
-            grid=(2, c_count),
-            in_specs=[pl.BlockSpec((tok_rows, local), lambda i, j, t: (i * c_count + j, 0))]
+            grid=(2, 2),
+            in_specs=[pl.BlockSpec((blocks, chips * tok_rows, block), lambda i, j, t: (0, 2 * i + j, 0))]
             + [fixed(d.shape) for d in downs],
-            out_specs=pl.BlockSpec((1, 1, tok_rows, width), lambda i, j, t: (t[j], i, 0, 0)),
+            out_specs=pl.BlockSpec(
+                (chips, 1, 1, tok_rows, width), lambda i, j, t: (0, t[1] ^ j, i, 0, 0)
+            ),
         ),
-        out_shape=jax.ShapeDtypeStruct((c_count, 2, tok_rows, width), LOW),
+        out_shape=jax.ShapeDtypeStruct((chips, 2, 2, tok_rows, width), LOW),
         compiler_params=pltpu.CompilerParams(vmem_limit_bytes=VMEM_LIMIT),
         cost_estimate=pl.CostEstimate(flops=0, bytes_accessed=8 << 20, transcendentals=0),
         name="down_terms",
-    )(table, acts, *downs)
+    )(place_of, acts, *downs)
+    return out.reshape(c_count * 2 * tok_rows, width)
 
 
 def inverse_rms(rows):
@@ -585,7 +592,7 @@
     ]
     qkv_piece = (jnp.concatenate(shares, axis=2).astype(WIDE) * attn_scale[:, :, None]).astype(LOW)
     qkv_piece = qkv_piece.transpose(1, 0, 2)
-    qkv_piece, w_gate_in, w_out = tie(qkv_piece, w_gate, w_out)
+    qkv_piece, w_out, w_down = tie(qkv_piece, w_out, w_down)
     qkv_piece = exchange_ctx(qkv_piece).reshape(1, c_count * piece, qkv_width)
     out_route = [(f_count * c + j, j * c_count + c) for c in range(c_count) for j in range(f_count)]
     out_piece = lax.ppermute(w_out, ("fsdp", "ctx"), out_route)
@@ -593,12 +600,16 @@
     for bit in [2 ** j for j in range(1, c_count.bit_length() - 1)] + [1]:
         small = jnp.concatenate([small, swap(small, "ctx", bit)], axis=0)
     int_places = small.reshape(-1)
-    gate_up = columns_by_device(w_gate_in, w_up, mlp_scale, ff_block)
-
-    qkv_piece, out_piece, near_tokens = tie(qkv_piece, out_piece, near_tokens)
+    down_half = ff_block // 2
+    down_tops = [swap(w_down[:down_half], "fsdp", r) for r in range(1, top_bit)]
+
+    qkv_piece, out_piece, near_tokens, own_cot, w_gate_in = tie(
+        qkv_piece, out_piece, near_tokens, own_cot, w_gate
+    )
     even_tokens = gather_far(own_tokens, near_tokens)
-    qkv_piece = qkv_piece[0]
-    qkv_parts = [qkv_piece] + [swap(qkv_piece, "fsdp", r) for r in range(1, f_count)]
+    qkv_parts = double_fsdp([qkv_piece], top_bit, 2)
+    own_cots = lax.all_gather(own_cot, "ctx", axis=0, tiled=True)
+    columns = columns_by_device(w_gate_in, w_up, mlp_scale, ff_block)
     half_dim = HEAD_DIM // 2
     frequency = jnp.power(ROPE_BASE, -2.0 * jnp.arange(half_dim, dtype=WIDE) / HEAD_DIM)
     angles = int_places.astype(WIDE)[:, None] * frequency[None, :]
@@ -606,9 +617,14 @@
     cosine = jnp.concatenate([cosine] * 4, axis=1)
     sine = jnp.concatenate([-sine, sine, -sine, sine], axis=1)
 
-    out_piece, cosine, sine, even_tokens = tie(out_piece, cosine, sine, even_tokens)
+    qkv_parts, out_piece, cosine, sine, even_tokens, down_tops, columns, own_cot = tie(
+        qkv_parts, out_piece, cosine, sine, even_tokens, down_tops, columns, own_cot
+    )
+    half = tok_rows // 2
+    cot_top = swap(own_cot[:half], "fsdp", top_bit)
     quad_tokens, other_tokens = gather_core(even_tokens)
-    w_out_rows = lax.all_gather(out_piece, "fsdp", axis=0, tiled=True)
+    qkv_parts = double_fsdp(qkv_parts, 1, 1)
+    out_parts = double_fsdp([out_piece[None]], top_bit, 2)
 
     def first_norm(rows):
         rows = rows.astype(WIDE)
@@ -616,29 +632,35 @@
 
     normed_first = [first_norm(quad_tokens), first_norm(other_tokens)]
 
-    qkv_parts, gate_up, own_cot, normed_first, w_down = tie(
-        qkv_parts, gate_up, own_cot, normed_first, w_down
-    )
-    gate_up = lax.all_to_all(gate_up, ("fsdp", "ctx"), 0, 0, tiled=True)
-    side_cot = swap(own_cot, "fsdp", top_bit)
-    downs = [w_down] + [swap(w_down, "fsdp", r) for r in range(1, top_bit)]
-    w_qkv = place([(r, 0, part) for r, part in enumerate(qkv_parts)], f_index, f_count)
+    qkv_parts, out_parts, normed_first, columns, cot_top, own_cot = tie(
+        qkv_parts, out_parts, normed_first, columns, cot_top, own_cot
+    )
+    exchange_all = lambda stack: lax.all_to_all(stack, ("fsdp", "ctx"), 0, 0, tiled=True)
+    columns = exchange_all(columns)
+    out_parts = double_fsdp(out_parts, 1, 1)
+    w_qkv = place(qkv_parts, f_order, f_index)
     qkv = jnp.concatenate([dot(rows, w_qkv) for rows in normed_first], axis=0)
     mixed, lse, q_scaled, k_rot, v_low = attention_forward(qkv, cosine, sine, int_places, heads)
 
-    mixed, side_cot, downs = tie(mixed, side_cot, downs)
-    cots = lax.all_gather(jnp.stack([own_cot, side_cot], axis=0), "ctx", axis=1, tiled=True)
+    mixed, out_parts, columns, own_cot = tie(mixed, out_parts, columns, own_cot)
+    cut = width // 2
+    own_columns = columns.reshape(width, 2 * ff_block)
+    tops = [swap(own_columns[:cut], "fsdp", r) for r in range(1, top_bit)]
+    cot_low = swap(own_cot[half:], "fsdp", top_bit)
+    w_out_rows = place(out_parts, f_order, f_index)
     middle = mixed.shape[0] // 2
     odd_out = scatter_core(dot(mixed[middle:], w_out_rows, out=LOW))
     even_out = dot(mixed[:middle], w_out_rows, out=LOW)
-    state = scatter_far(even_out, odd_out)
+    state = scatter_far(scatter_sum(even_out, odd_out))
     inputs = own_tokens.astype(WIDE)
     inv_first = inverse_rms(inputs)
     hat_first = inputs * inv_first
-    state, hat_first, gate_up = tie(state, hat_first, gate_up)
-    gate_ups = [gate_up.reshape(width, 2 * ff_block)]
-    halves = [gate_ups[0][: width // 2], gate_ups[0][width // 2 :]]
-    tops = [swap(halves[0], "fsdp", r) for r in range(1, top_bit)]
+    all_first = jnp.concatenate(normed_first, axis=0)
+    state, hat_first, all_first, own_columns, tops, cot_low = tie(
+        state, hat_first, all_first, own_columns, tops, cot_low
+    )
+    side_cots = lax.all_gather(jnp.concatenate([cot_top, cot_low], axis=0), "ctx", axis=0, tiled=True)
+    lows = [swap(own_columns[cut:], "fsdp", r) for r in range(1, top_bit)]
     hidden = inputs + scatter_end(scatter_near(state))
     inv_second = inverse_rms(hidden)
     hat_second = hidden * inv_second
@@ -646,61 +668,72 @@
 
     near_norm = gather_near(normed_own)
     side_norm = swap(normed_own, "fsdp", top_bit)
-    near_norm, side_norm, tops, halves = tie(near_norm, side_norm, tops, halves)
-    lows = [swap(halves[1], "fsdp", r) for r in range(1, top_bit)]
+    near_norm, side_norm, own_columns, w_down, lows = tie(near_norm, side_norm, own_columns, w_down, lows)
+    columns = [own_columns] + [jnp.concatenate(parts, axis=0) for parts in zip(tops, lows)]
+    down_lows = [swap(w_down[down_half:], "fsdp", r) for r in range(1, top_bit)]
     even_norm = gather_far(normed_own, near_norm)
     near_side = gather_near(side_norm)
     norm_pieces = list(gather_core(even_norm))
-    near_side, norm_pieces, cots, lows = tie(near_side, norm_pieces, cots, lows)
-    gate_ups += [jnp.concatenate(parts, axis=0) for parts in zip(tops, lows)]
+    near_side, norm_pieces, own_cots, down_lows = tie(near_side, norm_pieces, own_cots, down_lows)
+    downs = [w_down] + [jnp.concatenate(parts, axis=0) for parts in zip(down_tops, down_lows)]
     even_side = gather_far(side_norm, near_side)
-    cots = cots.reshape(2, c_count, tok_rows, width)
     table = jnp.array(c_order, jnp.int32) ^ c_index
-
-    *buffers, even_zero, odd_zero = feed_forward(0, *norm_pieces, cots, table, gate_ups, downs, [])
+    by_block = lambda rows: rows.reshape(c_count, tok_rows, width)
+
+    weights = (table, columns, downs)
+    *buffers, even_zero, odd_zero = feed_forward(0, *norm_pieces, by_block(own_cots), *weights, [])
     even_side, buffers, even_zero, odd_zero = tie(even_side, buffers, even_zero, odd_zero)
-    norm_pieces = gather_core(even_side)
-    odd_zero = scatter_core(odd_zero)
-    state_zero = scatter_far(even_zero, odd_zero)
-    norm_pieces, state_zero = tie(norm_pieces, state_zero)
-    *buffers, even_one, odd_one = feed_forward(1, *norm_pieces, cots, table, gate_ups, downs, buffers)
+    side_norms = gather_core(even_side)
+    quad_zero = scatter_sum(even_zero, scatter_core(odd_zero))
+    side_norms, quad_zero, buffers, side_cots = tie(side_norms, quad_zero, buffers, side_cots)
+    state_zero = scatter_far(quad_zero)
+    *buffers, even_one, odd_one = feed_forward(1, *side_norms, by_block(side_cots), *weights, buffers)
     all_norms, all_cots, all_acts, all_lows = buffers
-    state_zero, odd_one = tie(state_zero, odd_one)
+    state_zero, odd_one, even_one, all_norms = tie(state_zero, odd_one, even_one, all_norms)
     odd_one = scatter_core(odd_one)
     state_zero = scatter_near(state_zero)
-    state_zero, odd_one = tie(state_zero, odd_one)
-    state_one = scatter_far(even_one, odd_one)
-
-    act_of = lambda j: all_acts[:, j * ff_block : (j + 1) * ff_block]
-    gate_up_away = [dot(all_norms, all_lows[j], ((0,), (0,)), LOW) for j in range(1, len(downs))]
-    state_one, gate_up_away, all_lows = tie(state_one, gate_up_away, all_lows)
+
+    blocks = range(1, top_bit)
+    gate_away = [dot(all_norms, all_lows[2 * j], ((0,), (0,)), LOW) for j in blocks]
+    quad_one = scatter_sum(even_one, odd_one)
+    quad_one, state_zero, gate_away, all_norms = tie(quad_one, state_zero, gate_away, all_norms)
+    state_one = scatter_far(quad_one)
+    gate_received = [swap(part, "fsdp", r) for r, part in enumerate(gate_away, 1)]
+    up_away = [dot(all_norms, all_lows[2 * j + 1], ((0,), (0,)), LOW) for j in blocks]
+    state_one, up_away, all_norms, all_acts, all_cots = tie(
+        state_one, up_away, all_norms, all_acts, all_cots
+    )
     state_one = scatter_near(state_one)
-    cut = width // 2
-    tops = [swap(part[:cut], "fsdp", r) for r, part in enumerate(gate_up_away, 1)]
-    gate_up_own = dot(all_norms, all_lows[0], ((0,), (0,)))
-    down_away = [dot(act_of(j), all_cots, ((0,), (0,)), LOW) for j in range(1, len(downs))]
+    down_away = [dot(all_acts[j], all_cots, ((0,), (0,)), LOW) for j in blocks]
+    state_one, down_away, all_norms, all_acts = tie(state_one, down_away, all_norms, all_acts)
     side_one = swap(scatter_end(state_one).astype(LOW), "fsdp", top_bit)
-    side_one, tops, gate_up_away, gate_up_own, down_away = tie(
-        side_one, tops, gate_up_away, gate_up_own, down_away
-    )
-    lows = [swap(part[cut:], "fsdp", r) for r, part in enumerate(gate_up_away, 1)]
+    gate_own = dot(all_norms, all_lows[0], ((0,), (0,)), LOW)
+    down_terms = down_terms_by_device(all_acts, c_index, c_count, downs, tok_rows)
+    side_one, gate_own, all_norms, up_away, down_terms = tie(
+        side_one, gate_own, all_norms, up_away, down_terms
+    )
     grad_normed = scatter_end(state_zero) + side_one.astype(WIDE)
 
     grad_hidden = own_cot.astype(WIDE) + norm_back(grad_normed, hat_second, inv_second)
     hidden_low = grad_hidden.astype(LOW)
     near_hidden = gather_near(hidden_low)
-    down_terms = down_terms_by_device(all_acts, table, downs, tok_rows)
-    near_hidden, down_terms, lows, down_away = tie(near_hidden, down_terms, lows, down_away)
+    up_received = [swap(part, "fsdp", r) for r, part in enumerate(up_away, 1)]
+    up_own = dot(all_norms, all_lows[1], ((0,), (0,)), LOW)
+    near_hidden, up_own = tie(near_hidden, up_own)
     even_hidden = gather_far(hidden_low, near_hidden)
-    out_rows = lax.psum_scatter(down_terms.reshape(-1, width), "ctx", scatter_dimension=0, tiled=True)
+    even_hidden, up_received, gate_received, down_terms = tie(
+        even_hidden, up_received, gate_received, down_terms
+    )
+    out_rows = lax.psum_scatter(down_terms, "ctx", scatter_dimension=0, tiled=True)
     out_rows = out_rows.reshape(2, tok_rows, width)
-    received = [jnp.concatenate(parts, axis=0) for parts in zip(tops, lows)]
-    gate_up_sum = sum([part.astype(WIDE) for part in received], gate_up_own).astype(LOW)
-    even_hidden, gate_up_sum = tie(even_hidden, gate_up_sum)
     hidden_halves = gather_core(even_hidden)
-    gate_up_sum = lax.all_to_all(
-        gate_up_sum.reshape(devices, piece, 2 * ff_block), ("fsdp", "ctx"), 0, 0, tiled=True
-    )
+
+    def sum_by_device(own, parts):
+        total = sum([part.astype(WIDE) for part in parts], own.astype(WIDE)).astype(LOW)
+        return total.reshape(devices, piece, ff_block)
+
+    both_sums = [sum_by_device(gate_own, gate_received), sum_by_device(up_own, up_received)]
+    both_sums = exchange_all(jnp.concatenate(both_sums, axis=2))
     grad_mixed = jnp.concatenate([dot(h, w_out_rows, ((1,), (1,)), LOW) for h in hidden_halves], axis=0)
     out_part = dot(mixed[:middle], hidden_halves[0], ((0,), (0,))) + dot(
         mixed[middle:], hidden_halves[1], ((0,), (0,))
@@ -709,35 +742,35 @@
 
     grad_mixed, out_part = tie(grad_mixed, out_part)
     out_sum = halve_near(out_part, f_index)
-    down_sum = dot(act_of(0), all_cots, ((0,), (0,)))
-    grad_q, grad_kv = attention_backward(
+    grad_qkv = attention_backward(
         q_scaled, k_rot, v_low, grad_mixed, lse, cosine, sine, int_places, heads
     )
-    grad_qkv = jnp.concatenate([grad_q, grad_kv], axis=1)
-    grad_qkv, out_sum = tie(grad_qkv, out_sum)
-
-    halves = [grad_qkv[middle:], grad_qkv[:middle]]
-    odd = scatter_core(dot(halves[0], w_qkv, ((1,), (1,)), LOW))
-    qkv_part = dot(normed_first[0], halves[1], ((0,), (0,))) + dot(normed_first[1], halves[0], ((0,), (0,)))
-    qkv_part = qkv_part.astype(LOW).reshape(f_count, c_count * piece, qkv_width)
-    even = dot(halves[1], w_qkv, ((1,), (1,)), LOW)
-    odd, even, qkv_part = tie(odd, even, qkv_part)
-    state = scatter_far(even, odd)
+
+    grad_qkv, all_first = tie(grad_qkv, all_first)
+    qkv_part = dot(all_first, grad_qkv, ((0,), (0,)), LOW)
+    qkv_part = qkv_part.reshape(f_count, c_count * piece, qkv_width)
+    grad_qkv, qkv_part = tie(grad_qkv, qkv_part)
     qkv_sum = halve_near(qkv_part, f_index)
+    grad_qkv, both_sums, out_sum = tie(grad_qkv, both_sums, out_sum)
+    odd = scatter_core(dot(grad_qkv[middle:], w_qkv, ((1,), (1,)), LOW))
+    even = dot(grad_qkv[:middle], w_qkv, ((1,), (1,)), LOW)
+    quad = scatter_sum(even, odd)
     out_sum = halve_far(out_sum, f_index, top_bit)
-    state, qkv_sum, out_sum, down_away = tie(state, qkv_sum, out_sum, down_away)
-    state = scatter_near(state)
+    qkv_sum, quad, down_away, out_sum = tie(qkv_sum, quad, down_away, out_sum)
+    state = scatter_far(quad)
     qkv_sum = halve_far(qkv_sum, f_index, top_bit)
     out_grad = lax.ppermute(out_sum, ("fsdp", "ctx"), [(d, s) for s, d in out_route]).astype(WIDE)
-    for r, part in enumerate(down_away, 1):
-        down_sum = down_sum + swap(part, "fsdp", r).astype(WIDE)
-    down_grad = down_sum
-    state, qkv_sum, out_rows = tie(state, qkv_sum, out_rows)
+    down_received = [swap(part, "fsdp", r) for r, part in enumerate(down_away, 1)]
+    state, qkv_sum, out_grad, all_cots, out_rows = tie(state, qkv_sum, out_grad, all_cots, out_rows)
+    state = scatter_near(state)
     qkv_sum = exchange_ctx(qkv_sum.reshape(c_count, piece, qkv_width))
     side_out = swap(out_rows[1], "fsdp", top_bit)
+    down_grad = dot(all_acts[0], all_cots, ((0,), (0,)))
+    for part in down_received:
+        down_grad = down_grad + part.astype(WIDE)
     grad_normed = scatter_end(state)
     input_grad = grad_hidden + norm_back(grad_normed, hat_first, inv_first)
-    gate_grad, up_grad, mlp_gain_grad = assemble_columns(gate_up_sum, w_gate, w_up, mlp_scale)
+    gate_grad, up_grad, mlp_gain_grad = assemble_columns(both_sums, w_gate, w_up, mlp_scale)
     mlp_gain_grad = mlp_gain_grad[:, 0]
     output = hidden + out_rows[0].astype(WIDE) + side_out.astype(WIDE)
 

time: 645 us -> 614 us (0.952)
  waiting for transfers between devices: 266 us -> 191 us
  local copies, waits for them, and re-layouts: 29.4 us -> 43.8 us
  starting transfers between devices: 125 us -> 139 us
  matrix products: 50.5 us -> 62.9 us
    ppermute x1, waiting for transfers between devices: 40.4 us -> 2.85 us  [per_device(): lax.ppermute(out_sum, ('fsdp', 'ctx'), [(d, s) for s, d in out_route])]
    ppermute x68 -> x71, waiting for transfers between devices: 220 us -> 184 us  [swap(): return lax.ppermute(block, axis, [(i, i ^ mask) for i in range(count)])]
    dot_general x16 -> x17, matrix products: 50.5 us -> 62.9 us  [dot(): lax.dot_general(left, right, (dims, ((), ())), preferred_element_type=WIDE)]
    ppermute x68 -> x71, starting transfers between devices: 95.5 us -> 106 us  [swap(): return lax.ppermute(block, axis, [(i, i ^ mask) for i in range(count)])]
    unnamed x133 -> x172, local copies, waits for them, and re-layouts: 14.4 us -> 17.4 us
    pallas_call x2 -> x3, Pallas kernels: 17.8 us -> 15 us  [the longest x1 9.32 us: down_terms_by_device(): pl.pallas_call(functools.partial(down_kernel, blocks), grid_spec=pltpu.Pr...]
  transfers between devices with their start and end apart: 77 -> 80, of which waited for: 40 -> 37; matrix products, arithmetic and copies ran while one was open for 18% -> 25% of each run, Pallas kernels for 13% -> 16%
where the time goes in v3:
time: 614 us; the launch traced here: 605 us
  waiting for transfers between devices  191 us (31%)
  starting transfers between devices  139 us (23%)
  Pallas kernels  97.3 us (16%)
  matrix products  62.9 us (10%)
  other arithmetic  56 us (9%)
  local copies, waits for them, and re-layouts  43.8 us (7%)
  between operations  15.3 us (2%)
    ppermute x71, waiting for transfers between devices, swap(): return lax.ppermute(block, axis, [(i, i ^ mask) for i in range(count)])  184 us
    ppermute x71, starting transfers between devices, swap(): return lax.ppermute(block, axis, [(i, i ^ mask) for i in range(count)])  106 us
    dot_general x17, matrix products, dot(): lax.dot_general(left, right, (dims, ((), ())), preferred_element_type=WIDE)  62.9 us
    pallas_call x2, Pallas kernels, feed_forward(): pl.pallas_call(functools.partial(feed_kernel, blocks, steps, per_step), g...  39.5 us
    pallas_call x1, Pallas kernels, attention_backward(): pl.pallas_call(functools.partial(backward_kernel, heads, steps), grid=(st...  18 us
    unnamed x172, local copies, waits for them, and re-layouts  17.4 us
    pallas_call x1, Pallas kernels, attention_forward(): pl.pallas_call(functools.partial(forward_kernel, heads), grid=(length //...  15.8 us
    all_to_all x2, starting transfers between devices, per_device(): lax.all_to_all(stack, ('fsdp', 'ctx'), 0, 0, tiled=True)  14.5 us
  transfers between devices with their start and end apart: 80, of which 37 were waited for; matrix products, arithmetic and copies ran while one was open for 25% of the time, Pallas kernels for 16%

profile of v3, /device:TPU:1, one launch (start us, length us, event | category | flops | bytes accessed | tf_op | source)
XLA Modules:
  0.0 605.2 jit_solution(7660798737160144796)
XLA Ops:
  15.4 4.9 all-to-all-start
  20.3 3.2 collective-permute-start
  28.5 2.4 collective-permute-start.6
  31.9 5.6 collective-permute-start.3
  38.2 3.3 collective-permute-start.7
  45.9 4.0 columns_by_device.1
  51.7 2.9 collective-permute-done.3.refs_1_
  57.5 2.4 collective-permute-start.11
  64.4 15.8 %collective-permute-done.11.refs_1_ = bf16[1,64,2048]{2,1,0:T(8,128)(2,1)S(1)} collective-permute-done((bf16[1,64,2048]{2,1,0:T(8,128)(2,1)S(1)}, bf16[1,64,2048]{2,1,0:T(8,128)(2,1)S(1)}, u32[]{:S(2)}, u32[]{:S(2)}) %collective-permute-start.11) | collective-permute-done | bytes 262176 | tf_op jit(solution)/shard_map/ppermute | solution.py:30
  80.2 5.6 collective-permute-done.13
  87.9 7.9 %all-to-all-start.1 = ((bf16[32,64,512]{2,1,0:T(8,128)(2,1)}), bf16[32,64,512]{2,1,0:T(8,128)(2,1)S(1)}, u32[]{:S(2)}, u32[]{:S(2)}) async-start(bf16[32,64,512]{2,1,0:T(8,128)(2,1)} %columns_by_device.1), calls=%async_computation.1 | async-start | bytes 4194304 | tf_op jit(solution)/shard_map/all_to_all | solution.py:638
  100.5 2.6 place.2
  103.2 2.8 fusion.42
  108.5 15.8 %attention_forward.1 = (bf16[1024,256]{1,0:T(8,128)(2,1)}, f32[8,1024]{1,0:T(8,128)}, bf16[1024,256]{1,0:T(8,128)(2,1)}, bf16[1024,64]{1,0:T(8,128)(2,1)}, bf16[1024,64]{1,0:T(8,128)(2,1)}) custom-call(f32[1024,384]{1,0:T(8,128)} %pad_maximum_fusion.2.q_ref.kv_ref, f32[1024,384]{1,0:T(8,128)} %pad_maximum_fusion.2.q_ref.kv_ref, ...), custom_call_target="tpu_custom_call" | custom-call | bytes 2097152 | tf_op jit(solution)/shard_map/attention_forward/pallas_call | solution.py:283
  124.4 17.3 %collective-permute-done.14.refs_2_ = bf16[2,64,2048]{2,1,0:T(8,128)(2,1)} collective-permute-done((bf16[2,64,2048]{2,1,0:T(8,128)(2,1)S(1)}, bf16[2,64,2048]{2,1,0:T(8,128)(2,1)}, u32[]{:S(2)}, u32[]{:S(2)}) %collective-permute-start.14) | collective-permute-done | bytes 524320 | tf_op jit(solution)/shard_map/ppermute | solution.py:30
  141.7 2.6 all-to-all-done.1
  144.2 3.0 place.3
  157.4 22.6 %collective-permute-done.21 = bf16[64,2048]{1,0:T(8,128)(2,1)S(1)} collective-permute-done((bf16[64,2048]{1,0:T(8,128)(2,1)S(1)}, bf16[64,2048]{1,0:T(8,128)(2,1)S(1)}, u32[]{:S(2)}, u32[]{:S(2)}) %collective-permute-start.21) | collective-permute-done | bytes 262176 | tf_op jit(solution)/shard_map/ppermute | solution.py:30
  181.0 2.6 pad_maximum_fusion
  184.5 2.5 collective-permute-done.19
  192.1 3.3 collective-permute-start.27
  200.7 2.7 collective-permute-start.26
  203.5 13.7 %collective-permute-done.24 = bf16[128,2048]{1,0:T(8,128)(2,1)S(1)} collective-permute-done((bf16[128,2048]{1,0:T(8,128)(2,1)S(1)}, bf16[128,2048]{1,0:T(8,128)(2,1)S(1)}, u32[]{:S(2)}, u32[]{:S(2)}) %collective-permute-start.24) | collective-permute-done | bytes 524320 | tf_op jit(solution)/shard_map/ppermute | solution.py:30
  217.5 9.6 %collective-permute-done.26 = bf16[128,2048]{1,0:T(8,128)(2,1)} collective-permute-done((bf16[128,2048]{1,0:T(8,128)(2,1)S(1)}, bf16[128,2048]{1,0:T(8,128)(2,1)}, u32[]{:S(2)}, u32[]{:S(2)}) %collective-permute-start.26) | collective-permute-done | bytes 524320 | tf_op jit(solution)/shard_map/ppermute | solution.py:30
  230.5 9.0 %collective-permute-done.30 = bf16[64,2048]{1,0:T(8,128)(2,1)S(1)} collective-permute-done((bf16[64,2048]{1,0:T(8,128)(2,1)S(1)}, bf16[64,2048]{1,0:T(8,128)(2,1)S(1)}, u32[]{:S(2)}, u32[]{:S(2)}) %collective-permute-start.30) | collective-permute-done | bytes 262176 | tf_op jit(solution)/shard_map/ppermute | solution.py:30
  249.7 6.6 %collective-permute-done.28 = bf16[128,2048]{1,0:T(8,128)(2,1)} collective-permute-done((bf16[128,2048]{1,0:T(8,128)(2,1)}, bf16[128,2048]{1,0:T(8,128)(2,1)}, u32[]{:S(2)}, u32[]{:S(2)}) %collective-permute-start.28) | collective-permute-done | bytes 524320 | tf_op jit(solution)/shard_map/ppermute | solution.py:30
  265.3 19.7 %feed_forward.2 = (bf16[2048,2048]{1,0:T(8,128)(2,1)}, bf16[2048,2048]{1,0:T(8,128)(2,1)}, bf16[2,2048,256]{2,1,0:T(8,128)(2,1)}, bf16[4,2048,256]{2,1,0:T(8,128...) custom-call(s32[8]{0:T(128)} %broadcast_xor_fusion.table_ref, ...), custom_call_target="tpu_custom_call" | custom-call | bytes 8388608 | tf_op jit(solution)/shard_map/feed_forward/pallas_call | solution.py:497
  292.0 2.7 collective-permute-done.36.refs_1_
  298.5 19.8 %feed_forward.3 = (bf16[2048,2048]{1,0:T(8,128)(2,1)}, bf16[2048,2048]{1,0:T(8,128)(2,1)}, bf16[2,2048,256]{2,1,0:T(8,128)(2,1)}, bf16[4,2048,256]{2,1,0:T(8,128...) custom-call(s32[8]{0:T(128)} %broadcast_xor_fusion.table_ref, ...), custom_call_target="tpu_custom_call", output_to_operand_aliasing={{0}: (9, {}), {1}: (10, {}), {2}: (11, {}), {3}: (12, {})} | custom-call | bytes 8388608 | tf_op jit(solution)/shard_map/feed_forward/pallas_call | solution.py:497
  325.1 7.2 %convolution_convert_fusion.9 = bf16[2048,256]{1,0:T(8,128)(2,1)} fusion(bf16[2048,2048]{1,0:T(8,128)(2,1)} %get-tuple-element.320, bf16[4,2048,256]{2,1,0:T(8,128)(2,1)} %get-tuple-element.291), kind=kOutput, calls=%fused_computation.25 | convolution fusion | flops 2148007936 | bytes 10485760 | tf_op jit(solution)/shard_map/dot_general | solution.py:21
  337.5 3.6 convolution_convert_fusion.8
  342.6 4.9 collective-permute-done.47
  349.4 3.3 convolution_convert_fusion.7
  358.2 9.3 %down_terms.1 = bf16[4,2,2,128,2048]{4,3,2,1,0:T(8,128)(2,1)} custom-call(s32[2]{0:T(128)} %pad_add_fusion.3.table_ref, bf16[2,2048,256]{2,1,0:T(8,128)(2,1)} %get-tuple-element.318.act_ref, bf16[256,2048]{1,0:T(8,128)(2,1)} %refs_0_, bf16[256,2048]{1,0:T(8,128)(2,1)} %copy-done.13), custom_call_target="tpu_custom_call" | custom-call | bytes 8388608 | tf_op jit(solution)/shard_map/down_terms/pallas_call | solution.py:540
  367.5 7.0 %convolution_convert_fusion.6 = bf16[2048,256]{1,0:T(8,128)(2,1)} fusion(bf16[2048,2048]{1,0:T(8,128)(2,1)} %get-tuple-element.320, bf16[4,2048,256]{2,1,0:T(8,128)(2,1)S(1)} %copy-done.31), kind=kOutput, calls=%fused_computation.22 | convolution fusion | flops 2148007936 | bytes 10485760 | tf_op jit(solution)/shard_map/dot_general | solution.py:21
  376.1 2.6 fusion.35
  380.2 4.8 collective-permute-start.56
  384.9 7.1 %convolution_convert_fusion.5 = bf16[2048,256]{1,0:T(8,128)(2,1)} fusion(bf16[2048,2048]{1,0:T(8,128)(2,1)} %get-tuple-element.320, bf16[4,2048,256]{2,1,0:T(8,128)(2,1)} %get-tuple-element.291), kind=kOutput, calls=%fused_computation.21 | convolution fusion | flops 2148007936 | bytes 10485760 | tf_op jit(solution)/shard_map/dot_general | solution.py:21
  393.9 4.8 collective-permute-done.54
  400.0 3.2 collective-permute-done.56
  407.2 5.9 collective-permute-start.58
  417.8 6.6 %all-to-all-start.2 = ((bf16[32,64,512]{2,1,0:T(8,128)(2,1)}), bf16[32,64,512]{2,1,0:T(8,128)(2,1)}, u32[]{:S(2)}, u32[]{:S(2)}) async-start(bf16[32,64,512]{2,1,0:T(8,128)(2,1)} %pad_maximum_fusion.1), calls=%async_computation.2 | async-start | bytes 4194304 | tf_op jit(solution)/shard_map/all_to_all | solution.py:638
  424.5 2.8 convolution_convert_fusion.11
  427.3 2.5 convolution_convert_fusion.10
  430.6 2.3 fusion.29
  432.9 2.3 fusion.4
  438.5 18.0 %attention_backward.1 = bf16[1024,384]{1,0:T(8,128)(2,1)} custom-call(bf16[1024,256]{1,0:T(8,128)(2,1)} %get-tuple-element.233.q_ref, bf16[1024,64]{1,0:T(8,128)(2,1)} %get-tuple-element.234.k_ref, bf16[1024,64]{1,0:T(8,128)(2,1)} %get-tuple-element.235.v_ref, bf16[1024,256]{1,0:T(8,128)(2,1)} %pad_maximum_fusion.10.do_ref, ...), custom_call_target="tpu_custom_call" | custom-call | bytes 2097152 | tf_op jit(solution)/shard_map/attention_backward/pallas_call | solution.py:321
  456.6 4.9 convolution_convert_fusion.4
  461.5 8.6 %collective-permute-done.60 = bf16[2,64,2048]{2,1,0:T(8,128)(2,1)} collective-permute-done((bf16[2,64,2048]{2,1,0:T(8,128)(2,1)}, bf16[2,64,2048]{2,1,0:T(8,128)(2,1)}, u32[]{:S(2)}, u32[]{:S(2)}) %collective-permute-start.60) | collective-permute-done | bytes 524320 | tf_op jit(solution)/shard_map/ppermute | solution.py:30
  472.8 2.6 convolution_convert_fusion.2
  481.4 20.9 %collective-permute-done.59 = bf16[2,512,384]{2,1,0:T(8,128)(2,1)} collective-permute-done((bf16[2,512,384]{2,1,0:T(8,128)(2,1)}, bf16[2,512,384]{2,1,0:T(8,128)(2,1)}, u32[]{:S(2)}, u32[]{:S(2)}) %collective-permute-start.59) | collective-permute-done | bytes 786464 | tf_op jit(solution)/shard_map/ppermute | solution.py:30
  504.1 3.1 add_convert_fusion
  509.1 4.1 collective-permute-start.68
  514.3 3.1 collective-permute-start.63
  517.9 2.9 collective-permute-done.68
  520.8 3.4 collective-permute-start.66
  524.2 4.9 assemble_columns.1
  531.3 2.2 collective-permute-done.67
  533.4 14.0 %collective-permute-start.72 = (bf16[256,2048]{1,0:T(8,128)(2,1)}, bf16[256,2048]{1,0:T(8,128)(2,1)}, u32[]{:S(2)}, u32[]{:S(2)}) collective-permute-start(bf16[256,2048]{1,0:T(8,128)(2,1)} %convolution_convert_fusion.7), channel_id=1, source_target_pairs={{0,8},{8,0},{16,24},{24,16},{1,9},{9,1},{17,25},{25,17},{2,10},{10... | collective-permute-start | bytes 3145736 | tf_op jit(solution)/shard_map/ppermute | solution.py:30
  551.3 3.7 collective-permute-start.69
  559.8 5.7 all-to-all-start.3
  565.5 16.2 %collective-permute-done.72 = bf16[256,2048]{1,0:T(8,128)(2,1)} collective-permute-done((bf16[256,2048]{1,0:T(8,128)(2,1)}, bf16[256,2048]{1,0:T(8,128)(2,1)}, u32[]{:S(2)}, u32[]{:S(2)}) %collective-permute-start.72) | collective-permute-done | bytes 1048608 | tf_op jit(solution)/shard_map/ppermute | solution.py:30
  581.7 7.4 %convolution_add_fusion.1 = f32[256,2048]{1,0:T(8,128)} fusion(bf16[2048,2048]{1,0:T(8,128)(2,1)} %get-tuple-element.365, bf16[256,2048]{1,0:T(8,128)(2,1)} %collective-permute-done.72, bf16[2,2048,256]{2,1,0:T(8,128)(2,1)S(1)} %copy-done.3), kind=kOutput, calls=%fused_computation.19 | convolution fusion | flops 2148532224 | bytes 12582912 | tf_op jit(solution)/shard_map/dot_general | solution.py:21
  596.3 2.1 fusion.23
  (414 shorter events, 164.8 us)
Async XLA Ops:
  7.2 24.6 %collective-permute-start.1 = (bf16[128,2048]{1,0:T(8,128)(2,1)}, bf16[128,2048]{1,0:T(8,128)(2,1)S(1)}, u32[]{:S(2)}, u32[]{:S(2)}) collective-permute-start(bf16[128,2048]{1,0:T(8,128)(2,1)} %bitcast.127), channel_id=1, source_target_pairs={{0,2},{1,3},{2,0},{3,1},{4,6},{5,7},{6,4},{7,5},{8,10},{9,11},{10,... | collective-permute-start | bytes 1572872 | tf_op jit(solution)/shard_map/ppermute | solution.py:30
  9.3 22.5 %collective-permute-start.2 = (bf16[128,2048]{1,0:T(8,128)(2,1)}, bf16[128,2048]{1,0:T(8,128)(2,1)S(1)}, u32[]{:S(2)}, u32[]{:S(2)}) collective-permute-start(bf16[128,2048]{1,0:T(8,128)(2,1)} %bitcast.128), channel_id=1, source_target_pairs={{0,4},{1,5},{2,6},{3,7},{4,0},{5,1},{6,2},{7,3},{8,12},{9,13},{10,... | collective-permute-start | bytes 1572872 | tf_op jit(solution)/shard_map/ppermute | solution.py:30
  10.6 15.4 %collective-permute-start.4 = (s32[1,128]{1,0:T(1,128)}, s32[1,128]{1,0:T(1,128)S(1)}, u32[]{:S(2)}, u32[]{:S(2)}) collective-permute-start(s32[1,128]{1,0:T(1,128)} %param.14), channel_id=1, source_target_pairs={{0,2},{1,3},{2,0},{3,1},{4,6},{5,7},{6,4},{7,5},{8,10},{9,11},{10,... | collective-permute-start | bytes 1544 | tf_op jit(solution)/shard_map/ppermute | solution.py:30
  15.4 16.4 %all-to-all-start = ((bf16[8,64,384]{2,1,0:T(8,128)(2,1)}), bf16[8,64,384]{2,1,0:T(8,128)(2,1)S(1)}, u32[]{:S(2)}, u32[]{:S(2)}) async-start(bf16[8,64,384]{2,1,0:T(8,128)(2,1)} %fusion.24), calls=%async_computation | async-start | bytes 786432 | tf_op jit(solution)/shard_map/all_to_all | solution.py:123
  20.3 11.6 %collective-permute-start = (bf16[64,2048]{1,0:T(8,128)(2,1)S(1)}, bf16[64,2048]{1,0:T(8,128)(2,1)S(1)}, u32[]{:S(2)}, u32[]{:S(2)}) collective-permute-start(bf16[64,2048]{1,0:T(8,128)(2,1)S(1)} %copy-done.70), channel_id=1, source_target_pairs={{0,0},{1,8},{2,16},{3,24},{4,1},{5,9},{6,17},{7,25},{8,2},{9,10},{... | collective-permute-start | bytes 786440 | tf_op jit(solution)/shard_map/ppermute | solution.py:598
  24.3 27.3 %collective-permute-start.9 = (bf16[128,2048]{1,0:T(8,128)(2,1)}, bf16[128,2048]{1,0:T(8,128)(2,1)}, u32[]{:S(2)}, u32[]{:S(2)}) collective-permute-start(bf16[128,2048]{1,0:T(8,128)(2,1)} %slice.241), channel_id=1, source_target_pairs={{0,8},{8,0},{16,24},{24,16},{1,9},{9,1},{17,25},{25,17},{2,10},{10... | collective-permute-start | bytes 1572872 | tf_op jit(solution)/shard_map/ppermute | solution.py:30
  31.9 22.7 %collective-permute-start.3 = (bf16[1,512,384]{2,1,0:T(8,128)(2,1)S(1)}, bf16[1,512,384]{2,1,0:T(8,128)(2,1)S(1)}, u32[]{:S(2)}, u32[]{:S(2)}) collective-permute-start(bf16[1,512,384]{2,1,0:T(8,128)(2,1)S(1)} %bitcast.144), channel_id=1, source_target_pairs={{0,16},{8,24},{16,0},{24,8},{1,17},{9,25},{17,1},{25,9},{2,18},{10... | collective-permute-start | bytes 1179656 | tf_op jit(solution)/shard_map/ppermute | solution.py:30
  38.2 13.5 %collective-permute-start.7 = (bf16[64,2048]{1,0:T(8,128)(2,1)}, bf16[64,2048]{1,0:T(8,128)(2,1)S(1)}, u32[]{:S(2)}, u32[]{:S(2)}) collective-permute-start(bf16[64,2048]{1,0:T(8,128)(2,1)} %slice.239), channel_id=1, source_target_pairs={{0,2},{1,3},{2,0},{3,1},{4,6},{5,7},{6,4},{7,5},{8,10},{9,11},{10,... | collective-permute-start | bytes 786440 | tf_op jit(solution)/shard_map/ppermute | solution.py:30
  42.1 9.5 %collective-permute-start.8 = (bf16[64,2048]{1,0:T(8,128)(2,1)}, bf16[64,2048]{1,0:T(8,128)(2,1)}, u32[]{:S(2)}, u32[]{:S(2)}) collective-permute-start(bf16[64,2048]{1,0:T(8,128)(2,1)} %slice.240), channel_id=1, source_target_pairs={{0,4},{1,5},{2,6},{3,7},{4,0},{5,1},{6,2},{7,3},{8,12},{9,13},{10,... | collective-permute-start | bytes 786440 | tf_op jit(solution)/shard_map/ppermute | solution.py:30
  57.4 30.5 %collective-permute-start.10 = (bf16[2,512,384]{2,1,0:T(8,128)(2,1)S(1)}, bf16[2,512,384]{2,1,0:T(8,128)(2,1)}, u32[]{:S(2)}, u32[]{:S(2)}) collective-permute-start(bf16[2,512,384]{2,1,0:T(8,128)(2,1)S(1)} %pad_maximum_fusion.4), channel_id=1, source_target_pairs={{0,8},{8,0},{16,24},{24,16},{1,9},{9,1},{17,25},{25,17},{2,10},{10... | collective-permute-start | bytes 2359304 | tf_op jit(solution)/shard_map/ppermute | solution.py:30
  57.5 22.7 %collective-permute-start.11 = (bf16[1,64,2048]{2,1,0:T(8,128)(2,1)S(1)}, bf16[1,64,2048]{2,1,0:T(8,128)(2,1)S(1)}, u32[]{:S(2)}, u32[]{:S(2)}) collective-permute-start(bf16[1,64,2048]{2,1,0:T(8,128)(2,1)S(1)} %bitcast.153), channel_id=1, source_target_pairs={{0,16},{8,24},{16,0},{24,8},{1,17},{9,25},{17,1},{25,9},{2,18},{10... | collective-permute-start | bytes 786440 | tf_op jit(solution)/shard_map/ppermute | solution.py:30
  59.9 26.0 %collective-permute-start.13 = (bf16[64,2048]{1,0:T(8,128)(2,1)S(1)}, bf16[64,2048]{1,0:T(8,128)(2,1)S(1)}, u32[]{:S(2)}, u32[]{:S(2)}) collective-permute-start(bf16[64,2048]{1,0:T(8,128)(2,1)S(1)} %slice.242), channel_id=1, source_target_pairs={{0,16},{8,24},{16,0},{24,8},{1,17},{9,25},{17,1},{25,9},{2,18},{10... | collective-permute-start | bytes 786440 | tf_op jit(solution)/shard_map/ppermute | solution.py:30
  87.9 56.3 %all-to-all-start.1 = ((bf16[32,64,512]{2,1,0:T(8,128)(2,1)}), bf16[32,64,512]{2,1,0:T(8,128)(2,1)S(1)}, u32[]{:S(2)}, u32[]{:S(2)}) async-start(bf16[32,64,512]{2,1,0:T(8,128)(2,1)} %columns_by_device.1), calls=%async_computation.1 | async-start | bytes 4194304 | tf_op jit(solution)/shard_map/all_to_all | solution.py:638
  95.8 153.9 %all-gather.3.cloned.1.call-start = ((), (), s32[]{:S(2)}) async-start(), calls=%async_computation.5 | async-start | bytes 4718592 | tf_op jit(solution)/shard_map/all_gather | solution.py:611
  96.5 198.2 %all-gather.5.cloned.1.call-start = ((), (), s32[]{:S(2)}) async-start(), calls=%async_computation.6 | async-start | bytes 4718592 | tf_op jit(solution)/shard_map/all_gather | solution.py:662
  99.1 42.6 %collective-permute-start.14 = (bf16[2,64,2048]{2,1,0:T(8,128)(2,1)S(1)}, bf16[2,64,2048]{2,1,0:T(8,128)(2,1)}, u32[]{:S(2)}, u32[]{:S(2)}) collective-permute-start(bf16[2,64,2048]{2,1,0:T(8,128)(2,1)S(1)} %pad_maximum_fusion.7), channel_id=1, source_target_pairs={{0,8},{8,0},{16,24},{24,16},{1,9},{9,1},{17,25},{25,17},{2,10},{10... | collective-permute-start | bytes 1572872 | tf_op jit(solution)/shard_map/ppermute | solution.py:30
  151.6 32.9 %collective-permute-start.20 = (bf16[1024,512]{1,0:T(8,128)(2,1)S(1)}, bf16[1024,512]{1,0:T(8,128)(2,1)S(1)}, u32[]{:S(2)}, u32[]{:S(2)}) collective-permute-start(bf16[1024,512]{1,0:T(8,128)(2,1)S(1)} %bitcast.152), channel_id=1, source_target_pairs={{0,8},{8,0},{16,24},{24,16},{1,9},{9,1},{17,25},{25,17},{2,10},{10... | collective-permute-start | bytes 3145736 | tf_op jit(solution)/shard_map/ppermute | solution.py:30
  151.7 28.2 %collective-permute-start.21 = (bf16[64,2048]{1,0:T(8,128)(2,1)S(1)}, bf16[64,2048]{1,0:T(8,128)(2,1)S(1)}, u32[]{:S(2)}, u32[]{:S(2)}) collective-permute-start(bf16[64,2048]{1,0:T(8,128)(2,1)S(1)} %slice.254), channel_id=1, source_target_pairs={{0,16},{8,24},{16,0},{24,8},{1,17},{9,25},{17,1},{25,9},{2,18},{10... | collective-permute-start | bytes 786440 | tf_op jit(solution)/shard_map/ppermute | solution.py:30
  154.9 29.6 %collective-permute-start.16 = (bf16[64,2048]{1,0:T(8,128)(2,1)S(1)}, bf16[64,2048]{1,0:T(8,128)(2,1)S(1)}, u32[]{:S(2)}, u32[]{:S(2)}) collective-permute-start(bf16[64,2048]{1,0:T(8,128)(2,1)S(1)} %get-tuple-element.392), channel_id=1, source_target_pairs={{0,2},{1,3},{2,0},{3,1},{4,6},{5,7},{6,4},{7,5},{8,10},{9,11},{10,... | collective-permute-start | bytes 786440 | tf_op jit(solution)/shard_map/ppermute | solution.py:30
  156.0 28.6 %collective-permute-start.17 = (bf16[64,2048]{1,0:T(8,128)(2,1)S(1)}, bf16[64,2048]{1,0:T(8,128)(2,1)S(1)}, u32[]{:S(2)}, u32[]{:S(2)}) collective-permute-start(bf16[64,2048]{1,0:T(8,128)(2,1)S(1)} %get-tuple-element.391), channel_id=1, source_target_pairs={{0,4},{1,5},{2,6},{3,7},{4,0},{5,1},{6,2},{7,3},{8,12},{9,13},{10,... | collective-permute-start | bytes 786440 | tf_op jit(solution)/shard_map/ppermute | solution.py:30
  157.1 27.4 %collective-permute-start.18 = (bf16[64,2048]{1,0:T(8,128)(2,1)S(1)}, bf16[64,2048]{1,0:T(8,128)(2,1)S(1)}, u32[]{:S(2)}, u32[]{:S(2)}) collective-permute-start(bf16[64,2048]{1,0:T(8,128)(2,1)S(1)} %get-tuple-element.390), channel_id=1, source_target_pairs={{0,2},{1,3},{2,0},{3,1},{4,6},{5,7},{6,4},{7,5},{8,10},{9,11},{10,... | collective-permute-start | bytes 786440 | tf_op jit(solution)/shard_map/ppermute | solution.py:30
  192.1 36.1 %collective-permute-start.27 = (bf16[1024,512]{1,0:T(8,128)(2,1)}, bf16[1024,512]{1,0:T(8,128)(2,1)S(1)}, u32[]{:S(2)}, u32[]{:S(2)}) collective-permute-start(bf16[1024,512]{1,0:T(8,128)(2,1)} %slice.257), channel_id=1, source_target_pairs={{0,8},{8,0},{16,24},{24,16},{1,9},{9,1},{17,25},{25,17},{2,10},{10... | collective-permute-start | bytes 3145736 | tf_op jit(solution)/shard_map/ppermute | solution.py:30
  196.3 353.1 %reduce-scatter.2.cloned.1.call-start = ((), (), s32[]{:S(2)}) async-start(), calls=%async_computation.7 | async-start | bytes 9437184 | tf_op jit(solution)/shard_map/reduce_scatter | solution.py:727
  200.3 16.9 %collective-permute-start.24 = (bf16[128,2048]{1,0:T(8,128)(2,1)S(1)}, bf16[128,2048]{1,0:T(8,128)(2,1)S(1)}, u32[]{:S(2)}, u32[]{:S(2)}) collective-permute-start(bf16[128,2048]{1,0:T(8,128)(2,1)S(1)} %get-tuple-element.370), channel_id=1, source_target_pairs={{0,2},{1,3},{2,0},{3,1},{4,6},{5,7},{6,4},{7,5},{8,10},{9,11},{10,... | collective-permute-start | bytes 1572872 | tf_op jit(solution)/shard_map/ppermute | solution.py:30
  200.6 16.9 %collective-permute-start.25 = (bf16[128,2048]{1,0:T(8,128)(2,1)S(1)}, bf16[128,2048]{1,0:T(8,128)(2,1)S(1)}, u32[]{:S(2)}, u32[]{:S(2)}) collective-permute-start(bf16[128,2048]{1,0:T(8,128)(2,1)S(1)} %get-tuple-element.370), channel_id=1, source_target_pairs={{0,4},{1,5},{2,6},{3,7},{4,0},{5,1},{6,2},{7,3},{8,12},{9,13},{10,... | collective-permute-start | bytes 1572872 | tf_op jit(solution)/shard_map/ppermute | solution.py:30
  200.7 26.3 %collective-permute-start.26 = (bf16[128,2048]{1,0:T(8,128)(2,1)S(1)}, bf16[128,2048]{1,0:T(8,128)(2,1)}, u32[]{:S(2)}, u32[]{:S(2)}) collective-permute-start(bf16[128,2048]{1,0:T(8,128)(2,1)S(1)} %get-tuple-element.370), channel_id=1, source_target_pairs={{0,16},{8,24},{16,0},{24,8},{1,17},{9,25},{17,1},{25,9},{2,18},{10... | collective-permute-start | bytes 1572872 | tf_op jit(solution)/shard_map/ppermute | solution.py:30
  228.2 11.3 %collective-permute-start.30 = (bf16[64,2048]{1,0:T(8,128)(2,1)S(1)}, bf16[64,2048]{1,0:T(8,128)(2,1)S(1)}, u32[]{:S(2)}, u32[]{:S(2)}) collective-permute-start(bf16[64,2048]{1,0:T(8,128)(2,1)S(1)} %slice.258), channel_id=1, source_target_pairs={{0,2},{1,3},{2,0},{3,1},{4,6},{5,7},{6,4},{7,5},{8,10},{9,11},{10,... | collective-permute-start | bytes 786440 | tf_op jit(solution)/shard_map/ppermute | solution.py:30
  229.5 10.8 %collective-permute-start.31 = (bf16[64,2048]{1,0:T(8,128)(2,1)S(1)}, bf16[64,2048]{1,0:T(8,128)(2,1)S(1)}, u32[]{:S(2)}, u32[]{:S(2)}) collective-permute-start(bf16[64,2048]{1,0:T(8,128)(2,1)S(1)} %slice.259), channel_id=1, source_target_pairs={{0,4},{1,5},{2,6},{3,7},{4,0},{5,1},{6,2},{7,3},{8,12},{9,13},{10,... | collective-permute-start | bytes 786440 | tf_op jit(solution)/shard_map/ppermute | solution.py:30
  241.0 17.0 %collective-permute-start.32 = (bf16[512,2048]{1,0:T(8,128)(2,1)}, bf16[512,2048]{1,0:T(8,128)(2,1)}, u32[]{:S(2)}, u32[]{:S(2)}) collective-permute-start(bf16[512,2048]{1,0:T(8,128)(2,1)} %constant_dynamic-update-slice_fusion.5.refs_0_), channel_id=1, source_target_pairs={{0,1},{1,0},{2,3},{3,2},{4,5},{5,4},{6,7},{7,6},{8,9},{9,8},{10,11... | collective-permute-start | bytes 6291464 | tf_op jit(solution)/shard_map/ppermute | solution.py:30
  242.5 13.9 %collective-permute-start.28 = (bf16[128,2048]{1,0:T(8,128)(2,1)}, bf16[128,2048]{1,0:T(8,128)(2,1)}, u32[]{:S(2)}, u32[]{:S(2)}) collective-permute-start(bf16[128,2048]{1,0:T(8,128)(2,1)} %collective-permute-done.26), channel_id=1, source_target_pairs={{0,2},{1,3},{2,0},{3,1},{4,6},{5,7},{6,4},{7,5},{8,10},{9,11},{10,... | collective-permute-start | bytes 1572872 | tf_op jit(solution)/shard_map/ppermute | solution.py:30
  242.9 13.6 %collective-permute-start.29 = (bf16[128,2048]{1,0:T(8,128)(2,1)}, bf16[128,2048]{1,0:T(8,128)(2,1)}, u32[]{:S(2)}, u32[]{:S(2)}) collective-permute-start(bf16[128,2048]{1,0:T(8,128)(2,1)} %collective-permute-done.26), channel_id=1, source_target_pairs={{0,4},{1,5},{2,6},{3,7},{4,0},{5,1},{6,2},{7,3},{8,12},{9,13},{10,... | collective-permute-start | bytes 1572872 | tf_op jit(solution)/shard_map/ppermute | solution.py:30
  244.8 13.2 %collective-permute-start.33 = (bf16[128,2048]{1,0:T(8,128)(2,1)}, bf16[128,2048]{1,0:T(8,128)(2,1)}, u32[]{:S(2)}, u32[]{:S(2)}) collective-permute-start(bf16[128,2048]{1,0:T(8,128)(2,1)} %slice.260), channel_id=1, source_target_pairs={{0,8},{8,0},{16,24},{24,16},{1,9},{9,1},{17,25},{25,17},{2,10},{10... | collective-permute-start | bytes 1572872 | tf_op jit(solution)/shard_map/ppermute | solution.py:30
  259.0 26.0 %collective-permute-start.34 = (bf16[64,2048]{1,0:T(8,128)(2,1)S(1)}, bf16[64,2048]{1,0:T(8,128)(2,1)S(1)}, u32[]{:S(2)}, u32[]{:S(2)}) collective-permute-start(bf16[64,2048]{1,0:T(8,128)(2,1)S(1)} %slice.261), channel_id=1, source_target_pairs={{0,2},{1,3},{2,0},{3,1},{4,6},{5,7},{6,4},{7,5},{8,10},{9,11},{10,... | collective-permute-start | bytes 786440 | tf_op jit(solution)/shard_map/ppermute | solution.py:30
  261.2 23.8 %collective-permute-start.35 = (bf16[64,2048]{1,0:T(8,128)(2,1)S(1)}, bf16[64,2048]{1,0:T(8,128)(2,1)S(1)}, u32[]{:S(2)}, u32[]{:S(2)}) collective-permute-start(bf16[64,2048]{1,0:T(8,128)(2,1)S(1)} %slice.262), channel_id=1, source_target_pairs={{0,4},{1,5},{2,6},{3,7},{4,0},{5,1},{6,2},{7,3},{8,12},{9,13},{10,... | collective-permute-start | bytes 786440 | tf_op jit(solution)/shard_map/ppermute | solution.py:30
  295.6 22.8 %collective-permute-start.38 = (bf16[64,2048]{1,0:T(8,128)(2,1)S(1)}, bf16[64,2048]{1,0:T(8,128)(2,1)S(1)}, u32[]{:S(2)}, u32[]{:S(2)}) collective-permute-start(bf16[64,2048]{1,0:T(8,128)(2,1)S(1)} %get-tuple-element.386), channel_id=1, source_target_pairs={{0,2},{1,3},{2,0},{3,1},{4,6},{5,7},{6,4},{7,5},{8,10},{9,11},{10,... | collective-permute-start | bytes 786440 | tf_op jit(solution)/shard_map/ppermute | solution.py:30
  296.0 22.4 %collective-permute-start.39 = (bf16[64,2048]{1,0:T(8,128)(2,1)S(1)}, bf16[64,2048]{1,0:T(8,128)(2,1)S(1)}, u32[]{:S(2)}, u32[]{:S(2)}) collective-permute-start(bf16[64,2048]{1,0:T(8,128)(2,1)S(1)} %get-tuple-element.385), channel_id=1, source_target_pairs={{0,4},{1,5},{2,6},{3,7},{4,0},{5,1},{6,2},{7,3},{8,12},{9,13},{10,... | collective-permute-start | bytes 786440 | tf_op jit(solution)/shard_map/ppermute | solution.py:30
  297.1 21.3 %collective-permute-start.40 = (bf16[64,2048]{1,0:T(8,128)(2,1)S(1)}, bf16[64,2048]{1,0:T(8,128)(2,1)S(1)}, u32[]{:S(2)}, u32[]{:S(2)}) collective-permute-start(bf16[64,2048]{1,0:T(8,128)(2,1)S(1)} %get-tuple-element.384), channel_id=1, source_target_pairs={{0,2},{1,3},{2,0},{3,1},{4,6},{5,7},{6,4},{7,5},{8,10},{9,11},{10,... | collective-permute-start | bytes 786440 | tf_op jit(solution)/shard_map/ppermute | solution.py:30
  298.2 20.2 %collective-permute-start.41 = (bf16[64,2048]{1,0:T(8,128)(2,1)S(1)}, bf16[64,2048]{1,0:T(8,128)(2,1)S(1)}, u32[]{:S(2)}, u32[]{:S(2)}) collective-permute-start(bf16[64,2048]{1,0:T(8,128)(2,1)S(1)} %get-tuple-element.383), channel_id=1, source_target_pairs={{0,4},{1,5},{2,6},{3,7},{4,0},{5,1},{6,2},{7,3},{8,12},{9,13},{10,... | collective-permute-start | bytes 786440 | tf_op jit(solution)/shard_map/ppermute | solution.py:30
  319.3 13.0 %collective-permute-start.42 = (bf16[512,2048]{1,0:T(8,128)(2,1)}, bf16[512,2048]{1,0:T(8,128)(2,1)S(1)}, u32[]{:S(2)}, u32[]{:S(2)}) collective-permute-start(bf16[512,2048]{1,0:T(8,128)(2,1)} %get-tuple-element.282), channel_id=1, source_target_pairs={{0,1},{1,0},{2,3},{3,2},{4,5},{5,4},{6,7},{7,6},{8,9},{9,8},{10,11... | collective-permute-start | bytes 6291464 | tf_op jit(solution)/shard_map/ppermute | solution.py:30
  322.3 10.8 %collective-permute-start.43 = (bf16[64,2048]{1,0:T(8,128)(2,1)S(1)}, bf16[64,2048]{1,0:T(8,128)(2,1)S(1)}, u32[]{:S(2)}, u32[]{:S(2)}) collective-permute-start(bf16[64,2048]{1,0:T(8,128)(2,1)S(1)} %add_convert_fusion.16), channel_id=1, source_target_pairs={{0,2},{1,3},{2,0},{3,1},{4,6},{5,7},{6,4},{7,5},{8,10},{9,11},{10,... | collective-permute-start | bytes 786440 | tf_op jit(solution)/shard_map/ppermute | solution.py:30
  335.9 11.6 %collective-permute-start.47 = (bf16[64,2048]{1,0:T(8,128)(2,1)S(1)}, bf16[64,2048]{1,0:T(8,128)(2,1)S(1)}, u32[]{:S(2)}, u32[]{:S(2)}) collective-permute-start(bf16[64,2048]{1,0:T(8,128)(2,1)S(1)} %get-tuple-element.378), channel_id=1, source_target_pairs={{0,2},{1,3},{2,0},{3,1},{4,6},{5,7},{6,4},{7,5},{8,10},{9,11},{10,... | collective-permute-start | bytes 786440 | tf_op jit(solution)/shard_map/ppermute | solution.py:30
  336.4 12.0 %collective-permute-start.48 = (bf16[64,2048]{1,0:T(8,128)(2,1)S(1)}, bf16[64,2048]{1,0:T(8,128)(2,1)S(1)}, u32[]{:S(2)}, u32[]{:S(2)}) collective-permute-start(bf16[64,2048]{1,0:T(8,128)(2,1)S(1)} %get-tuple-element.377), channel_id=1, source_target_pairs={{0,4},{1,5},{2,6},{3,7},{4,0},{5,1},{6,2},{7,3},{8,12},{9,13},{10,... | collective-permute-start | bytes 786440 | tf_op jit(solution)/shard_map/ppermute | solution.py:30
  341.1 52.7 %collective-permute-start.57 = (bf16[2048,256]{1,0:T(8,128)(2,1)}, bf16[2048,256]{1,0:T(8,128)(2,1)}, u32[]{:S(2)}, u32[]{:S(2)}) collective-permute-start(bf16[2048,256]{1,0:T(8,128)(2,1)} %convolution_convert_fusion.9), channel_id=1, source_target_pairs={{0,8},{8,0},{16,24},{24,16},{1,9},{9,1},{17,25},{25,17},{2,10},{10... | collective-permute-start | bytes 3145736 | tf_op jit(solution)/shard_map/ppermute | solution.py:30
  356.1 18.6 %collective-permute-start.51 = (bf16[128,2048]{1,0:T(8,128)(2,1)}, bf16[128,2048]{1,0:T(8,128)(2,1)}, u32[]{:S(2)}, u32[]{:S(2)}) collective-permute-start(bf16[128,2048]{1,0:T(8,128)(2,1)} %pad_maximum_fusion.9), channel_id=1, source_target_pairs={{0,16},{8,24},{16,0},{24,8},{1,17},{9,25},{17,1},{25,9},{2,18},{10... | collective-permute-start | bytes 1572872 | tf_op jit(solution)/shard_map/ppermute | solution.py:30
  378.7 13.3 %collective-permute-start.52 = (bf16[128,2048]{1,0:T(8,128)(2,1)S(1)}, bf16[128,2048]{1,0:T(8,128)(2,1)S(1)}, u32[]{:S(2)}, u32[]{:S(2)}) collective-permute-start(bf16[128,2048]{1,0:T(8,128)(2,1)S(1)} %get-tuple-element.326), channel_id=1, source_target_pairs={{0,2},{1,3},{2,0},{3,1},{4,6},{5,7},{6,4},{7,5},{8,10},{9,11},{10,... | collective-permute-start | bytes 1572872 | tf_op jit(solution)/shard_map/ppermute | solution.py:30
  379.9 12.2 %collective-permute-start.53 = (bf16[128,2048]{1,0:T(8,128)(2,1)S(1)}, bf16[128,2048]{1,0:T(8,128)(2,1)S(1)}, u32[]{:S(2)}, u32[]{:S(2)}) collective-permute-start(bf16[128,2048]{1,0:T(8,128)(2,1)S(1)} %get-tuple-element.326), channel_id=1, source_target_pairs={{0,4},{1,5},{2,6},{3,7},{4,0},{5,1},{6,2},{7,3},{8,12},{9,13},{10,... | collective-permute-start | bytes 1572872 | tf_op jit(solution)/shard_map/ppermute | solution.py:30
  380.2 23.0 %collective-permute-start.56 = (bf16[2048,256]{1,0:T(8,128)(2,1)S(1)}, bf16[2048,256]{1,0:T(8,128)(2,1)}, u32[]{:S(2)}, u32[]{:S(2)}) collective-permute-start(bf16[2048,256]{1,0:T(8,128)(2,1)S(1)} %copy-done.69), channel_id=1, source_target_pairs={{0,8},{8,0},{16,24},{24,16},{1,9},{9,1},{17,25},{25,17},{2,10},{10... | collective-permute-start | bytes 3145736 | tf_op jit(solution)/shard_map/ppermute | solution.py:30
  407.2 20.1 %collective-permute-start.58 = (bf16[512,2048]{1,0:T(8,128)(2,1)}, bf16[512,2048]{1,0:T(8,128)(2,1)}, u32[]{:S(2)}, u32[]{:S(2)}) collective-permute-start(bf16[512,2048]{1,0:T(8,128)(2,1)} %constant_dynamic-update-slice_fusion.19), channel_id=1, source_target_pairs={{0,1},{1,0},{2,3},{3,2},{4,5},{5,4},{6,7},{7,6},{8,9},{9,8},{10,11... | collective-permute-start | bytes 6291464 | tf_op jit(solution)/shard_map/ppermute | solution.py:30
  417.8 55.0 %all-to-all-start.2 = ((bf16[32,64,512]{2,1,0:T(8,128)(2,1)}), bf16[32,64,512]{2,1,0:T(8,128)(2,1)}, u32[]{:S(2)}, u32[]{:S(2)}) async-start(bf16[32,64,512]{2,1,0:T(8,128)(2,1)} %pad_maximum_fusion.1), calls=%async_computation.2 | async-start | bytes 4194304 | tf_op jit(solution)/shard_map/all_to_all | solution.py:638
  437.1 33.0 %collective-permute-start.60 = (bf16[2,64,2048]{2,1,0:T(8,128)(2,1)}, bf16[2,64,2048]{2,1,0:T(8,128)(2,1)}, u32[]{:S(2)}, u32[]{:S(2)}) collective-permute-start(bf16[2,64,2048]{2,1,0:T(8,128)(2,1)} %dynamic-slice_bitcast_fusion.1), channel_id=1, source_target_pairs={{0,8},{8,0},{16,24},{24,16},{1,9},{9,1},{17,25},{25,17},{2,10},{10... | collective-permute-start | bytes 1572872 | tf_op jit(solution)/shard_map/ppermute | solution.py:30
  475.4 28.6 %collective-permute-start.61 = (bf16[512,2048]{1,0:T(8,128)(2,1)}, bf16[512,2048]{1,0:T(8,128)(2,1)}, u32[]{:S(2)}, u32[]{:S(2)}) collective-permute-start(bf16[512,2048]{1,0:T(8,128)(2,1)} %convolution_convert_fusion.2), channel_id=1, source_target_pairs={{0,1},{1,0},{2,3},{3,2},{4,5},{5,4},{6,7},{7,6},{8,9},{9,8},{10,11... | collective-permute-start | bytes 6291464 | tf_op jit(solution)/shard_map/ppermute | solution.py:30
  477.3 25.1 %collective-permute-start.59 = (bf16[2,512,384]{2,1,0:T(8,128)(2,1)}, bf16[2,512,384]{2,1,0:T(8,128)(2,1)}, u32[]{:S(2)}, u32[]{:S(2)}) collective-permute-start(bf16[2,512,384]{2,1,0:T(8,128)(2,1)} %dynamic-slice_bitcast_fusion), channel_id=1, source_target_pairs={{0,8},{8,0},{16,24},{24,16},{1,9},{9,1},{17,25},{25,17},{2,10},{10... | collective-permute-start | bytes 2359304 | tf_op jit(solution)/shard_map/ppermute | solution.py:30
  479.7 24.3 %collective-permute-start.62 = (bf16[1,64,2048]{2,1,0:T(8,128)(2,1)S(1)}, bf16[1,64,2048]{2,1,0:T(8,128)(2,1)S(1)}, u32[]{:S(2)}, u32[]{:S(2)}) collective-permute-start(bf16[1,64,2048]{2,1,0:T(8,128)(2,1)S(1)} %constant_dynamic-slice_fusion.1), channel_id=1, source_target_pairs={{0,16},{8,24},{16,0},{24,8},{1,17},{9,25},{17,1},{25,9},{2,18},{10... | collective-permute-start | bytes 786440 | tf_op jit(solution)/shard_map/ppermute | solution.py:30
  508.1 25.4 %collective-permute-start.67 = (bf16[1,512,384]{2,1,0:T(8,128)(2,1)}, bf16[1,512,384]{2,1,0:T(8,128)(2,1)}, u32[]{:S(2)}, u32[]{:S(2)}) collective-permute-start(bf16[1,512,384]{2,1,0:T(8,128)(2,1)} %constant_dynamic-slice_fusion), channel_id=1, source_target_pairs={{0,16},{8,24},{16,0},{24,8},{1,17},{9,25},{17,1},{25,9},{2,18},{10... | collective-permute-start | bytes 1179656 | tf_op jit(solution)/shard_map/ppermute | solution.py:30
  509.1 11.7 %collective-permute-start.68 = (bf16[64,2048]{1,0:T(8,128)(2,1)S(1)}, bf16[64,2048]{1,0:T(8,128)(2,1)S(1)}, u32[]{:S(2)}, u32[]{:S(2)}) collective-permute-start(bf16[64,2048]{1,0:T(8,128)(2,1)S(1)} %fusion.28), channel_id=1, source_target_pairs={{0,0},{8,1},{16,2},{24,3},{1,4},{9,5},{17,6},{25,7},{2,8},{10,9},{... | collective-permute-start | bytes 786440 | tf_op jit(solution)/shard_map/ppermute | solution.py:762
  514.3 35.0 %collective-permute-start.63 = (bf16[64,2048]{1,0:T(8,128)(2,1)}, bf16[64,2048]{1,0:T(8,128)(2,1)}, u32[]{:S(2)}, u32[]{:S(2)}) collective-permute-start(bf16[64,2048]{1,0:T(8,128)(2,1)} %get-tuple-element.374), channel_id=1, source_target_pairs={{0,2},{1,3},{2,0},{3,1},{4,6},{5,7},{6,4},{7,5},{8,10},{9,11},{10,... | collective-permute-start | bytes 786440 | tf_op jit(solution)/shard_map/ppermute | solution.py:30
  517.4 31.9 %collective-permute-start.64 = (bf16[64,2048]{1,0:T(8,128)(2,1)}, bf16[64,2048]{1,0:T(8,128)(2,1)}, u32[]{:S(2)}, u32[]{:S(2)}) collective-permute-start(bf16[64,2048]{1,0:T(8,128)(2,1)} %get-tuple-element.373), channel_id=1, source_target_pairs={{0,4},{1,5},{2,6},{3,7},{4,0},{5,1},{6,2},{7,3},{8,12},{9,13},{10,... | collective-permute-start | bytes 786440 | tf_op jit(solution)/shard_map/ppermute | solution.py:30
  517.9 31.5 %collective-permute-start.65 = (bf16[64,2048]{1,0:T(8,128)(2,1)}, bf16[64,2048]{1,0:T(8,128)(2,1)}, u32[]{:S(2)}, u32[]{:S(2)}) collective-permute-start(bf16[64,2048]{1,0:T(8,128)(2,1)} %get-tuple-element.372), channel_id=1, source_target_pairs={{0,2},{1,3},{2,0},{3,1},{4,6},{5,7},{6,4},{7,5},{8,10},{9,11},{10,... | collective-permute-start | bytes 786440 | tf_op jit(solution)/shard_map/ppermute | solution.py:30
  520.8 28.6 %collective-permute-start.66 = (bf16[64,2048]{1,0:T(8,128)(2,1)}, bf16[64,2048]{1,0:T(8,128)(2,1)}, u32[]{:S(2)}, u32[]{:S(2)}) collective-permute-start(bf16[64,2048]{1,0:T(8,128)(2,1)} %get-tuple-element.371), channel_id=1, source_target_pairs={{0,4},{1,5},{2,6},{3,7},{4,0},{5,1},{6,2},{7,3},{8,12},{9,13},{10,... | collective-permute-start | bytes 786440 | tf_op jit(solution)/shard_map/ppermute | solution.py:30
  533.4 48.3 %collective-permute-start.72 = (bf16[256,2048]{1,0:T(8,128)(2,1)}, bf16[256,2048]{1,0:T(8,128)(2,1)}, u32[]{:S(2)}, u32[]{:S(2)}) collective-permute-start(bf16[256,2048]{1,0:T(8,128)(2,1)} %convolution_convert_fusion.7), channel_id=1, source_target_pairs={{0,8},{8,0},{16,24},{24,16},{1,9},{9,1},{17,25},{25,17},{2,10},{10... | collective-permute-start | bytes 3145736 | tf_op jit(solution)/shard_map/ppermute | solution.py:30
  551.3 45.0 %collective-permute-start.69 = (bf16[128,2048]{1,0:T(8,128)(2,1)}, bf16[128,2048]{1,0:T(8,128)(2,1)}, u32[]{:S(2)}, u32[]{:S(2)}) collective-permute-start(bf16[128,2048]{1,0:T(8,128)(2,1)} %slice_bitcast_fusion.1), channel_id=1, source_target_pairs={{0,16},{8,24},{16,0},{24,8},{1,17},{9,25},{17,1},{25,9},{2,18},{10... | collective-permute-start | bytes 1572872 | tf_op jit(solution)/shard_map/ppermute | solution.py:30
  556.8 32.3 %collective-permute-start.70 = (bf16[64,2048]{1,0:T(8,128)(2,1)}, bf16[64,2048]{1,0:T(8,128)(2,1)}, u32[]{:S(2)}, u32[]{:S(2)}) collective-permute-start(bf16[64,2048]{1,0:T(8,128)(2,1)} %add_convert_fusion.9), channel_id=1, source_target_pairs={{0,2},{1,3},{2,0},{3,1},{4,6},{5,7},{6,4},{7,5},{8,10},{9,11},{10,... | collective-permute-start | bytes 786440 | tf_op jit(solution)/shard_map/ppermute | solution.py:30
  558.5 30.6 %collective-permute-start.71 = (bf16[64,2048]{1,0:T(8,128)(2,1)}, bf16[64,2048]{1,0:T(8,128)(2,1)}, u32[]{:S(2)}, u32[]{:S(2)}) collective-permute-start(bf16[64,2048]{1,0:T(8,128)(2,1)} %add_convert_fusion.8), channel_id=1, source_target_pairs={{0,4},{1,5},{2,6},{3,7},{4,0},{5,1},{6,2},{7,3},{8,12},{9,13},{10,... | collective-permute-start | bytes 786440 | tf_op jit(solution)/shard_map/ppermute | solution.py:30
  559.8 32.3 %all-to-all-start.3 = ((bf16[8,64,384]{2,1,0:T(8,128)(2,1)}), bf16[8,64,384]{2,1,0:T(8,128)(2,1)S(1)}, u32[]{:S(2)}, u32[]{:S(2)}) async-start(bf16[8,64,384]{2,1,0:T(8,128)(2,1)} %bitcast.150), calls=%async_computation.4 | async-start | bytes 786432 | tf_op jit(solution)/shard_map/all_to_all | solution.py:123
  (96 other events, 980.3 us)
Sparse Core Ops, SparseCore 0:
  98.5 47.8 all-gather.2
  196.4 43.4 all-gather.4
  403.4 90.4 reduce-scatter.1

commit v4 on v3

--- a/solution.py
+++ b/solution.py
@@ -13,6 +13,43 @@
 EPSILON = 1e-05
 ROPE_BASE = 500000.0
 VMEM_LIMIT = 56 * 1024 * 1024
+
+WHEN = {
+    "out_route": (0, 1),
+    "down_a": (0, 2),
+    "down_b": (6, 9),
+    "own_cots": (1, 9),
+    "columns": (1, 2),
+    "out_far": (2, 3),
+    "cot_a": (2, 3),
+    "out_near": (3, 99),
+    "columns_all": (3, 4),
+    "cot_b": (4, 6),
+    "move_0": (5, 7),
+    "move_1": (5, 6),
+    "move_2": (6, 8),
+    "move_3": (6, 8),
+    "side_cots": (6, 11),
+    "gate_away": (12, 13),
+    "gate_move": (13, 18),
+    "up_away": (13, 14),
+    "down_away": (14, 15),
+    "gate_own": (15, 16),
+    "down_terms": (15, 16),
+    "up_move": (16, 18),
+    "up_own": (16, 17),
+    "out_rows": (18, 23),
+    "both_all": (18, 22),
+    "down_move": (21, 24),
+    "out_part": (18, 19),
+    "out_halved": (19, 21),
+    "out_sum": (21, 23),
+    "out_grad": (23, 25),
+    "side_out": (23, 25),
+    "down_own": (20, 22),
+    "assembled": (23, 24),
+}
+COST = {"forward": 0, "backward": 0, "feed": 0, "split_out": 1, "split_last": 2, "split_hidden": 2}
 LOW = jnp.bfloat16
 WIDE = jnp.float32
 
@@ -23,6 +60,34 @@
 
 def tie(*values):
     return lax.optimization_barrier(values)
+
+
+class Steps:
+    def __init__(self):
+        self.waiting, self.flying, self.ended = {}, {}, {}
+
+    def add(self, name, needs, operand, task):
+        self.waiting[name] = (needs, operand, task)
+
+    def result(self, name):
+        if name in self.waiting:
+            _, operand, task = self.waiting.pop(name)
+            self.flying[name] = task(operand())
+        return self.ended[name] if name in self.ended else self.flying[name]
+
+    def barrier(self, step, *values):
+        starting = [n for n in self.waiting if WHEN[n][0] <= step]
+        later = [n for n in starting if any(need in self.waiting for need in self.waiting[n][0])]
+        tasks = [(n, *self.waiting.pop(n)[1:]) for n in starting if n not in later]
+        operands = [operand() for _, operand, _ in tasks]
+        ending = [n for n in self.flying if WHEN[n][1] <= step and n not in self.ended]
+        values, operands, results = tie(values, operands, [self.flying[n] for n in ending])
+        self.ended.update(zip(ending, results))
+        for (name, _, task), operand in zip(tasks, operands):
+            self.flying[name] = task(operand)
+        for name in later:
+            self.result(name)
+        return values
 
 
 def swap(block, axis, mask):
@@ -68,13 +133,19 @@
     return even
 
 
-def gather_core(even):
+def swap_core(rows, parts):
+    size = rows.shape[0] // parts
+    pieces = [swap(rows[j * size : (j + 1) * size], "ctx", 1) for j in range(parts)]
+    return pieces[0] if parts == 1 else jnp.concatenate(pieces, axis=0)
+
+
+def gather_core(even, parts=1):
     quad = jnp.concatenate(even, axis=0)
-    return quad, swap(quad, "ctx", 1)
-
-
-def scatter_core(odd):
-    return swap(odd, "ctx", 1)
+    return quad, swap_core(quad, parts)
+
+
+def scatter_core(odd, parts=1):
+    return swap_core(odd, parts)
 
 
 def scatter_sum(even, odd):
@@ -305,7 +376,7 @@
             dimension_semantics=("arbitrary",), vmem_limit_bytes=VMEM_LIMIT
         ),
         cost_estimate=pl.CostEstimate(
-            flops=0, bytes_accessed=8 * length * width, transcendentals=0
+            flops=COST["forward"] * 10**9, bytes_accessed=8 * length * width, transcendentals=0
         ),
         name="attention_forward",
     )(qkv, qkv, cosine, sine, cosine, sine, places[None, :], places[:, None])
@@ -338,7 +409,7 @@
             dimension_semantics=("arbitrary",), vmem_limit_bytes=VMEM_LIMIT
         ),
         cost_estimate=pl.CostEstimate(
-            flops=0, bytes_accessed=8 * length * width, transcendentals=0
+            flops=COST["backward"] * 10**9, bytes_accessed=8 * length * width, transcendentals=0
         ),
         name="attention_backward",
     )(
@@ -514,7 +585,7 @@
         compiler_params=pltpu.CompilerParams(
             dimension_semantics=("arbitrary",), vmem_limit_bytes=VMEM_LIMIT
         ),
-        cost_estimate=pl.CostEstimate(flops=0, bytes_accessed=8 << 20, transcendentals=0),
+        cost_estimate=pl.CostEstimate(flops=COST["feed"] * 10**9, bytes_accessed=8 << 20, transcendentals=0),
         name="feed_forward",
     )(table, *inputs)
 
@@ -592,39 +663,55 @@
     ]
     qkv_piece = (jnp.concatenate(shares, axis=2).astype(WIDE) * attn_scale[:, :, None]).astype(LOW)
     qkv_piece = qkv_piece.transpose(1, 0, 2)
-    qkv_piece, w_out, w_down = tie(qkv_piece, w_out, w_down)
+    steps = Steps()
+    add, result, barrier = steps.add, steps.result, steps.barrier
+    blocks = range(1, top_bit)
+    away = lambda rows: [swap(rows, "fsdp", r) for r in blocks]
+    exchange_all = lambda stack: lax.all_to_all(stack, ("fsdp", "ctx"), 0, 0, tiled=True)
+    joined = lambda lists: [jnp.concatenate(parts, axis=0) for parts in zip(*lists)]
+    half, unit_half, quarter = tok_rows // 2, ff_block // 2, width // 4
+    out_route = [(f_count * c + j, j * c_count + c) for c in range(c_count) for j in range(f_count)]
+    back_route = [(d, s) for s, d in out_route]
+
+    add("out_route", (), lambda: w_out, lambda w: lax.ppermute(w, ("fsdp", "ctx"), out_route)[None])
+    add("out_far", ("out_route",), lambda: [result("out_route")], lambda s: double_fsdp(s, top_bit, 2))
+    add("out_near", ("out_far",), lambda: result("out_far"), lambda s: double_fsdp(s, 1, 1))
+    add("down_a", (), lambda: w_down[:unit_half], away)
+    add("down_b", (), lambda: w_down[unit_half:], away)
+    add("columns", (), lambda: (w_gate, w_up), lambda w: columns_by_device(*w, mlp_scale, ff_block))
+    add(
+        "columns_all", ("columns",), lambda: result("columns"),
+        lambda stack: exchange_all(stack).reshape(width, 2 * ff_block),
+    )
+    for j in range(4):
+        add(f"move_{j}", ("columns_all",), lambda: result("columns_all"), lambda c, j=j: away(c[j * quarter : (j + 1) * quarter]))
+    gather_rows = lambda rows: lax.all_gather(rows, "ctx", axis=0, tiled=True)
+    add("own_cots", (), lambda: own_cot, gather_rows)
+    add("cot_a", (), lambda: own_cot[:half], lambda rows: swap(rows, "fsdp", top_bit))
+    add("cot_b", (), lambda: own_cot[half:], lambda rows: swap(rows, "fsdp", top_bit))
+    add(
+        "side_cots", ("cot_a", "cot_b"), lambda: (result("cot_a"), result("cot_b")),
+        lambda parts: gather_rows(jnp.concatenate(parts, axis=0)),
+    )
+
+    (qkv_piece,) = barrier(0, qkv_piece)
     qkv_piece = exchange_ctx(qkv_piece).reshape(1, c_count * piece, qkv_width)
-    out_route = [(f_count * c + j, j * c_count + c) for c in range(c_count) for j in range(f_count)]
-    out_piece = lax.ppermute(w_out, ("fsdp", "ctx"), out_route)
     small = positions
     for bit in [2 ** j for j in range(1, c_count.bit_length() - 1)] + [1]:
         small = jnp.concatenate([small, swap(small, "ctx", bit)], axis=0)
     int_places = small.reshape(-1)
-    down_half = ff_block // 2
-    down_tops = [swap(w_down[:down_half], "fsdp", r) for r in range(1, top_bit)]
-
-    qkv_piece, out_piece, near_tokens, own_cot, w_gate_in = tie(
-        qkv_piece, out_piece, near_tokens, own_cot, w_gate
-    )
+    qkv_piece, near_tokens = barrier(1, qkv_piece, near_tokens)
     even_tokens = gather_far(own_tokens, near_tokens)
     qkv_parts = double_fsdp([qkv_piece], top_bit, 2)
-    own_cots = lax.all_gather(own_cot, "ctx", axis=0, tiled=True)
-    columns = columns_by_device(w_gate_in, w_up, mlp_scale, ff_block)
     half_dim = HEAD_DIM // 2
     frequency = jnp.power(ROPE_BASE, -2.0 * jnp.arange(half_dim, dtype=WIDE) / HEAD_DIM)
     angles = int_places.astype(WIDE)[:, None] * frequency[None, :]
     cosine, sine = jnp.cos(angles), jnp.sin(angles)
     cosine = jnp.concatenate([cosine] * 4, axis=1)
     sine = jnp.concatenate([-sine, sine, -sine, sine], axis=1)
-
-    qkv_parts, out_piece, cosine, sine, even_tokens, down_tops, columns, own_cot = tie(
-        qkv_parts, out_piece, cosine, sine, even_tokens, down_tops, columns, own_cot
-    )
-    half = tok_rows // 2
-    cot_top = swap(own_cot[:half], "fsdp", top_bit)
+    qkv_parts, cosine, sine, even_tokens = barrier(2, qkv_parts, cosine, sine, even_tokens)
     quad_tokens, other_tokens = gather_core(even_tokens)
     qkv_parts = double_fsdp(qkv_parts, 1, 1)
-    out_parts = double_fsdp([out_piece[None]], top_bit, 2)
 
     def first_norm(rows):
         rows = rows.astype(WIDE)
@@ -632,146 +719,156 @@
 
     normed_first = [first_norm(quad_tokens), first_norm(other_tokens)]
 
-    qkv_parts, out_parts, normed_first, columns, cot_top, own_cot = tie(
-        qkv_parts, out_parts, normed_first, columns, cot_top, own_cot
-    )
-    exchange_all = lambda stack: lax.all_to_all(stack, ("fsdp", "ctx"), 0, 0, tiled=True)
-    columns = exchange_all(columns)
-    out_parts = double_fsdp(out_parts, 1, 1)
+    qkv_parts, normed_first = barrier(3, qkv_parts, normed_first)
     w_qkv = place(qkv_parts, f_order, f_index)
     qkv = jnp.concatenate([dot(rows, w_qkv) for rows in normed_first], axis=0)
     mixed, lse, q_scaled, k_rot, v_low = attention_forward(qkv, cosine, sine, int_places, heads)
-
-    mixed, out_parts, columns, own_cot = tie(mixed, out_parts, columns, own_cot)
-    cut = width // 2
-    own_columns = columns.reshape(width, 2 * ff_block)
-    tops = [swap(own_columns[:cut], "fsdp", r) for r in range(1, top_bit)]
-    cot_low = swap(own_cot[half:], "fsdp", top_bit)
-    w_out_rows = place(out_parts, f_order, f_index)
+    (mixed,) = barrier(4, mixed)
+
+    w_out_rows = place(result("out_near"), f_order, f_index)
     middle = mixed.shape[0] // 2
-    odd_out = scatter_core(dot(mixed[middle:], w_out_rows, out=LOW))
+    odd_out = scatter_core(dot(mixed[middle:], w_out_rows, out=LOW), COST["split_out"])
     even_out = dot(mixed[:middle], w_out_rows, out=LOW)
+    odd_out, even_out = barrier(5, odd_out, even_out)
     state = scatter_far(scatter_sum(even_out, odd_out))
     inputs = own_tokens.astype(WIDE)
     inv_first = inverse_rms(inputs)
     hat_first = inputs * inv_first
     all_first = jnp.concatenate(normed_first, axis=0)
-    state, hat_first, all_first, own_columns, tops, cot_low = tie(
-        state, hat_first, all_first, own_columns, tops, cot_low
-    )
-    side_cots = lax.all_gather(jnp.concatenate([cot_top, cot_low], axis=0), "ctx", axis=0, tiled=True)
-    lows = [swap(own_columns[cut:], "fsdp", r) for r in range(1, top_bit)]
-    hidden = inputs + scatter_end(scatter_near(state))
+    state, hat_first, all_first = barrier(6, state, hat_first, all_first)
+    (state,) = barrier(7, scatter_near(state))
+    hidden = inputs + scatter_end(state)
     inv_second = inverse_rms(hidden)
     hat_second = hidden * inv_second
     normed_own = hat_second.astype(LOW)
 
     near_norm = gather_near(normed_own)
     side_norm = swap(normed_own, "fsdp", top_bit)
-    near_norm, side_norm, own_columns, w_down, lows = tie(near_norm, side_norm, own_columns, w_down, lows)
-    columns = [own_columns] + [jnp.concatenate(parts, axis=0) for parts in zip(tops, lows)]
-    down_lows = [swap(w_down[down_half:], "fsdp", r) for r in range(1, top_bit)]
+    near_norm, side_norm = barrier(8, near_norm, side_norm)
     even_norm = gather_far(normed_own, near_norm)
     near_side = gather_near(side_norm)
     norm_pieces = list(gather_core(even_norm))
-    near_side, norm_pieces, own_cots, down_lows = tie(near_side, norm_pieces, own_cots, down_lows)
-    downs = [w_down] + [jnp.concatenate(parts, axis=0) for parts in zip(down_tops, down_lows)]
-    even_side = gather_far(side_norm, near_side)
+    (norm_pieces,) = barrier(9, norm_pieces)
+    columns = [result("columns_all")] + joined([result(f"move_{j}") for j in range(4)])
+    downs = [w_down] + joined([result("down_a"), result("down_b")])
     table = jnp.array(c_order, jnp.int32) ^ c_index
     by_block = lambda rows: rows.reshape(c_count, tok_rows, width)
 
     weights = (table, columns, downs)
-    *buffers, even_zero, odd_zero = feed_forward(0, *norm_pieces, by_block(own_cots), *weights, [])
-    even_side, buffers, even_zero, odd_zero = tie(even_side, buffers, even_zero, odd_zero)
-    side_norms = gather_core(even_side)
+    *buffers, even_zero, odd_zero = feed_forward(0, *norm_pieces, by_block(result("own_cots")), *weights, [])
+    near_side, buffers, even_zero, odd_zero = barrier(10, near_side, buffers, even_zero, odd_zero)
+    side_norms = gather_core(gather_far(side_norm, near_side))
     quad_zero = scatter_sum(even_zero, scatter_core(odd_zero))
-    side_norms, quad_zero, buffers, side_cots = tie(side_norms, quad_zero, buffers, side_cots)
+    side_norms, quad_zero, buffers, side_cots = barrier(
+        11, side_norms, quad_zero, buffers, result("side_cots")
+    )
     state_zero = scatter_far(quad_zero)
     *buffers, even_one, odd_one = feed_forward(1, *side_norms, by_block(side_cots), *weights, buffers)
     all_norms, all_cots, all_acts, all_lows = buffers
-    state_zero, odd_one, even_one, all_norms = tie(state_zero, odd_one, even_one, all_norms)
-    odd_one = scatter_core(odd_one)
-    state_zero = scatter_near(state_zero)
-
-    blocks = range(1, top_bit)
-    gate_away = [dot(all_norms, all_lows[2 * j], ((0,), (0,)), LOW) for j in blocks]
-    quad_one = scatter_sum(even_one, odd_one)
-    quad_one, state_zero, gate_away, all_norms = tie(quad_one, state_zero, gate_away, all_norms)
-    state_one = scatter_far(quad_one)
-    gate_received = [swap(part, "fsdp", r) for r, part in enumerate(gate_away, 1)]
-    up_away = [dot(all_norms, all_lows[2 * j + 1], ((0,), (0,)), LOW) for j in blocks]
-    state_one, up_away, all_norms, all_acts, all_cots = tie(
-        state_one, up_away, all_norms, all_acts, all_cots
-    )
-    state_one = scatter_near(state_one)
-    down_away = [dot(all_acts[j], all_cots, ((0,), (0,)), LOW) for j in blocks]
-    state_one, down_away, all_norms, all_acts = tie(state_one, down_away, all_norms, all_acts)
-    side_one = swap(scatter_end(state_one).astype(LOW), "fsdp", top_bit)
-    gate_own = dot(all_norms, all_lows[0], ((0,), (0,)), LOW)
-    down_terms = down_terms_by_device(all_acts, c_index, c_count, downs, tok_rows)
-    side_one, gate_own, all_norms, up_away, down_terms = tie(
-        side_one, gate_own, all_norms, up_away, down_terms
-    )
-    grad_normed = scatter_end(state_zero) + side_one.astype(WIDE)
-
-    grad_hidden = own_cot.astype(WIDE) + norm_back(grad_normed, hat_second, inv_second)
-    hidden_low = grad_hidden.astype(LOW)
-    near_hidden = gather_near(hidden_low)
-    up_received = [swap(part, "fsdp", r) for r, part in enumerate(up_away, 1)]
-    up_own = dot(all_norms, all_lows[1], ((0,), (0,)), LOW)
-    near_hidden, up_own = tie(near_hidden, up_own)
-    even_hidden = gather_far(hidden_low, near_hidden)
-    even_hidden, up_received, gate_received, down_terms = tie(
-        even_hidden, up_received, gate_received, down_terms
-    )
-    out_rows = lax.psum_scatter(down_terms, "ctx", scatter_dimension=0, tiled=True)
-    out_rows = out_rows.reshape(2, tok_rows, width)
-    hidden_halves = gather_core(even_hidden)
+
+    product = lambda left, right: dot(left, right, ((0,), (0,)), LOW)
+    add(
+        "gate_away", (), lambda: (all_norms, all_lows),
+        lambda p: [product(p[0], p[1][2 * j]) for j in blocks],
+    )
+    add(
+        "up_away", (), lambda: (all_norms, all_lows),
+        lambda p: [product(p[0], p[1][2 * j + 1]) for j in blocks],
+    )
+    add("down_away", (), lambda: (all_acts, all_cots), lambda p: [product(p[0][j], p[1]) for j in blocks])
+    add("gate_own", (), lambda: (all_norms, all_lows), lambda p: product(p[0], p[1][0]))
+    add("up_own", (), lambda: (all_norms, all_lows), lambda p: product(p[0], p[1][1]))
+    move_back = lambda parts: [swap(part, "fsdp", r) for r, part in enumerate(parts, 1)]
+    add("gate_move", ("gate_away",), lambda: result("gate_away"), move_back)
+    add("up_move", ("up_away",), lambda: result("up_away"), move_back)
+    add("down_move", ("down_away",), lambda: result("down_away"), move_back)
+    add(
+        "down_terms", (), lambda: all_acts,
+        lambda acts: down_terms_by_device(acts, c_index, c_count, downs, tok_rows),
+    )
+    add(
+        "out_rows", ("down_terms",), lambda: result("down_terms"),
+        lambda t: lax.psum_scatter(t, "ctx", scatter_dimension=0, tiled=True).reshape(2, tok_rows, width),
+    )
+    add("side_out", ("out_rows",), lambda: result("out_rows")[1], lambda rows: swap(rows, "fsdp", top_bit))
 
     def sum_by_device(own, parts):
         total = sum([part.astype(WIDE) for part in parts], own.astype(WIDE)).astype(LOW)
         return total.reshape(devices, piece, ff_block)
 
-    both_sums = [sum_by_device(gate_own, gate_received), sum_by_device(up_own, up_received)]
-    both_sums = exchange_all(jnp.concatenate(both_sums, axis=2))
+    add(
+        "both_all", ("gate_own", "gate_move", "up_own", "up_move"), lambda: [result(n) for n in ("gate_own", "gate_move", "up_own", "up_move")],
+        lambda p: exchange_all(
+            jnp.concatenate([sum_by_device(p[0], p[1]), sum_by_device(p[2], p[3])], axis=2)
+        ),
+    )
+    add(
+        "down_own", (), lambda: (all_acts, all_cots),
+        lambda p: dot(p[0][0], p[1], ((0,), (0,))),
+    )
+    add(
+        "assembled",
+        ("both_all",),
+        lambda: result("both_all"),
+        lambda parts: assemble_columns(parts, w_gate, w_up, mlp_scale),
+    )
+    state_zero, odd_one, even_one = barrier(12, state_zero, odd_one, even_one)
+    odd_one = scatter_core(odd_one)
+    state_zero = scatter_near(state_zero)
+    quad_one = scatter_sum(even_one, odd_one)
+    quad_one, state_zero = barrier(13, quad_one, state_zero)
+    (state_one,) = barrier(14, scatter_far(quad_one))
+    (state_one,) = barrier(15, scatter_near(state_one))
+    side_one = swap(scatter_end(state_one).astype(LOW), "fsdp", top_bit)
+    (side_one,) = barrier(16, side_one)
+    grad_normed = scatter_end(state_zero) + side_one.astype(WIDE)
+
+    grad_hidden = own_cot.astype(WIDE) + norm_back(grad_normed, hat_second, inv_second)
+    hidden_low = grad_hidden.astype(LOW)
+    (near_hidden,) = barrier(17, gather_near(hidden_low))
+    (even_hidden,) = barrier(18, gather_far(hidden_low, near_hidden))
+    hidden_halves = gather_core(even_hidden, COST["split_hidden"])
     grad_mixed = jnp.concatenate([dot(h, w_out_rows, ((1,), (1,)), LOW) for h in hidden_halves], axis=0)
-    out_part = dot(mixed[:middle], hidden_halves[0], ((0,), (0,))) + dot(
-        mixed[middle:], hidden_halves[1], ((0,), (0,))
-    )
-    out_part = out_part.astype(LOW).reshape(f_count, piece, width)
-
-    grad_mixed, out_part = tie(grad_mixed, out_part)
-    out_sum = halve_near(out_part, f_index)
+
+    def out_product(p):
+        total = dot(p[0][:middle], p[1][0], ((0,), (0,))) + dot(p[0][middle:], p[1][1], ((0,), (0,)))
+        return total.astype(LOW).reshape(f_count, piece, width)
+
+    add("out_part", (), lambda: (mixed, hidden_halves), out_product)
+    add("out_halved", ("out_part",), lambda: result("out_part"), lambda p: halve_near(p, f_index))
+    add("out_sum", ("out_halved",), lambda: result("out_halved"), lambda p: halve_far(p, f_index, top_bit))
+    add("out_grad", ("out_sum",), lambda: result("out_sum"), lambda p: lax.ppermute(p, ("fsdp", "ctx"), back_route))
+
+    (grad_mixed,) = barrier(19, grad_mixed)
     grad_qkv = attention_backward(
         q_scaled, k_rot, v_low, grad_mixed, lse, cosine, sine, int_places, heads
     )
-
-    grad_qkv, all_first = tie(grad_qkv, all_first)
+    grad_qkv, all_first = barrier(20, grad_qkv, all_first)
+
     qkv_part = dot(all_first, grad_qkv, ((0,), (0,)), LOW)
     qkv_part = qkv_part.reshape(f_count, c_count * piece, qkv_width)
     grad_qkv, qkv_part = tie(grad_qkv, qkv_part)
     qkv_sum = halve_near(qkv_part, f_index)
-    grad_qkv, both_sums, out_sum = tie(grad_qkv, both_sums, out_sum)
-    odd = scatter_core(dot(grad_qkv[middle:], w_qkv, ((1,), (1,)), LOW))
+    (grad_qkv,) = barrier(21, grad_qkv)
+    odd = scatter_core(dot(grad_qkv[middle:], w_qkv, ((1,), (1,)), LOW), COST["split_last"])
     even = dot(grad_qkv[:middle], w_qkv, ((1,), (1,)), LOW)
     quad = scatter_sum(even, odd)
-    out_sum = halve_far(out_sum, f_index, top_bit)
-    qkv_sum, quad, down_away, out_sum = tie(qkv_sum, quad, down_away, out_sum)
+    qkv_sum, quad = barrier(22, qkv_sum, quad)
     state = scatter_far(quad)
     qkv_sum = halve_far(qkv_sum, f_index, top_bit)
-    out_grad = lax.ppermute(out_sum, ("fsdp", "ctx"), [(d, s) for s, d in out_route]).astype(WIDE)
-    down_received = [swap(part, "fsdp", r) for r, part in enumerate(down_away, 1)]
-    state, qkv_sum, out_grad, all_cots, out_rows = tie(state, qkv_sum, out_grad, all_cots, out_rows)
-    state = scatter_near(state)
+    state, qkv_sum = barrier(23, state, qkv_sum)
     qkv_sum = exchange_ctx(qkv_sum.reshape(c_count, piece, qkv_width))
-    side_out = swap(out_rows[1], "fsdp", top_bit)
-    down_grad = dot(all_acts[0], all_cots, ((0,), (0,)))
-    for part in down_received:
-        down_grad = down_grad + part.astype(WIDE)
+    (state,) = barrier(24, scatter_near(state))
+    (qkv_sum,) = barrier(25, qkv_sum)
     grad_normed = scatter_end(state)
     input_grad = grad_hidden + norm_back(grad_normed, hat_first, inv_first)
-    gate_grad, up_grad, mlp_gain_grad = assemble_columns(both_sums, w_gate, w_up, mlp_scale)
+    gate_grad, up_grad, mlp_gain_grad = result("assembled")
     mlp_gain_grad = mlp_gain_grad[:, 0]
+    out_grad = result("out_grad").astype(WIDE)
+    down_grad = result("down_own")
+    for part in result("down_move"):
+        down_grad = down_grad + part.astype(WIDE)
+    side_out, out_rows = result("side_out"), result("out_rows")
     output = hidden + out_rows[0].astype(WIDE) + side_out.astype(WIDE)
 
     qkv_sum = qkv_sum.astype(WIDE)

time: 614 us -> 587 us (0.956)
  starting transfers between devices: 139 us -> 106 us
  waiting for transfers between devices: 191 us -> 202 us
  matrix products: 62.9 us -> 52.3 us
    ppermute x71 -> x75, starting transfers between devices: 106 us -> 80 us  [swap(): return lax.ppermute(block, axis, [(i, i ^ mask) for i in range(count)])]
    dot_general x17, matrix products: 62.9 us -> 52.3 us  [dot(): lax.dot_general(left, right, (dims, ((), ())), preferred_element_type=WIDE)]
    ppermute x71 -> x75, waiting for transfers between devices: 184 us -> 192 us  [swap(): return lax.ppermute(block, axis, [(i, i ^ mask) for i in range(count)])]
    ppermute x2, waiting for transfers between devices: 2.85 us -> 9.6 us  [the longest x1 9.6 us: per_device(): lax.ppermute(p, ('fsdp', 'ctx'), back_route)]
    unnamed x172 -> x177, local copies, waits for them, and re-layouts: 17.4 us -> 20.4 us
  transfers between devices with their start and end apart: 80 -> 84, of which waited for: 37 -> 34; matrix products, arithmetic and copies ran while one was open for 25% -> 24% of each run, Pallas kernels for 16% -> 17%
where the time goes in v4:
time: 587 us; the launch traced here: 580 us
  waiting for transfers between devices  202 us (34%)
  starting transfers between devices  106 us (18%)
  Pallas kernels  97.4 us (17%)
  other arithmetic  60.7 us (10%)
  matrix products  52.3 us (9%)
  local copies, waits for them, and re-layouts  45.7 us (8%)
  between operations  15.3 us (3%)
    ppermute x75, waiting for transfers between devices, swap(): return lax.ppermute(block, axis, [(i, i ^ mask) for i in range(count)])  192 us
    ppermute x75, starting transfers between devices, swap(): return lax.ppermute(block, axis, [(i, i ^ mask) for i in range(count)])  80 us
    dot_general x17, matrix products, dot(): lax.dot_general(left, right, (dims, ((), ())), preferred_element_type=WIDE)  52.3 us
    pallas_call x2, Pallas kernels, feed_forward(): pl.pallas_call(functools.partial(feed_kernel, blocks, steps, per_step), g...  39.6 us
    unnamed x177, local copies, waits for them, and re-layouts  20.4 us
    pallas_call x1, Pallas kernels, attention_backward(): pl.pallas_call(functools.partial(backward_kernel, heads, steps), grid=(st...  18.4 us
    pallas_call x1, Pallas kernels, attention_forward(): pl.pallas_call(functools.partial(forward_kernel, heads), grid=(length //...  15.9 us
  transfers between devices with their start and end apart: 84, of which 34 were waited for; matrix products, arithmetic and copies ran while one was open for 24% of the time, Pallas kernels for 17%

profile of v4, /device:TPU:1, one launch (start us, length us, event | category | flops | bytes accessed | tf_op | source)
XLA Modules:
  0.0 579.6 jit_solution(186060253649915428)
XLA Ops:
  7.2 2.1 collective-permute-start
  16.2 4.6 all-to-all-start
  20.8 3.2 collective-permute-start.2
  24.0 3.3 collective-permute-start.4
  33.4 7.4 %collective-permute-start.3 = (bf16[1,512,384]{2,1,0:T(8,128)(2,1)S(1)}, bf16[1,512,384]{2,1,0:T(8,128)(2,1)S(1)}, u32[]{:S(2)}, u32[]{:S(2)}) collective-permute-start(bf16[1,512,384]{2,1,0:T(8,128)(2,1)S(1)} %bitcast.150), channel_id=1, source_target_pairs={{0,16},{8,24},{16,0},{24,8},{1,17},{9,25},{17,1},{25,9},{2,18},{10... | collective-permute-start | bytes 1179656 | tf_op jit(solution)/shard_map/ppermute | solution.py:95
  47.2 4.0 columns_by_device.1
  51.3 7.2 %collective-permute-done.3.refs_1_ = bf16[1,512,384]{2,1,0:T(8,128)(2,1)S(1)} collective-permute-done((bf16[1,512,384]{2,1,0:T(8,128)(2,1)S(1)}, bf16[1,512,384]{2,1,0:T(8,128)(2,1)S(1)}, u32[]{:S(2)}, u32[]{:S(2)}) %collective-permute-start.3) | collective-permute-done | bytes 393248 | tf_op jit(solution)/shard_map/ppermute | solution.py:95
  60.8 2.6 collective-permute-start.12
  67.9 15.6 %collective-permute-done.12.refs_1_ = bf16[1,64,2048]{2,1,0:T(8,128)(2,1)S(1)} collective-permute-done((bf16[1,64,2048]{2,1,0:T(8,128)(2,1)S(1)}, bf16[1,64,2048]{2,1,0:T(8,128)(2,1)S(1)}, u32[]{:S(2)}, u32[]{:S(2)}) %collective-permute-start.12) | collective-permute-done | bytes 262176 | tf_op jit(solution)/shard_map/ppermute | solution.py:95
  83.5 5.6 collective-permute-done.13
  92.0 5.3 all-to-all-start.1
  101.6 2.7 place.2
  104.4 2.8 fusion.47
  109.7 15.9 %attention_forward.1 = (bf16[1024,256]{1,0:T(8,128)(2,1)}, f32[8,1024]{1,0:T(8,128)}, bf16[1024,256]{1,0:T(8,128)(2,1)}, bf16[1024,64]{1,0:T(8,128)(2,1)}, bf16[1024,64]{1,0:T(8,128)(2,1)}) custom-call(f32[1024,384]{1,0:T(8,128)} %pad_maximum_fusion.2.q_ref.kv_ref, f32[1024,384]{1,0:T(8,128)} %pad_maximum_fusion.2.q_ref.kv_ref, ...), custom_call_target="tpu_custom_call" | custom-call | bytes 2097152 | tf_op jit(solution)/shard_map/attention_forward/pallas_call | solution.py:354
  125.6 17.6 %collective-permute-done.14.refs_2_ = bf16[2,64,2048]{2,1,0:T(8,128)(2,1)} collective-permute-done((bf16[2,64,2048]{2,1,0:T(8,128)(2,1)}, bf16[2,64,2048]{2,1,0:T(8,128)(2,1)}, u32[]{:S(2)}, u32[]{:S(2)}) %collective-permute-start.14) | collective-permute-done | bytes 524320 | tf_op jit(solution)/shard_map/ppermute | solution.py:95
  143.2 2.3 place.3
  145.7 2.7 convolution_convert_fusion.1
  150.8 3.5 collective-permute-start.20
  159.0 7.6 %collective-permute-done.20 = bf16[64,2048]{1,0:T(8,128)(2,1)S(1)} collective-permute-done((bf16[64,2048]{1,0:T(8,128)(2,1)S(1)}, bf16[64,2048]{1,0:T(8,128)(2,1)S(1)}, u32[]{:S(2)}, u32[]{:S(2)}) %collective-permute-start.20) | collective-permute-done | bytes 262176 | tf_op jit(solution)/shard_map/ppermute | solution.py:95
  168.0 2.7 pad_maximum_fusion
  171.5 2.2 collective-permute-done.19
  188.0 2.1 collective-permute-start.26
  190.2 16.7 %collective-permute-done.28 = bf16[512,512]{1,0:T(8,128)(2,1)} collective-permute-done((bf16[512,512]{1,0:T(8,128)(2,1)}, bf16[512,512]{1,0:T(8,128)(2,1)}, u32[]{:S(2)}, u32[]{:S(2)}) %collective-permute-start.28) | collective-permute-done | bytes 524320 | tf_op jit(solution)/shard_map/ppermute | solution.py:95
  206.9 11.2 %collective-permute-done.29 = bf16[512,512]{1,0:T(8,128)(2,1)S(1)} collective-permute-done((bf16[512,512]{1,0:T(8,128)(2,1)}, bf16[512,512]{1,0:T(8,128)(2,1)S(1)}, u32[]{:S(2)}, u32[]{:S(2)}) %collective-permute-start.29) | collective-permute-done | bytes 524320 | tf_op jit(solution)/shard_map/ppermute | solution.py:95
  220.2 2.2 collective-permute-start.33
  225.1 2.3 collective-permute-done.33
  228.1 2.2 collective-permute-start.34
  240.1 4.7 collective-permute-done.35
  246.9 19.8 %feed_forward.2 = (bf16[2048,2048]{1,0:T(8,128)(2,1)}, bf16[2048,2048]{1,0:T(8,128)(2,1)}, bf16[2,2048,256]{2,1,0:T(8,128)(2,1)}, bf16[4,2048,256]{2,1,0:T(8,128...) custom-call(s32[8]{0:T(128)} %broadcast_xor_fusion.table_ref, ...), custom_call_target="tpu_custom_call" | custom-call | bytes 8388608 | tf_op jit(solution)/shard_map/feed_forward/pallas_call | solution.py:568
  270.2 3.7 collective-permute-done.36
  276.9 3.1 collective-permute-done.38.refs_1_
  283.8 19.8 %feed_forward.3 = (bf16[2048,2048]{1,0:T(8,128)(2,1)}, bf16[2048,2048]{1,0:T(8,128)(2,1)}, bf16[2,2048,256]{2,1,0:T(8,128)(2,1)}, bf16[4,2048,256]{2,1,0:T(8,128...) custom-call(s32[8]{0:T(128)} %broadcast_xor_fusion.table_ref, ...), custom_call_target="tpu_custom_call", output_to_operand_aliasing={{0}: (9, {}), {1}: (10, {}), {2}: (11, {}), {3}: (12, {})} | custom-call | bytes 8388608 | tf_op jit(solution)/shard_map/feed_forward/pallas_call | solution.py:568
  311.7 7.4 %convolution_convert_fusion.9 = bf16[2048,256]{1,0:T(8,128)(2,1)} fusion(bf16[2048,2048]{1,0:T(8,128)(2,1)} %get-tuple-element.352, bf16[4,2048,256]{2,1,0:T(8,128)(2,1)} %get-tuple-element.353), kind=kOutput, calls=%fused_computation.24 | convolution fusion | flops 2148007936 | bytes 10485760 | tf_op jit(solution)/shard_map/dot_general | solution.py:58
  324.4 3.6 convolution_convert_fusion.8
  328.7 5.7 collective-permute-done.49
  335.9 3.3 convolution_convert_fusion.7
  343.6 9.3 %down_terms.1 = bf16[4,2,2,128,2048]{4,3,2,1,0:T(8,128)(2,1)} custom-call(s32[2]{0:T(128)} %pad_add_fusion.3.table_ref, bf16[2,2048,256]{2,1,0:T(8,128)(2,1)} %get-tuple-element.382.act_ref, bf16[256,2048]{1,0:T(8,128)(2,1)} %refs_0_.1, bf16[256,2048]{1,0:T(8,128)(2,1)} %copy-done.7), custom_call_target="tpu_custom_call" | custom-call | bytes 8388608 | tf_op jit(solution)/shard_map/down_terms/pallas_call | solution.py:611
  353.0 7.0 %convolution_convert_fusion.6 = bf16[2048,256]{1,0:T(8,128)(2,1)} fusion(bf16[2048,2048]{1,0:T(8,128)(2,1)} %get-tuple-element.352, bf16[4,2048,256]{2,1,0:T(8,128)(2,1)S(1)} %copy-done.27), kind=kOutput, calls=%fused_computation.21 | convolution fusion | flops 2148007936 | bytes 10485760 | tf_op jit(solution)/shard_map/dot_general | solution.py:58
  359.9 7.5 %collective-permute-done.53 = bf16[128,2048]{1,0:T(8,128)(2,1)} collective-permute-done((bf16[128,2048]{1,0:T(8,128)(2,1)}, bf16[128,2048]{1,0:T(8,128)(2,1)}, u32[]{:S(2)}, u32[]{:S(2)}) %collective-permute-start.53) | collective-permute-done | bytes 524320 | tf_op jit(solution)/shard_map/ppermute | solution.py:95
  368.8 2.6 fusion.38
  371.9 7.2 %convolution_convert_fusion.5 = bf16[2048,256]{1,0:T(8,128)(2,1)} fusion(bf16[2048,2048]{1,0:T(8,128)(2,1)} %get-tuple-element.352, bf16[4,2048,256]{2,1,0:T(8,128)(2,1)} %get-tuple-element.353), kind=kOutput, calls=%fused_computation.20 | convolution fusion | flops 2148007936 | bytes 10485760 | tf_op jit(solution)/shard_map/dot_general | solution.py:58
  379.1 3.4 collective-permute-done.54
  383.9 4.6 collective-permute-done.56
  389.5 4.2 collective-permute-done.59
  394.9 3.8 collective-permute-start.60
  408.1 3.6 all-to-all-start.2
  414.2 2.3 convolution_convert_fusion.11
  420.8 18.4 %attention_backward.1 = bf16[1024,384]{1,0:T(8,128)(2,1)} custom-call(bf16[1024,256]{1,0:T(8,128)(2,1)} %get-tuple-element.265.q_ref, bf16[1024,64]{1,0:T(8,128)(2,1)} %get-tuple-element.266.k_ref, bf16[1024,64]{1,0:T(8,128)(2,1)} %get-tuple-element.267.v_ref, bf16[1024,256]{1,0:T(8,128)(2,1)} %pad_maximum_fusion.12.do_ref, ...), custom_call_target="tpu_custom_call" | custom-call | bytes 2097152 | tf_op jit(solution)/shard_map/attention_backward/pallas_call | solution.py:392
  439.9 2.5 fusion.4
  444.0 2.4 convolution_convert_fusion.4
  447.3 17.1 %collective-permute-done.63 = bf16[2,64,2048]{2,1,0:T(8,128)(2,1)S(1)} collective-permute-done((bf16[2,64,2048]{2,1,0:T(8,128)(2,1)S(1)}, bf16[2,64,2048]{2,1,0:T(8,128)(2,1)S(1)}, u32[]{:S(2)}, u32[]{:S(2)}) %collective-permute-start.63) | collective-permute-done | bytes 524320 | tf_op jit(solution)/shard_map/ppermute | solution.py:95
  467.9 3.7 fusion.10
  472.3 11.5 %collective-permute-done.62 = bf16[2,512,384]{2,1,0:T(8,128)(2,1)S(1)} collective-permute-done((bf16[2,512,384]{2,1,0:T(8,128)(2,1)S(1)}, bf16[2,512,384]{2,1,0:T(8,128)(2,1)S(1)}, u32[]{:S(2)}, u32[]{:S(2)}) %collective-permute-start.62) | collective-permute-done | bytes 786464 | tf_op jit(solution)/shard_map/ppermute | solution.py:95
  484.0 2.6 add_convert_fusion
  486.7 2.4 fusion.39
  493.9 17.5 %collective-permute-done.70 = bf16[1,512,384]{2,1,0:T(8,128)(2,1)S(1)} collective-permute-done((bf16[1,512,384]{2,1,0:T(8,128)(2,1)S(1)}, bf16[1,512,384]{2,1,0:T(8,128)(2,1)S(1)}, u32[]{:S(2)}, u32[]{:S(2)}) %collective-permute-start.70) | collective-permute-done | bytes 393248 | tf_op jit(solution)/shard_map/ppermute | solution.py:95
  518.6 4.4 all-to-all-start.3
  524.6 3.8 collective-permute-start.73
  528.5 5.0 assemble_columns.1
  533.5 11.4 %collective-permute-done.76 = bf16[256,2048]{1,0:T(8,128)(2,1)} collective-permute-done((bf16[256,2048]{1,0:T(8,128)(2,1)}, bf16[256,2048]{1,0:T(8,128)(2,1)}, u32[]{:S(2)}, u32[]{:S(2)}) %collective-permute-start.76) | collective-permute-done | bytes 1048608 | tf_op jit(solution)/shard_map/ppermute | solution.py:95
  545.7 3.0 convert_add_fusion
  552.6 2.4 fusion.23
  555.0 9.6 %collective-permute-done.73 = bf16[64,2048]{1,0:T(8,128)(2,1)} collective-permute-done((bf16[64,2048]{1,0:T(8,128)(2,1)}, bf16[64,2048]{1,0:T(8,128)(2,1)}, u32[]{:S(2)}, u32[]{:S(2)}) %collective-permute-start.73) | collective-permute-done | bytes 262176 | tf_op jit(solution)/shard_map/ppermute | solution.py:840
  569.3 2.1 fusion.24
  (435 shorter events, 159.8 us)
Async XLA Ops:
  7.2 26.2 %collective-permute-start = (bf16[128,2048]{1,0:T(8,128)(2,1)}, bf16[128,2048]{1,0:T(8,128)(2,1)S(1)}, u32[]{:S(2)}, u32[]{:S(2)}) collective-permute-start(bf16[128,2048]{1,0:T(8,128)(2,1)} %bitcast.136), channel_id=1, source_target_pairs={{0,2},{1,3},{2,0},{3,1},{4,6},{5,7},{6,4},{7,5},{8,10},{9,11},{10,... | collective-permute-start | bytes 1572872 | tf_op jit(solution)/shard_map/ppermute | solution.py:95
  9.3 24.1 %collective-permute-start.1 = (bf16[128,2048]{1,0:T(8,128)(2,1)}, bf16[128,2048]{1,0:T(8,128)(2,1)S(1)}, u32[]{:S(2)}, u32[]{:S(2)}) collective-permute-start(bf16[128,2048]{1,0:T(8,128)(2,1)} %bitcast.137), channel_id=1, source_target_pairs={{0,4},{1,5},{2,6},{3,7},{4,0},{5,1},{6,2},{7,3},{8,12},{9,13},{10,... | collective-permute-start | bytes 1572872 | tf_op jit(solution)/shard_map/ppermute | solution.py:95
  16.2 17.2 %all-to-all-start = ((bf16[8,64,384]{2,1,0:T(8,128)(2,1)}), bf16[8,64,384]{2,1,0:T(8,128)(2,1)S(1)}, u32[]{:S(2)}, u32[]{:S(2)}) async-start(bf16[8,64,384]{2,1,0:T(8,128)(2,1)} %fusion.25), calls=%async_computation | async-start | bytes 786432 | tf_op jit(solution)/shard_map/all_to_all | solution.py:194
  20.8 12.5 %collective-permute-start.2 = (bf16[64,2048]{1,0:T(8,128)(2,1)}, bf16[64,2048]{1,0:T(8,128)(2,1)S(1)}, u32[]{:S(2)}, u32[]{:S(2)}) collective-permute-start(bf16[64,2048]{1,0:T(8,128)(2,1)} %param.19), channel_id=1, source_target_pairs={{0,0},{1,8},{2,16},{3,24},{4,1},{5,9},{6,17},{7,25},{8,2},{9,10},{... | collective-permute-start | bytes 786440 | tf_op jit(solution)/shard_map/ppermute | solution.py:676
  27.3 23.9 %collective-permute-start.9 = (bf16[128,2048]{1,0:T(8,128)(2,1)}, bf16[128,2048]{1,0:T(8,128)(2,1)S(1)}, u32[]{:S(2)}, u32[]{:S(2)}) collective-permute-start(bf16[128,2048]{1,0:T(8,128)(2,1)} %get-tuple-element.221), channel_id=1, source_target_pairs={{0,8},{8,0},{16,24},{24,16},{1,9},{9,1},{17,25},{25,17},{2,10},{10... | collective-permute-start | bytes 1572872 | tf_op jit(solution)/shard_map/ppermute | solution.py:95
  33.4 25.1 %collective-permute-start.3 = (bf16[1,512,384]{2,1,0:T(8,128)(2,1)S(1)}, bf16[1,512,384]{2,1,0:T(8,128)(2,1)S(1)}, u32[]{:S(2)}, u32[]{:S(2)}) collective-permute-start(bf16[1,512,384]{2,1,0:T(8,128)(2,1)S(1)} %bitcast.150), channel_id=1, source_target_pairs={{0,16},{8,24},{16,0},{24,8},{1,17},{9,25},{17,1},{25,9},{2,18},{10... | collective-permute-start | bytes 1179656 | tf_op jit(solution)/shard_map/ppermute | solution.py:95
  41.5 9.8 %collective-permute-start.7 = (bf16[64,2048]{1,0:T(8,128)(2,1)}, bf16[64,2048]{1,0:T(8,128)(2,1)S(1)}, u32[]{:S(2)}, u32[]{:S(2)}) collective-permute-start(bf16[64,2048]{1,0:T(8,128)(2,1)} %slice.264), channel_id=1, source_target_pairs={{0,2},{1,3},{2,0},{3,1},{4,6},{5,7},{6,4},{7,5},{8,10},{9,11},{10,... | collective-permute-start | bytes 786440 | tf_op jit(solution)/shard_map/ppermute | solution.py:95
  60.7 30.4 %collective-permute-start.10 = (bf16[2,512,384]{2,1,0:T(8,128)(2,1)S(1)}, bf16[2,512,384]{2,1,0:T(8,128)(2,1)S(1)}, u32[]{:S(2)}, u32[]{:S(2)}) collective-permute-start(bf16[2,512,384]{2,1,0:T(8,128)(2,1)S(1)} %pad_maximum_fusion.6), channel_id=1, source_target_pairs={{0,8},{8,0},{16,24},{24,16},{1,9},{9,1},{17,25},{25,17},{2,10},{10... | collective-permute-start | bytes 2359304 | tf_op jit(solution)/shard_map/ppermute | solution.py:95
  60.8 22.7 %collective-permute-start.12 = (bf16[1,64,2048]{2,1,0:T(8,128)(2,1)S(1)}, bf16[1,64,2048]{2,1,0:T(8,128)(2,1)S(1)}, u32[]{:S(2)}, u32[]{:S(2)}) collective-permute-start(bf16[1,64,2048]{2,1,0:T(8,128)(2,1)S(1)} %bitcast.157), channel_id=1, source_target_pairs={{0,16},{8,24},{16,0},{24,8},{1,17},{9,25},{17,1},{25,9},{2,18},{10... | collective-permute-start | bytes 786440 | tf_op jit(solution)/shard_map/ppermute | solution.py:95
  63.4 25.8 %collective-permute-start.13 = (bf16[64,2048]{1,0:T(8,128)(2,1)S(1)}, bf16[64,2048]{1,0:T(8,128)(2,1)S(1)}, u32[]{:S(2)}, u32[]{:S(2)}) collective-permute-start(bf16[64,2048]{1,0:T(8,128)(2,1)S(1)} %copy-done.65), channel_id=1, source_target_pairs={{0,16},{8,24},{16,0},{24,8},{1,17},{9,25},{17,1},{25,9},{2,18},{10... | collective-permute-start | bytes 786440 | tf_op jit(solution)/shard_map/ppermute | solution.py:95
  92.0 53.7 %all-to-all-start.1 = ((bf16[32,64,512]{2,1,0:T(8,128)(2,1)}), bf16[32,64,512]{2,1,0:T(8,128)(2,1)S(1)}, u32[]{:S(2)}, u32[]{:S(2)}) async-start(bf16[32,64,512]{2,1,0:T(8,128)(2,1)} %columns_by_device.1), calls=%async_computation.1 | async-start | bytes 4194304 | tf_op jit(solution)/shard_map/all_to_all | solution.py:670
  97.3 142.8 %all-gather.3.cloned.1.call-start = ((), (), s32[]{:S(2)}) async-start(), calls=%async_computation.5 | async-start | bytes 4718592 | tf_op jit(solution)/shard_map/all_gather | solution.py:688
  98.0 182.0 %all-gather.5.cloned.1.call-start = ((), (), s32[]{:S(2)}) async-start(), calls=%async_computation.6 | async-start | bytes 4718592 | tf_op jit(solution)/shard_map/all_gather | solution.py:688
  100.3 43.0 %collective-permute-start.14 = (bf16[2,64,2048]{2,1,0:T(8,128)(2,1)}, bf16[2,64,2048]{2,1,0:T(8,128)(2,1)}, u32[]{:S(2)}, u32[]{:S(2)}) collective-permute-start(bf16[2,64,2048]{2,1,0:T(8,128)(2,1)} %pad_maximum_fusion.9), channel_id=1, source_target_pairs={{0,8},{8,0},{16,24},{24,16},{1,9},{9,1},{17,25},{25,17},{2,10},{10... | collective-permute-start | bytes 1572872 | tf_op jit(solution)/shard_map/ppermute | solution.py:95
  150.8 15.8 %collective-permute-start.20 = (bf16[64,2048]{1,0:T(8,128)(2,1)S(1)}, bf16[64,2048]{1,0:T(8,128)(2,1)S(1)}, u32[]{:S(2)}, u32[]{:S(2)}) collective-permute-start(bf16[64,2048]{1,0:T(8,128)(2,1)S(1)} %copy-done.62), channel_id=1, source_target_pairs={{0,16},{8,24},{16,0},{24,8},{1,17},{9,25},{17,1},{25,9},{2,18},{10... | collective-permute-start | bytes 786440 | tf_op jit(solution)/shard_map/ppermute | solution.py:95
  155.0 18.8 %collective-permute-start.21 = (bf16[512,512]{1,0:T(8,128)(2,1)S(1)}, bf16[512,512]{1,0:T(8,128)(2,1)S(1)}, u32[]{:S(2)}, u32[]{:S(2)}) collective-permute-start(bf16[512,512]{1,0:T(8,128)(2,1)S(1)} %slice.280), channel_id=1, source_target_pairs={{0,8},{8,0},{16,24},{24,16},{1,9},{9,1},{17,25},{25,17},{2,10},{10... | collective-permute-start | bytes 1572872 | tf_op jit(solution)/shard_map/ppermute | solution.py:95
  156.1 15.4 %collective-permute-start.16 = (bf16[64,2048]{1,0:T(8,128)(2,1)S(1)}, bf16[64,2048]{1,0:T(8,128)(2,1)S(1)}, u32[]{:S(2)}, u32[]{:S(2)}) collective-permute-start(bf16[64,2048]{1,0:T(8,128)(2,1)S(1)} %get-tuple-element.446), channel_id=1, source_target_pairs={{0,2},{1,3},{2,0},{3,1},{4,6},{5,7},{6,4},{7,5},{8,10},{9,11},{10,... | collective-permute-start | bytes 786440 | tf_op jit(solution)/shard_map/ppermute | solution.py:95
  157.2 14.3 %collective-permute-start.17 = (bf16[64,2048]{1,0:T(8,128)(2,1)S(1)}, bf16[64,2048]{1,0:T(8,128)(2,1)S(1)}, u32[]{:S(2)}, u32[]{:S(2)}) collective-permute-start(bf16[64,2048]{1,0:T(8,128)(2,1)S(1)} %get-tuple-element.445), channel_id=1, source_target_pairs={{0,4},{1,5},{2,6},{3,7},{4,0},{5,1},{6,2},{7,3},{8,12},{9,13},{10,... | collective-permute-start | bytes 786440 | tf_op jit(solution)/shard_map/ppermute | solution.py:95
  158.7 12.9 %collective-permute-start.18 = (bf16[64,2048]{1,0:T(8,128)(2,1)S(1)}, bf16[64,2048]{1,0:T(8,128)(2,1)S(1)}, u32[]{:S(2)}, u32[]{:S(2)}) collective-permute-start(bf16[64,2048]{1,0:T(8,128)(2,1)S(1)} %get-tuple-element.444), channel_id=1, source_target_pairs={{0,2},{1,3},{2,0},{3,1},{4,6},{5,7},{6,4},{7,5},{8,10},{9,11},{10,... | collective-permute-start | bytes 786440 | tf_op jit(solution)/shard_map/ppermute | solution.py:95
  171.5 12.9 %collective-permute-start.24 = (bf16[512,512]{1,0:T(8,128)(2,1)}, bf16[512,512]{1,0:T(8,128)(2,1)}, u32[]{:S(2)}, u32[]{:S(2)}) collective-permute-start(bf16[512,512]{1,0:T(8,128)(2,1)} %slice.281), channel_id=1, source_target_pairs={{0,8},{8,0},{16,24},{24,16},{1,9},{9,1},{17,25},{25,17},{2,10},{10... | collective-permute-start | bytes 1572872 | tf_op jit(solution)/shard_map/ppermute | solution.py:95
  174.7 9.7 %collective-permute-start.22 = (bf16[64,2048]{1,0:T(8,128)(2,1)}, bf16[64,2048]{1,0:T(8,128)(2,1)}, u32[]{:S(2)}, u32[]{:S(2)}) collective-permute-start(bf16[64,2048]{1,0:T(8,128)(2,1)} %add_convert_fusion.18), channel_id=1, source_target_pairs={{0,2},{1,3},{2,0},{3,1},{4,6},{5,7},{6,4},{7,5},{8,10},{9,11},{10,... | collective-permute-start | bytes 786440 | tf_op jit(solution)/shard_map/ppermute | solution.py:95
  178.9 28.0 %collective-permute-start.28 = (bf16[512,512]{1,0:T(8,128)(2,1)}, bf16[512,512]{1,0:T(8,128)(2,1)}, u32[]{:S(2)}, u32[]{:S(2)}) collective-permute-start(bf16[512,512]{1,0:T(8,128)(2,1)} %slice.284), channel_id=1, source_target_pairs={{0,8},{8,0},{16,24},{24,16},{1,9},{9,1},{17,25},{25,17},{2,10},{10... | collective-permute-start | bytes 1572872 | tf_op jit(solution)/shard_map/ppermute | solution.py:95
  179.7 38.4 %collective-permute-start.29 = (bf16[512,512]{1,0:T(8,128)(2,1)}, bf16[512,512]{1,0:T(8,128)(2,1)S(1)}, u32[]{:S(2)}, u32[]{:S(2)}) collective-permute-start(bf16[512,512]{1,0:T(8,128)(2,1)} %slice.285), channel_id=1, source_target_pairs={{0,8},{8,0},{16,24},{24,16},{1,9},{9,1},{17,25},{25,17},{2,10},{10... | collective-permute-start | bytes 1572872 | tf_op jit(solution)/shard_map/ppermute | solution.py:95
  182.1 330.1 %reduce-scatter.2.cloned.1.call-start = ((), (), s32[]{:S(2)}) async-start(), calls=%async_computation.7 | async-start | bytes 9437184 | tf_op jit(solution)/shard_map/reduce_scatter | solution.py:791
  186.9 31.2 %collective-permute-start.25 = (bf16[128,2048]{1,0:T(8,128)(2,1)S(1)}, bf16[128,2048]{1,0:T(8,128)(2,1)S(1)}, u32[]{:S(2)}, u32[]{:S(2)}) collective-permute-start(bf16[128,2048]{1,0:T(8,128)(2,1)S(1)} %get-tuple-element.422), channel_id=1, source_target_pairs={{0,2},{1,3},{2,0},{3,1},{4,6},{5,7},{6,4},{7,5},{8,10},{9,11},{10,... | collective-permute-start | bytes 1572872 | tf_op jit(solution)/shard_map/ppermute | solution.py:95
  188.0 30.1 %collective-permute-start.26 = (bf16[128,2048]{1,0:T(8,128)(2,1)S(1)}, bf16[128,2048]{1,0:T(8,128)(2,1)S(1)}, u32[]{:S(2)}, u32[]{:S(2)}) collective-permute-start(bf16[128,2048]{1,0:T(8,128)(2,1)S(1)} %get-tuple-element.422), channel_id=1, source_target_pairs={{0,4},{1,5},{2,6},{3,7},{4,0},{5,1},{6,2},{7,3},{8,12},{9,13},{10,... | collective-permute-start | bytes 1572872 | tf_op jit(solution)/shard_map/ppermute | solution.py:95
  190.2 28.0 %collective-permute-start.27 = (bf16[128,2048]{1,0:T(8,128)(2,1)S(1)}, bf16[128,2048]{1,0:T(8,128)(2,1)}, u32[]{:S(2)}, u32[]{:S(2)}) collective-permute-start(bf16[128,2048]{1,0:T(8,128)(2,1)S(1)} %get-tuple-element.422), channel_id=1, source_target_pairs={{0,16},{8,24},{16,0},{24,8},{1,17},{9,25},{17,1},{25,9},{2,18},{10... | collective-permute-start | bytes 1572872 | tf_op jit(solution)/shard_map/ppermute | solution.py:95
  228.1 16.7 %collective-permute-start.34 = (bf16[512,2048]{1,0:T(8,128)(2,1)}, bf16[512,2048]{1,0:T(8,128)(2,1)}, u32[]{:S(2)}, u32[]{:S(2)}) collective-permute-start(bf16[512,2048]{1,0:T(8,128)(2,1)} %constant_dynamic-update-slice_fusion.5.refs_0_), channel_id=1, source_target_pairs={{0,1},{1,0},{2,3},{3,2},{4,5},{5,4},{6,7},{7,6},{8,9},{9,8},{10,11... | collective-permute-start | bytes 6291464 | tf_op jit(solution)/shard_map/ppermute | solution.py:95
  230.9 13.9 %collective-permute-start.35 = (bf16[128,2048]{1,0:T(8,128)(2,1)}, bf16[128,2048]{1,0:T(8,128)(2,1)}, u32[]{:S(2)}, u32[]{:S(2)}) collective-permute-start(bf16[128,2048]{1,0:T(8,128)(2,1)} %get-tuple-element.274), channel_id=1, source_target_pairs={{0,8},{8,0},{16,24},{24,16},{1,9},{9,1},{17,25},{25,17},{2,10},{10... | collective-permute-start | bytes 1572872 | tf_op jit(solution)/shard_map/ppermute | solution.py:95
  233.7 33.0 %collective-permute-start.30 = (bf16[128,2048]{1,0:T(8,128)(2,1)}, bf16[128,2048]{1,0:T(8,128)(2,1)S(1)}, u32[]{:S(2)}, u32[]{:S(2)}) collective-permute-start(bf16[128,2048]{1,0:T(8,128)(2,1)} %collective-permute-done.27), channel_id=1, source_target_pairs={{0,2},{1,3},{2,0},{3,1},{4,6},{5,7},{6,4},{7,5},{8,10},{9,11},{10,... | collective-permute-start | bytes 1572872 | tf_op jit(solution)/shard_map/ppermute | solution.py:95
  234.1 32.6 %collective-permute-start.31 = (bf16[128,2048]{1,0:T(8,128)(2,1)}, bf16[128,2048]{1,0:T(8,128)(2,1)S(1)}, u32[]{:S(2)}, u32[]{:S(2)}) collective-permute-start(bf16[128,2048]{1,0:T(8,128)(2,1)} %collective-permute-done.27), channel_id=1, source_target_pairs={{0,4},{1,5},{2,6},{3,7},{4,0},{5,1},{6,2},{7,3},{8,12},{9,13},{10,... | collective-permute-start | bytes 1572872 | tf_op jit(solution)/shard_map/ppermute | solution.py:95
  280.9 22.8 %collective-permute-start.40 = (bf16[64,2048]{1,0:T(8,128)(2,1)S(1)}, bf16[64,2048]{1,0:T(8,128)(2,1)S(1)}, u32[]{:S(2)}, u32[]{:S(2)}) collective-permute-start(bf16[64,2048]{1,0:T(8,128)(2,1)S(1)} %get-tuple-element.440), channel_id=1, source_target_pairs={{0,2},{1,3},{2,0},{3,1},{4,6},{5,7},{6,4},{7,5},{8,10},{9,11},{10,... | collective-permute-start | bytes 786440 | tf_op jit(solution)/shard_map/ppermute | solution.py:95
  282.0 21.7 %collective-permute-start.41 = (bf16[64,2048]{1,0:T(8,128)(2,1)S(1)}, bf16[64,2048]{1,0:T(8,128)(2,1)S(1)}, u32[]{:S(2)}, u32[]{:S(2)}) collective-permute-start(bf16[64,2048]{1,0:T(8,128)(2,1)S(1)} %get-tuple-element.439), channel_id=1, source_target_pairs={{0,4},{1,5},{2,6},{3,7},{4,0},{5,1},{6,2},{7,3},{8,12},{9,13},{10,... | collective-permute-start | bytes 786440 | tf_op jit(solution)/shard_map/ppermute | solution.py:95
  283.5 20.2 %collective-permute-start.42 = (bf16[64,2048]{1,0:T(8,128)(2,1)S(1)}, bf16[64,2048]{1,0:T(8,128)(2,1)S(1)}, u32[]{:S(2)}, u32[]{:S(2)}) collective-permute-start(bf16[64,2048]{1,0:T(8,128)(2,1)S(1)} %get-tuple-element.438), channel_id=1, source_target_pairs={{0,2},{1,3},{2,0},{3,1},{4,6},{5,7},{6,4},{7,5},{8,10},{9,11},{10,... | collective-permute-start | bytes 786440 | tf_op jit(solution)/shard_map/ppermute | solution.py:95
  283.8 19.9 %collective-permute-start.43 = (bf16[64,2048]{1,0:T(8,128)(2,1)S(1)}, bf16[64,2048]{1,0:T(8,128)(2,1)S(1)}, u32[]{:S(2)}, u32[]{:S(2)}) collective-permute-start(bf16[64,2048]{1,0:T(8,128)(2,1)S(1)} %get-tuple-element.437), channel_id=1, source_target_pairs={{0,4},{1,5},{2,6},{3,7},{4,0},{5,1},{6,2},{7,3},{8,12},{9,13},{10,... | collective-permute-start | bytes 786440 | tf_op jit(solution)/shard_map/ppermute | solution.py:95
  304.6 14.5 %collective-permute-start.44 = (bf16[512,2048]{1,0:T(8,128)(2,1)}, bf16[512,2048]{1,0:T(8,128)(2,1)S(1)}, u32[]{:S(2)}, u32[]{:S(2)}) collective-permute-start(bf16[512,2048]{1,0:T(8,128)(2,1)} %get-tuple-element.313), channel_id=1, source_target_pairs={{0,1},{1,0},{2,3},{3,2},{4,5},{5,4},{6,7},{7,6},{8,9},{9,8},{10,11... | collective-permute-start | bytes 6291464 | tf_op jit(solution)/shard_map/ppermute | solution.py:95
  307.8 12.1 %collective-permute-start.45 = (bf16[64,2048]{1,0:T(8,128)(2,1)S(1)}, bf16[64,2048]{1,0:T(8,128)(2,1)S(1)}, u32[]{:S(2)}, u32[]{:S(2)}) collective-permute-start(bf16[64,2048]{1,0:T(8,128)(2,1)S(1)} %add_convert_fusion.16), channel_id=1, source_target_pairs={{0,2},{1,3},{2,0},{3,1},{4,6},{5,7},{6,4},{7,5},{8,10},{9,11},{10,... | collective-permute-start | bytes 786440 | tf_op jit(solution)/shard_map/ppermute | solution.py:95
  310.1 9.8 %collective-permute-start.46 = (bf16[64,2048]{1,0:T(8,128)(2,1)S(1)}, bf16[64,2048]{1,0:T(8,128)(2,1)S(1)}, u32[]{:S(2)}, u32[]{:S(2)}) collective-permute-start(bf16[64,2048]{1,0:T(8,128)(2,1)S(1)} %add_convert_fusion.15), channel_id=1, source_target_pairs={{0,4},{1,5},{2,6},{3,7},{4,0},{5,1},{6,2},{7,3},{8,12},{9,13},{10,... | collective-permute-start | bytes 786440 | tf_op jit(solution)/shard_map/ppermute | solution.py:95
  321.5 12.9 %collective-permute-start.49 = (bf16[64,2048]{1,0:T(8,128)(2,1)S(1)}, bf16[64,2048]{1,0:T(8,128)(2,1)S(1)}, u32[]{:S(2)}, u32[]{:S(2)}) collective-permute-start(bf16[64,2048]{1,0:T(8,128)(2,1)S(1)} %get-tuple-element.432), channel_id=1, source_target_pairs={{0,2},{1,3},{2,0},{3,1},{4,6},{5,7},{6,4},{7,5},{8,10},{9,11},{10,... | collective-permute-start | bytes 786440 | tf_op jit(solution)/shard_map/ppermute | solution.py:95
  322.7 11.7 %collective-permute-start.50 = (bf16[64,2048]{1,0:T(8,128)(2,1)S(1)}, bf16[64,2048]{1,0:T(8,128)(2,1)S(1)}, u32[]{:S(2)}, u32[]{:S(2)}) collective-permute-start(bf16[64,2048]{1,0:T(8,128)(2,1)S(1)} %get-tuple-element.431), channel_id=1, source_target_pairs={{0,4},{1,5},{2,6},{3,7},{4,0},{5,1},{6,2},{7,3},{8,12},{9,13},{10,... | collective-permute-start | bytes 786440 | tf_op jit(solution)/shard_map/ppermute | solution.py:95
  324.2 59.7 %collective-permute-start.58 = (bf16[2048,256]{1,0:T(8,128)(2,1)}, bf16[2048,256]{1,0:T(8,128)(2,1)}, u32[]{:S(2)}, u32[]{:S(2)}) collective-permute-start(bf16[2048,256]{1,0:T(8,128)(2,1)} %convolution_convert_fusion.9), channel_id=1, source_target_pairs={{0,8},{8,0},{16,24},{24,16},{1,9},{9,1},{17,25},{25,17},{2,10},{10... | collective-permute-start | bytes 3145736 | tf_op jit(solution)/shard_map/ppermute | solution.py:95
  343.1 24.4 %collective-permute-start.53 = (bf16[128,2048]{1,0:T(8,128)(2,1)}, bf16[128,2048]{1,0:T(8,128)(2,1)}, u32[]{:S(2)}, u32[]{:S(2)}) collective-permute-start(bf16[128,2048]{1,0:T(8,128)(2,1)} %pad_maximum_fusion.11), channel_id=1, source_target_pairs={{0,16},{8,24},{16,0},{24,8},{1,17},{9,25},{17,1},{25,9},{2,18},{10... | collective-permute-start | bytes 1572872 | tf_op jit(solution)/shard_map/ppermute | solution.py:95
  371.4 11.1 %collective-permute-start.54 = (bf16[128,2048]{1,0:T(8,128)(2,1)S(1)}, bf16[128,2048]{1,0:T(8,128)(2,1)S(1)}, u32[]{:S(2)}, u32[]{:S(2)}) collective-permute-start(bf16[128,2048]{1,0:T(8,128)(2,1)S(1)} %get-tuple-element.361), channel_id=1, source_target_pairs={{0,2},{1,3},{2,0},{3,1},{4,6},{5,7},{6,4},{7,5},{8,10},{9,11},{10,... | collective-permute-start | bytes 1572872 | tf_op jit(solution)/shard_map/ppermute | solution.py:95
  371.9 10.9 %collective-permute-start.55 = (bf16[128,2048]{1,0:T(8,128)(2,1)S(1)}, bf16[128,2048]{1,0:T(8,128)(2,1)S(1)}, u32[]{:S(2)}, u32[]{:S(2)}) collective-permute-start(bf16[128,2048]{1,0:T(8,128)(2,1)S(1)} %get-tuple-element.361), channel_id=1, source_target_pairs={{0,4},{1,5},{2,6},{3,7},{4,0},{5,1},{6,2},{7,3},{8,12},{9,13},{10,... | collective-permute-start | bytes 1572872 | tf_op jit(solution)/shard_map/ppermute | solution.py:95
  371.9 21.9 %collective-permute-start.59 = (bf16[2048,256]{1,0:T(8,128)(2,1)S(1)}, bf16[2048,256]{1,0:T(8,128)(2,1)}, u32[]{:S(2)}, u32[]{:S(2)}) collective-permute-start(bf16[2048,256]{1,0:T(8,128)(2,1)S(1)} %copy-done.69), channel_id=1, source_target_pairs={{0,8},{8,0},{16,24},{24,16},{1,9},{9,1},{17,25},{25,17},{2,10},{10... | collective-permute-start | bytes 3145736 | tf_op jit(solution)/shard_map/ppermute | solution.py:95
  394.9 21.6 %collective-permute-start.60 = (bf16[256,2048]{1,0:T(8,128)(2,1)}, bf16[256,2048]{1,0:T(8,128)(2,1)}, u32[]{:S(2)}, u32[]{:S(2)}) collective-permute-start(bf16[256,2048]{1,0:T(8,128)(2,1)} %pad_maximum_fusion.3), channel_id=1, source_target_pairs={{0,1},{1,0},{2,3},{3,2},{4,5},{5,4},{6,7},{7,6},{8,9},{9,8},{10,11... | collective-permute-start | bytes 3145736 | tf_op jit(solution)/shard_map/ppermute | solution.py:95
  400.7 17.2 %collective-permute-start.61 = (bf16[256,2048]{1,0:T(8,128)(2,1)}, bf16[256,2048]{1,0:T(8,128)(2,1)}, u32[]{:S(2)}, u32[]{:S(2)}) collective-permute-start(bf16[256,2048]{1,0:T(8,128)(2,1)} %pad_maximum_fusion.4), channel_id=1, source_target_pairs={{0,1},{1,0},{2,3},{3,2},{4,5},{5,4},{6,7},{7,6},{8,9},{9,8},{10,11... | collective-permute-start | bytes 3145736 | tf_op jit(solution)/shard_map/ppermute | solution.py:95
  408.1 78.5 %all-to-all-start.2 = ((bf16[32,64,512]{2,1,0:T(8,128)(2,1)}), bf16[32,64,512]{2,1,0:T(8,128)(2,1)}, u32[]{:S(2)}, u32[]{:S(2)}) async-start(bf16[32,64,512]{2,1,0:T(8,128)(2,1)} %pad_maximum_fusion.1), calls=%async_computation.2 | async-start | bytes 4194304 | tf_op jit(solution)/shard_map/all_to_all | solution.py:670
  442.5 21.9 %collective-permute-start.63 = (bf16[2,64,2048]{2,1,0:T(8,128)(2,1)S(1)}, bf16[2,64,2048]{2,1,0:T(8,128)(2,1)S(1)}, u32[]{:S(2)}, u32[]{:S(2)}) collective-permute-start(bf16[2,64,2048]{2,1,0:T(8,128)(2,1)S(1)} %dynamic-slice_bitcast_fusion.1), channel_id=1, source_target_pairs={{0,8},{8,0},{16,24},{24,16},{1,9},{9,1},{17,25},{25,17},{2,10},{10... | collective-permute-start | bytes 1572872 | tf_op jit(solution)/shard_map/ppermute | solution.py:95
  446.6 37.2 %collective-permute-start.62 = (bf16[2,512,384]{2,1,0:T(8,128)(2,1)S(1)}, bf16[2,512,384]{2,1,0:T(8,128)(2,1)S(1)}, u32[]{:S(2)}, u32[]{:S(2)}) collective-permute-start(bf16[2,512,384]{2,1,0:T(8,128)(2,1)S(1)} %dynamic-slice_bitcast_fusion), channel_id=1, source_target_pairs={{0,8},{8,0},{16,24},{24,16},{1,9},{9,1},{17,25},{25,17},{2,10},{10... | collective-permute-start | bytes 2359304 | tf_op jit(solution)/shard_map/ppermute | solution.py:95
  466.0 18.0 %collective-permute-start.65 = (bf16[256,2048]{1,0:T(8,128)(2,1)S(1)}, bf16[256,2048]{1,0:T(8,128)(2,1)S(1)}, u32[]{:S(2)}, u32[]{:S(2)}) collective-permute-start(bf16[256,2048]{1,0:T(8,128)(2,1)S(1)} %get-tuple-element.430), channel_id=1, source_target_pairs={{0,1},{1,0},{2,3},{3,2},{4,5},{5,4},{6,7},{7,6},{8,9},{9,8},{10,11... | collective-permute-start | bytes 3145736 | tf_op jit(solution)/shard_map/ppermute | solution.py:95
  467.1 16.9 %collective-permute-start.64 = (bf16[256,2048]{1,0:T(8,128)(2,1)S(1)}, bf16[256,2048]{1,0:T(8,128)(2,1)S(1)}, u32[]{:S(2)}, u32[]{:S(2)}) collective-permute-start(bf16[256,2048]{1,0:T(8,128)(2,1)S(1)} %get-tuple-element.429), channel_id=1, source_target_pairs={{0,1},{1,0},{2,3},{3,2},{4,5},{5,4},{6,7},{7,6},{8,9},{9,8},{10,11... | collective-permute-start | bytes 3145736 | tf_op jit(solution)/shard_map/ppermute | solution.py:95
  472.3 19.7 %collective-permute-start.71 = (bf16[1,64,2048]{2,1,0:T(8,128)(2,1)}, bf16[1,64,2048]{2,1,0:T(8,128)(2,1)}, u32[]{:S(2)}, u32[]{:S(2)}) collective-permute-start(bf16[1,64,2048]{2,1,0:T(8,128)(2,1)} %constant_dynamic-slice_fusion), channel_id=1, source_target_pairs={{0,16},{8,24},{16,0},{24,8},{1,17},{9,25},{17,1},{25,9},{2,18},{10... | collective-permute-start | bytes 786440 | tf_op jit(solution)/shard_map/ppermute | solution.py:95
  489.0 25.0 %collective-permute-start.66 = (bf16[64,2048]{1,0:T(8,128)(2,1)}, bf16[64,2048]{1,0:T(8,128)(2,1)}, u32[]{:S(2)}, u32[]{:S(2)}) collective-permute-start(bf16[64,2048]{1,0:T(8,128)(2,1)} %get-tuple-element.426), channel_id=1, source_target_pairs={{0,2},{1,3},{2,0},{3,1},{4,6},{5,7},{6,4},{7,5},{8,10},{9,11},{10,... | collective-permute-start | bytes 786440 | tf_op jit(solution)/shard_map/ppermute | solution.py:95
  490.1 24.0 %collective-permute-start.67 = (bf16[64,2048]{1,0:T(8,128)(2,1)}, bf16[64,2048]{1,0:T(8,128)(2,1)}, u32[]{:S(2)}, u32[]{:S(2)}) collective-permute-start(bf16[64,2048]{1,0:T(8,128)(2,1)} %get-tuple-element.425), channel_id=1, source_target_pairs={{0,4},{1,5},{2,6},{3,7},{4,0},{5,1},{6,2},{7,3},{8,12},{9,13},{10,... | collective-permute-start | bytes 786440 | tf_op jit(solution)/shard_map/ppermute | solution.py:95
  491.3 22.7 %collective-permute-start.68 = (bf16[64,2048]{1,0:T(8,128)(2,1)}, bf16[64,2048]{1,0:T(8,128)(2,1)}, u32[]{:S(2)}, u32[]{:S(2)}) collective-permute-start(bf16[64,2048]{1,0:T(8,128)(2,1)} %get-tuple-element.424), channel_id=1, source_target_pairs={{0,2},{1,3},{2,0},{3,1},{4,6},{5,7},{6,4},{7,5},{8,10},{9,11},{10,... | collective-permute-start | bytes 786440 | tf_op jit(solution)/shard_map/ppermute | solution.py:95
  491.7 22.4 %collective-permute-start.69 = (bf16[64,2048]{1,0:T(8,128)(2,1)}, bf16[64,2048]{1,0:T(8,128)(2,1)}, u32[]{:S(2)}, u32[]{:S(2)}) collective-permute-start(bf16[64,2048]{1,0:T(8,128)(2,1)} %get-tuple-element.423), channel_id=1, source_target_pairs={{0,4},{1,5},{2,6},{3,7},{4,0},{5,1},{6,2},{7,3},{8,12},{9,13},{10,... | collective-permute-start | bytes 786440 | tf_op jit(solution)/shard_map/ppermute | solution.py:95
  492.0 19.3 %collective-permute-start.70 = (bf16[1,512,384]{2,1,0:T(8,128)(2,1)S(1)}, bf16[1,512,384]{2,1,0:T(8,128)(2,1)S(1)}, u32[]{:S(2)}, u32[]{:S(2)}) collective-permute-start(bf16[1,512,384]{2,1,0:T(8,128)(2,1)S(1)} %constant_dynamic-slice_fusion.1), channel_id=1, source_target_pairs={{0,16},{8,24},{16,0},{24,8},{1,17},{9,25},{17,1},{25,9},{2,18},{10... | collective-permute-start | bytes 1179656 | tf_op jit(solution)/shard_map/ppermute | solution.py:95
  511.3 33.6 %collective-permute-start.76 = (bf16[256,2048]{1,0:T(8,128)(2,1)}, bf16[256,2048]{1,0:T(8,128)(2,1)}, u32[]{:S(2)}, u32[]{:S(2)}) collective-permute-start(bf16[256,2048]{1,0:T(8,128)(2,1)} %convolution_convert_fusion.7), channel_id=1, source_target_pairs={{0,8},{8,0},{16,24},{24,16},{1,9},{9,1},{17,25},{25,17},{2,10},{10... | collective-permute-start | bytes 3145736 | tf_op jit(solution)/shard_map/ppermute | solution.py:95
  515.1 29.8 %collective-permute-start.74 = (bf16[64,2048]{1,0:T(8,128)(2,1)S(1)}, bf16[64,2048]{1,0:T(8,128)(2,1)S(1)}, u32[]{:S(2)}, u32[]{:S(2)}) collective-permute-start(bf16[64,2048]{1,0:T(8,128)(2,1)S(1)} %add_convert_fusion.9), channel_id=1, source_target_pairs={{0,2},{1,3},{2,0},{3,1},{4,6},{5,7},{6,4},{7,5},{8,10},{9,11},{10,... | collective-permute-start | bytes 786440 | tf_op jit(solution)/shard_map/ppermute | solution.py:95
  517.2 27.7 %collective-permute-start.75 = (bf16[64,2048]{1,0:T(8,128)(2,1)S(1)}, bf16[64,2048]{1,0:T(8,128)(2,1)S(1)}, u32[]{:S(2)}, u32[]{:S(2)}) collective-permute-start(bf16[64,2048]{1,0:T(8,128)(2,1)S(1)} %add_convert_fusion.8), channel_id=1, source_target_pairs={{0,4},{1,5},{2,6},{3,7},{4,0},{5,1},{6,2},{7,3},{8,12},{9,13},{10,... | collective-permute-start | bytes 786440 | tf_op jit(solution)/shard_map/ppermute | solution.py:95
  518.6 46.0 %all-to-all-start.3 = ((bf16[8,64,384]{2,1,0:T(8,128)(2,1)}), bf16[8,64,384]{2,1,0:T(8,128)(2,1)S(1)}, u32[]{:S(2)}, u32[]{:S(2)}) async-start(bf16[8,64,384]{2,1,0:T(8,128)(2,1)} %bitcast.37), calls=%async_computation.4 | async-start | bytes 786432 | tf_op jit(solution)/shard_map/all_to_all | solution.py:194
  523.0 41.6 %collective-permute-start.72 = (bf16[128,2048]{1,0:T(8,128)(2,1)}, bf16[128,2048]{1,0:T(8,128)(2,1)}, u32[]{:S(2)}, u32[]{:S(2)}) collective-permute-start(bf16[128,2048]{1,0:T(8,128)(2,1)} %slice.346), channel_id=1, source_target_pairs={{0,16},{8,24},{16,0},{24,8},{1,17},{9,25},{17,1},{25,9},{2,18},{10... | collective-permute-start | bytes 1572872 | tf_op jit(solution)/shard_map/ppermute | solution.py:95
  524.6 40.0 %collective-permute-start.73 = (bf16[64,2048]{1,0:T(8,128)(2,1)}, bf16[64,2048]{1,0:T(8,128)(2,1)}, u32[]{:S(2)}, u32[]{:S(2)}) collective-permute-start(bf16[64,2048]{1,0:T(8,128)(2,1)} %fusion.31), channel_id=1, source_target_pairs={{0,0},{8,1},{16,2},{24,3},{1,4},{9,5},{17,6},{25,7},{2,8},{10,9},{... | collective-permute-start | bytes 786440 | tf_op jit(solution)/shard_map/ppermute | solution.py:840
  (102 other events, 973.3 us)
Sparse Core Ops, SparseCore 0:
  100.0 47.8 all-gather.2
  182.2 40.2 all-gather.4
  393.9 86.8 reduce-scatter.1

commit v5 on v4

--- a/solution.py
+++ b/solution.py
@@ -40,14 +40,15 @@
     "up_own": (16, 17),
     "out_rows": (18, 23),
     "both_all": (18, 22),
-    "down_move": (21, 24),
     "out_part": (18, 19),
-    "out_halved": (19, 21),
-    "out_sum": (21, 23),
+    "out_halved": (19, 20),
+    "out_sum": (20, 22),
     "out_grad": (23, 25),
     "side_out": (23, 25),
     "down_own": (20, 22),
     "assembled": (23, 24),
+    "down_move_a": (21, 24),
+    "down_move_b": (21, 24),
 }
 COST = {"forward": 0, "backward": 0, "feed": 0, "split_out": 1, "split_last": 2, "split_hidden": 2}
 LOW = jnp.bfloat16
@@ -781,7 +782,8 @@
     move_back = lambda parts: [swap(part, "fsdp", r) for r, part in enumerate(parts, 1)]
     add("gate_move", ("gate_away",), lambda: result("gate_away"), move_back)
     add("up_move", ("up_away",), lambda: result("up_away"), move_back)
-    add("down_move", ("down_away",), lambda: result("down_away"), move_back)
+    add("down_move_a", ("down_away",), lambda: [p[:unit_half] for p in result("down_away")], move_back)
+    add("down_move_b", ("down_away",), lambda: [p[unit_half:] for p in result("down_away")], move_back)
     add(
         "down_terms", (), lambda: all_acts,
         lambda acts: down_terms_by_device(acts, c_index, c_count, downs, tok_rows),
@@ -866,7 +868,7 @@
     mlp_gain_grad = mlp_gain_grad[:, 0]
     out_grad = result("out_grad").astype(WIDE)
     down_grad = result("down_own")
-    for part in result("down_move"):
+    for part in joined([result("down_move_a"), result("down_move_b")]):
         down_grad = down_grad + part.astype(WIDE)
     side_out, out_rows = result("side_out"), result("out_rows")
     output = hidden + out_rows[0].astype(WIDE) + side_out.astype(WIDE)

time: 587 us -> 577 us (0.983)
  waiting for transfers between devices: 202 us -> 194 us
  starting transfers between devices: 106 us -> 112 us
    ppermute x75 -> x76, waiting for transfers between devices: 192 us -> 180 us  [swap(): return lax.ppermute(block, axis, [(i, i ^ mask) for i in range(count)])]
    ppermute x75 -> x76, starting transfers between devices: 80 us -> 82.9 us  [swap(): return lax.ppermute(block, axis, [(i, i ^ mask) for i in range(count)])]
    unnamed x177 -> x183, local copies, waits for them, and re-layouts: 20.4 us -> 18.1 us
  transfers between devices with their start and end apart: 84 -> 85, of which waited for: 34 -> 35; matrix products, arithmetic and copies ran while one was open for 24% -> 24% of each run, Pallas kernels for 17% -> 17%
where the time goes in v5:
time: 577 us; the launch traced here: 569 us
  waiting for transfers between devices  194 us (34%)
  starting transfers between devices  112 us (19%)
  Pallas kernels  97.3 us (17%)
  other arithmetic  59.2 us (10%)
  matrix products  51.5 us (9%)
  local copies, waits for them, and re-layouts  41 us (7%)
  between operations  15.4 us (3%)
    ppermute x76, waiting for transfers between devices, swap(): return lax.ppermute(block, axis, [(i, i ^ mask) for i in range(count)])  180 us
    ppermute x76, starting transfers between devices, swap(): return lax.ppermute(block, axis, [(i, i ^ mask) for i in range(count)])  82.9 us
    dot_general x17, matrix products, dot(): lax.dot_general(left, right, (dims, ((), ())), preferred_element_type=WIDE)  51.5 us
    pallas_call x2, Pallas kernels, feed_forward(): pl.pallas_call(functools.partial(feed_kernel, blocks, steps, per_step), g...  39.6 us
    pallas_call x1, Pallas kernels, attention_backward(): pl.pallas_call(functools.partial(backward_kernel, heads, steps), grid=(st...  18.2 us
    unnamed x183, local copies, waits for them, and re-layouts  18.1 us
    pallas_call x1, Pallas kernels, attention_forward(): pl.pallas_call(functools.partial(forward_kernel, heads), grid=(length //...  15.9 us
    ppermute x1, waiting for transfers between devices, per_device(): lax.ppermute(p, ('fsdp', 'ctx'), back_route)  13 us
  transfers between devices with their start and end apart: 85, of which 35 were waited for; matrix products, arithmetic and copies ran while one was open for 24% of the time, Pallas kernels for 17%

profile of v5, /device:TPU:1, one launch (start us, length us, event | category | flops | bytes accessed | tf_op | source)
XLA Modules:
  0.0 569.4 jit_solution(14678684670719552948)
XLA Ops:
  7.2 2.1 collective-permute-start
  16.3 4.6 all-to-all-start
  20.9 3.2 collective-permute-start.2
  24.1 3.3 collective-permute-start.4
  33.5 7.4 %collective-permute-start.3 = (bf16[1,512,384]{2,1,0:T(8,128)(2,1)S(1)}, bf16[1,512,384]{2,1,0:T(8,128)(2,1)S(1)}, u32[]{:S(2)}, u32[]{:S(2)}) collective-permute-start(bf16[1,512,384]{2,1,0:T(8,128)(2,1)S(1)} %bitcast.150), channel_id=1, source_target_pairs={{0,16},{8,24},{16,0},{24,8},{1,17},{9,25},{17,1},{25,9},{2,18},{10... | collective-permute-start | bytes 1179656 | tf_op jit(solution)/shard_map/ppermute | solution.py:96
  42.9 1.9 fusion.37
  46.6 4.0 columns_by_device.1
  51.1 7.5 %collective-permute-done.3.refs_1_ = bf16[1,512,384]{2,1,0:T(8,128)(2,1)S(1)} collective-permute-done((bf16[1,512,384]{2,1,0:T(8,128)(2,1)S(1)}, bf16[1,512,384]{2,1,0:T(8,128)(2,1)S(1)}, u32[]{:S(2)}, u32[]{:S(2)}) %collective-permute-start.3) | collective-permute-done | bytes 393248 | tf_op jit(solution)/shard_map/ppermute | solution.py:96
  59.9 2.9 collective-permute-start.12
  67.3 14.8 %collective-permute-done.12.refs_1_ = bf16[1,64,2048]{2,1,0:T(8,128)(2,1)S(1)} collective-permute-done((bf16[1,64,2048]{2,1,0:T(8,128)(2,1)S(1)}, bf16[1,64,2048]{2,1,0:T(8,128)(2,1)S(1)}, u32[]{:S(2)}, u32[]{:S(2)}) %collective-permute-start.12) | collective-permute-done | bytes 262176 | tf_op jit(solution)/shard_map/ppermute | solution.py:96
  82.1 5.6 collective-permute-done.13
  87.7 2.1 collective-permute-done.10.refs_2_
  89.8 5.8 %all-to-all-start.1 = ((bf16[32,64,512]{2,1,0:T(8,128)(2,1)}), bf16[32,64,512]{2,1,0:T(8,128)(2,1)S(1)}, u32[]{:S(2)}, u32[]{:S(2)}) async-start(bf16[32,64,512]{2,1,0:T(8,128)(2,1)} %columns_by_device.1), calls=%async_computation.1 | async-start | bytes 4194304 | tf_op jit(solution)/shard_map/all_to_all | solution.py:671
  100.1 2.7 place.2
  102.8 2.8 fusion.48
  108.2 15.9 %attention_forward.1 = (bf16[1024,256]{1,0:T(8,128)(2,1)}, f32[8,1024]{1,0:T(8,128)}, bf16[1024,256]{1,0:T(8,128)(2,1)}, bf16[1024,64]{1,0:T(8,128)(2,1)}, bf16[1024,64]{1,0:T(8,128)(2,1)}) custom-call(f32[1024,384]{1,0:T(8,128)} %pad_maximum_fusion.2.q_ref.kv_ref, f32[1024,384]{1,0:T(8,128)} %pad_maximum_fusion.2.q_ref.kv_ref, ...), custom_call_target="tpu_custom_call" | custom-call | bytes 2097152 | tf_op jit(solution)/shard_map/attention_forward/pallas_call | solution.py:355
  124.1 17.5 %collective-permute-done.14.refs_2_ = bf16[2,64,2048]{2,1,0:T(8,128)(2,1)} collective-permute-done((bf16[2,64,2048]{2,1,0:T(8,128)(2,1)}, bf16[2,64,2048]{2,1,0:T(8,128)(2,1)}, u32[]{:S(2)}, u32[]{:S(2)}) %collective-permute-start.14) | collective-permute-done | bytes 524320 | tf_op jit(solution)/shard_map/ppermute | solution.py:96
  141.6 2.3 place.3
  144.1 2.7 convolution_convert_fusion.1
  149.1 3.5 collective-permute-start.20
  157.3 7.6 %collective-permute-done.20 = bf16[64,2048]{1,0:T(8,128)(2,1)S(1)} collective-permute-done((bf16[64,2048]{1,0:T(8,128)(2,1)S(1)}, bf16[64,2048]{1,0:T(8,128)(2,1)S(1)}, u32[]{:S(2)}, u32[]{:S(2)}) %collective-permute-start.20) | collective-permute-done | bytes 262176 | tf_op jit(solution)/shard_map/ppermute | solution.py:96
  166.3 2.6 pad_maximum_fusion
  180.5 3.0 collective-permute-done.24
  189.2 16.8 %collective-permute-done.28 = bf16[512,512]{1,0:T(8,128)(2,1)} collective-permute-done((bf16[512,512]{1,0:T(8,128)(2,1)}, bf16[512,512]{1,0:T(8,128)(2,1)}, u32[]{:S(2)}, u32[]{:S(2)}) %collective-permute-start.28) | collective-permute-done | bytes 524320 | tf_op jit(solution)/shard_map/ppermute | solution.py:96
  206.0 11.2 %collective-permute-done.29 = bf16[512,512]{1,0:T(8,128)(2,1)S(1)} collective-permute-done((bf16[512,512]{1,0:T(8,128)(2,1)}, bf16[512,512]{1,0:T(8,128)(2,1)S(1)}, u32[]{:S(2)}, u32[]{:S(2)}) %collective-permute-start.29) | collective-permute-done | bytes 524320 | tf_op jit(solution)/shard_map/ppermute | solution.py:96
  221.4 2.1 collective-permute-done.32
  225.9 2.9 collective-permute-start.34
  237.5 1.9 constant_dynamic-update-slice_fusion.20
  239.4 5.0 collective-permute-done.35
  246.4 19.8 %feed_forward.2 = (bf16[2048,2048]{1,0:T(8,128)(2,1)}, bf16[2048,2048]{1,0:T(8,128)(2,1)}, bf16[2,2048,256]{2,1,0:T(8,128)(2,1)}, bf16[4,2048,256]{2,1,0:T(8,128...) custom-call(s32[8]{0:T(128)} %broadcast_xor_fusion.table_ref, ...), custom_call_target="tpu_custom_call" | custom-call | bytes 8388608 | tf_op jit(solution)/shard_map/feed_forward/pallas_call | solution.py:569
  269.4 4.0 collective-permute-done.36
  273.6 2.0 collective-permute-start.38
  276.5 3.1 collective-permute-done.38.refs_1_
  283.4 19.9 %feed_forward.3 = (bf16[2048,2048]{1,0:T(8,128)(2,1)}, bf16[2048,2048]{1,0:T(8,128)(2,1)}, bf16[2,2048,256]{2,1,0:T(8,128)(2,1)}, bf16[4,2048,256]{2,1,0:T(8,128...) custom-call(s32[8]{0:T(128)} %broadcast_xor_fusion.table_ref, ...), custom_call_target="tpu_custom_call", output_to_operand_aliasing={{0}: (9, {}), {1}: (10, {}), {2}: (11, {}), {3}: (12, {})} | custom-call | bytes 8388608 | tf_op jit(solution)/shard_map/feed_forward/pallas_call | solution.py:569
  311.1 7.3 %convolution_convert_fusion.9 = bf16[2048,256]{1,0:T(8,128)(2,1)} fusion(bf16[2048,2048]{1,0:T(8,128)(2,1)} %get-tuple-element.355, bf16[4,2048,256]{2,1,0:T(8,128)(2,1)} %get-tuple-element.356), kind=kOutput, calls=%fused_computation.24 | convolution fusion | flops 2148007936 | bytes 10485760 | tf_op jit(solution)/shard_map/dot_general | solution.py:59
  323.8 3.6 convolution_convert_fusion.8
  327.7 5.7 %collective-permute-done.49 = bf16[64,2048]{1,0:T(8,128)(2,1)S(1)} collective-permute-done((bf16[64,2048]{1,0:T(8,128)(2,1)S(1)}, bf16[64,2048]{1,0:T(8,128)(2,1)S(1)}, u32[]{:S(2)}, u32[]{:S(2)}) %collective-permute-start.49) | collective-permute-done | bytes 262176 | tf_op jit(solution)/shard_map/ppermute | solution.py:96
  335.5 3.3 convolution_convert_fusion.7
  342.8 9.6 %down_terms.1 = bf16[4,2,2,128,2048]{4,3,2,1,0:T(8,128)(2,1)} custom-call(s32[2]{0:T(128)} %pad_add_fusion.3.table_ref, bf16[2,2048,256]{2,1,0:T(8,128)(2,1)} %get-tuple-element.385.act_ref, bf16[256,2048]{1,0:T(8,128)(2,1)} %refs_0_.1, bf16[256,2048]{1,0:T(8,128)(2,1)} %copy-done.7), custom_call_target="tpu_custom_call" | custom-call | bytes 8388608 | tf_op jit(solution)/shard_map/down_terms/pallas_call | solution.py:612
  352.4 6.9 %convolution_convert_fusion.6 = bf16[2048,256]{1,0:T(8,128)(2,1)} fusion(bf16[2048,2048]{1,0:T(8,128)(2,1)} %get-tuple-element.355, bf16[4,2048,256]{2,1,0:T(8,128)(2,1)S(1)} %copy-done.27), kind=kOutput, calls=%fused_computation.21 | convolution fusion | flops 2148007936 | bytes 10485760 | tf_op jit(solution)/shard_map/dot_general | solution.py:59
  359.3 6.5 %collective-permute-done.53 = bf16[128,2048]{1,0:T(8,128)(2,1)} collective-permute-done((bf16[128,2048]{1,0:T(8,128)(2,1)}, bf16[128,2048]{1,0:T(8,128)(2,1)}, u32[]{:S(2)}, u32[]{:S(2)}) %collective-permute-start.53) | collective-permute-done | bytes 524320 | tf_op jit(solution)/shard_map/ppermute | solution.py:96
  367.2 2.6 fusion.38
  371.8 7.2 %convolution_convert_fusion.5 = bf16[2048,256]{1,0:T(8,128)(2,1)} fusion(bf16[2048,2048]{1,0:T(8,128)(2,1)} %get-tuple-element.355, bf16[4,2048,256]{2,1,0:T(8,128)(2,1)} %get-tuple-element.356), kind=kOutput, calls=%fused_computation.20 | convolution fusion | flops 2148007936 | bytes 10485760 | tf_op jit(solution)/shard_map/dot_general | solution.py:59
  383.4 3.3 collective-permute-done.56
  387.6 6.1 %collective-permute-done.59 = bf16[2048,256]{1,0:T(8,128)(2,1)} collective-permute-done((bf16[2048,256]{1,0:T(8,128)(2,1)S(1)}, bf16[2048,256]{1,0:T(8,128)(2,1)}, u32[]{:S(2)}, u32[]{:S(2)}) %collective-permute-start.59) | collective-permute-done | bytes 1048608 | tf_op jit(solution)/shard_map/ppermute | solution.py:96
  393.9 3.9 collective-permute-start.60
  410.3 4.2 all-to-all-start.2
  415.6 18.2 %attention_backward.1 = bf16[1024,384]{1,0:T(8,128)(2,1)} custom-call(bf16[1024,256]{1,0:T(8,128)(2,1)} %get-tuple-element.268.q_ref, bf16[1024,64]{1,0:T(8,128)(2,1)} %get-tuple-element.269.k_ref, bf16[1024,64]{1,0:T(8,128)(2,1)} %get-tuple-element.270.v_ref, bf16[1024,256]{1,0:T(8,128)(2,1)} %pad_maximum_fusion.12.do_ref, ...), custom_call_target="tpu_custom_call" | custom-call | bytes 2097152 | tf_op jit(solution)/shard_map/attention_backward/pallas_call | solution.py:393
  435.0 5.0 convolution_convert_fusion.4
  443.9 2.2 collective-permute-start.66
  446.1 3.7 fusion.10
  449.8 26.1 %collective-permute-done.66 = bf16[1,64,2048]{2,1,0:T(8,128)(2,1)S(1)} collective-permute-done((bf16[1,64,2048]{2,1,0:T(8,128)(2,1)S(1)}, bf16[1,64,2048]{2,1,0:T(8,128)(2,1)S(1)}, u32[]{:S(2)}, u32[]{:S(2)}) %collective-permute-start.66) | collective-permute-done | bytes 262176 | tf_op jit(solution)/shard_map/ppermute | solution.py:96
  478.6 2.6 add_convert_fusion
  482.7 2.4 fusion.39
  488.1 13.1 %collective-permute-done.71 = bf16[1,512,384]{2,1,0:T(8,128)(2,1)S(1)} collective-permute-done((bf16[1,512,384]{2,1,0:T(8,128)(2,1)S(1)}, bf16[1,512,384]{2,1,0:T(8,128)(2,1)S(1)}, u32[]{:S(2)}, u32[]{:S(2)}) %collective-permute-start.71) | collective-permute-done | bytes 393248 | tf_op jit(solution)/shard_map/ppermute | solution.py:96
  502.0 1.9 slice.354
  508.9 6.3 %all-to-all-start.3 = ((bf16[8,64,384]{2,1,0:T(8,128)(2,1)}), bf16[8,64,384]{2,1,0:T(8,128)(2,1)S(1)}, u32[]{:S(2)}, u32[]{:S(2)}) async-start(bf16[8,64,384]{2,1,0:T(8,128)(2,1)} %bitcast.37), calls=%async_computation.4 | async-start | bytes 786432 | tf_op jit(solution)/shard_map/all_to_all | solution.py:195
  515.3 4.9 assemble_columns.1
  520.2 3.8 collective-permute-start.73
  524.1 7.5 %collective-permute-done.77 = bf16[128,2048]{1,0:T(8,128)(2,1)} collective-permute-done((bf16[128,2048]{1,0:T(8,128)(2,1)}, bf16[128,2048]{1,0:T(8,128)(2,1)}, u32[]{:S(2)}, u32[]{:S(2)}) %collective-permute-start.77) | collective-permute-done | bytes 524320 | tf_op jit(solution)/shard_map/ppermute | solution.py:96
  534.7 2.8 convert_add_fusion
  538.9 2.4 fusion.23
  541.4 13.0 %collective-permute-done.73 = bf16[64,2048]{1,0:T(8,128)(2,1)} collective-permute-done((bf16[64,2048]{1,0:T(8,128)(2,1)}, bf16[64,2048]{1,0:T(8,128)(2,1)}, u32[]{:S(2)}, u32[]{:S(2)}) %collective-permute-start.73) | collective-permute-done | bytes 262176 | tf_op jit(solution)/shard_map/ppermute | solution.py:842
  559.2 2.1 fusion.24
  (443 shorter events, 151.1 us)
Async XLA Ops:
  7.2 26.3 %collective-permute-start = (bf16[128,2048]{1,0:T(8,128)(2,1)}, bf16[128,2048]{1,0:T(8,128)(2,1)S(1)}, u32[]{:S(2)}, u32[]{:S(2)}) collective-permute-start(bf16[128,2048]{1,0:T(8,128)(2,1)} %bitcast.136), channel_id=1, source_target_pairs={{0,2},{1,3},{2,0},{3,1},{4,6},{5,7},{6,4},{7,5},{8,10},{9,11},{10,... | collective-permute-start | bytes 1572872 | tf_op jit(solution)/shard_map/ppermute | solution.py:96
  9.3 24.2 %collective-permute-start.1 = (bf16[128,2048]{1,0:T(8,128)(2,1)}, bf16[128,2048]{1,0:T(8,128)(2,1)S(1)}, u32[]{:S(2)}, u32[]{:S(2)}) collective-permute-start(bf16[128,2048]{1,0:T(8,128)(2,1)} %bitcast.137), channel_id=1, source_target_pairs={{0,4},{1,5},{2,6},{3,7},{4,0},{5,1},{6,2},{7,3},{8,12},{9,13},{10,... | collective-permute-start | bytes 1572872 | tf_op jit(solution)/shard_map/ppermute | solution.py:96
  16.3 17.2 %all-to-all-start = ((bf16[8,64,384]{2,1,0:T(8,128)(2,1)}), bf16[8,64,384]{2,1,0:T(8,128)(2,1)S(1)}, u32[]{:S(2)}, u32[]{:S(2)}) async-start(bf16[8,64,384]{2,1,0:T(8,128)(2,1)} %fusion.25), calls=%async_computation | async-start | bytes 786432 | tf_op jit(solution)/shard_map/all_to_all | solution.py:195
  20.9 12.5 %collective-permute-start.2 = (bf16[64,2048]{1,0:T(8,128)(2,1)S(1)}, bf16[64,2048]{1,0:T(8,128)(2,1)S(1)}, u32[]{:S(2)}, u32[]{:S(2)}) collective-permute-start(bf16[64,2048]{1,0:T(8,128)(2,1)S(1)} %copy-done.72), channel_id=1, source_target_pairs={{0,0},{1,8},{2,16},{3,24},{4,1},{5,9},{6,17},{7,25},{8,2},{9,10},{... | collective-permute-start | bytes 786440 | tf_op jit(solution)/shard_map/ppermute | solution.py:677
  27.4 23.7 %collective-permute-start.9 = (bf16[128,2048]{1,0:T(8,128)(2,1)}, bf16[128,2048]{1,0:T(8,128)(2,1)}, u32[]{:S(2)}, u32[]{:S(2)}) collective-permute-start(bf16[128,2048]{1,0:T(8,128)(2,1)} %get-tuple-element.224), channel_id=1, source_target_pairs={{0,8},{8,0},{16,24},{24,16},{1,9},{9,1},{17,25},{25,17},{2,10},{10... | collective-permute-start | bytes 1572872 | tf_op jit(solution)/shard_map/ppermute | solution.py:96
  33.5 25.1 %collective-permute-start.3 = (bf16[1,512,384]{2,1,0:T(8,128)(2,1)S(1)}, bf16[1,512,384]{2,1,0:T(8,128)(2,1)S(1)}, u32[]{:S(2)}, u32[]{:S(2)}) collective-permute-start(bf16[1,512,384]{2,1,0:T(8,128)(2,1)S(1)} %bitcast.150), channel_id=1, source_target_pairs={{0,16},{8,24},{16,0},{24,8},{1,17},{9,25},{17,1},{25,9},{2,18},{10... | collective-permute-start | bytes 1179656 | tf_op jit(solution)/shard_map/ppermute | solution.py:96
  40.9 10.2 %collective-permute-start.7 = (bf16[64,2048]{1,0:T(8,128)(2,1)S(1)}, bf16[64,2048]{1,0:T(8,128)(2,1)S(1)}, u32[]{:S(2)}, u32[]{:S(2)}) collective-permute-start(bf16[64,2048]{1,0:T(8,128)(2,1)S(1)} %slice.270), channel_id=1, source_target_pairs={{0,2},{1,3},{2,0},{3,1},{4,6},{5,7},{6,4},{7,5},{8,10},{9,11},{10,... | collective-permute-start | bytes 786440 | tf_op jit(solution)/shard_map/ppermute | solution.py:96
  59.8 30.0 %collective-permute-start.10 = (bf16[2,512,384]{2,1,0:T(8,128)(2,1)S(1)}, bf16[2,512,384]{2,1,0:T(8,128)(2,1)}, u32[]{:S(2)}, u32[]{:S(2)}) collective-permute-start(bf16[2,512,384]{2,1,0:T(8,128)(2,1)S(1)} %pad_maximum_fusion.6), channel_id=1, source_target_pairs={{0,8},{8,0},{16,24},{24,16},{1,9},{9,1},{17,25},{25,17},{2,10},{10... | collective-permute-start | bytes 2359304 | tf_op jit(solution)/shard_map/ppermute | solution.py:96
  59.9 22.3 %collective-permute-start.12 = (bf16[1,64,2048]{2,1,0:T(8,128)(2,1)S(1)}, bf16[1,64,2048]{2,1,0:T(8,128)(2,1)S(1)}, u32[]{:S(2)}, u32[]{:S(2)}) collective-permute-start(bf16[1,64,2048]{2,1,0:T(8,128)(2,1)S(1)} %bitcast.157), channel_id=1, source_target_pairs={{0,16},{8,24},{16,0},{24,8},{1,17},{9,25},{17,1},{25,9},{2,18},{10... | collective-permute-start | bytes 786440 | tf_op jit(solution)/shard_map/ppermute | solution.py:96
  62.8 25.0 %collective-permute-start.13 = (bf16[64,2048]{1,0:T(8,128)(2,1)S(1)}, bf16[64,2048]{1,0:T(8,128)(2,1)S(1)}, u32[]{:S(2)}, u32[]{:S(2)}) collective-permute-start(bf16[64,2048]{1,0:T(8,128)(2,1)S(1)} %copy-done.67), channel_id=1, source_target_pairs={{0,16},{8,24},{16,0},{24,8},{1,17},{9,25},{17,1},{25,9},{2,18},{10... | collective-permute-start | bytes 786440 | tf_op jit(solution)/shard_map/ppermute | solution.py:96
  89.8 54.2 %all-to-all-start.1 = ((bf16[32,64,512]{2,1,0:T(8,128)(2,1)}), bf16[32,64,512]{2,1,0:T(8,128)(2,1)S(1)}, u32[]{:S(2)}, u32[]{:S(2)}) async-start(bf16[32,64,512]{2,1,0:T(8,128)(2,1)} %columns_by_device.1), calls=%async_computation.1 | async-start | bytes 4194304 | tf_op jit(solution)/shard_map/all_to_all | solution.py:671
  95.6 143.7 %all-gather.3.cloned.1.call-start = ((), (), s32[]{:S(2)}) async-start(), calls=%async_computation.5 | async-start | bytes 4718592 | tf_op jit(solution)/shard_map/all_gather | solution.py:689
  96.4 183.3 %all-gather.5.cloned.1.call-start = ((), (), s32[]{:S(2)}) async-start(), calls=%async_computation.6 | async-start | bytes 4718592 | tf_op jit(solution)/shard_map/all_gather | solution.py:689
  98.8 42.8 %collective-permute-start.14 = (bf16[2,64,2048]{2,1,0:T(8,128)(2,1)}, bf16[2,64,2048]{2,1,0:T(8,128)(2,1)}, u32[]{:S(2)}, u32[]{:S(2)}) collective-permute-start(bf16[2,64,2048]{2,1,0:T(8,128)(2,1)} %pad_maximum_fusion.9), channel_id=1, source_target_pairs={{0,8},{8,0},{16,24},{24,16},{1,9},{9,1},{17,25},{25,17},{2,10},{10... | collective-permute-start | bytes 1572872 | tf_op jit(solution)/shard_map/ppermute | solution.py:96
  149.1 15.8 %collective-permute-start.20 = (bf16[64,2048]{1,0:T(8,128)(2,1)S(1)}, bf16[64,2048]{1,0:T(8,128)(2,1)S(1)}, u32[]{:S(2)}, u32[]{:S(2)}) collective-permute-start(bf16[64,2048]{1,0:T(8,128)(2,1)S(1)} %copy-done.64), channel_id=1, source_target_pairs={{0,16},{8,24},{16,0},{24,8},{1,17},{9,25},{17,1},{25,9},{2,18},{10... | collective-permute-start | bytes 786440 | tf_op jit(solution)/shard_map/ppermute | solution.py:96
  153.3 18.8 %collective-permute-start.21 = (bf16[512,512]{1,0:T(8,128)(2,1)S(1)}, bf16[512,512]{1,0:T(8,128)(2,1)S(1)}, u32[]{:S(2)}, u32[]{:S(2)}) collective-permute-start(bf16[512,512]{1,0:T(8,128)(2,1)S(1)} %slice.286), channel_id=1, source_target_pairs={{0,8},{8,0},{16,24},{24,16},{1,9},{9,1},{17,25},{25,17},{2,10},{10... | collective-permute-start | bytes 1572872 | tf_op jit(solution)/shard_map/ppermute | solution.py:96
  154.4 16.2 %collective-permute-start.16 = (bf16[64,2048]{1,0:T(8,128)(2,1)S(1)}, bf16[64,2048]{1,0:T(8,128)(2,1)S(1)}, u32[]{:S(2)}, u32[]{:S(2)}) collective-permute-start(bf16[64,2048]{1,0:T(8,128)(2,1)S(1)} %get-tuple-element.452), channel_id=1, source_target_pairs={{0,2},{1,3},{2,0},{3,1},{4,6},{5,7},{6,4},{7,5},{8,10},{9,11},{10,... | collective-permute-start | bytes 786440 | tf_op jit(solution)/shard_map/ppermute | solution.py:96
  155.6 15.1 %collective-permute-start.17 = (bf16[64,2048]{1,0:T(8,128)(2,1)S(1)}, bf16[64,2048]{1,0:T(8,128)(2,1)S(1)}, u32[]{:S(2)}, u32[]{:S(2)}) collective-permute-start(bf16[64,2048]{1,0:T(8,128)(2,1)S(1)} %get-tuple-element.451), channel_id=1, source_target_pairs={{0,4},{1,5},{2,6},{3,7},{4,0},{5,1},{6,2},{7,3},{8,12},{9,13},{10,... | collective-permute-start | bytes 786440 | tf_op jit(solution)/shard_map/ppermute | solution.py:96
  157.0 13.7 %collective-permute-start.18 = (bf16[64,2048]{1,0:T(8,128)(2,1)S(1)}, bf16[64,2048]{1,0:T(8,128)(2,1)S(1)}, u32[]{:S(2)}, u32[]{:S(2)}) collective-permute-start(bf16[64,2048]{1,0:T(8,128)(2,1)S(1)} %get-tuple-element.450), channel_id=1, source_target_pairs={{0,2},{1,3},{2,0},{3,1},{4,6},{5,7},{6,4},{7,5},{8,10},{9,11},{10,... | collective-permute-start | bytes 786440 | tf_op jit(solution)/shard_map/ppermute | solution.py:96
  170.6 12.9 %collective-permute-start.24 = (bf16[512,512]{1,0:T(8,128)(2,1)}, bf16[512,512]{1,0:T(8,128)(2,1)}, u32[]{:S(2)}, u32[]{:S(2)}) collective-permute-start(bf16[512,512]{1,0:T(8,128)(2,1)} %slice.287), channel_id=1, source_target_pairs={{0,8},{8,0},{16,24},{24,16},{1,9},{9,1},{17,25},{25,17},{2,10},{10... | collective-permute-start | bytes 1572872 | tf_op jit(solution)/shard_map/ppermute | solution.py:96
  173.0 10.6 %collective-permute-start.22 = (bf16[64,2048]{1,0:T(8,128)(2,1)}, bf16[64,2048]{1,0:T(8,128)(2,1)S(1)}, u32[]{:S(2)}, u32[]{:S(2)}) collective-permute-start(bf16[64,2048]{1,0:T(8,128)(2,1)} %add_convert_fusion.18), channel_id=1, source_target_pairs={{0,2},{1,3},{2,0},{3,1},{4,6},{5,7},{6,4},{7,5},{8,10},{9,11},{10,... | collective-permute-start | bytes 786440 | tf_op jit(solution)/shard_map/ppermute | solution.py:96
  174.8 9.4 %collective-permute-start.23 = (bf16[64,2048]{1,0:T(8,128)(2,1)}, bf16[64,2048]{1,0:T(8,128)(2,1)}, u32[]{:S(2)}, u32[]{:S(2)}) collective-permute-start(bf16[64,2048]{1,0:T(8,128)(2,1)} %add_convert_fusion.17), channel_id=1, source_target_pairs={{0,4},{1,5},{2,6},{3,7},{4,0},{5,1},{6,2},{7,3},{8,12},{9,13},{10,... | collective-permute-start | bytes 786440 | tf_op jit(solution)/shard_map/ppermute | solution.py:96
  177.2 28.8 %collective-permute-start.28 = (bf16[512,512]{1,0:T(8,128)(2,1)}, bf16[512,512]{1,0:T(8,128)(2,1)}, u32[]{:S(2)}, u32[]{:S(2)}) collective-permute-start(bf16[512,512]{1,0:T(8,128)(2,1)} %slice.290), channel_id=1, source_target_pairs={{0,8},{8,0},{16,24},{24,16},{1,9},{9,1},{17,25},{25,17},{2,10},{10... | collective-permute-start | bytes 1572872 | tf_op jit(solution)/shard_map/ppermute | solution.py:96
  178.0 39.2 %collective-permute-start.29 = (bf16[512,512]{1,0:T(8,128)(2,1)}, bf16[512,512]{1,0:T(8,128)(2,1)S(1)}, u32[]{:S(2)}, u32[]{:S(2)}) collective-permute-start(bf16[512,512]{1,0:T(8,128)(2,1)} %slice.291), channel_id=1, source_target_pairs={{0,8},{8,0},{16,24},{24,16},{1,9},{9,1},{17,25},{25,17},{2,10},{10... | collective-permute-start | bytes 1572872 | tf_op jit(solution)/shard_map/ppermute | solution.py:96
  180.3 321.7 %reduce-scatter.2.cloned.1.call-start = ((), (), s32[]{:S(2)}) async-start(), calls=%async_computation.7 | async-start | bytes 9437184 | tf_op jit(solution)/shard_map/reduce_scatter | solution.py:793
  186.9 30.3 %collective-permute-start.25 = (bf16[128,2048]{1,0:T(8,128)(2,1)S(1)}, bf16[128,2048]{1,0:T(8,128)(2,1)S(1)}, u32[]{:S(2)}, u32[]{:S(2)}) collective-permute-start(bf16[128,2048]{1,0:T(8,128)(2,1)S(1)} %get-tuple-element.428), channel_id=1, source_target_pairs={{0,2},{1,3},{2,0},{3,1},{4,6},{5,7},{6,4},{7,5},{8,10},{9,11},{10,... | collective-permute-start | bytes 1572872 | tf_op jit(solution)/shard_map/ppermute | solution.py:96
  188.0 29.2 %collective-permute-start.26 = (bf16[128,2048]{1,0:T(8,128)(2,1)S(1)}, bf16[128,2048]{1,0:T(8,128)(2,1)S(1)}, u32[]{:S(2)}, u32[]{:S(2)}) collective-permute-start(bf16[128,2048]{1,0:T(8,128)(2,1)S(1)} %get-tuple-element.428), channel_id=1, source_target_pairs={{0,4},{1,5},{2,6},{3,7},{4,0},{5,1},{6,2},{7,3},{8,12},{9,13},{10,... | collective-permute-start | bytes 1572872 | tf_op jit(solution)/shard_map/ppermute | solution.py:96
  189.2 28.0 %collective-permute-start.27 = (bf16[128,2048]{1,0:T(8,128)(2,1)S(1)}, bf16[128,2048]{1,0:T(8,128)(2,1)}, u32[]{:S(2)}, u32[]{:S(2)}) collective-permute-start(bf16[128,2048]{1,0:T(8,128)(2,1)S(1)} %get-tuple-element.428), channel_id=1, source_target_pairs={{0,16},{8,24},{16,0},{24,8},{1,17},{9,25},{17,1},{25,9},{2,18},{10... | collective-permute-start | bytes 1572872 | tf_op jit(solution)/shard_map/ppermute | solution.py:96
  225.9 18.5 %collective-permute-start.34 = (bf16[512,2048]{1,0:T(8,128)(2,1)}, bf16[512,2048]{1,0:T(8,128)(2,1)}, u32[]{:S(2)}, u32[]{:S(2)}) collective-permute-start(bf16[512,2048]{1,0:T(8,128)(2,1)} %constant_dynamic-update-slice_fusion.5.refs_0_), channel_id=1, source_target_pairs={{0,1},{1,0},{2,3},{3,2},{4,5},{5,4},{6,7},{7,6},{8,9},{9,8},{10,11... | collective-permute-start | bytes 6291464 | tf_op jit(solution)/shard_map/ppermute | solution.py:96
  230.4 13.9 %collective-permute-start.35 = (bf16[128,2048]{1,0:T(8,128)(2,1)}, bf16[128,2048]{1,0:T(8,128)(2,1)}, u32[]{:S(2)}, u32[]{:S(2)}) collective-permute-start(bf16[128,2048]{1,0:T(8,128)(2,1)} %get-tuple-element.277), channel_id=1, source_target_pairs={{0,8},{8,0},{16,24},{24,16},{1,9},{9,1},{17,25},{25,17},{2,10},{10... | collective-permute-start | bytes 1572872 | tf_op jit(solution)/shard_map/ppermute | solution.py:96
  233.2 33.0 %collective-permute-start.30 = (bf16[128,2048]{1,0:T(8,128)(2,1)}, bf16[128,2048]{1,0:T(8,128)(2,1)S(1)}, u32[]{:S(2)}, u32[]{:S(2)}) collective-permute-start(bf16[128,2048]{1,0:T(8,128)(2,1)} %collective-permute-done.27), channel_id=1, source_target_pairs={{0,2},{1,3},{2,0},{3,1},{4,6},{5,7},{6,4},{7,5},{8,10},{9,11},{10,... | collective-permute-start | bytes 1572872 | tf_op jit(solution)/shard_map/ppermute | solution.py:96
  233.6 32.6 %collective-permute-start.31 = (bf16[128,2048]{1,0:T(8,128)(2,1)}, bf16[128,2048]{1,0:T(8,128)(2,1)S(1)}, u32[]{:S(2)}, u32[]{:S(2)}) collective-permute-start(bf16[128,2048]{1,0:T(8,128)(2,1)} %collective-permute-done.27), channel_id=1, source_target_pairs={{0,4},{1,5},{2,6},{3,7},{4,0},{5,1},{6,2},{7,3},{8,12},{9,13},{10,... | collective-permute-start | bytes 1572872 | tf_op jit(solution)/shard_map/ppermute | solution.py:96
  280.4 22.8 %collective-permute-start.40 = (bf16[64,2048]{1,0:T(8,128)(2,1)S(1)}, bf16[64,2048]{1,0:T(8,128)(2,1)S(1)}, u32[]{:S(2)}, u32[]{:S(2)}) collective-permute-start(bf16[64,2048]{1,0:T(8,128)(2,1)S(1)} %get-tuple-element.446), channel_id=1, source_target_pairs={{0,2},{1,3},{2,0},{3,1},{4,6},{5,7},{6,4},{7,5},{8,10},{9,11},{10,... | collective-permute-start | bytes 786440 | tf_op jit(solution)/shard_map/ppermute | solution.py:96
  281.5 21.8 %collective-permute-start.41 = (bf16[64,2048]{1,0:T(8,128)(2,1)S(1)}, bf16[64,2048]{1,0:T(8,128)(2,1)S(1)}, u32[]{:S(2)}, u32[]{:S(2)}) collective-permute-start(bf16[64,2048]{1,0:T(8,128)(2,1)S(1)} %get-tuple-element.445), channel_id=1, source_target_pairs={{0,4},{1,5},{2,6},{3,7},{4,0},{5,1},{6,2},{7,3},{8,12},{9,13},{10,... | collective-permute-start | bytes 786440 | tf_op jit(solution)/shard_map/ppermute | solution.py:96
  282.7 20.6 %collective-permute-start.42 = (bf16[64,2048]{1,0:T(8,128)(2,1)S(1)}, bf16[64,2048]{1,0:T(8,128)(2,1)S(1)}, u32[]{:S(2)}, u32[]{:S(2)}) collective-permute-start(bf16[64,2048]{1,0:T(8,128)(2,1)S(1)} %get-tuple-element.444), channel_id=1, source_target_pairs={{0,2},{1,3},{2,0},{3,1},{4,6},{5,7},{6,4},{7,5},{8,10},{9,11},{10,... | collective-permute-start | bytes 786440 | tf_op jit(solution)/shard_map/ppermute | solution.py:96
  283.0 20.3 %collective-permute-start.43 = (bf16[64,2048]{1,0:T(8,128)(2,1)S(1)}, bf16[64,2048]{1,0:T(8,128)(2,1)S(1)}, u32[]{:S(2)}, u32[]{:S(2)}) collective-permute-start(bf16[64,2048]{1,0:T(8,128)(2,1)S(1)} %get-tuple-element.443), channel_id=1, source_target_pairs={{0,4},{1,5},{2,6},{3,7},{4,0},{5,1},{6,2},{7,3},{8,12},{9,13},{10,... | collective-permute-start | bytes 786440 | tf_op jit(solution)/shard_map/ppermute | solution.py:96
  304.2 14.2 %collective-permute-start.44 = (bf16[512,2048]{1,0:T(8,128)(2,1)}, bf16[512,2048]{1,0:T(8,128)(2,1)S(1)}, u32[]{:S(2)}, u32[]{:S(2)}) collective-permute-start(bf16[512,2048]{1,0:T(8,128)(2,1)} %get-tuple-element.316), channel_id=1, source_target_pairs={{0,1},{1,0},{2,3},{3,2},{4,5},{5,4},{6,7},{7,6},{8,9},{9,8},{10,11... | collective-permute-start | bytes 6291464 | tf_op jit(solution)/shard_map/ppermute | solution.py:96
  307.5 11.7 %collective-permute-start.45 = (bf16[64,2048]{1,0:T(8,128)(2,1)S(1)}, bf16[64,2048]{1,0:T(8,128)(2,1)S(1)}, u32[]{:S(2)}, u32[]{:S(2)}) collective-permute-start(bf16[64,2048]{1,0:T(8,128)(2,1)S(1)} %add_convert_fusion.16), channel_id=1, source_target_pairs={{0,2},{1,3},{2,0},{3,1},{4,6},{5,7},{6,4},{7,5},{8,10},{9,11},{10,... | collective-permute-start | bytes 786440 | tf_op jit(solution)/shard_map/ppermute | solution.py:96
  321.3 12.1 %collective-permute-start.49 = (bf16[64,2048]{1,0:T(8,128)(2,1)S(1)}, bf16[64,2048]{1,0:T(8,128)(2,1)S(1)}, u32[]{:S(2)}, u32[]{:S(2)}) collective-permute-start(bf16[64,2048]{1,0:T(8,128)(2,1)S(1)} %get-tuple-element.438), channel_id=1, source_target_pairs={{0,2},{1,3},{2,0},{3,1},{4,6},{5,7},{6,4},{7,5},{8,10},{9,11},{10,... | collective-permute-start | bytes 786440 | tf_op jit(solution)/shard_map/ppermute | solution.py:96
  322.4 11.0 %collective-permute-start.50 = (bf16[64,2048]{1,0:T(8,128)(2,1)S(1)}, bf16[64,2048]{1,0:T(8,128)(2,1)S(1)}, u32[]{:S(2)}, u32[]{:S(2)}) collective-permute-start(bf16[64,2048]{1,0:T(8,128)(2,1)S(1)} %get-tuple-element.437), channel_id=1, source_target_pairs={{0,4},{1,5},{2,6},{3,7},{4,0},{5,1},{6,2},{7,3},{8,12},{9,13},{10,... | collective-permute-start | bytes 786440 | tf_op jit(solution)/shard_map/ppermute | solution.py:96
  323.5 59.8 %collective-permute-start.58 = (bf16[2048,256]{1,0:T(8,128)(2,1)}, bf16[2048,256]{1,0:T(8,128)(2,1)}, u32[]{:S(2)}, u32[]{:S(2)}) collective-permute-start(bf16[2048,256]{1,0:T(8,128)(2,1)} %convolution_convert_fusion.9), channel_id=1, source_target_pairs={{0,8},{8,0},{16,24},{24,16},{1,9},{9,1},{17,25},{25,17},{2,10},{10... | collective-permute-start | bytes 3145736 | tf_op jit(solution)/shard_map/ppermute | solution.py:96
  341.8 24.0 %collective-permute-start.53 = (bf16[128,2048]{1,0:T(8,128)(2,1)}, bf16[128,2048]{1,0:T(8,128)(2,1)}, u32[]{:S(2)}, u32[]{:S(2)}) collective-permute-start(bf16[128,2048]{1,0:T(8,128)(2,1)} %pad_maximum_fusion.11), channel_id=1, source_target_pairs={{0,16},{8,24},{16,0},{24,8},{1,17},{9,25},{17,1},{25,9},{2,18},{10... | collective-permute-start | bytes 1572872 | tf_op jit(solution)/shard_map/ppermute | solution.py:96
  369.8 10.7 %collective-permute-start.54 = (bf16[128,2048]{1,0:T(8,128)(2,1)S(1)}, bf16[128,2048]{1,0:T(8,128)(2,1)S(1)}, u32[]{:S(2)}, u32[]{:S(2)}) collective-permute-start(bf16[128,2048]{1,0:T(8,128)(2,1)S(1)} %get-tuple-element.364), channel_id=1, source_target_pairs={{0,2},{1,3},{2,0},{3,1},{4,6},{5,7},{6,4},{7,5},{8,10},{9,11},{10,... | collective-permute-start | bytes 1572872 | tf_op jit(solution)/shard_map/ppermute | solution.py:96
  370.3 10.7 %collective-permute-start.55 = (bf16[128,2048]{1,0:T(8,128)(2,1)S(1)}, bf16[128,2048]{1,0:T(8,128)(2,1)S(1)}, u32[]{:S(2)}, u32[]{:S(2)}) collective-permute-start(bf16[128,2048]{1,0:T(8,128)(2,1)S(1)} %get-tuple-element.364), channel_id=1, source_target_pairs={{0,4},{1,5},{2,6},{3,7},{4,0},{5,1},{6,2},{7,3},{8,12},{9,13},{10,... | collective-permute-start | bytes 1572872 | tf_op jit(solution)/shard_map/ppermute | solution.py:96
  371.8 21.8 %collective-permute-start.59 = (bf16[2048,256]{1,0:T(8,128)(2,1)S(1)}, bf16[2048,256]{1,0:T(8,128)(2,1)}, u32[]{:S(2)}, u32[]{:S(2)}) collective-permute-start(bf16[2048,256]{1,0:T(8,128)(2,1)S(1)} %copy-done.71), channel_id=1, source_target_pairs={{0,8},{8,0},{16,24},{24,16},{1,9},{9,1},{17,25},{25,17},{2,10},{10... | collective-permute-start | bytes 3145736 | tf_op jit(solution)/shard_map/ppermute | solution.py:96
  393.9 9.9 %collective-permute-start.60 = (bf16[256,2048]{1,0:T(8,128)(2,1)S(1)}, bf16[256,2048]{1,0:T(8,128)(2,1)S(1)}, u32[]{:S(2)}, u32[]{:S(2)}) collective-permute-start(bf16[256,2048]{1,0:T(8,128)(2,1)S(1)} %pad_maximum_fusion.3), channel_id=1, source_target_pairs={{0,1},{1,0},{2,3},{3,2},{4,5},{5,4},{6,7},{7,6},{8,9},{9,8},{10,11... | collective-permute-start | bytes 3145736 | tf_op jit(solution)/shard_map/ppermute | solution.py:96
  408.8 25.0 %collective-permute-start.62 = (bf16[2,64,2048]{2,1,0:T(8,128)(2,1)}, bf16[2,64,2048]{2,1,0:T(8,128)(2,1)S(1)}, u32[]{:S(2)}, u32[]{:S(2)}) collective-permute-start(bf16[2,64,2048]{2,1,0:T(8,128)(2,1)} %dynamic-slice_bitcast_fusion.1), channel_id=1, source_target_pairs={{0,8},{8,0},{16,24},{24,16},{1,9},{9,1},{17,25},{25,17},{2,10},{10... | collective-permute-start | bytes 1572872 | tf_op jit(solution)/shard_map/ppermute | solution.py:96
  410.3 70.9 %all-to-all-start.2 = ((bf16[32,64,512]{2,1,0:T(8,128)(2,1)}), bf16[32,64,512]{2,1,0:T(8,128)(2,1)}, u32[]{:S(2)}, u32[]{:S(2)}) async-start(bf16[32,64,512]{2,1,0:T(8,128)(2,1)} %pad_maximum_fusion.1), calls=%async_computation.2 | async-start | bytes 4194304 | tf_op jit(solution)/shard_map/all_to_all | solution.py:671
  440.2 38.2 %collective-permute-start.63 = (bf16[2,512,384]{2,1,0:T(8,128)(2,1)S(1)}, bf16[2,512,384]{2,1,0:T(8,128)(2,1)S(1)}, u32[]{:S(2)}, u32[]{:S(2)}) collective-permute-start(bf16[2,512,384]{2,1,0:T(8,128)(2,1)S(1)} %dynamic-slice_bitcast_fusion), channel_id=1, source_target_pairs={{0,8},{8,0},{16,24},{24,16},{1,9},{9,1},{17,25},{25,17},{2,10},{10... | collective-permute-start | bytes 2359304 | tf_op jit(solution)/shard_map/ppermute | solution.py:96
  443.0 35.5 %collective-permute-start.65 = (bf16[256,2048]{1,0:T(8,128)(2,1)S(1)}, bf16[256,2048]{1,0:T(8,128)(2,1)S(1)}, u32[]{:S(2)}, u32[]{:S(2)}) collective-permute-start(bf16[256,2048]{1,0:T(8,128)(2,1)S(1)} %get-tuple-element.436), channel_id=1, source_target_pairs={{0,1},{1,0},{2,3},{3,2},{4,5},{5,4},{6,7},{7,6},{8,9},{9,8},{10,11... | collective-permute-start | bytes 3145736 | tf_op jit(solution)/shard_map/ppermute | solution.py:96
  443.8 34.7 %collective-permute-start.64 = (bf16[256,2048]{1,0:T(8,128)(2,1)S(1)}, bf16[256,2048]{1,0:T(8,128)(2,1)S(1)}, u32[]{:S(2)}, u32[]{:S(2)}) collective-permute-start(bf16[256,2048]{1,0:T(8,128)(2,1)S(1)} %get-tuple-element.435), channel_id=1, source_target_pairs={{0,1},{1,0},{2,3},{3,2},{4,5},{5,4},{6,7},{7,6},{8,9},{9,8},{10,11... | collective-permute-start | bytes 3145736 | tf_op jit(solution)/shard_map/ppermute | solution.py:96
  443.9 31.9 %collective-permute-start.66 = (bf16[1,64,2048]{2,1,0:T(8,128)(2,1)S(1)}, bf16[1,64,2048]{2,1,0:T(8,128)(2,1)S(1)}, u32[]{:S(2)}, u32[]{:S(2)}) collective-permute-start(bf16[1,64,2048]{2,1,0:T(8,128)(2,1)S(1)} %constant_dynamic-slice_fusion.1), channel_id=1, source_target_pairs={{0,16},{8,24},{16,0},{24,8},{1,17},{9,25},{17,1},{25,9},{2,18},{10... | collective-permute-start | bytes 786440 | tf_op jit(solution)/shard_map/ppermute | solution.py:96
  481.2 19.9 %collective-permute-start.71 = (bf16[1,512,384]{2,1,0:T(8,128)(2,1)S(1)}, bf16[1,512,384]{2,1,0:T(8,128)(2,1)S(1)}, u32[]{:S(2)}, u32[]{:S(2)}) collective-permute-start(bf16[1,512,384]{2,1,0:T(8,128)(2,1)S(1)} %constant_dynamic-slice_fusion), channel_id=1, source_target_pairs={{0,16},{8,24},{16,0},{24,8},{1,17},{9,25},{17,1},{25,9},{2,18},{10... | collective-permute-start | bytes 1179656 | tf_op jit(solution)/shard_map/ppermute | solution.py:96
  485.1 18.8 %collective-permute-start.67 = (bf16[64,2048]{1,0:T(8,128)(2,1)}, bf16[64,2048]{1,0:T(8,128)(2,1)S(1)}, u32[]{:S(2)}, u32[]{:S(2)}) collective-permute-start(bf16[64,2048]{1,0:T(8,128)(2,1)} %get-tuple-element.432), channel_id=1, source_target_pairs={{0,2},{1,3},{2,0},{3,1},{4,6},{5,7},{6,4},{7,5},{8,10},{9,11},{10,... | collective-permute-start | bytes 786440 | tf_op jit(solution)/shard_map/ppermute | solution.py:96
  485.4 20.0 %collective-permute-start.68 = (bf16[64,2048]{1,0:T(8,128)(2,1)}, bf16[64,2048]{1,0:T(8,128)(2,1)S(1)}, u32[]{:S(2)}, u32[]{:S(2)}) collective-permute-start(bf16[64,2048]{1,0:T(8,128)(2,1)} %get-tuple-element.431), channel_id=1, source_target_pairs={{0,4},{1,5},{2,6},{3,7},{4,0},{5,1},{6,2},{7,3},{8,12},{9,13},{10,... | collective-permute-start | bytes 786440 | tf_op jit(solution)/shard_map/ppermute | solution.py:96
  485.7 19.6 %collective-permute-start.69 = (bf16[64,2048]{1,0:T(8,128)(2,1)}, bf16[64,2048]{1,0:T(8,128)(2,1)}, u32[]{:S(2)}, u32[]{:S(2)}) collective-permute-start(bf16[64,2048]{1,0:T(8,128)(2,1)} %get-tuple-element.430), channel_id=1, source_target_pairs={{0,2},{1,3},{2,0},{3,1},{4,6},{5,7},{6,4},{7,5},{8,10},{9,11},{10,... | collective-permute-start | bytes 786440 | tf_op jit(solution)/shard_map/ppermute | solution.py:96
  486.9 18.5 %collective-permute-start.70 = (bf16[64,2048]{1,0:T(8,128)(2,1)}, bf16[64,2048]{1,0:T(8,128)(2,1)}, u32[]{:S(2)}, u32[]{:S(2)}) collective-permute-start(bf16[64,2048]{1,0:T(8,128)(2,1)} %get-tuple-element.429), channel_id=1, source_target_pairs={{0,4},{1,5},{2,6},{3,7},{4,0},{5,1},{6,2},{7,3},{8,12},{9,13},{10,... | collective-permute-start | bytes 786440 | tf_op jit(solution)/shard_map/ppermute | solution.py:96
  501.1 19.1 %collective-permute-start.76 = (bf16[128,2048]{1,0:T(8,128)(2,1)}, bf16[128,2048]{1,0:T(8,128)(2,1)}, u32[]{:S(2)}, u32[]{:S(2)}) collective-permute-start(bf16[128,2048]{1,0:T(8,128)(2,1)} %get-tuple-element.405), channel_id=1, source_target_pairs={{0,8},{8,0},{16,24},{24,16},{1,9},{9,1},{17,25},{25,17},{2,10},{10... | collective-permute-start | bytes 1572872 | tf_op jit(solution)/shard_map/ppermute | solution.py:96
  503.9 27.7 %collective-permute-start.77 = (bf16[128,2048]{1,0:T(8,128)(2,1)}, bf16[128,2048]{1,0:T(8,128)(2,1)}, u32[]{:S(2)}, u32[]{:S(2)}) collective-permute-start(bf16[128,2048]{1,0:T(8,128)(2,1)} %get-tuple-element.406), channel_id=1, source_target_pairs={{0,8},{8,0},{16,24},{24,16},{1,9},{9,1},{17,25},{25,17},{2,10},{10... | collective-permute-start | bytes 1572872 | tf_op jit(solution)/shard_map/ppermute | solution.py:96
  507.2 24.4 %collective-permute-start.74 = (bf16[64,2048]{1,0:T(8,128)(2,1)}, bf16[64,2048]{1,0:T(8,128)(2,1)S(1)}, u32[]{:S(2)}, u32[]{:S(2)}) collective-permute-start(bf16[64,2048]{1,0:T(8,128)(2,1)} %add_convert_fusion.9), channel_id=1, source_target_pairs={{0,2},{1,3},{2,0},{3,1},{4,6},{5,7},{6,4},{7,5},{8,10},{9,11},{10,... | collective-permute-start | bytes 786440 | tf_op jit(solution)/shard_map/ppermute | solution.py:96
  508.9 22.7 %collective-permute-start.75 = (bf16[64,2048]{1,0:T(8,128)(2,1)}, bf16[64,2048]{1,0:T(8,128)(2,1)}, u32[]{:S(2)}, u32[]{:S(2)}) collective-permute-start(bf16[64,2048]{1,0:T(8,128)(2,1)} %add_convert_fusion.8), channel_id=1, source_target_pairs={{0,4},{1,5},{2,6},{3,7},{4,0},{5,1},{6,2},{7,3},{8,12},{9,13},{10,... | collective-permute-start | bytes 786440 | tf_op jit(solution)/shard_map/ppermute | solution.py:96
  508.9 45.5 %all-to-all-start.3 = ((bf16[8,64,384]{2,1,0:T(8,128)(2,1)}), bf16[8,64,384]{2,1,0:T(8,128)(2,1)S(1)}, u32[]{:S(2)}, u32[]{:S(2)}) async-start(bf16[8,64,384]{2,1,0:T(8,128)(2,1)} %bitcast.37), calls=%async_computation.4 | async-start | bytes 786432 | tf_op jit(solution)/shard_map/all_to_all | solution.py:195
  515.2 39.2 %collective-permute-start.72 = (bf16[128,2048]{1,0:T(8,128)(2,1)}, bf16[128,2048]{1,0:T(8,128)(2,1)}, u32[]{:S(2)}, u32[]{:S(2)}) collective-permute-start(bf16[128,2048]{1,0:T(8,128)(2,1)} %slice.354), channel_id=1, source_target_pairs={{0,16},{8,24},{16,0},{24,8},{1,17},{9,25},{17,1},{25,9},{2,18},{10... | collective-permute-start | bytes 1572872 | tf_op jit(solution)/shard_map/ppermute | solution.py:96
  520.2 34.2 %collective-permute-start.73 = (bf16[64,2048]{1,0:T(8,128)(2,1)}, bf16[64,2048]{1,0:T(8,128)(2,1)}, u32[]{:S(2)}, u32[]{:S(2)}) collective-permute-start(bf16[64,2048]{1,0:T(8,128)(2,1)} %fusion.31), channel_id=1, source_target_pairs={{0,0},{8,1},{16,2},{24,3},{1,4},{9,5},{17,6},{25,7},{2,8},{10,9},{... | collective-permute-start | bytes 786440 | tf_op jit(solution)/shard_map/ppermute | solution.py:842
  (105 other events, 919.6 us)
Sparse Core Ops, SparseCore 0:
  98.3 47.8 all-gather.2
  180.4 41.4 all-gather.4
  393.8 89.7 reduce-scatter.1

commit v6 on v5

--- a/solution.py
+++ b/solution.py
@@ -30,9 +30,9 @@
     "move_2": (6, 8),
     "move_3": (6, 8),
     "side_cots": (6, 11),
-    "gate_away": (12, 13),
-    "gate_move": (13, 18),
-    "up_away": (13, 14),
+    "gate_away": (13, 14),
+    "gate_move": (14, 18),
+    "up_away": (14, 15),
     "down_away": (14, 15),
     "gate_own": (15, 16),
     "down_terms": (15, 16),

time: 577 us -> 575 us (level)
  the two profiles are of different devices: /device:TPU:1 before, /device:TPU:2 now
where the time goes in v6:
time: 575 us; the launch traced here: 567 us
  waiting for transfers between devices  190 us (33%)
  starting transfers between devices  112 us (19%)
  Pallas kernels  97.3 us (17%)
  other arithmetic  60.8 us (11%)
  matrix products  49 us (9%)
  local copies, waits for them, and re-layouts  41.9 us (7%)
  between operations  15.4 us (3%)
    ppermute x76, waiting for transfers between devices, swap(): return lax.ppermute(block, axis, [(i, i ^ mask) for i in range(count)])  174 us
    ppermute x76, starting transfers between devices, swap(): return lax.ppermute(block, axis, [(i, i ^ mask) for i in range(count)])  84.5 us
    dot_general x17, matrix products, dot(): lax.dot_general(left, right, (dims, ((), ())), preferred_element_type=WIDE)  49 us
    pallas_call x2, Pallas kernels, feed_forward(): pl.pallas_call(functools.partial(feed_kernel, blocks, steps, per_step), g...  39.7 us
    unnamed x179, local copies, waits for them, and re-layouts  19.2 us
    pallas_call x1, Pallas kernels, attention_backward(): pl.pallas_call(functools.partial(backward_kernel, heads, steps), grid=(st...  18.2 us
    pallas_call x1, Pallas kernels, attention_forward(): pl.pallas_call(functools.partial(forward_kernel, heads), grid=(length //...  15.9 us
    ppermute x1, waiting for transfers between devices, per_device(): lax.ppermute(p, ('fsdp', 'ctx'), back_route)  15 us
  transfers between devices with their start and end apart: 85, of which 33 were waited for; matrix products, arithmetic and copies ran while one was open for 24% of the time, Pallas kernels for 17%

profile of v6, /device:TPU:2, one launch (start us, length us, event | category | flops | bytes accessed | tf_op | source)
XLA Modules:
  0.0 566.9 jit_solution(6969704076398796155)
XLA Ops:
  7.3 2.0 collective-permute-start.1
  15.1 4.9 all-to-all-start
  19.9 4.0 collective-permute-start.2
  29.1 2.1 collective-permute-done.5
  32.5 6.5 %collective-permute-start.3 = (bf16[1,512,384]{2,1,0:T(8,128)(2,1)S(1)}, bf16[1,512,384]{2,1,0:T(8,128)(2,1)S(1)}, u32[]{:S(2)}, u32[]{:S(2)}) collective-permute-start(bf16[1,512,384]{2,1,0:T(8,128)(2,1)S(1)} %bitcast.148), channel_id=1, source_target_pairs={{0,16},{8,24},{16,0},{24,8},{1,17},{9,25},{17,1},{25,9},{2,18},{10... | collective-permute-start | bytes 1179656 | tf_op jit(solution)/shard_map/ppermute | solution.py:96
  46.6 4.0 columns_by_device.1
  50.6 6.5 %collective-permute-done.3.refs_1_ = bf16[1,512,384]{2,1,0:T(8,128)(2,1)S(1)} collective-permute-done((bf16[1,512,384]{2,1,0:T(8,128)(2,1)S(1)}, bf16[1,512,384]{2,1,0:T(8,128)(2,1)S(1)}, u32[]{:S(2)}, u32[]{:S(2)}) %collective-permute-start.3) | collective-permute-done | bytes 393248 | tf_op jit(solution)/shard_map/ppermute | solution.py:96
  59.2 3.4 collective-permute-start.12
  67.1 15.6 %collective-permute-done.12.refs_1_ = bf16[1,64,2048]{2,1,0:T(8,128)(2,1)S(1)} collective-permute-done((bf16[1,64,2048]{2,1,0:T(8,128)(2,1)S(1)}, bf16[1,64,2048]{2,1,0:T(8,128)(2,1)S(1)}, u32[]{:S(2)}, u32[]{:S(2)}) %collective-permute-start.12) | collective-permute-done | bytes 262176 | tf_op jit(solution)/shard_map/ppermute | solution.py:96
  82.7 4.7 collective-permute-done.13
  88.8 5.8 %all-to-all-start.1 = ((bf16[32,64,512]{2,1,0:T(8,128)(2,1)}), bf16[32,64,512]{2,1,0:T(8,128)(2,1)S(1)}, u32[]{:S(2)}, u32[]{:S(2)}) async-start(bf16[32,64,512]{2,1,0:T(8,128)(2,1)} %columns_by_device.1), calls=%async_computation.1 | async-start | bytes 4194304 | tf_op jit(solution)/shard_map/all_to_all | solution.py:671
  99.3 2.7 place.2
  102.0 2.8 fusion.48
  107.3 15.9 %attention_forward.1 = (bf16[1024,256]{1,0:T(8,128)(2,1)}, f32[8,1024]{1,0:T(8,128)}, bf16[1024,256]{1,0:T(8,128)(2,1)}, bf16[1024,64]{1,0:T(8,128)(2,1)}, bf16[1024,64]{1,0:T(8,128)(2,1)}) custom-call(f32[1024,384]{1,0:T(8,128)} %pad_maximum_fusion.2.q_ref.kv_ref, f32[1024,384]{1,0:T(8,128)} %pad_maximum_fusion.2.q_ref.kv_ref, ...), custom_call_target="tpu_custom_call" | custom-call | bytes 2097152 | tf_op jit(solution)/shard_map/attention_forward/pallas_call | solution.py:355
  123.2 17.8 %collective-permute-done.14.refs_2_ = bf16[2,64,2048]{2,1,0:T(8,128)(2,1)} collective-permute-done((bf16[2,64,2048]{2,1,0:T(8,128)(2,1)}, bf16[2,64,2048]{2,1,0:T(8,128)(2,1)}, u32[]{:S(2)}, u32[]{:S(2)}) %collective-permute-start.14) | collective-permute-done | bytes 524320 | tf_op jit(solution)/shard_map/ppermute | solution.py:96
  141.0 2.3 place.3
  143.4 2.7 convolution_convert_fusion.1
  147.5 3.7 collective-permute-start.20
  156.9 7.0 %collective-permute-done.20 = bf16[64,2048]{1,0:T(8,128)(2,1)S(1)} collective-permute-done((bf16[64,2048]{1,0:T(8,128)(2,1)S(1)}, bf16[64,2048]{1,0:T(8,128)(2,1)S(1)}, u32[]{:S(2)}, u32[]{:S(2)}) %collective-permute-start.20) | collective-permute-done | bytes 262176 | tf_op jit(solution)/shard_map/ppermute | solution.py:96
  165.6 2.6 pad_maximum_fusion
  177.7 2.0 collective-permute-start.29
  180.8 4.3 collective-permute-done.24
  189.7 17.9 %collective-permute-done.28 = bf16[512,512]{1,0:T(8,128)(2,1)} collective-permute-done((bf16[512,512]{1,0:T(8,128)(2,1)}, bf16[512,512]{1,0:T(8,128)(2,1)}, u32[]{:S(2)}, u32[]{:S(2)}) %collective-permute-start.28) | collective-permute-done | bytes 524320 | tf_op jit(solution)/shard_map/ppermute | solution.py:96
  207.6 9.7 %collective-permute-done.29 = bf16[512,512]{1,0:T(8,128)(2,1)S(1)} collective-permute-done((bf16[512,512]{1,0:T(8,128)(2,1)}, bf16[512,512]{1,0:T(8,128)(2,1)S(1)}, u32[]{:S(2)}, u32[]{:S(2)}) %collective-permute-start.29) | collective-permute-done | bytes 524320 | tf_op jit(solution)/shard_map/ppermute | solution.py:96
  220.7 3.7 collective-permute-done.32
  238.5 4.3 collective-permute-done.35
  244.9 19.8 %feed_forward.2 = (bf16[2048,2048]{1,0:T(8,128)(2,1)}, bf16[2048,2048]{1,0:T(8,128)(2,1)}, bf16[2,2048,256]{2,1,0:T(8,128)(2,1)}, bf16[4,2048,256]{2,1,0:T(8,128...) custom-call(s32[8]{0:T(128)} %broadcast_xor_fusion.table_ref, ...), custom_call_target="tpu_custom_call" | custom-call | bytes 8388608 | tf_op jit(solution)/shard_map/feed_forward/pallas_call | solution.py:569
  267.9 4.9 collective-permute-done.36
  275.4 3.0 collective-permute-done.38.refs_1_
  283.3 19.9 %feed_forward.3 = (bf16[2048,2048]{1,0:T(8,128)(2,1)}, bf16[2048,2048]{1,0:T(8,128)(2,1)}, bf16[2,2048,256]{2,1,0:T(8,128)(2,1)}, bf16[4,2048,256]{2,1,0:T(8,128...) custom-call(s32[8]{0:T(128)} %broadcast_xor_fusion.table_ref, ...), custom_call_target="tpu_custom_call", output_to_operand_aliasing={{0}: (9, {}), {1}: (10, {}), {2}: (11, {}), {3}: (12, {})} | custom-call | bytes 8388608 | tf_op jit(solution)/shard_map/feed_forward/pallas_call | solution.py:569
  309.1 2.5 add_convert_fusion.1
  311.7 3.0 collective-permute-done.45
  320.5 4.9 convolution_convert_fusion.9
  327.0 2.6 collective-permute-done.49
  333.4 3.6 convolution_convert_fusion.8
  337.1 3.3 convolution_convert_fusion.7
  341.5 2.2 collective-permute-start.53
  343.7 9.6 %down_terms.1 = bf16[4,2,2,128,2048]{4,3,2,1,0:T(8,128)(2,1)} custom-call(s32[2]{0:T(128)} %pad_add_fusion.3.table_ref, bf16[2,2048,256]{2,1,0:T(8,128)(2,1)} %get-tuple-element.385.act_ref, bf16[256,2048]{1,0:T(8,128)(2,1)} %refs_0_.1, bf16[256,2048]{1,0:T(8,128)(2,1)} %copy-done.7), custom_call_target="tpu_custom_call" | custom-call | bytes 8388608 | tf_op jit(solution)/shard_map/down_terms/pallas_call | solution.py:612
  353.4 6.9 %convolution_convert_fusion.6 = bf16[2048,256]{1,0:T(8,128)(2,1)} fusion(bf16[2048,2048]{1,0:T(8,128)(2,1)} %get-tuple-element.355, bf16[4,2048,256]{2,1,0:T(8,128)(2,1)S(1)} %copy-done.28), kind=kOutput, calls=%fused_computation.21 | convolution fusion | flops 2148007936 | bytes 10485760 | tf_op jit(solution)/shard_map/dot_general | solution.py:59
  360.3 5.0 collective-permute-done.53
  366.7 2.6 fusion.38
  371.2 3.6 collective-permute-start.59
  374.8 7.2 %convolution_convert_fusion.5 = bf16[2048,256]{1,0:T(8,128)(2,1)} fusion(bf16[2048,2048]{1,0:T(8,128)(2,1)} %get-tuple-element.355, bf16[4,2048,256]{2,1,0:T(8,128)(2,1)} %get-tuple-element.356), kind=kOutput, calls=%fused_computation.20 | convolution fusion | flops 2148007936 | bytes 10485760 | tf_op jit(solution)/shard_map/dot_general | solution.py:59
  383.9 4.6 collective-permute-done.56
  389.2 5.2 collective-permute-done.59
  409.6 3.9 all-to-all-start.2
  414.6 18.2 %attention_backward.1 = bf16[1024,384]{1,0:T(8,128)(2,1)} custom-call(bf16[1024,256]{1,0:T(8,128)(2,1)} %get-tuple-element.268.q_ref, bf16[1024,64]{1,0:T(8,128)(2,1)} %get-tuple-element.269.k_ref, bf16[1024,64]{1,0:T(8,128)(2,1)} %get-tuple-element.270.v_ref, bf16[1024,256]{1,0:T(8,128)(2,1)} %pad_maximum_fusion.12.do_ref, ...), custom_call_target="tpu_custom_call" | custom-call | bytes 2097152 | tf_op jit(solution)/shard_map/attention_backward/pallas_call | solution.py:393
  434.0 5.1 convolution_convert_fusion.4
  442.8 2.5 collective-permute-start.66
  445.3 3.7 fusion.10
  449.0 26.6 %collective-permute-done.66 = bf16[1,64,2048]{2,1,0:T(8,128)(2,1)S(1)} collective-permute-done((bf16[1,64,2048]{2,1,0:T(8,128)(2,1)S(1)}, bf16[1,64,2048]{2,1,0:T(8,128)(2,1)S(1)}, u32[]{:S(2)}, u32[]{:S(2)}) %collective-permute-start.66) | collective-permute-done | bytes 262176 | tf_op jit(solution)/shard_map/ppermute | solution.py:96
  476.5 2.6 add_convert_fusion
  479.2 3.4 collective-permute-start.71
  482.6 2.4 fusion.39
  489.1 10.0 %collective-permute-done.71 = bf16[1,512,384]{2,1,0:T(8,128)(2,1)S(1)} collective-permute-done((bf16[1,512,384]{2,1,0:T(8,128)(2,1)S(1)}, bf16[1,512,384]{2,1,0:T(8,128)(2,1)S(1)}, u32[]{:S(2)}, u32[]{:S(2)}) %collective-permute-start.71) | collective-permute-done | bytes 393248 | tf_op jit(solution)/shard_map/ppermute | solution.py:96
  501.8 2.0 collective-permute-start.77
  509.6 4.8 all-to-all-start.3
  514.6 4.9 assemble_columns.1
  519.5 3.5 collective-permute-start.73
  523.1 4.0 collective-permute-done.77
  530.2 2.8 convert_add_fusion
  534.4 2.4 fusion.23
  536.9 15.0 %collective-permute-done.73 = bf16[64,2048]{1,0:T(8,128)(2,1)} collective-permute-done((bf16[64,2048]{1,0:T(8,128)(2,1)}, bf16[64,2048]{1,0:T(8,128)(2,1)}, u32[]{:S(2)}, u32[]{:S(2)}) %collective-permute-start.73) | collective-permute-done | bytes 262176 | tf_op jit(solution)/shard_map/ppermute | solution.py:842
  556.6 2.1 fusion.24
  (438 shorter events, 158.0 us)
Async XLA Ops:
  7.2 25.3 %collective-permute-start = (bf16[128,2048]{1,0:T(8,128)(2,1)}, bf16[128,2048]{1,0:T(8,128)(2,1)S(1)}, u32[]{:S(2)}, u32[]{:S(2)}) collective-permute-start(bf16[128,2048]{1,0:T(8,128)(2,1)} %bitcast.136), channel_id=1, source_target_pairs={{0,2},{1,3},{2,0},{3,1},{4,6},{5,7},{6,4},{7,5},{8,10},{9,11},{10,... | collective-permute-start | bytes 1572872 | tf_op jit(solution)/shard_map/ppermute | solution.py:96
  7.3 25.2 %collective-permute-start.1 = (bf16[128,2048]{1,0:T(8,128)(2,1)}, bf16[128,2048]{1,0:T(8,128)(2,1)S(1)}, u32[]{:S(2)}, u32[]{:S(2)}) collective-permute-start(bf16[128,2048]{1,0:T(8,128)(2,1)} %bitcast.137), channel_id=1, source_target_pairs={{0,4},{1,5},{2,6},{3,7},{4,0},{5,1},{6,2},{7,3},{8,12},{9,13},{10,... | collective-permute-start | bytes 1572872 | tf_op jit(solution)/shard_map/ppermute | solution.py:96
  15.1 17.4 %all-to-all-start = ((bf16[8,64,384]{2,1,0:T(8,128)(2,1)}), bf16[8,64,384]{2,1,0:T(8,128)(2,1)S(1)}, u32[]{:S(2)}, u32[]{:S(2)}) async-start(bf16[8,64,384]{2,1,0:T(8,128)(2,1)} %fusion.25), calls=%async_computation | async-start | bytes 786432 | tf_op jit(solution)/shard_map/all_to_all | solution.py:195
  19.9 12.5 %collective-permute-start.2 = (bf16[64,2048]{1,0:T(8,128)(2,1)S(1)}, bf16[64,2048]{1,0:T(8,128)(2,1)S(1)}, u32[]{:S(2)}, u32[]{:S(2)}) collective-permute-start(bf16[64,2048]{1,0:T(8,128)(2,1)S(1)} %copy-done.72), channel_id=1, source_target_pairs={{0,0},{1,8},{2,16},{3,24},{4,1},{5,9},{6,17},{7,25},{8,2},{9,10},{... | collective-permute-start | bytes 786440 | tf_op jit(solution)/shard_map/ppermute | solution.py:677
  24.1 26.6 %collective-permute-start.9 = (bf16[128,2048]{1,0:T(8,128)(2,1)}, bf16[128,2048]{1,0:T(8,128)(2,1)}, u32[]{:S(2)}, u32[]{:S(2)}) collective-permute-start(bf16[128,2048]{1,0:T(8,128)(2,1)} %get-tuple-element.224), channel_id=1, source_target_pairs={{0,8},{8,0},{16,24},{24,16},{1,9},{9,1},{17,25},{25,17},{2,10},{10... | collective-permute-start | bytes 1572872 | tf_op jit(solution)/shard_map/ppermute | solution.py:96
  32.5 24.6 %collective-permute-start.3 = (bf16[1,512,384]{2,1,0:T(8,128)(2,1)S(1)}, bf16[1,512,384]{2,1,0:T(8,128)(2,1)S(1)}, u32[]{:S(2)}, u32[]{:S(2)}) collective-permute-start(bf16[1,512,384]{2,1,0:T(8,128)(2,1)S(1)} %bitcast.148), channel_id=1, source_target_pairs={{0,16},{8,24},{16,0},{24,8},{1,17},{9,25},{17,1},{25,9},{2,18},{10... | collective-permute-start | bytes 1179656 | tf_op jit(solution)/shard_map/ppermute | solution.py:96
  38.9 11.7 %collective-permute-start.7 = (bf16[64,2048]{1,0:T(8,128)(2,1)S(1)}, bf16[64,2048]{1,0:T(8,128)(2,1)S(1)}, u32[]{:S(2)}, u32[]{:S(2)}) collective-permute-start(bf16[64,2048]{1,0:T(8,128)(2,1)S(1)} %slice.270), channel_id=1, source_target_pairs={{0,2},{1,3},{2,0},{3,1},{4,6},{5,7},{6,4},{7,5},{8,10},{9,11},{10,... | collective-permute-start | bytes 786440 | tf_op jit(solution)/shard_map/ppermute | solution.py:96
  41.3 9.3 %collective-permute-start.8 = (bf16[64,2048]{1,0:T(8,128)(2,1)}, bf16[64,2048]{1,0:T(8,128)(2,1)S(1)}, u32[]{:S(2)}, u32[]{:S(2)}) collective-permute-start(bf16[64,2048]{1,0:T(8,128)(2,1)} %slice.271), channel_id=1, source_target_pairs={{0,4},{1,5},{2,6},{3,7},{4,0},{5,1},{6,2},{7,3},{8,12},{9,13},{10,... | collective-permute-start | bytes 786440 | tf_op jit(solution)/shard_map/ppermute | solution.py:96
  58.0 30.9 %collective-permute-start.10 = (bf16[2,512,384]{2,1,0:T(8,128)(2,1)S(1)}, bf16[2,512,384]{2,1,0:T(8,128)(2,1)}, u32[]{:S(2)}, u32[]{:S(2)}) collective-permute-start(bf16[2,512,384]{2,1,0:T(8,128)(2,1)S(1)} %pad_maximum_fusion.6), channel_id=1, source_target_pairs={{0,8},{8,0},{16,24},{24,16},{1,9},{9,1},{17,25},{25,17},{2,10},{10... | collective-permute-start | bytes 2359304 | tf_op jit(solution)/shard_map/ppermute | solution.py:96
  59.2 23.5 %collective-permute-start.12 = (bf16[1,64,2048]{2,1,0:T(8,128)(2,1)S(1)}, bf16[1,64,2048]{2,1,0:T(8,128)(2,1)S(1)}, u32[]{:S(2)}, u32[]{:S(2)}) collective-permute-start(bf16[1,64,2048]{2,1,0:T(8,128)(2,1)S(1)} %bitcast.155), channel_id=1, source_target_pairs={{0,16},{8,24},{16,0},{24,8},{1,17},{9,25},{17,1},{25,9},{2,18},{10... | collective-permute-start | bytes 786440 | tf_op jit(solution)/shard_map/ppermute | solution.py:96
  62.6 24.8 %collective-permute-start.13 = (bf16[64,2048]{1,0:T(8,128)(2,1)S(1)}, bf16[64,2048]{1,0:T(8,128)(2,1)S(1)}, u32[]{:S(2)}, u32[]{:S(2)}) collective-permute-start(bf16[64,2048]{1,0:T(8,128)(2,1)S(1)} %copy-done.67), channel_id=1, source_target_pairs={{0,16},{8,24},{16,0},{24,8},{1,17},{9,25},{17,1},{25,9},{2,18},{10... | collective-permute-start | bytes 786440 | tf_op jit(solution)/shard_map/ppermute | solution.py:96
  88.8 54.5 %all-to-all-start.1 = ((bf16[32,64,512]{2,1,0:T(8,128)(2,1)}), bf16[32,64,512]{2,1,0:T(8,128)(2,1)S(1)}, u32[]{:S(2)}, u32[]{:S(2)}) async-start(bf16[32,64,512]{2,1,0:T(8,128)(2,1)} %columns_by_device.1), calls=%async_computation.1 | async-start | bytes 4194304 | tf_op jit(solution)/shard_map/all_to_all | solution.py:671
  94.6 143.9 %all-gather.3.cloned.1.call-start = ((), (), s32[]{:S(2)}) async-start(), calls=%async_computation.5 | async-start | bytes 4718592 | tf_op jit(solution)/shard_map/all_gather | solution.py:689
  95.4 183.0 %all-gather.5.cloned.1.call-start = ((), (), s32[]{:S(2)}) async-start(), calls=%async_computation.6 | async-start | bytes 4718592 | tf_op jit(solution)/shard_map/all_gather | solution.py:689
  97.8 43.3 %collective-permute-start.14 = (bf16[2,64,2048]{2,1,0:T(8,128)(2,1)}, bf16[2,64,2048]{2,1,0:T(8,128)(2,1)}, u32[]{:S(2)}, u32[]{:S(2)}) collective-permute-start(bf16[2,64,2048]{2,1,0:T(8,128)(2,1)} %pad_maximum_fusion.9), channel_id=1, source_target_pairs={{0,8},{8,0},{16,24},{24,16},{1,9},{9,1},{17,25},{25,17},{2,10},{10... | collective-permute-start | bytes 1572872 | tf_op jit(solution)/shard_map/ppermute | solution.py:96
  147.5 16.4 %collective-permute-start.20 = (bf16[64,2048]{1,0:T(8,128)(2,1)S(1)}, bf16[64,2048]{1,0:T(8,128)(2,1)S(1)}, u32[]{:S(2)}, u32[]{:S(2)}) collective-permute-start(bf16[64,2048]{1,0:T(8,128)(2,1)S(1)} %copy-done.64), channel_id=1, source_target_pairs={{0,16},{8,24},{16,0},{24,8},{1,17},{9,25},{17,1},{25,9},{2,18},{10... | collective-permute-start | bytes 786440 | tf_op jit(solution)/shard_map/ppermute | solution.py:96
  152.0 20.0 %collective-permute-start.21 = (bf16[512,512]{1,0:T(8,128)(2,1)S(1)}, bf16[512,512]{1,0:T(8,128)(2,1)S(1)}, u32[]{:S(2)}, u32[]{:S(2)}) collective-permute-start(bf16[512,512]{1,0:T(8,128)(2,1)S(1)} %slice.286), channel_id=1, source_target_pairs={{0,8},{8,0},{16,24},{24,16},{1,9},{9,1},{17,25},{25,17},{2,10},{10... | collective-permute-start | bytes 1572872 | tf_op jit(solution)/shard_map/ppermute | solution.py:96
  153.3 16.7 %collective-permute-start.16 = (bf16[64,2048]{1,0:T(8,128)(2,1)S(1)}, bf16[64,2048]{1,0:T(8,128)(2,1)S(1)}, u32[]{:S(2)}, u32[]{:S(2)}) collective-permute-start(bf16[64,2048]{1,0:T(8,128)(2,1)S(1)} %get-tuple-element.452), channel_id=1, source_target_pairs={{0,2},{1,3},{2,0},{3,1},{4,6},{5,7},{6,4},{7,5},{8,10},{9,11},{10,... | collective-permute-start | bytes 786440 | tf_op jit(solution)/shard_map/ppermute | solution.py:96
  154.2 15.8 %collective-permute-start.17 = (bf16[64,2048]{1,0:T(8,128)(2,1)S(1)}, bf16[64,2048]{1,0:T(8,128)(2,1)S(1)}, u32[]{:S(2)}, u32[]{:S(2)}) collective-permute-start(bf16[64,2048]{1,0:T(8,128)(2,1)S(1)} %get-tuple-element.451), channel_id=1, source_target_pairs={{0,4},{1,5},{2,6},{3,7},{4,0},{5,1},{6,2},{7,3},{8,12},{9,13},{10,... | collective-permute-start | bytes 786440 | tf_op jit(solution)/shard_map/ppermute | solution.py:96
  155.4 14.6 %collective-permute-start.18 = (bf16[64,2048]{1,0:T(8,128)(2,1)S(1)}, bf16[64,2048]{1,0:T(8,128)(2,1)S(1)}, u32[]{:S(2)}, u32[]{:S(2)}) collective-permute-start(bf16[64,2048]{1,0:T(8,128)(2,1)S(1)} %get-tuple-element.450), channel_id=1, source_target_pairs={{0,2},{1,3},{2,0},{3,1},{4,6},{5,7},{6,4},{7,5},{8,10},{9,11},{10,... | collective-permute-start | bytes 786440 | tf_op jit(solution)/shard_map/ppermute | solution.py:96
  169.9 15.2 %collective-permute-start.24 = (bf16[512,512]{1,0:T(8,128)(2,1)}, bf16[512,512]{1,0:T(8,128)(2,1)}, u32[]{:S(2)}, u32[]{:S(2)}) collective-permute-start(bf16[512,512]{1,0:T(8,128)(2,1)} %slice.287), channel_id=1, source_target_pairs={{0,8},{8,0},{16,24},{24,16},{1,9},{9,1},{17,25},{25,17},{2,10},{10... | collective-permute-start | bytes 1572872 | tf_op jit(solution)/shard_map/ppermute | solution.py:96
  172.9 12.2 %collective-permute-start.22 = (bf16[64,2048]{1,0:T(8,128)(2,1)}, bf16[64,2048]{1,0:T(8,128)(2,1)S(1)}, u32[]{:S(2)}, u32[]{:S(2)}) collective-permute-start(bf16[64,2048]{1,0:T(8,128)(2,1)} %add_convert_fusion.18), channel_id=1, source_target_pairs={{0,2},{1,3},{2,0},{3,1},{4,6},{5,7},{6,4},{7,5},{8,10},{9,11},{10,... | collective-permute-start | bytes 786440 | tf_op jit(solution)/shard_map/ppermute | solution.py:96
  174.3 11.5 %collective-permute-start.23 = (bf16[64,2048]{1,0:T(8,128)(2,1)}, bf16[64,2048]{1,0:T(8,128)(2,1)}, u32[]{:S(2)}, u32[]{:S(2)}) collective-permute-start(bf16[64,2048]{1,0:T(8,128)(2,1)} %add_convert_fusion.17), channel_id=1, source_target_pairs={{0,4},{1,5},{2,6},{3,7},{4,0},{5,1},{6,2},{7,3},{8,12},{9,13},{10,... | collective-permute-start | bytes 786440 | tf_op jit(solution)/shard_map/ppermute | solution.py:96
  176.9 30.7 %collective-permute-start.28 = (bf16[512,512]{1,0:T(8,128)(2,1)}, bf16[512,512]{1,0:T(8,128)(2,1)}, u32[]{:S(2)}, u32[]{:S(2)}) collective-permute-start(bf16[512,512]{1,0:T(8,128)(2,1)} %slice.290), channel_id=1, source_target_pairs={{0,8},{8,0},{16,24},{24,16},{1,9},{9,1},{17,25},{25,17},{2,10},{10... | collective-permute-start | bytes 1572872 | tf_op jit(solution)/shard_map/ppermute | solution.py:96
  177.7 39.6 %collective-permute-start.29 = (bf16[512,512]{1,0:T(8,128)(2,1)}, bf16[512,512]{1,0:T(8,128)(2,1)S(1)}, u32[]{:S(2)}, u32[]{:S(2)}) collective-permute-start(bf16[512,512]{1,0:T(8,128)(2,1)} %slice.291), channel_id=1, source_target_pairs={{0,8},{8,0},{16,24},{24,16},{1,9},{9,1},{17,25},{25,17},{2,10},{10... | collective-permute-start | bytes 1572872 | tf_op jit(solution)/shard_map/ppermute | solution.py:96
  180.6 319.3 %reduce-scatter.2.cloned.1.call-start = ((), (), s32[]{:S(2)}) async-start(), calls=%async_computation.7 | async-start | bytes 9437184 | tf_op jit(solution)/shard_map/reduce_scatter | solution.py:793
  188.6 28.7 %collective-permute-start.25 = (bf16[128,2048]{1,0:T(8,128)(2,1)S(1)}, bf16[128,2048]{1,0:T(8,128)(2,1)S(1)}, u32[]{:S(2)}, u32[]{:S(2)}) collective-permute-start(bf16[128,2048]{1,0:T(8,128)(2,1)S(1)} %get-tuple-element.428), channel_id=1, source_target_pairs={{0,2},{1,3},{2,0},{3,1},{4,6},{5,7},{6,4},{7,5},{8,10},{9,11},{10,... | collective-permute-start | bytes 1572872 | tf_op jit(solution)/shard_map/ppermute | solution.py:96
  189.1 28.2 %collective-permute-start.26 = (bf16[128,2048]{1,0:T(8,128)(2,1)S(1)}, bf16[128,2048]{1,0:T(8,128)(2,1)S(1)}, u32[]{:S(2)}, u32[]{:S(2)}) collective-permute-start(bf16[128,2048]{1,0:T(8,128)(2,1)S(1)} %get-tuple-element.428), channel_id=1, source_target_pairs={{0,4},{1,5},{2,6},{3,7},{4,0},{5,1},{6,2},{7,3},{8,12},{9,13},{10,... | collective-permute-start | bytes 1572872 | tf_op jit(solution)/shard_map/ppermute | solution.py:96
  189.6 27.7 %collective-permute-start.27 = (bf16[128,2048]{1,0:T(8,128)(2,1)S(1)}, bf16[128,2048]{1,0:T(8,128)(2,1)}, u32[]{:S(2)}, u32[]{:S(2)}) collective-permute-start(bf16[128,2048]{1,0:T(8,128)(2,1)S(1)} %get-tuple-element.428), channel_id=1, source_target_pairs={{0,16},{8,24},{16,0},{24,8},{1,17},{9,25},{17,1},{25,9},{2,18},{10... | collective-permute-start | bytes 1572872 | tf_op jit(solution)/shard_map/ppermute | solution.py:96
  226.5 16.4 %collective-permute-start.34 = (bf16[512,2048]{1,0:T(8,128)(2,1)}, bf16[512,2048]{1,0:T(8,128)(2,1)}, u32[]{:S(2)}, u32[]{:S(2)}) collective-permute-start(bf16[512,2048]{1,0:T(8,128)(2,1)} %constant_dynamic-update-slice_fusion.5.refs_0_), channel_id=1, source_target_pairs={{0,1},{1,0},{2,3},{3,2},{4,5},{5,4},{6,7},{7,6},{8,9},{9,8},{10,11... | collective-permute-start | bytes 6291464 | tf_op jit(solution)/shard_map/ppermute | solution.py:96
  228.1 14.7 %collective-permute-start.35 = (bf16[128,2048]{1,0:T(8,128)(2,1)}, bf16[128,2048]{1,0:T(8,128)(2,1)}, u32[]{:S(2)}, u32[]{:S(2)}) collective-permute-start(bf16[128,2048]{1,0:T(8,128)(2,1)} %get-tuple-element.277), channel_id=1, source_target_pairs={{0,8},{8,0},{16,24},{24,16},{1,9},{9,1},{17,25},{25,17},{2,10},{10... | collective-permute-start | bytes 1572872 | tf_op jit(solution)/shard_map/ppermute | solution.py:96
  231.2 33.6 %collective-permute-start.30 = (bf16[128,2048]{1,0:T(8,128)(2,1)}, bf16[128,2048]{1,0:T(8,128)(2,1)S(1)}, u32[]{:S(2)}, u32[]{:S(2)}) collective-permute-start(bf16[128,2048]{1,0:T(8,128)(2,1)} %collective-permute-done.27), channel_id=1, source_target_pairs={{0,2},{1,3},{2,0},{3,1},{4,6},{5,7},{6,4},{7,5},{8,10},{9,11},{10,... | collective-permute-start | bytes 1572872 | tf_op jit(solution)/shard_map/ppermute | solution.py:96
  232.5 32.3 %collective-permute-start.31 = (bf16[128,2048]{1,0:T(8,128)(2,1)}, bf16[128,2048]{1,0:T(8,128)(2,1)S(1)}, u32[]{:S(2)}, u32[]{:S(2)}) collective-permute-start(bf16[128,2048]{1,0:T(8,128)(2,1)} %collective-permute-done.27), channel_id=1, source_target_pairs={{0,4},{1,5},{2,6},{3,7},{4,0},{5,1},{6,2},{7,3},{8,12},{9,13},{10,... | collective-permute-start | bytes 1572872 | tf_op jit(solution)/shard_map/ppermute | solution.py:96
  279.3 23.9 %collective-permute-start.40 = (bf16[64,2048]{1,0:T(8,128)(2,1)S(1)}, bf16[64,2048]{1,0:T(8,128)(2,1)S(1)}, u32[]{:S(2)}, u32[]{:S(2)}) collective-permute-start(bf16[64,2048]{1,0:T(8,128)(2,1)S(1)} %get-tuple-element.446), channel_id=1, source_target_pairs={{0,2},{1,3},{2,0},{3,1},{4,6},{5,7},{6,4},{7,5},{8,10},{9,11},{10,... | collective-permute-start | bytes 786440 | tf_op jit(solution)/shard_map/ppermute | solution.py:96
  279.9 23.3 %collective-permute-start.41 = (bf16[64,2048]{1,0:T(8,128)(2,1)S(1)}, bf16[64,2048]{1,0:T(8,128)(2,1)S(1)}, u32[]{:S(2)}, u32[]{:S(2)}) collective-permute-start(bf16[64,2048]{1,0:T(8,128)(2,1)S(1)} %get-tuple-element.445), channel_id=1, source_target_pairs={{0,4},{1,5},{2,6},{3,7},{4,0},{5,1},{6,2},{7,3},{8,12},{9,13},{10,... | collective-permute-start | bytes 786440 | tf_op jit(solution)/shard_map/ppermute | solution.py:96
  281.3 21.9 %collective-permute-start.42 = (bf16[64,2048]{1,0:T(8,128)(2,1)S(1)}, bf16[64,2048]{1,0:T(8,128)(2,1)S(1)}, u32[]{:S(2)}, u32[]{:S(2)}) collective-permute-start(bf16[64,2048]{1,0:T(8,128)(2,1)S(1)} %get-tuple-element.444), channel_id=1, source_target_pairs={{0,2},{1,3},{2,0},{3,1},{4,6},{5,7},{6,4},{7,5},{8,10},{9,11},{10,... | collective-permute-start | bytes 786440 | tf_op jit(solution)/shard_map/ppermute | solution.py:96
  282.8 20.5 %collective-permute-start.43 = (bf16[64,2048]{1,0:T(8,128)(2,1)S(1)}, bf16[64,2048]{1,0:T(8,128)(2,1)S(1)}, u32[]{:S(2)}, u32[]{:S(2)}) collective-permute-start(bf16[64,2048]{1,0:T(8,128)(2,1)S(1)} %get-tuple-element.443), channel_id=1, source_target_pairs={{0,4},{1,5},{2,6},{3,7},{4,0},{5,1},{6,2},{7,3},{8,12},{9,13},{10,... | collective-permute-start | bytes 786440 | tf_op jit(solution)/shard_map/ppermute | solution.py:96
  316.3 9.3 %collective-permute-start.47 = (bf16[64,2048]{1,0:T(8,128)(2,1)S(1)}, bf16[64,2048]{1,0:T(8,128)(2,1)S(1)}, u32[]{:S(2)}, u32[]{:S(2)}) collective-permute-start(bf16[64,2048]{1,0:T(8,128)(2,1)S(1)} %get-tuple-element.440), channel_id=1, source_target_pairs={{0,2},{1,3},{2,0},{3,1},{4,6},{5,7},{6,4},{7,5},{8,10},{9,11},{10,... | collective-permute-start | bytes 786440 | tf_op jit(solution)/shard_map/ppermute | solution.py:96
  319.3 10.4 %collective-permute-start.49 = (bf16[64,2048]{1,0:T(8,128)(2,1)S(1)}, bf16[64,2048]{1,0:T(8,128)(2,1)S(1)}, u32[]{:S(2)}, u32[]{:S(2)}) collective-permute-start(bf16[64,2048]{1,0:T(8,128)(2,1)S(1)} %get-tuple-element.438), channel_id=1, source_target_pairs={{0,2},{1,3},{2,0},{3,1},{4,6},{5,7},{6,4},{7,5},{8,10},{9,11},{10,... | collective-permute-start | bytes 786440 | tf_op jit(solution)/shard_map/ppermute | solution.py:96
  319.8 10.9 %collective-permute-start.50 = (bf16[64,2048]{1,0:T(8,128)(2,1)S(1)}, bf16[64,2048]{1,0:T(8,128)(2,1)S(1)}, u32[]{:S(2)}, u32[]{:S(2)}) collective-permute-start(bf16[64,2048]{1,0:T(8,128)(2,1)S(1)} %get-tuple-element.437), channel_id=1, source_target_pairs={{0,4},{1,5},{2,6},{3,7},{4,0},{5,1},{6,2},{7,3},{8,12},{9,13},{10,... | collective-permute-start | bytes 786440 | tf_op jit(solution)/shard_map/ppermute | solution.py:96
  330.8 9.6 %collective-permute-start.51 = (bf16[64,2048]{1,0:T(8,128)(2,1)S(1)}, bf16[64,2048]{1,0:T(8,128)(2,1)S(1)}, u32[]{:S(2)}, u32[]{:S(2)}) collective-permute-start(bf16[64,2048]{1,0:T(8,128)(2,1)S(1)} %add_convert_fusion.14), channel_id=1, source_target_pairs={{0,2},{1,3},{2,0},{3,1},{4,6},{5,7},{6,4},{7,5},{8,10},{9,11},{10,... | collective-permute-start | bytes 786440 | tf_op jit(solution)/shard_map/ppermute | solution.py:96
  333.1 50.8 %collective-permute-start.58 = (bf16[2048,256]{1,0:T(8,128)(2,1)}, bf16[2048,256]{1,0:T(8,128)(2,1)}, u32[]{:S(2)}, u32[]{:S(2)}) collective-permute-start(bf16[2048,256]{1,0:T(8,128)(2,1)} %convolution_convert_fusion.9), channel_id=1, source_target_pairs={{0,8},{8,0},{16,24},{24,16},{1,9},{9,1},{17,25},{25,17},{2,10},{10... | collective-permute-start | bytes 3145736 | tf_op jit(solution)/shard_map/ppermute | solution.py:96
  341.5 23.8 %collective-permute-start.53 = (bf16[128,2048]{1,0:T(8,128)(2,1)}, bf16[128,2048]{1,0:T(8,128)(2,1)}, u32[]{:S(2)}, u32[]{:S(2)}) collective-permute-start(bf16[128,2048]{1,0:T(8,128)(2,1)} %pad_maximum_fusion.11), channel_id=1, source_target_pairs={{0,16},{8,24},{16,0},{24,8},{1,17},{9,25},{17,1},{25,9},{2,18},{10... | collective-permute-start | bytes 1572872 | tf_op jit(solution)/shard_map/ppermute | solution.py:96
  369.3 12.7 %collective-permute-start.54 = (bf16[128,2048]{1,0:T(8,128)(2,1)S(1)}, bf16[128,2048]{1,0:T(8,128)(2,1)S(1)}, u32[]{:S(2)}, u32[]{:S(2)}) collective-permute-start(bf16[128,2048]{1,0:T(8,128)(2,1)S(1)} %get-tuple-element.364), channel_id=1, source_target_pairs={{0,2},{1,3},{2,0},{3,1},{4,6},{5,7},{6,4},{7,5},{8,10},{9,11},{10,... | collective-permute-start | bytes 1572872 | tf_op jit(solution)/shard_map/ppermute | solution.py:96
  370.7 11.3 %collective-permute-start.55 = (bf16[128,2048]{1,0:T(8,128)(2,1)S(1)}, bf16[128,2048]{1,0:T(8,128)(2,1)S(1)}, u32[]{:S(2)}, u32[]{:S(2)}) collective-permute-start(bf16[128,2048]{1,0:T(8,128)(2,1)S(1)} %get-tuple-element.364), channel_id=1, source_target_pairs={{0,4},{1,5},{2,6},{3,7},{4,0},{5,1},{6,2},{7,3},{8,12},{9,13},{10,... | collective-permute-start | bytes 1572872 | tf_op jit(solution)/shard_map/ppermute | solution.py:96
  371.2 23.2 %collective-permute-start.59 = (bf16[2048,256]{1,0:T(8,128)(2,1)S(1)}, bf16[2048,256]{1,0:T(8,128)(2,1)}, u32[]{:S(2)}, u32[]{:S(2)}) collective-permute-start(bf16[2048,256]{1,0:T(8,128)(2,1)S(1)} %copy-done.71), channel_id=1, source_target_pairs={{0,8},{8,0},{16,24},{24,16},{1,9},{9,1},{17,25},{25,17},{2,10},{10... | collective-permute-start | bytes 3145736 | tf_op jit(solution)/shard_map/ppermute | solution.py:96
  406.2 26.6 %collective-permute-start.62 = (bf16[2,64,2048]{2,1,0:T(8,128)(2,1)}, bf16[2,64,2048]{2,1,0:T(8,128)(2,1)S(1)}, u32[]{:S(2)}, u32[]{:S(2)}) collective-permute-start(bf16[2,64,2048]{2,1,0:T(8,128)(2,1)} %dynamic-slice_bitcast_fusion.1), channel_id=1, source_target_pairs={{0,8},{8,0},{16,24},{24,16},{1,9},{9,1},{17,25},{25,17},{2,10},{10... | collective-permute-start | bytes 1572872 | tf_op jit(solution)/shard_map/ppermute | solution.py:96
  409.6 69.5 %all-to-all-start.2 = ((bf16[32,64,512]{2,1,0:T(8,128)(2,1)}), bf16[32,64,512]{2,1,0:T(8,128)(2,1)}, u32[]{:S(2)}, u32[]{:S(2)}) async-start(bf16[32,64,512]{2,1,0:T(8,128)(2,1)} %pad_maximum_fusion.1), calls=%async_computation.2 | async-start | bytes 4194304 | tf_op jit(solution)/shard_map/all_to_all | solution.py:671
  439.2 37.1 %collective-permute-start.63 = (bf16[2,512,384]{2,1,0:T(8,128)(2,1)S(1)}, bf16[2,512,384]{2,1,0:T(8,128)(2,1)S(1)}, u32[]{:S(2)}, u32[]{:S(2)}) collective-permute-start(bf16[2,512,384]{2,1,0:T(8,128)(2,1)S(1)} %dynamic-slice_bitcast_fusion), channel_id=1, source_target_pairs={{0,8},{8,0},{16,24},{24,16},{1,9},{9,1},{17,25},{25,17},{2,10},{10... | collective-permute-start | bytes 2359304 | tf_op jit(solution)/shard_map/ppermute | solution.py:96
  442.2 34.3 %collective-permute-start.65 = (bf16[256,2048]{1,0:T(8,128)(2,1)S(1)}, bf16[256,2048]{1,0:T(8,128)(2,1)S(1)}, u32[]{:S(2)}, u32[]{:S(2)}) collective-permute-start(bf16[256,2048]{1,0:T(8,128)(2,1)S(1)} %get-tuple-element.436), channel_id=1, source_target_pairs={{0,1},{1,0},{2,3},{3,2},{4,5},{5,4},{6,7},{7,6},{8,9},{9,8},{10,11... | collective-permute-start | bytes 3145736 | tf_op jit(solution)/shard_map/ppermute | solution.py:96
  442.3 34.2 %collective-permute-start.64 = (bf16[256,2048]{1,0:T(8,128)(2,1)S(1)}, bf16[256,2048]{1,0:T(8,128)(2,1)S(1)}, u32[]{:S(2)}, u32[]{:S(2)}) collective-permute-start(bf16[256,2048]{1,0:T(8,128)(2,1)S(1)} %get-tuple-element.435), channel_id=1, source_target_pairs={{0,1},{1,0},{2,3},{3,2},{4,5},{5,4},{6,7},{7,6},{8,9},{9,8},{10,11... | collective-permute-start | bytes 3145736 | tf_op jit(solution)/shard_map/ppermute | solution.py:96
  442.8 32.7 %collective-permute-start.66 = (bf16[1,64,2048]{2,1,0:T(8,128)(2,1)S(1)}, bf16[1,64,2048]{2,1,0:T(8,128)(2,1)S(1)}, u32[]{:S(2)}, u32[]{:S(2)}) collective-permute-start(bf16[1,64,2048]{2,1,0:T(8,128)(2,1)S(1)} %constant_dynamic-slice_fusion.1), channel_id=1, source_target_pairs={{0,16},{8,24},{16,0},{24,8},{1,17},{9,25},{17,1},{25,9},{2,18},{10... | collective-permute-start | bytes 786440 | tf_op jit(solution)/shard_map/ppermute | solution.py:96
  479.2 19.8 %collective-permute-start.71 = (bf16[1,512,384]{2,1,0:T(8,128)(2,1)S(1)}, bf16[1,512,384]{2,1,0:T(8,128)(2,1)S(1)}, u32[]{:S(2)}, u32[]{:S(2)}) collective-permute-start(bf16[1,512,384]{2,1,0:T(8,128)(2,1)S(1)} %constant_dynamic-slice_fusion), channel_id=1, source_target_pairs={{0,16},{8,24},{16,0},{24,8},{1,17},{9,25},{17,1},{25,9},{2,18},{10... | collective-permute-start | bytes 1179656 | tf_op jit(solution)/shard_map/ppermute | solution.py:96
  485.0 16.8 %collective-permute-start.67 = (bf16[64,2048]{1,0:T(8,128)(2,1)}, bf16[64,2048]{1,0:T(8,128)(2,1)S(1)}, u32[]{:S(2)}, u32[]{:S(2)}) collective-permute-start(bf16[64,2048]{1,0:T(8,128)(2,1)} %get-tuple-element.432), channel_id=1, source_target_pairs={{0,2},{1,3},{2,0},{3,1},{4,6},{5,7},{6,4},{7,5},{8,10},{9,11},{10,... | collective-permute-start | bytes 786440 | tf_op jit(solution)/shard_map/ppermute | solution.py:96
  485.8 18.0 %collective-permute-start.68 = (bf16[64,2048]{1,0:T(8,128)(2,1)}, bf16[64,2048]{1,0:T(8,128)(2,1)S(1)}, u32[]{:S(2)}, u32[]{:S(2)}) collective-permute-start(bf16[64,2048]{1,0:T(8,128)(2,1)} %get-tuple-element.431), channel_id=1, source_target_pairs={{0,4},{1,5},{2,6},{3,7},{4,0},{5,1},{6,2},{7,3},{8,12},{9,13},{10,... | collective-permute-start | bytes 786440 | tf_op jit(solution)/shard_map/ppermute | solution.py:96
  486.9 16.9 %collective-permute-start.69 = (bf16[64,2048]{1,0:T(8,128)(2,1)}, bf16[64,2048]{1,0:T(8,128)(2,1)}, u32[]{:S(2)}, u32[]{:S(2)}) collective-permute-start(bf16[64,2048]{1,0:T(8,128)(2,1)} %get-tuple-element.430), channel_id=1, source_target_pairs={{0,2},{1,3},{2,0},{3,1},{4,6},{5,7},{6,4},{7,5},{8,10},{9,11},{10,... | collective-permute-start | bytes 786440 | tf_op jit(solution)/shard_map/ppermute | solution.py:96
  488.3 15.5 %collective-permute-start.70 = (bf16[64,2048]{1,0:T(8,128)(2,1)}, bf16[64,2048]{1,0:T(8,128)(2,1)}, u32[]{:S(2)}, u32[]{:S(2)}) collective-permute-start(bf16[64,2048]{1,0:T(8,128)(2,1)} %get-tuple-element.429), channel_id=1, source_target_pairs={{0,4},{1,5},{2,6},{3,7},{4,0},{5,1},{6,2},{7,3},{8,12},{9,13},{10,... | collective-permute-start | bytes 786440 | tf_op jit(solution)/shard_map/ppermute | solution.py:96
  499.1 20.5 %collective-permute-start.76 = (bf16[128,2048]{1,0:T(8,128)(2,1)}, bf16[128,2048]{1,0:T(8,128)(2,1)}, u32[]{:S(2)}, u32[]{:S(2)}) collective-permute-start(bf16[128,2048]{1,0:T(8,128)(2,1)} %get-tuple-element.405), channel_id=1, source_target_pairs={{0,8},{8,0},{16,24},{24,16},{1,9},{9,1},{17,25},{25,17},{2,10},{10... | collective-permute-start | bytes 1572872 | tf_op jit(solution)/shard_map/ppermute | solution.py:96
  501.8 25.3 %collective-permute-start.77 = (bf16[128,2048]{1,0:T(8,128)(2,1)}, bf16[128,2048]{1,0:T(8,128)(2,1)}, u32[]{:S(2)}, u32[]{:S(2)}) collective-permute-start(bf16[128,2048]{1,0:T(8,128)(2,1)} %get-tuple-element.406), channel_id=1, source_target_pairs={{0,8},{8,0},{16,24},{24,16},{1,9},{9,1},{17,25},{25,17},{2,10},{10... | collective-permute-start | bytes 1572872 | tf_op jit(solution)/shard_map/ppermute | solution.py:96
  505.6 21.4 %collective-permute-start.74 = (bf16[64,2048]{1,0:T(8,128)(2,1)}, bf16[64,2048]{1,0:T(8,128)(2,1)S(1)}, u32[]{:S(2)}, u32[]{:S(2)}) collective-permute-start(bf16[64,2048]{1,0:T(8,128)(2,1)} %add_convert_fusion.9), channel_id=1, source_target_pairs={{0,2},{1,3},{2,0},{3,1},{4,6},{5,7},{6,4},{7,5},{8,10},{9,11},{10,... | collective-permute-start | bytes 786440 | tf_op jit(solution)/shard_map/ppermute | solution.py:96
  508.1 18.9 %collective-permute-start.75 = (bf16[64,2048]{1,0:T(8,128)(2,1)}, bf16[64,2048]{1,0:T(8,128)(2,1)}, u32[]{:S(2)}, u32[]{:S(2)}) collective-permute-start(bf16[64,2048]{1,0:T(8,128)(2,1)} %add_convert_fusion.8), channel_id=1, source_target_pairs={{0,4},{1,5},{2,6},{3,7},{4,0},{5,1},{6,2},{7,3},{8,12},{9,13},{10,... | collective-permute-start | bytes 786440 | tf_op jit(solution)/shard_map/ppermute | solution.py:96
  509.6 42.3 %all-to-all-start.3 = ((bf16[8,64,384]{2,1,0:T(8,128)(2,1)}), bf16[8,64,384]{2,1,0:T(8,128)(2,1)S(1)}, u32[]{:S(2)}, u32[]{:S(2)}) async-start(bf16[8,64,384]{2,1,0:T(8,128)(2,1)} %bitcast.37), calls=%async_computation.4 | async-start | bytes 786432 | tf_op jit(solution)/shard_map/all_to_all | solution.py:195
  514.4 37.5 %collective-permute-start.72 = (bf16[128,2048]{1,0:T(8,128)(2,1)}, bf16[128,2048]{1,0:T(8,128)(2,1)}, u32[]{:S(2)}, u32[]{:S(2)}) collective-permute-start(bf16[128,2048]{1,0:T(8,128)(2,1)} %slice.354), channel_id=1, source_target_pairs={{0,16},{8,24},{16,0},{24,8},{1,17},{9,25},{17,1},{25,9},{2,18},{10... | collective-permute-start | bytes 1572872 | tf_op jit(solution)/shard_map/ppermute | solution.py:96
  519.5 32.4 %collective-permute-start.73 = (bf16[64,2048]{1,0:T(8,128)(2,1)}, bf16[64,2048]{1,0:T(8,128)(2,1)}, u32[]{:S(2)}, u32[]{:S(2)}) collective-permute-start(bf16[64,2048]{1,0:T(8,128)(2,1)} %fusion.31), channel_id=1, source_target_pairs={{0,0},{8,1},{16,2},{24,3},{1,4},{9,5},{17,6},{25,7},{2,8},{10,9},{... | collective-permute-start | bytes 786440 | tf_op jit(solution)/shard_map/ppermute | solution.py:842
  (103 other events, 870.6 us)
Sparse Core Ops, SparseCore 0:
  97.4 46.8 all-gather.2
  180.7 39.8 all-gather.4
  394.6 88.0 reduce-scatter.1
